TPU v7x, 256 devices: a whole 4x4x8 slice. The times are simulated.
256 devices in a mesh: dp: 4 (over x), gy: 8 (over y, core), gx: 8 (over z).
Axes of the slice: x: 4, y: 4, z: 8, core: 2. Of those that a mesh axis runs over, the one named last changes fastest.
Arguments:
- tiles: bfloat16 [4, 128, 256, 768], P('dp', 'gy', 'gx'), may hold values from -6 to 6
- cotangent: bfloat16 [4, 128, 256, 768], P('dp', 'gy', 'gx'), may hold values from -6 to 6
- tissue: int32 [4, 128, 256], P('dp', 'gy', 'gx'), may hold values from 0 to 1, as said below
- w_qkv: bfloat16 [768, 2304], replicated, may hold values from -0.21875 to 0.21875
- w_proj: bfloat16 [768, 768], replicated, may hold values from -0.21875 to 0.21875
Outputs:
- out_tiles: bfloat16 [4, 128, 256, 768], P('dp', 'gy', 'gx')
- grad_tiles: bfloat16 [4, 128, 256, 768], P('dp', 'gy', 'gx')
- grad_qkv: float32 [768, 2304], P(('dp', 'gy', 'gx'))
- grad_proj: float32 [768, 768], P(('dp', 'gy', 'gx'))
Inputs may be any that keep to these rules, and one draw needn't show every extreme that they name: Within each slide, grid row of 16 tiles and block of 32 tile columns, every window either holds no tissue tile or holds one at its centre cell. Two blocks of the same slide and grid row whose column block indices differ by half their number hold together at most 2 windows with tissue; in every draw some such pair holds exactly 2, all in one block.
All inputs are finite; a program needn't handle non-finite values.
Results may differ from a plain program's by a relative error of at most 0.0095.
Values may be sent and summed in bfloat16 or wider, within the bound.
No kernel may reach another device: no remote copies, remote signals or barrier semaphores. Data moves between devices by JAX's collectives and lax.ppermute only.
A program may use at most 128 MiB of HBM per device.

v0:
```python
import math

import jax
import jax.numpy as jnp
from jax import lax
from jax.sharding import PartitionSpec as P

HEADS = 12
WIN = 16


def from_behind(value, axis, by):
    devices = lax.axis_size(axis)
    return lax.ppermute(value, axis, [(i, (i + by) % devices) for i in range(devices)])


def window_pass(tiles_win, cot_win, tissue_win, w_qkv, w_proj, heads):
    slots, cells, width = tiles_win.shape
    head_size = width // heads
    scale = 1.0 / math.sqrt(head_size)
    xf = tiles_win.astype(jnp.float32)
    mean = jnp.mean(xf, -1, keepdims=True)
    centred = xf - mean
    inv = lax.rsqrt(jnp.mean(centred * centred, -1, keepdims=True) + 1e-05)
    normed = centred * inv
    hidden = normed.astype(jnp.bfloat16).reshape(slots * cells, width)
    qkv = jnp.dot(hidden, w_qkv, preferred_element_type=jnp.float32).astype(jnp.bfloat16)
    qkv = qkv.reshape(slots, cells, 3, heads, head_size)
    query = qkv[:, :, 0]
    keys = qkv[:, :, 1]
    values = qkv[:, :, 2]
    empty = (jnp.sum(tissue_win, -1, keepdims=True) == 0).astype(jnp.float32)
    live = jnp.maximum(tissue_win, empty)
    scores = jnp.einsum("sqhe,skhe->shqk", query, keys, preferred_element_type=jnp.float32) * scale
    weights = jnp.exp(scores) * live[:, None, None, :]
    probs = weights / jnp.sum(weights, -1, keepdims=True)
    probs_b = probs.astype(jnp.bfloat16)
    attended = jnp.einsum("shqk,skhe->sqhe", probs_b, values, preferred_element_type=jnp.float32)
    attended = attended.astype(jnp.bfloat16).reshape(slots * cells, width)
    branch = jnp.dot(attended, w_proj, preferred_element_type=jnp.float32).reshape(
        slots, cells, width
    )
    qmask = tissue_win[..., None]
    out = (xf + qmask * branch).astype(jnp.bfloat16)
    cot_f = cot_win.astype(jnp.float32)
    dbranch = (cot_f * qmask).astype(jnp.bfloat16).reshape(slots * cells, width)
    grad_proj = jnp.einsum("td,te->de", attended, dbranch, preferred_element_type=jnp.float32)
    dattended = jnp.einsum("te,de->td", dbranch, w_proj, preferred_element_type=jnp.float32)
    dattended = dattended.astype(jnp.bfloat16).reshape(slots, cells, heads, head_size)
    dprobs = jnp.einsum("sqhe,skhe->shqk", dattended, values, preferred_element_type=jnp.float32)
    dvalues = jnp.einsum("shqk,sqhe->skhe", probs_b, dattended, preferred_element_type=jnp.float32)
    dscores = (probs * (dprobs - jnp.sum(probs * dprobs, -1, keepdims=True))).astype(jnp.bfloat16)
    dquery = (
        jnp.einsum("shqk,skhe->sqhe", dscores, keys, preferred_element_type=jnp.float32) * scale
    )
    dkeys = (
        jnp.einsum("shqk,sqhe->skhe", dscores, query, preferred_element_type=jnp.float32) * scale
    )
    dqkv = jnp.stack([dquery, dkeys, dvalues], axis=2).astype(jnp.bfloat16)
    dqkv = dqkv.reshape(slots * cells, 3 * width)
    grad_qkv = jnp.einsum("td,te->de", hidden, dqkv, preferred_element_type=jnp.float32)
    dhidden = jnp.einsum("te,de->td", dqkv, w_qkv, preferred_element_type=jnp.float32)
    dhidden = dhidden.reshape(slots, cells, width)
    dnorm = inv * (
        dhidden
        - jnp.mean(dhidden, -1, keepdims=True)
        - normed * jnp.mean(dhidden * normed, -1, keepdims=True)
    )
    grad_in = (cot_f + dnorm).astype(jnp.bfloat16)
    return (out, grad_in, grad_qkv, grad_proj)


def to_windows(block, count):
    feats = block.shape[3]
    block = block.reshape(WIN, count, WIN, feats)
    return block.transpose(1, 0, 2, 3).reshape(count, WIN * WIN, feats)


def from_windows(field, count):
    feats = field.shape[2]
    field = field.reshape(count, WIN, WIN, feats).transpose(1, 0, 2, 3)
    return field.reshape(1, WIN, count * WIN, feats)


def shards(tiles, cotangent, tissue, w_qkv, w_proj):
    half_win = WIN // 2
    below = from_behind(tiles[:, :half_win], "gy", -1)
    rows_done = jnp.concatenate([tiles[:, half_win:], below], axis=1)
    beside = from_behind(rows_done[:, :, :half_win], "gx", -1)
    shifted = jnp.concatenate([rows_done[:, :, half_win:], beside], axis=2)
    count = shifted.shape[2] // WIN
    tiles_win = to_windows(shifted, count)
    cot_win = to_windows(cotangent, count)
    tissue_win = to_windows(tissue.astype(jnp.float32)[..., None], count)[..., 0]
    out_win, grad_win, grad_qkv, grad_proj = window_pass(
        tiles_win, cot_win, tissue_win, w_qkv, w_proj, HEADS
    )
    sum_qkv, sum_proj = (
        lax.psum_scatter(grad_qkv, ("dp", "gy", "gx"), scatter_dimension=0, tiled=True),
        lax.psum_scatter(grad_proj, ("dp", "gy", "gx"), scatter_dimension=0, tiled=True),
    )
    windows_all = lax.axis_size("dp") * lax.axis_size("gy") * lax.axis_size("gx") * count
    scale = 1.0 / math.sqrt(windows_all)
    return (
        from_windows(out_win, count),
        from_windows(grad_win, count),
        sum_qkv * scale,
        sum_proj * scale,
    )


def solution(mesh):
    in_specs = (P("dp", "gy", "gx", None), P("dp", "gy", "gx", None), P("dp", "gy", "gx"), P(), P())
    out_specs = (
        P("dp", "gy", "gx", None),
        P("dp", "gy", "gx", None),
        P(("dp", "gy", "gx"), None),
        P(("dp", "gy", "gx"), None),
    )
    return jax.shard_map(shards, mesh=mesh, in_specs=in_specs, out_specs=out_specs, check_vma=False)
```

profile of v0, /device:TPU:6, one launch (start us, length us, event | category | flops | bytes accessed | tf_op | source)
XLA Modules:
  0.0 378.0 jit_solution(13255381878479183681)
XLA Ops:
  7.2 2.2 fusion.31
  9.4 2.5 collective-permute-start
  16.5 2.5 copy.55
  19.7 2.2 fusion.10
  23.2 2.5 fusion.4
  26.8 3.2 convolution_convert_fusion.1
  30.1 1.6 pad_maximum_fusion.1
  31.7 5.9 %collective-permute-start.1 = (bf16[1,16,8,768]{3,2,1,0:T(8,128)(2,1)}, bf16[1,16,8,768]{3,2,1,0:T(8,128)(2,1)}, u32[]{:S(2)}, u32[]{:S(2)}) collective-permute-start(bf16[1,16,8,768]{3,2,1,0:T(8,128)(2,1)} %pad_maximum_fusion.1), channel_id=1, source_target_pairs={{0,7},{1,0},{2,1},{3,2},{4,3},{5,4},{6,5},{7,6},{8,15},{9,8},{10,9... | collective-permute-start | bytes 589832 | tf_op jit(solution)/shard_map/ppermute | solution.py:14
  38.2 2.3 copy.56
  40.5 2.9 reshape.171
  45.5 1.4 copy.46
  48.8 1.3 add_rsqrt_fusion
  50.1 1.4 rsqrt.17
  51.5 1.6 fusion.7
  53.1 3.4 convolution_convert_fusion
  56.6 4.3 %copy.48 = bf16[512,2304]{0,1:T(8,128)(2,1)} copy(bf16[512,2304]{1,0:T(8,128)(2,1)} %convolution_convert_fusion) | data formatting | bytes 4718592 | tf_op jit(solution)/shard_map/convert_element_type | solution.py:27
  60.9 6.1 %reshape.168 = bf16[2,256,3,12,64]{1,0,4,3,2:T(2,128)(2,1)} reshape(bf16[512,2304]{0,1:T(8,128)(2,1)} %copy.48) | data formatting | bytes 4718592 | tf_op jit(solution)/shard_map/reshape | solution.py:28
  66.9 2.9 fusion.30
  69.8 1.8 fusion.1
  71.7 1.4 fusion.18
  73.1 1.5 fusion.15
  74.6 2.2 multiply_reduce_fusion
  76.8 2.1 multiply_convert_fusion
  81.7 2.5 copy.65
  85.7 5.0 %fusion.32 = f32[768,2304]{1,0:T(8,128)} fusion(bf16[512,768]{1,0:T(8,128)(2,1)S(1)} %bitcast.142, bf16[512,2304]{0,1:T(8,128)(2,1)S(1)} %bitcast.140), kind=kOutput, calls=%fused_computation.63 | convolution fusion | flops 1811939328 | bytes 10223616 | tf_op jit(solution)/shard_map/td,te->de/dot_general | solution.py:61
  90.7 2.2 fusion.33
  92.9 1.4 rsqrt.18
  95.0 2.1 copy.62
  99.5 2.4 fusion.29
  103.3 264.9 %all-reduce.5.cloned.1.call-done = (f32[768,2304]{1,0:T(8,128)}, f32[768,768]{1,0:T(8,128)}) async-done(((f32[768,2304]{1,0:T(8,128)}, f32[768,768]{1,0:T(8,128)}), (f32[768,2304]{1,0:T(8,128)}, f32[768,768]{1,0:T(8,128)})) %all-reduce.5.cloned.1.call-update) | async-done | bytes 9437200
  368.2 1.5 dynamic-slice_multiply_fusion
  369.7 1.4 dynamic-slice_multiply_fusion.1
  (73 shorter events, 21.0 us)
Async XLA Ops:
  7.2 46.0 %copy-start = (bf16[768,2304]{1,0:T(8,128)(2,1)S(1)}, bf16[768,2304]{1,0:T(8,128)(2,1)}, u32[]{:S(2)}) copy-start(bf16[768,2304]{1,0:T(8,128)(2,1)} %param.8) | copy-start | bytes 10616836
  7.2 361.0 %all-reduce.5.cloned.1.call-start = ((), (), s32[]{:S(2)}) async-start(), calls=%async_computation | async-start | bytes 18874368
  9.4 20.6 %collective-permute-start = (bf16[1,8,32,768]{3,2,1,0:T(8,128)(2,1)}, bf16[1,8,32,768]{3,2,1,0:T(8,128)(2,1)}, u32[]{:S(2)}, u32[]{:S(2)}) collective-permute-start(bf16[1,8,32,768]{3,2,1,0:T(8,128)(2,1)} %get-tuple-element.12), channel_id=1, source_target_pairs={{0,56},{8,0},{16,8},{24,16},{32,24},{40,32},{48,40},{56,48},{1,57}... | collective-permute-start | bytes 1179656 | tf_op jit(solution)/shard_map/ppermute | solution.py:14
  23.2 2.5 copy-start.18
  26.8 3.3 copy-start.6
  26.8 10.7 %copy-start.15 = (f32[2,256]{1,0:T(2,128)S(1)}, f32[2,256]{1,0:T(2,128)}, u32[]{:S(2)}) copy-start(f32[2,256]{1,0:T(2,128)} %mul.111) | copy-start | bytes 6148
  26.8 10.7 %copy-start.17 = (f32[2]{0:T(128)S(1)}, f32[2]{0:T(128)}, u32[]{:S(2)}) copy-start(f32[2]{0:T(128)} %compare_convert_fusion) | copy-start | bytes 28
  31.7 12.8 %collective-permute-start.1 = (bf16[1,16,8,768]{3,2,1,0:T(8,128)(2,1)}, bf16[1,16,8,768]{3,2,1,0:T(8,128)(2,1)}, u32[]{:S(2)}, u32[]{:S(2)}) collective-permute-start(bf16[1,16,8,768]{3,2,1,0:T(8,128)(2,1)} %pad_maximum_fusion.1), channel_id=1, source_target_pairs={{0,7},{1,0},{2,1},{3,2},{4,3},{5,4},{6,5},{7,6},{8,15},{9,8},{10,9... | collective-permute-start | bytes 589832 | tf_op jit(solution)/shard_map/ppermute | solution.py:14
  45.5 1.6 copy-start.2
  66.9 2.9 copy-start.12
  71.6 1.4 copy-start.10
  73.1 11.6 %copy-start.8 = (bf16[2,12,64,256]{3,2,1,0:T(8,128)(2,1)}, bf16[2,12,64,256]{3,2,1,0:T(8,128)(2,1)S(1)}, u32[]{:S(2)}) copy-start(bf16[2,12,64,256]{3,2,1,0:T(8,128)(2,1)S(1)} %fusion.18) | copy-start | bytes 2359300
  80.1 1.1 copy-start.3
  80.1 1.1 copy-start.11
  81.7 2.5 copy-start.1
  85.7 5.0 %copy-start.7 = (bf16[2,16,16,768]{3,2,1,0:T(8,128)(2,1)S(1)}, bf16[2,16,16,768]{3,2,1,0:T(8,128)(2,1)}, u32[]{:S(2)}) copy-start(bf16[2,16,16,768]{3,2,1,0:T(8,128)(2,1)} %fusion.10) | copy-start | bytes 2359300
  95.0 2.1 copy-start.4
  95.0 2.3 copy-start.9
  95.0 2.3 copy-start.16
  95.0 2.7 copy-start.19
  97.7 1.8 copy-start.13
  97.7 1.8 copy-start.14
  99.5 2.4 copy-start.5
Sparse Core Ops, SparseCore 0:
  93.0 275.0 all-reduce.4
where the time goes:
time: 379 us; the launch traced here: 378 us
  waiting for transfers between devices  265 us (70%)
  local copies, waits for them, and re-layouts  41.8 us (11%)
  matrix products  25.6 us (7%)
  other arithmetic  22.9 us (6%)
  between operations  14.3 us (4%)
  starting transfers between devices  8.35 us (2%)
    unnamed x2, waiting for transfers between devices  265 us
    ppermute x2, starting transfers between devices, from_behind(): lax.ppermute(value, axis, [(i, (i + by) % devices) for i in range(devices)])  8.31 us
  transfers between devices with their start and end apart: 3, of which 1 were waited for; matrix products, arithmetic and copies ran while one was open for 9% of the time, Pallas kernels for 0%

commit v1 on v0

v1 whole, which is shorter than its diff:
```python
import math

import jax
import jax.numpy as jnp
from jax import lax
from jax.experimental import pallas as pl
from jax.experimental.pallas import tpu as pltpu
from jax.sharding import PartitionSpec as P

F32 = jnp.float32
BF = jnp.bfloat16
D = 768
WIN = 16
CELLS = WIN * WIN
GROUPS = 3
GW = D // GROUPS
HEAD_SCALE = 0.125
VMEM = 56 * 1024 * 1024


def nn(a, b):
    return lax.dot_general(a, b, (((1,), (0,)), ((), ())), preferred_element_type=F32)


def nt(a, b):
    return lax.dot_general(a, b, (((1,), (1,)), ((), ())), preferred_element_type=F32)


def tn(a, b):
    return lax.dot_general(a, b, (((0,), (0,)), ((), ())), preferred_element_type=F32)


def full(shape):
    return pl.BlockSpec(shape, lambda *g: (0,) * len(shape))


def cost(flops, size):
    return pl.CostEstimate(flops=int(flops), bytes_accessed=int(size), transcendentals=0)


def branch_kernel(cot_ref, tis_ref, wp_ref, db_ref, da_ref):
    for w in range(2):
        db = cot_ref[:, w].reshape(CELLS, D) * jnp.tile(tis_ref[w], (1, D // 128))
        db_ref[w] = db
        da_ref[w] = nt(db, wp_ref[...]).astype(BF)


def branch(cot, tis, w_proj):
    shape = jax.ShapeDtypeStruct((2, CELLS, D), BF)
    return pl.pallas_call(
        branch_kernel,
        out_shape=[shape, shape],
        compiler_params=pltpu.CompilerParams(vmem_limit_bytes=VMEM),
        cost_estimate=cost(6e8, 4e6),
        name="branch",
    )(cot, tis, w_proj)


def moments(x):
    mean = jnp.mean(x, -1, keepdims=True)
    centred = x - mean
    inv = lax.rsqrt(jnp.mean(centred * centred, -1, keepdims=True) + 1e-05)
    return centred * inv, inv


def head_pair(q2, k2, v2, da2, ones2):
    lane = lax.broadcasted_iota(jnp.int32, (1, 128), 1)
    sel_a = (lane < 64).astype(BF)
    sel_b = (lane >= 64).astype(BF)
    ka, kb, va, vb = k2 * sel_a, k2 * sel_b, v2 * sel_a, v2 * sel_b
    wa = jnp.exp(nt(q2, ka)).astype(BF)
    wb = jnp.exp(nt(q2, kb)).astype(BF)
    both = nn(wa, jnp.concatenate([va, ones2 * sel_a], 1)) + nn(
        wb, jnp.concatenate([vb, ones2 * sel_b], 1)
    )
    rinv = 1.0 / both[:, 128:]
    attended = both[:, :128] * rinv
    lhs = jnp.concatenate([da2, (da2.astype(F32) * attended).astype(BF)], 1)
    minus_a = jnp.broadcast_to(-sel_a, (CELLS, 128))
    minus_b = jnp.broadcast_to(-sel_b, (CELLS, 128))
    dsa = (wa.astype(F32) * nt(lhs, jnp.concatenate([va, minus_a], 1))).astype(BF)
    dsb = (wb.astype(F32) * nt(lhs, jnp.concatenate([vb, minus_b], 1))).astype(BF)
    dq = (nn(dsa, ka) + nn(dsb, kb)) * (rinv * HEAD_SCALE)
    dan = (da2.astype(F32) * rinv).astype(BF)
    qn = (q2.astype(F32) * rinv).astype(BF)
    dv = tn(wa, dan * sel_a) + tn(wb, dan * sel_b)
    dk = tn(dsa, qn * sel_a) + tn(dsb, qn * sel_b)
    return attended.astype(BF), dq.astype(BF), dk.astype(BF), dv.astype(BF)


def main_kernel(
    tiles_ref, below_ref, right_ref, diag_ref, src_ref, tis_ref, live_ref,
    wq_ref, wk_ref, wv_ref, da_ref, db_ref,
    keep_ref, send_ref, att_ref, dqkv_ref, xw_ref,
    hid_ref, hid_t_ref, alls_ref,
):
    step = pl.program_id(0)

    def order():
        column = lax.broadcasted_iota(jnp.int32, (D, D), 1)
        return jnp.where(column == src_ref[...], 1.0, 0.0).astype(BF)

    def put(grad):
        keep_ref[...] = grad[: D // 2].astype(BF)
        send_ref[...] = grad[D // 2 :].astype(BF)

    @pl.when(step == 0)
    def _():
        own = tiles_ref[8:16].astype(F32)
        low = below_ref[...].astype(F32)
        right = right_ref[...].astype(F32)
        diag = diag_ref[...].astype(F32)
        perm = order()
        for w in range(2):
            if w == 0:
                top, bottom = own[:, 8:24], low[:, 8:24]
            else:
                top = jnp.concatenate([own[:, 24:32], right], 1)
                bottom = jnp.concatenate([low[:, 24:32], diag], 1)
            x = jnp.concatenate([top, bottom], 0).reshape(CELLS, D)
            xw_ref[w] = x.astype(BF)
            normed, _ = moments(x)
            hidden = normed.astype(BF)
            hid_ref[w] = hidden
            hid_t_ref[:, w * CELLS : (w + 1) * CELLS] = nt(perm, hidden).astype(BF)

    @pl.when(step < GROUPS)
    def _():
        for w in range(2):
            hidden = hid_ref[w]
            query = (nn(hidden, wq_ref[...])).astype(BF) * BF(HEAD_SCALE)
            tis2 = tis_ref[w]
            tis4 = jnp.concatenate([tis2, tis2], 1)
            key = nn(hidden, wk_ref[...]).astype(BF) * tis4
            value = nn(hidden, wv_ref[...]).astype(BF) * tis4
            for p in range(2):
                s = slice(p * 128, (p + 1) * 128)
                att, dq, dk, dv = head_pair(
                    query[:, s], key[:, s], value[:, s], da_ref[w, :, s], live_ref[w]
                )
                att_ref[w, :, s] = att
                dqkv_ref[0, w, :, s] = dq
                dqkv_ref[0, w, :, slice(GW + p * 128, GW + (p + 1) * 128)] = dk * tis2
                dqkv_ref[0, w, :, slice(2 * GW + p * 128, 2 * GW + (p + 1) * 128)] = dv * tis2
        alls_ref[step] = att_ref[...].reshape(2 * CELLS, GW)
        put(nn(hid_t_ref[...], dqkv_ref[0].reshape(2 * CELLS, D)))

    @pl.when(step == GROUPS)
    def _():
        attended = jnp.concatenate([alls_ref[g] for g in range(GROUPS)], 1)
        att_t = nt(order(), attended).astype(BF)
        put(nn(att_t, db_ref[...].reshape(2 * CELLS, D)))


def main(tiles, below, right, diag, src, tis, live, w_qkv, da, db):
    def columns(block):
        return pl.BlockSpec((D, GW), lambda g: (0, block * GROUPS + jnp.minimum(g, GROUPS - 1)))

    part = pl.BlockSpec((2, CELLS, GW), lambda g: (0, 0, jnp.minimum(g, GROUPS - 1)))
    half = pl.BlockSpec((D // 2, D), lambda g: (0, g))
    wide = (GROUPS + 1) * D
    return pl.pallas_call(
        main_kernel,
        grid=(GROUPS + 1,),
        in_specs=[
            full((16, 32, D)), full((8, 32, D)), full((8, 8, D)), full((8, 8, D)),
            full((D, 1)), full((2, CELLS, 128)), full((2, CELLS, 128)),
            columns(0), columns(1), columns(2), part, full((2, CELLS, D)),
        ],
        out_specs=[
            half, half, part,
            pl.BlockSpec((1, 2, CELLS, D), lambda g: (jnp.minimum(g, GROUPS - 1), 0, 0, 0)),
            full((2, CELLS, D)),
        ],
        out_shape=[
            jax.ShapeDtypeStruct((D // 2, wide), BF),
            jax.ShapeDtypeStruct((D // 2, wide), BF),
            jax.ShapeDtypeStruct((2, CELLS, D), BF),
            jax.ShapeDtypeStruct((GROUPS, 2, CELLS, D), BF),
            jax.ShapeDtypeStruct((2, CELLS, D), BF),
        ],
        scratch_shapes=[
            pltpu.VMEM((2, CELLS, D), BF),
            pltpu.VMEM((D, 2 * CELLS), BF),
            pltpu.VMEM((GROUPS, 2 * CELLS, GW), BF),
        ],
        compiler_params=pltpu.CompilerParams(vmem_limit_bytes=VMEM),
        cost_estimate=cost(6e9, 16e6),
        name="heads",
    )(tiles, below, right, diag, src, tis, live, w_qkv, w_qkv, w_qkv, da, db)


def outs_kernel(
    xw_ref, cot_ref, tis_ref, att_ref, dqkv_ref, wq_ref, wk_ref, wv_ref, wp_ref,
    out_ref, grad_ref, acc_ref,
):
    step = pl.program_id(0)
    weights = jnp.concatenate([wq_ref[...], wk_ref[...], wv_ref[...]], 1)
    for w in range(2):
        part = nt(dqkv_ref[0, w], weights)

        @pl.when(step == 0)
        def _():
            acc_ref[w] = part

        @pl.when(step > 0)
        def _():
            acc_ref[w] += part

    @pl.when(step == GROUPS - 1)
    def _():
        for w in range(2):
            x = xw_ref[w].astype(F32)
            tis = jnp.tile(tis_ref[w].astype(F32), (1, D // 128))
            out = x + tis * nn(att_ref[w], wp_ref[...])
            out_ref[:, w] = out.astype(BF).reshape(WIN, WIN, D)
            normed, inv = moments(x)
            dh = acc_ref[w]
            dnorm = inv * (
                dh
                - jnp.mean(dh, -1, keepdims=True)
                - normed * jnp.mean(dh * normed, -1, keepdims=True)
            )
            grad = cot_ref[:, w].reshape(CELLS, D).astype(F32) + dnorm
            grad_ref[:, w] = grad.astype(BF).reshape(WIN, WIN, D)


def outs(xw, cot, tis, att, dqkv, w_qkv, w_proj):
    def columns(block):
        return pl.BlockSpec((D, GW), lambda g: (0, block * GROUPS + g))

    shape = jax.ShapeDtypeStruct((WIN, 2, WIN, D), BF)
    out, grad = pl.pallas_call(
        outs_kernel,
        grid=(GROUPS,),
        in_specs=[
            full((2, CELLS, D)), full((WIN, 2, WIN, D)), full((2, CELLS, 128)), full((2, CELLS, D)),
            pl.BlockSpec((1, 2, CELLS, D), lambda g: (g, 0, 0, 0)),
            columns(0), columns(1), columns(2), full((D, D)),
        ],
        out_specs=[full((WIN, 2, WIN, D))] * 2,
        out_shape=[shape, shape],
        scratch_shapes=[pltpu.VMEM((2, CELLS, D), F32)],
        compiler_params=pltpu.CompilerParams(vmem_limit_bytes=VMEM),
        cost_estimate=cost(2.4e9, 12e6),
        name="outs",
    )(xw, cot, tis, att, dqkv, w_qkv, w_qkv, w_qkv, w_proj)
    return out.reshape(1, WIN, 2 * WIN, D), grad.reshape(1, WIN, 2 * WIN, D)


def send(value, axis, move):
    devices = lax.axis_size(axis)
    return lax.ppermute(value, axis, [(i, move(i) % devices) for i in range(devices)])


def add(*terms):
    total = terms[0].astype(F32)
    for term in terms[1:]:
        total = total + term.astype(F32)
    return total.astype(BF)


def ring_of_four(blocks, axis, step):
    _, _, width = blocks.shape
    n = width // 2
    from_low = send(blocks[2, :, :n], axis, lambda j: j + step)
    from_high = send(blocks[2, :, n:], axis, lambda j: j - step)
    up = jnp.concatenate([add(blocks[1, :, :n], from_low), blocks[1, :, n:]], 1)
    down = jnp.concatenate([blocks[3, :, :n], add(blocks[3, :, n:], from_high)], 1)
    got_up = send(up, axis, lambda j: j + step)
    got_down = send(down, axis, lambda j: j - step)
    return add(blocks[0], got_up, got_down)


def row_order():
    dp = lax.axis_index("dp")
    gy = lax.axis_index("gy")
    y, core = gy // 2, gy % 2
    at = jnp.arange(D, dtype=jnp.int32)
    rest = at % 24
    y_of = (at // 24 % 4 + y) % 4
    dp_of = (at // 96 % 4 + dp) % 4
    core_of = (at // 384 + core) % 2
    return (((dp_of * 8 + y_of * 2 + core_of) * 24 + rest)[:, None]).astype(jnp.int32)


def shards(tiles, cotangent, tissue, w_qkv, w_proj):
    mine = tiles[0]
    below = send(mine[:8], "gy", lambda i: i - 1)
    right = send(mine[8:, :8], "gx", lambda i: i - 1)
    ny, nx = lax.axis_size("gy"), lax.axis_size("gx")
    diag = lax.ppermute(
        mine[:8, :8],
        ("gy", "gx"),
        [
            (a * nx + b, (a - 1) % ny * nx + (b - 1) % nx)
            for a in range(ny)
            for b in range(nx)
        ],
    )
    cells = tissue.reshape(WIN, 2, WIN).transpose(1, 0, 2).reshape(2, CELLS, 1)
    empty = jnp.max(cells, 1, keepdims=True) == 0
    tis = jnp.broadcast_to(cells.astype(BF), (2, CELLS, 128))
    live = jnp.broadcast_to(jnp.where(empty, 1, cells).astype(BF), (2, CELLS, 128))
    cot = cotangent.reshape(WIN, 2, WIN, D)
    db, da = branch(cot, tis, w_proj)
    keep, give, att, dqkv, xw = main(
        mine, below, right, diag, row_order(), tis, live, w_qkv, da, db
    )
    rows = add(keep, send(give, "gy", lambda i: i ^ 1))
    rows = ring_of_four(rows.reshape(4, 96, -1), "dp", 1)
    rows = ring_of_four(rows.reshape(4, 24, -1), "gy", 2)
    parts = lax.all_to_all(rows.reshape(8, 3, -1), "gx", 0, 0)
    total = jnp.sum(parts.astype(F32), 0) * (1.0 / math.sqrt(512))
    grad_qkv = total[:, : 3 * D].reshape(3, GROUPS, 3, GW).transpose(0, 2, 1, 3)
    out, grad = outs(xw, cot, tis, att, dqkv, w_qkv, w_proj)
    return out, grad, grad_qkv.reshape(3, 3 * D), total[:, 3 * D :]


def solution(mesh):
    block = P("dp", "gy", "gx", None)
    in_specs = (block, block, P("dp", "gy", "gx"), P(), P())
    out_specs = (block, block, P(("dp", "gy", "gx"), None), P(("dp", "gy", "gx"), None))
    return jax.shard_map(
        shards, mesh=mesh, in_specs=in_specs, out_specs=out_specs, check_vma=False
    )
```

time: 379 us -> 109 us (0.29)
  the two profiles are of different devices: /device:TPU:6 before, /device:TPU:32 now
where the time goes in v1:
time: 109 us; the launch traced here: 108 us
  waiting for transfers between devices  35.6 us (33%)
  Pallas kernels  33.2 us (30%)
  starting transfers between devices  26.2 us (24%)
  local copies, waits for them, and re-layouts  6.73 us (6%)
  other arithmetic  5.92 us (5%)
    ppermute x11, waiting for transfers between devices, send(): lax.ppermute(value, axis, [(i, move(i) % devices) for i in range(devices)])  35.6 us
    pallas_call x1, Pallas kernels, main(): pl.pallas_call(main_kernel, grid=(GROUPS + 1,), in_specs=[full((16, 32, D...  20.5 us
    ppermute x11, starting transfers between devices, send(): lax.ppermute(value, axis, [(i, move(i) % devices) for i in range(devices)])  19.8 us
    pallas_call x1, Pallas kernels, outs(): pl.pallas_call(outs_kernel, grid=(GROUPS,), in_specs=[full((2, CELLS, D))...  9.41 us
    all_to_all x1, starting transfers between devices, shards(): parts = lax.all_to_all(rows.reshape(8, 3, -1), 'gx', 0, 0)  4.3 us
    pallas_call x1, Pallas kernels, branch(): pl.pallas_call(branch_kernel, out_shape=[shape, shape], compiler_params=p...  3.28 us
    convert_element_type x5, other arithmetic, add(): return total.astype(BF)  3 us
  transfers between devices with their start and end apart: 13, of which 7 were waited for; matrix products, arithmetic and copies ran while one was open for 5% of the time, Pallas kernels for 12%

profile of v1, /device:TPU:32, one launch (start us, length us, event | category | flops | bytes accessed | tf_op | source)
XLA Modules:
  0.0 108.5 jit_solution(15014396055365846622)
XLA Ops:
  0.6 1.0 fusion.27
  1.6 2.1 %collective-permute-start.2 = (bf16[8,8,768]{2,1,0:T(8,128)(2,1)S(1)}, bf16[8,8,768]{2,1,0:T(8,128)(2,1)S(1)}, u32[]{:S(2)}, u32[]{:S(2)}) collective-permute-start(bf16[8,8,768]{2,1,0:T(8,128)(2,1)S(1)} %get-tuple-element.28), channel_id=1, source_target_pairs={{0,63},{1,56},{2,57},{3,58},{4,59},{5,60},{6,61},{7,62},{8,7},{9,0... | collective-permute-start | bytes 294920 | tf_op jit(solution)/shard_map/ppermute | solution.py:292
  3.7 5.9 %collective-permute-start.1 = (bf16[8,8,768]{2,1,0:T(8,128)(2,1)S(1)}, bf16[8,8,768]{2,1,0:T(8,128)(2,1)S(1)}, u32[]{:S(2)}, u32[]{:S(2)}) collective-permute-start(bf16[8,8,768]{2,1,0:T(8,128)(2,1)S(1)} %get-tuple-element.29), channel_id=1, source_target_pairs={{0,7},{1,0},{2,1},{3,2},{4,3},{5,4},{6,5},{7,6},{8,15},{9,8},{10,9... | collective-permute-start | bytes 294920 | tf_op jit(solution)/shard_map/ppermute | solution.py:253
  9.5 1.0 slice_bitcast_fusion
  10.5 0.6 collective-permute-start
  11.1 0.8 reshape.377
  11.9 0.7 reduce_max.10
  12.9 1.8 %fusion.14.src_ref = s32[768,1]{1,0:T(8,128)} fusion(s32[]{:T(128)S(6)} %select_n.128, s32[]{:T(128)S(6)} %select_n.125, s32[]{:T(128)S(6)} %axis_index.25), kind=kLoop, calls=%fused_computation.46 | loop fusion | flops 67584 | bytes 3084 | tf_op jit(solution)/shard_map/add | solution.py:284
  14.8 0.8 broadcast_in_dim.24.tis_ref
  15.6 3.3 %branch.1 = (bf16[2,256,768]{2,1,0:T(8,128)(2,1)}, bf16[2,256,768]{2,1,0:T(8,128)(2,1)}) custom-call(bf16[16,2,16,768]{3,2,1,0:T(8,128)(2,1)} %bitcast.50, bf16[2,256,128]{2,1,0:T(8,128)(2,1)} %broadcast_in_dim.24.tis_ref, bf16[768,768]{1,0:T(8,128)(2,1)} %wp_ref.3), custom_call_target="tpu_custom_call" | custom-call | flops 600000000 | bytes 4000000 | tf_op jit(solution)/shard_map/branch/pallas_call | solution.py:50
  18.9 0.8 broadcast_in_dim.27.live_ref
  19.7 20.5 %heads.1 = (bf16[384,3072]{1,0:T(8,128)(2,1)}, bf16[384,3072]{1,0:T(8,128)(2,1)}, bf16[2,256,768]{2,1,0:T(8,128)(2,1)}, bf16[3,2,256,768]{3,2,1,0:T(8,128)(2,1)}, bf16[2,256,768]{2,1,0:T(8,128)(2,1)}) custom-call(bf16[16,32,768]{2,1,0:T(8,128)(2,1)} %bitcast.53, bf16[8,32,768]{2,1,0:T(8,128)(2,1)} %copy-done, bf16[8,8,768]{2,1,0:T(8,128)(2,1)} %copy-done.2, ...), custom_call_target="tpu_custom_call" | custom-call | flops 6000000000 | bytes 16000000 | tf_op jit(solution)/shard_map/heads/pallas_call | solution.py:162
  40.3 4.7 %collective-permute-done.3 = bf16[384,3072]{1,0:T(8,128)(2,1)S(1)} collective-permute-done((bf16[384,3072]{1,0:T(8,128)(2,1)}, bf16[384,3072]{1,0:T(8,128)(2,1)S(1)}, u32[]{:S(2)}, u32[]{:S(2)}) %collective-permute-start.3) | collective-permute-done | bytes 2359328 | tf_op jit(solution)/shard_map/ppermute | solution.py:253
  45.1 2.5 %add_convert_fusion = bf16[384,3072]{1,0:T(8,128)(2,1)S(1)} fusion(bf16[384,3072]{1,0:T(8,128)(2,1)S(1)} %collective-permute-done.3, bf16[384,3072]{1,0:T(8,128)(2,1)} %get-tuple-element.20), kind=kLoop, calls=%fused_computation | loop fusion | flops 4718592 | bytes 7077888 | tf_op jit(solution)/shard_map/convert_element_type | solution.py:260
  47.7 1.7 %collective-permute-start.4 = (bf16[96,1536]{1,0:T(8,128)(2,1)S(1)}, bf16[96,1536]{1,0:T(8,128)(2,1)S(1)}, u32[]{:S(2)}, u32[]{:S(2)}) collective-permute-start(bf16[96,1536]{1,0:T(8,128)(2,1)S(1)} %get-tuple-element.24), channel_id=1, source_target_pairs={{0,64},{64,128},{128,192},{192,0},{1,65},{65,129},{129,193},{193,1... | collective-permute-start | bytes 884744 | tf_op jit(solution)/shard_map/ppermute | solution.py:253
  49.5 1.7 %collective-permute-start.6 = (bf16[96,1536]{1,0:T(8,128)(2,1)S(1)}, bf16[96,1536]{1,0:T(8,128)(2,1)S(1)}, u32[]{:S(2)}, u32[]{:S(2)}) collective-permute-start(bf16[96,1536]{1,0:T(8,128)(2,1)S(1)} %get-tuple-element.25), channel_id=1, source_target_pairs={{0,192},{64,0},{128,64},{192,128},{1,193},{65,1},{129,65},{193,129... | collective-permute-start | bytes 884744 | tf_op jit(solution)/shard_map/ppermute | solution.py:253
  51.2 7.0 %collective-permute-done.4 = bf16[96,1536]{1,0:T(8,128)(2,1)S(1)} collective-permute-done((bf16[96,1536]{1,0:T(8,128)(2,1)S(1)}, bf16[96,1536]{1,0:T(8,128)(2,1)S(1)}, u32[]{:S(2)}, u32[]{:S(2)}) %collective-permute-start.4) | collective-permute-done | bytes 294944 | tf_op jit(solution)/shard_map/ppermute | solution.py:253
  58.3 0.1 fusion.3
  58.5 3.0 %collective-permute-start.7 = (bf16[96,3072]{1,0:T(8,128)(2,1)S(1)}, bf16[96,3072]{1,0:T(8,128)(2,1)S(1)}, u32[]{:S(2)}, u32[]{:S(2)}) collective-permute-start(bf16[96,3072]{1,0:T(8,128)(2,1)S(1)} %pad_maximum_fusion.1), channel_id=1, source_target_pairs={{0,192},{64,0},{128,64},{192,128},{1,193},{65,1},{129,65},{193,129... | collective-permute-start | bytes 1769480 | tf_op jit(solution)/shard_map/ppermute | solution.py:253
  61.6 11.6 %collective-permute-done.7 = bf16[96,3072]{1,0:T(8,128)(2,1)S(1)} collective-permute-done((bf16[96,3072]{1,0:T(8,128)(2,1)S(1)}, bf16[96,3072]{1,0:T(8,128)(2,1)S(1)}, u32[]{:S(2)}, u32[]{:S(2)}) %collective-permute-start.7) | collective-permute-done | bytes 589856 | tf_op jit(solution)/shard_map/ppermute | solution.py:253
  73.2 3.5 %collective-permute-done.5 = bf16[96,3072]{1,0:T(8,128)(2,1)S(1)} collective-permute-done((bf16[96,3072]{1,0:T(8,128)(2,1)S(1)}, bf16[96,3072]{1,0:T(8,128)(2,1)S(1)}, u32[]{:S(2)}, u32[]{:S(2)}) %collective-permute-start.5) | collective-permute-done | bytes 589856 | tf_op jit(solution)/shard_map/ppermute | solution.py:253
  76.8 0.2 add_convert_fusion.1
  77.1 3.2 %collective-permute-start.10 = (bf16[24,1536]{1,0:T(8,128)(2,1)S(1)}, bf16[24,1536]{1,0:T(8,128)(2,1)S(1)}, u32[]{:S(2)}, u32[]{:S(2)}) collective-permute-start(bf16[24,1536]{1,0:T(8,128)(2,1)S(1)} %get-tuple-element.33), channel_id=1, source_target_pairs={{0,48},{8,56},{16,0},{24,8},{32,16},{40,24},{48,32},{56,40},{1,49}... | collective-permute-start | bytes 221192 | tf_op jit(solution)/shard_map/ppermute | solution.py:253
  80.3 2.3 %collective-permute-done.8 = bf16[24,1536]{1,0:T(8,128)(2,1)S(1)} collective-permute-done((bf16[24,1536]{1,0:T(8,128)(2,1)S(1)}, bf16[24,1536]{1,0:T(8,128)(2,1)S(1)}, u32[]{:S(2)}, u32[]{:S(2)}) %collective-permute-start.8) | collective-permute-done | bytes 73760 | tf_op jit(solution)/shard_map/ppermute | solution.py:253
  82.7 3.3 %collective-permute-start.11 = (bf16[24,3072]{1,0:T(8,128)(2,1)S(1)}, bf16[24,3072]{1,0:T(8,128)(2,1)S(1)}, u32[]{:S(2)}, u32[]{:S(2)}) collective-permute-start(bf16[24,3072]{1,0:T(8,128)(2,1)S(1)} %pad_maximum_fusion.3), channel_id=1, source_target_pairs={{0,48},{8,56},{16,0},{24,8},{32,16},{40,24},{48,32},{56,40},{1,49}... | collective-permute-start | bytes 442376 | tf_op jit(solution)/shard_map/ppermute | solution.py:253
  86.1 2.6 %collective-permute-done.11 = bf16[24,3072]{1,0:T(8,128)(2,1)S(1)} collective-permute-done((bf16[24,3072]{1,0:T(8,128)(2,1)S(1)}, bf16[24,3072]{1,0:T(8,128)(2,1)S(1)}, u32[]{:S(2)}, u32[]{:S(2)}) %collective-permute-start.11) | collective-permute-done | bytes 147488 | tf_op jit(solution)/shard_map/ppermute | solution.py:253
  88.7 3.8 %collective-permute-done.9 = bf16[24,3072]{1,0:T(8,128)(2,1)S(1)} collective-permute-done((bf16[24,3072]{1,0:T(8,128)(2,1)S(1)}, bf16[24,3072]{1,0:T(8,128)(2,1)S(1)}, u32[]{:S(2)}, u32[]{:S(2)}) %collective-permute-start.9) | collective-permute-done | bytes 147488 | tf_op jit(solution)/shard_map/ppermute | solution.py:253
  92.5 0.8 reshape.384
  93.3 4.3 %all-to-all-start = ((bf16[8,3,3072]{2,1,0:T(4,128)(2,1)}), bf16[8,3,3072]{2,1,0:T(4,128)(2,1)S(1)}, u32[]{:S(2)}, u32[]{:S(2)}) async-start(bf16[8,3,3072]{2,1,0:T(4,128)(2,1)} %reshape.384), calls=%async_computation | async-start | bytes 393216 | tf_op jit(solution)/shard_map/all_to_all | solution.py:313
  97.6 9.4 %outs.1 = (bf16[16,2,16,768]{3,2,1,0:T(8,128)(2,1)}, bf16[16,2,16,768]{3,2,1,0:T(8,128)(2,1)}) custom-call(bf16[2,256,768]{2,1,0:T(8,128)(2,1)} %get-tuple-element.15.xw_ref, bf16[16,2,16,768]{3,2,1,0:T(8,128)(2,1)} %bitcast.51, bf16[2,256,128]{2,1,0:T(8,128)(2,1)} %broadcast_in_dim.24.tis_ref, bf16[2,256,768]{2,1,0:T(8,128)(2,1)} %get-tuple-element.16.att_ref, ...), custom_call_target="tpu_custom_call" | custom-call | flops 2400000000 | bytes 12000000 | tf_op jit(solution)/shard_map/outs/pallas_call | solution.py:233
  107.2 0.6 slice.99
  107.8 0.6 reshape.386
  (35 shorter events, 1.2 us)
Async XLA Ops:
  1.6 17.3 %collective-permute-start.2 = (bf16[8,8,768]{2,1,0:T(8,128)(2,1)S(1)}, bf16[8,8,768]{2,1,0:T(8,128)(2,1)S(1)}, u32[]{:S(2)}, u32[]{:S(2)}) collective-permute-start(bf16[8,8,768]{2,1,0:T(8,128)(2,1)S(1)} %get-tuple-element.28), channel_id=1, source_target_pairs={{0,63},{1,56},{2,57},{3,58},{4,59},{5,60},{6,61},{7,62},{8,7},{9,0... | collective-permute-start | bytes 294920 | tf_op jit(solution)/shard_map/ppermute | solution.py:292
  3.7 15.2 %collective-permute-start.1 = (bf16[8,8,768]{2,1,0:T(8,128)(2,1)S(1)}, bf16[8,8,768]{2,1,0:T(8,128)(2,1)S(1)}, u32[]{:S(2)}, u32[]{:S(2)}) collective-permute-start(bf16[8,8,768]{2,1,0:T(8,128)(2,1)S(1)} %get-tuple-element.29), channel_id=1, source_target_pairs={{0,7},{1,0},{2,1},{3,2},{4,3},{5,4},{6,5},{7,6},{8,15},{9,8},{10,9... | collective-permute-start | bytes 294920 | tf_op jit(solution)/shard_map/ppermute | solution.py:253
  10.5 8.3 %collective-permute-start = (bf16[8,32,768]{2,1,0:T(8,128)(2,1)S(1)}, bf16[8,32,768]{2,1,0:T(8,128)(2,1)S(1)}, u32[]{:S(2)}, u32[]{:S(2)}) collective-permute-start(bf16[8,32,768]{2,1,0:T(8,128)(2,1)S(1)} %slice_bitcast_fusion), channel_id=1, source_target_pairs={{0,56},{8,0},{16,8},{24,16},{32,24},{40,32},{48,40},{56,48},{1,57}... | collective-permute-start | bytes 1179656 | tf_op jit(solution)/shard_map/ppermute | solution.py:253
  18.9 0.9 copy-start.1
  18.9 0.8 copy-start.2
  18.9 0.8 copy-start
  40.2 4.8 %collective-permute-start.3 = (bf16[384,3072]{1,0:T(8,128)(2,1)}, bf16[384,3072]{1,0:T(8,128)(2,1)S(1)}, u32[]{:S(2)}, u32[]{:S(2)}) collective-permute-start(bf16[384,3072]{1,0:T(8,128)(2,1)} %get-tuple-element.21), channel_id=1, source_target_pairs={{0,8},{8,0},{16,24},{24,16},{32,40},{40,32},{48,56},{56,48},{1,9},... | collective-permute-start | bytes 7077896 | tf_op jit(solution)/shard_map/ppermute | solution.py:253
  47.7 10.5 %collective-permute-start.4 = (bf16[96,1536]{1,0:T(8,128)(2,1)S(1)}, bf16[96,1536]{1,0:T(8,128)(2,1)S(1)}, u32[]{:S(2)}, u32[]{:S(2)}) collective-permute-start(bf16[96,1536]{1,0:T(8,128)(2,1)S(1)} %get-tuple-element.24), channel_id=1, source_target_pairs={{0,64},{64,128},{128,192},{192,0},{1,65},{65,129},{129,193},{193,1... | collective-permute-start | bytes 884744 | tf_op jit(solution)/shard_map/ppermute | solution.py:253
  49.5 8.8 %collective-permute-start.6 = (bf16[96,1536]{1,0:T(8,128)(2,1)S(1)}, bf16[96,1536]{1,0:T(8,128)(2,1)S(1)}, u32[]{:S(2)}, u32[]{:S(2)}) collective-permute-start(bf16[96,1536]{1,0:T(8,128)(2,1)S(1)} %get-tuple-element.25), channel_id=1, source_target_pairs={{0,192},{64,0},{128,64},{192,128},{1,193},{65,1},{129,65},{193,129... | collective-permute-start | bytes 884744 | tf_op jit(solution)/shard_map/ppermute | solution.py:253
  58.5 14.8 %collective-permute-start.7 = (bf16[96,3072]{1,0:T(8,128)(2,1)S(1)}, bf16[96,3072]{1,0:T(8,128)(2,1)S(1)}, u32[]{:S(2)}, u32[]{:S(2)}) collective-permute-start(bf16[96,3072]{1,0:T(8,128)(2,1)S(1)} %pad_maximum_fusion.1), channel_id=1, source_target_pairs={{0,192},{64,0},{128,64},{192,128},{1,193},{65,1},{129,65},{193,129... | collective-permute-start | bytes 1769480 | tf_op jit(solution)/shard_map/ppermute | solution.py:253
  61.5 15.2 %collective-permute-start.5 = (bf16[96,3072]{1,0:T(8,128)(2,1)S(1)}, bf16[96,3072]{1,0:T(8,128)(2,1)S(1)}, u32[]{:S(2)}, u32[]{:S(2)}) collective-permute-start(bf16[96,3072]{1,0:T(8,128)(2,1)S(1)} %pad_maximum_fusion), channel_id=1, source_target_pairs={{0,64},{64,128},{128,192},{192,0},{1,65},{65,129},{129,193},{193,1... | collective-permute-start | bytes 1769480 | tf_op jit(solution)/shard_map/ppermute | solution.py:253
  77.0 5.6 %collective-permute-start.8 = (bf16[24,1536]{1,0:T(8,128)(2,1)S(1)}, bf16[24,1536]{1,0:T(8,128)(2,1)S(1)}, u32[]{:S(2)}, u32[]{:S(2)}) collective-permute-start(bf16[24,1536]{1,0:T(8,128)(2,1)S(1)} %get-tuple-element.32), channel_id=1, source_target_pairs={{0,16},{8,24},{16,32},{24,40},{32,48},{40,56},{48,0},{56,8},{1,17}... | collective-permute-start | bytes 221192 | tf_op jit(solution)/shard_map/ppermute | solution.py:253
  77.1 5.6 %collective-permute-start.10 = (bf16[24,1536]{1,0:T(8,128)(2,1)S(1)}, bf16[24,1536]{1,0:T(8,128)(2,1)S(1)}, u32[]{:S(2)}, u32[]{:S(2)}) collective-permute-start(bf16[24,1536]{1,0:T(8,128)(2,1)S(1)} %get-tuple-element.33), channel_id=1, source_target_pairs={{0,48},{8,56},{16,0},{24,8},{32,16},{40,24},{48,32},{56,40},{1,49}... | collective-permute-start | bytes 221192 | tf_op jit(solution)/shard_map/ppermute | solution.py:253
  82.7 6.0 %collective-permute-start.11 = (bf16[24,3072]{1,0:T(8,128)(2,1)S(1)}, bf16[24,3072]{1,0:T(8,128)(2,1)S(1)}, u32[]{:S(2)}, u32[]{:S(2)}) collective-permute-start(bf16[24,3072]{1,0:T(8,128)(2,1)S(1)} %pad_maximum_fusion.3), channel_id=1, source_target_pairs={{0,48},{8,56},{16,0},{24,8},{32,16},{40,24},{48,32},{56,40},{1,49}... | collective-permute-start | bytes 442376 | tf_op jit(solution)/shard_map/ppermute | solution.py:253
  86.0 6.4 %collective-permute-start.9 = (bf16[24,3072]{1,0:T(8,128)(2,1)S(1)}, bf16[24,3072]{1,0:T(8,128)(2,1)S(1)}, u32[]{:S(2)}, u32[]{:S(2)}) collective-permute-start(bf16[24,3072]{1,0:T(8,128)(2,1)S(1)} %pad_maximum_fusion.2), channel_id=1, source_target_pairs={{0,16},{8,24},{16,32},{24,40},{32,48},{40,56},{48,0},{56,8},{1,17}... | collective-permute-start | bytes 442376 | tf_op jit(solution)/shard_map/ppermute | solution.py:253
  93.3 13.7 %all-to-all-start = ((bf16[8,3,3072]{2,1,0:T(4,128)(2,1)}), bf16[8,3,3072]{2,1,0:T(4,128)(2,1)S(1)}, u32[]{:S(2)}, u32[]{:S(2)}) async-start(bf16[8,3,3072]{2,1,0:T(4,128)(2,1)} %reshape.384), calls=%async_computation | async-start | bytes 393216 | tf_op jit(solution)/shard_map/all_to_all | solution.py:313

commit v2 on v1

v2 whole, which is shorter than its diff:
```python
import math

import jax
import jax.numpy as jnp
from jax import lax
from jax.experimental import pallas as pl
from jax.experimental.pallas import tpu as pltpu
from jax.sharding import PartitionSpec as P

F32 = jnp.float32
BF = jnp.bfloat16
D = 768
WIN = 16
CELLS = WIN * WIN
GROUPS = 3
GW = D // GROUPS
HEAD_SCALE = 0.125
VMEM = 56 * 1024 * 1024


def nn(a, b):
    return lax.dot_general(a, b, (((1,), (0,)), ((), ())), preferred_element_type=F32)


def nt(a, b):
    return lax.dot_general(a, b, (((1,), (1,)), ((), ())), preferred_element_type=F32)


def tn(a, b):
    return lax.dot_general(a, b, (((0,), (0,)), ((), ())), preferred_element_type=F32)


def full(shape):
    return pl.BlockSpec(shape, lambda *g: (0,) * len(shape))


def cost(flops, size):
    return pl.CostEstimate(flops=int(flops), bytes_accessed=int(size), transcendentals=0)


def branch_kernel(cot_ref, tissue_ref, wp_ref, db_ref, da_ref, tis_ref, live_ref):
    grid = tissue_ref[...].astype(F32).astype(BF)
    cell = lax.broadcasted_iota(jnp.int32, (CELLS, 1), 0)
    row_of = lax.broadcasted_iota(jnp.int32, (CELLS, WIN), 1) == (cell >> 4)
    rows = nn(row_of.astype(F32).astype(BF), grid)
    lane = lax.broadcasted_iota(jnp.int32, (CELLS, 2 * WIN), 1)
    ones = jnp.ones((2 * WIN, 128), BF)
    for w in range(2):
        own = jnp.where(lane == (cell & 15) + w * WIN, rows, 0.0).astype(BF)
        tis = nn(own, ones)
        some = jnp.max(jnp.max(tis, 0, keepdims=True), 1, keepdims=True)
        tis_ref[w] = tis.astype(BF)
        live_ref[w] = jnp.maximum(tis, 1.0 - some).astype(BF)
        db = cot_ref[:, w].reshape(CELLS, D) * jnp.tile(tis.astype(BF), (1, D // 128))
        db_ref[w] = db
        da_ref[w] = nt(db, wp_ref[...]).astype(BF)


def branch(cot, tissue, w_proj):
    shape = jax.ShapeDtypeStruct((2, CELLS, D), BF)
    mask = jax.ShapeDtypeStruct((2, CELLS, 128), BF)
    return pl.pallas_call(
        branch_kernel,
        out_shape=[shape, shape, mask, mask],
        compiler_params=pltpu.CompilerParams(vmem_limit_bytes=VMEM),
        cost_estimate=cost(6e8, 4e6),
        name="branch",
    )(cot, tissue, w_proj)


def row_order(first):
    gy = lax.axis_index("gy")
    dp, y, core = lax.axis_index("dp"), gy >> 1, gy & 1
    at = lax.broadcasted_iota(jnp.int32, (D, 1), 0)
    block = ((at.astype(F32) + 0.5) * (1.0 / 24)).astype(jnp.int32)
    outer, inner = (block >> 2) & 3, block & 3
    if first == "dp":
        dp_of, y_of = (outer + dp) & 3, (inner + y) & 3
    else:
        dp_of, y_of = (inner + dp) & 3, (outer + y) & 3
    core_of = ((block >> 4) + core) & 1
    source = (dp_of * 8 + y_of * 2 + core_of) * 24 + at - block * 24
    column = lax.broadcasted_iota(jnp.int32, (D, D), 1)
    return jnp.where(column == source, 1.0, 0.0).astype(BF)


def moments(x):
    mean = jnp.mean(x, -1, keepdims=True)
    centred = x - mean
    inv = lax.rsqrt(jnp.mean(centred * centred, -1, keepdims=True) + 1e-05)
    return centred * inv, inv


def head_pair(q2, k2, v2, da2, ones2):
    lane = lax.broadcasted_iota(jnp.int32, (1, 128), 1)
    sel_a = (lane < 64).astype(BF)
    sel_b = (lane >= 64).astype(BF)
    ka, kb, va, vb = k2 * sel_a, k2 * sel_b, v2 * sel_a, v2 * sel_b
    wa = jnp.exp(nt(q2, ka)).astype(BF)
    wb = jnp.exp(nt(q2, kb)).astype(BF)
    both = nn(wa, jnp.concatenate([va, ones2 * sel_a], 1)) + nn(
        wb, jnp.concatenate([vb, ones2 * sel_b], 1)
    )
    rinv = 1.0 / both[:, 128:]
    attended = both[:, :128] * rinv
    lhs = jnp.concatenate([da2, (da2.astype(F32) * attended).astype(BF)], 1)
    minus_a = jnp.broadcast_to(-sel_a, (CELLS, 128))
    minus_b = jnp.broadcast_to(-sel_b, (CELLS, 128))
    dsa = (wa.astype(F32) * nt(lhs, jnp.concatenate([va, minus_a], 1))).astype(BF)
    dsb = (wb.astype(F32) * nt(lhs, jnp.concatenate([vb, minus_b], 1))).astype(BF)
    dq = (nn(dsa, ka) + nn(dsb, kb)) * (rinv * HEAD_SCALE)
    dan = (da2.astype(F32) * rinv).astype(BF)
    qn = (q2.astype(F32) * rinv).astype(BF)
    dv = tn(wa, dan * sel_a) + tn(wb, dan * sel_b)
    dk = tn(dsa, qn * sel_a) + tn(dsb, qn * sel_b)
    return attended.astype(BF), dq.astype(BF), dk.astype(BF), dv.astype(BF)


def put(grad, keep_ref, send_ref):
    keep_ref[...] = grad[: D // 2].astype(BF)
    send_ref[...] = grad[D // 2 :].astype(BF)


def heads_group(
    hid_ref, hid_t_ref, tis_ref, live_ref, wq_ref, wk_ref, wv_ref, da_ref,
    keep_ref, send_ref, att_ref, dqkv_ref,
):
    for w in range(2):
        hidden = hid_ref[w]
        query = nn(hidden, wq_ref[...]).astype(BF) * BF(HEAD_SCALE)
        tis2 = tis_ref[w]
        tis4 = jnp.concatenate([tis2, tis2], 1)
        key = nn(hidden, wk_ref[...]).astype(BF) * tis4
        value = nn(hidden, wv_ref[...]).astype(BF) * tis4
        for p in range(2):
            s = slice(p * 128, (p + 1) * 128)
            att, dq, dk, dv = head_pair(
                query[:, s], key[:, s], value[:, s], da_ref[w, :, s], live_ref[w]
            )
            att_ref[w, :, s] = att
            dqkv_ref[0, w, :, s] = dq
            dqkv_ref[0, w, :, slice(GW + p * 128, GW + (p + 1) * 128)] = dk * tis2
            dqkv_ref[0, w, :, slice(2 * GW + p * 128, 2 * GW + (p + 1) * 128)] = dv * tis2
    put(nn(hid_t_ref[...], dqkv_ref[0].reshape(2 * CELLS, D)), keep_ref, send_ref)


def first_kernel(
    tiles_ref, below_ref, right_ref, diag_ref, tis_ref, live_ref,
    wq_ref, wk_ref, wv_ref, da_ref,
    keep_ref, send_ref, att_ref, dqkv_ref, xw_ref, hid_ref, hid_t_ref,
):
    @pl.when(pl.program_id(0) == 0)
    def _():
        own = tiles_ref[8:16].astype(F32)
        low = below_ref[...].astype(F32)
        right = right_ref[...].astype(F32)
        diag = diag_ref[...].astype(F32)
        perm = row_order("dp")
        for w in range(2):
            if w == 0:
                top, bottom = own[:, 8:24], low[:, 8:24]
            else:
                top = jnp.concatenate([own[:, 24:32], right], 1)
                bottom = jnp.concatenate([low[:, 24:32], diag], 1)
            x = jnp.concatenate([top, bottom], 0).reshape(CELLS, D)
            xw_ref[w] = x.astype(BF)
            normed, _ = moments(x)
            hidden = normed.astype(BF)
            hid_ref[w] = hidden
            hid_t_ref[:, w * CELLS : (w + 1) * CELLS] = nt(perm, hidden).astype(BF)

    heads_group(
        hid_ref, hid_t_ref, tis_ref, live_ref, wq_ref, wk_ref, wv_ref, da_ref,
        keep_ref, send_ref, att_ref, dqkv_ref,
    )


def last_kernel(
    hid_ref, tis_ref, live_ref, wq_ref, wk_ref, wv_ref, da_ref,
    keep_ref, send_ref, att_ref, dqkv_ref, hid_t_ref,
):
    perm = row_order("gy")
    for w in range(2):
        hid_t_ref[:, w * CELLS : (w + 1) * CELLS] = nt(perm, hid_ref[w]).astype(BF)
    heads_group(
        hid_ref, hid_t_ref, tis_ref, live_ref, wq_ref, wk_ref, wv_ref, da_ref,
        keep_ref, send_ref, att_ref, dqkv_ref,
    )


def columns(block, first):
    return pl.BlockSpec((D, GW), lambda g: (0, block * GROUPS + first + g))


def heads_specs(first, groups):
    inputs = [
        full((2, CELLS, 128)), full((2, CELLS, 128)),
        columns(0, first), columns(1, first), columns(2, first),
        pl.BlockSpec((2, CELLS, GW), lambda g: (0, 0, first + g)),
    ]
    half = pl.BlockSpec((D // 2, D), lambda g: (0, g))
    outputs = [
        half, half,
        pl.BlockSpec((2, CELLS, GW), lambda g: (0, 0, g)),
        pl.BlockSpec((1, 2, CELLS, D), lambda g: (g, 0, 0, 0)),
    ]
    shapes = [
        jax.ShapeDtypeStruct((D // 2, groups * D), BF),
        jax.ShapeDtypeStruct((D // 2, groups * D), BF),
        jax.ShapeDtypeStruct((2, CELLS, groups * GW), BF),
        jax.ShapeDtypeStruct((groups, 2, CELLS, D), BF),
    ]
    return inputs, outputs, shapes


def first_heads(tiles, below, right, diag, tis, live, w_qkv, da):
    inputs, outputs, shapes = heads_specs(0, 2)
    rows = jax.ShapeDtypeStruct((2, CELLS, D), BF)
    return pl.pallas_call(
        first_kernel,
        grid=(2,),
        in_specs=[full((16, 32, D)), full((8, 32, D)), full((8, 8, D)), full((8, 8, D))] + inputs,
        out_specs=outputs + [full((2, CELLS, D))] * 2,
        out_shape=shapes + [rows, rows],
        scratch_shapes=[pltpu.VMEM((D, 2 * CELLS), BF)],
        compiler_params=pltpu.CompilerParams(vmem_limit_bytes=VMEM),
        cost_estimate=cost(6e9, 10e6),
        name="first_heads",
    )(tiles, below, right, diag, tis, live, w_qkv, w_qkv, w_qkv, da)


def last_heads(hid, tis, live, w_qkv, da):
    inputs, outputs, shapes = heads_specs(2, 1)
    return pl.pallas_call(
        last_kernel,
        grid=(1,),
        in_specs=[full((2, CELLS, D))] + inputs,
        out_specs=outputs,
        out_shape=shapes,
        scratch_shapes=[pltpu.VMEM((D, 2 * CELLS), BF)],
        compiler_params=pltpu.CompilerParams(vmem_limit_bytes=VMEM),
        cost_estimate=cost(4e9, 6e6),
        name="last_heads",
    )(hid, tis, live, w_qkv, w_qkv, w_qkv, da)


def proj_kernel(att0_ref, att1_ref, db_ref, keep_ref, send_ref):
    attended = jnp.concatenate([att0_ref[...], att1_ref[...]], 2).reshape(2 * CELLS, D)
    att_t = nt(row_order("gy"), attended).astype(BF)
    put(nn(att_t, db_ref[...].reshape(2 * CELLS, D)), keep_ref, send_ref)


def proj_grad(att0, att1, db):
    shape = jax.ShapeDtypeStruct((D // 2, D), BF)
    return pl.pallas_call(
        proj_kernel,
        out_shape=[shape, shape],
        compiler_params=pltpu.CompilerParams(vmem_limit_bytes=VMEM),
        cost_estimate=cost(2e9, 4e6),
        name="proj_grad",
    )(att0, att1, db)


def outs_kernel(
    xw_ref, cot_ref, tis_ref, att0_ref, att1_ref, dqkv0_ref, dqkv1_ref,
    wq_ref, wk_ref, wv_ref, wp_ref, out_ref, grad_ref, acc_ref,
):
    step = pl.program_id(0)
    weights = jnp.concatenate([wq_ref[...], wk_ref[...], wv_ref[...]], 1)
    for w in range(2):
        dqkv = jnp.where(step < GROUPS - 1, dqkv0_ref[0, w], dqkv1_ref[0, w])
        part = nt(dqkv, weights)

        @pl.when(step == 0)
        def _():
            acc_ref[w] = part

        @pl.when(step > 0)
        def _():
            acc_ref[w] += part

    @pl.when(step == GROUPS - 1)
    def _():
        for w in range(2):
            x = xw_ref[w].astype(F32)
            tis = jnp.tile(tis_ref[w].astype(F32), (1, D // 128))
            attended = jnp.concatenate([att0_ref[w], att1_ref[w]], 1)
            out = x + tis * nn(attended, wp_ref[...])
            out_ref[:, w] = out.astype(BF).reshape(WIN, WIN, D)
            normed, inv = moments(x)
            dh = acc_ref[w]
            dnorm = inv * (
                dh
                - jnp.mean(dh, -1, keepdims=True)
                - normed * jnp.mean(dh * normed, -1, keepdims=True)
            )
            grad = cot_ref[:, w].reshape(CELLS, D).astype(F32) + dnorm
            grad_ref[:, w] = grad.astype(BF).reshape(WIN, WIN, D)


def outs(xw, cot, tis, att0, att1, dqkv0, dqkv1, w_qkv, w_proj):
    shape = jax.ShapeDtypeStruct((WIN, 2, WIN, D), BF)
    out, grad = pl.pallas_call(
        outs_kernel,
        grid=(GROUPS,),
        in_specs=[
            full((2, CELLS, D)), full((WIN, 2, WIN, D)), full((2, CELLS, 128)),
            full((2, CELLS, 2 * GW)), full((2, CELLS, GW)),
            pl.BlockSpec((1, 2, CELLS, D), lambda g: (jnp.minimum(g, 1), 0, 0, 0)),
            full((1, 2, CELLS, D)),
            columns(0, 0), columns(1, 0), columns(2, 0), full((D, D)),
        ],
        out_specs=[full((WIN, 2, WIN, D))] * 2,
        out_shape=[shape, shape],
        scratch_shapes=[pltpu.VMEM((2, CELLS, D), F32)],
        compiler_params=pltpu.CompilerParams(vmem_limit_bytes=VMEM),
        cost_estimate=cost(6e9, 12e6),
        name="outs",
    )(xw, cot, tis, att0, att1, dqkv0, dqkv1, w_qkv, w_qkv, w_qkv, w_proj)
    return out.reshape(1, WIN, 2 * WIN, D), grad.reshape(1, WIN, 2 * WIN, D)


def send(value, axis, move):
    devices = lax.axis_size(axis)
    return lax.ppermute(value, axis, [(i, move(i) % devices) for i in range(devices)])


def add(*terms):
    total = terms[0].astype(F32)
    for term in terms[1:]:
        total = total + term.astype(F32)
    return total.astype(BF)


def ring_start(low, high, axis, step):
    from_low = send(low[2], axis, lambda j: j + step)
    from_high = send(high[2], axis, lambda j: j - step)
    return from_low, from_high


def ring_pass(low, high, came, axis, step):
    up = jnp.concatenate([add(low[1], came[0]), high[1]], 1)
    down = jnp.concatenate([low[3], add(high[3], came[1])], 1)
    return send(up, axis, lambda j: j + step), send(down, axis, lambda j: j - step)


def ring_end(low, high, came):
    n = low.shape[2]
    up, down = came
    return add(low[0], up[:, :n], down[:, :n]), add(high[0], up[:, n:], down[:, n:])


def tie(*values):
    return lax.optimization_barrier(values)


def blocks(value):
    return value.reshape(4, value.shape[0] // 4, value.shape[1])


def shards(tiles, cotangent, tissue, w_qkv, w_proj):
    mine = tiles[0]
    below = send(mine[:8], "gy", lambda i: i - 1)
    right = send(mine[8:, :8], "gx", lambda i: i - 1)
    ny, nx = lax.axis_size("gy"), lax.axis_size("gx")
    diag = lax.ppermute(
        mine[:8, :8],
        ("gy", "gx"),
        [
            (a * nx + b, (a - 1) % ny * nx + (b - 1) % nx)
            for a in range(ny)
            for b in range(nx)
        ],
    )
    cot = cotangent.reshape(WIN, 2, WIN, D)
    db, da, tis, live = branch(cot, tissue[0], w_proj)
    keep0, send0, att0, dqkv0, xw, hid = first_heads(
        mine, below, right, diag, tis, live, w_qkv, da
    )
    first = add(keep0, send(send0, "gy", lambda i: i ^ 1))
    keep1, send1, att1, dqkv1 = last_heads(hid, tis, live, w_qkv, da)
    low_b = add(keep1, send(send1, "gy", lambda i: i ^ 1))
    first, att1 = tie(first, att1)
    low_a, high_a = blocks(first[:, :D]), blocks(first[:, D:])
    came_a = ring_start(low_a, high_a, "dp", 1)
    keep2, send2 = proj_grad(att0, att1, db)
    high_b = add(keep2, send(send2, "gy", lambda i: i ^ 1))
    low_b, high_b, came_a = tie(blocks(low_b), blocks(high_b), came_a)
    came_b = ring_start(low_b, high_b, "gy", 2)
    came_a = ring_pass(low_a, high_a, came_a, "dp", 1)
    came_b, xw = tie(came_b, xw)
    came_b = ring_pass(low_b, high_b, came_b, "gy", 2)
    out, grad = outs(xw, cot, tis, att0, att1, dqkv0, dqkv1, w_qkv, w_proj)
    out, came_a, came_b = tie(out, came_a, came_b)
    low_a, high_a = (blocks(v) for v in ring_end(low_a, high_a, came_a))
    low_b, high_b = (blocks(v) for v in ring_end(low_b, high_b, came_b))
    came_a = ring_start(low_a, high_a, "gy", 2)
    came_b = ring_start(low_b, high_b, "dp", 1)
    came_a = ring_pass(low_a, high_a, came_a, "gy", 2)
    came_b = ring_pass(low_b, high_b, came_b, "dp", 1)
    low_a, high_a = ring_end(low_a, high_a, came_a)
    low_b, high_b = ring_end(low_b, high_b, came_b)
    rows = jnp.concatenate([low_a, high_a, low_b, high_b], 1)
    parts = lax.all_to_all(rows.reshape(8, 3, -1), "gx", 0, 0)
    total = jnp.sum(parts.astype(F32), 0) * (1.0 / math.sqrt(512))
    grad_qkv = total[:, : 3 * D].reshape(3, GROUPS, 3, GW).transpose(0, 2, 1, 3)
    return out, grad, grad_qkv.reshape(3, 3 * D), total[:, 3 * D :]


def solution(mesh):
    block = P("dp", "gy", "gx", None)
    in_specs = (block, block, P("dp", "gy", "gx"), P(), P())
    out_specs = (block, block, P(("dp", "gy", "gx"), None), P(("dp", "gy", "gx"), None))
    return jax.shard_map(
        shards, mesh=mesh, in_specs=in_specs, out_specs=out_specs, check_vma=False
    )
```

time: 109 us -> 103 us (0.945)
  the two profiles are of different devices: /device:TPU:32 before, /device:TPU:6 now
where the time goes in v2:
time: 103 us
  Pallas kernels  39.6 us (38%)
  starting transfers between devices  32.8 us (32%)
  blocking collectives  13.3 us (13%)
  waiting for transfers between devices  10.9 us (11%)
  local copies, waits for them, and re-layouts  4.3 us (4%)
  other arithmetic  1.26 us (1%)
    ppermute x21, starting transfers between devices, send(): lax.ppermute(value, axis, [(i, move(i) % devices) for i in range(devices)])  32 us
    pallas_call x1, Pallas kernels, first_heads(): pl.pallas_call(first_kernel, grid=(2,), in_specs=[full((16, 32, D)), full...  13.8 us
    all_to_all x1, blocking collectives, shards(): parts = lax.all_to_all(rows.reshape(8, 3, -1), 'gx', 0, 0)  13.3 us
    ppermute x21, waiting for transfers between devices, send(): lax.ppermute(value, axis, [(i, move(i) % devices) for i in range(devices)])  10.5 us
    pallas_call x1, Pallas kernels, outs(): pl.pallas_call(outs_kernel, grid=(GROUPS,), in_specs=[full((2, CELLS, D))...  9.68 us
    pallas_call x1, Pallas kernels, last_heads(): pl.pallas_call(last_kernel, grid=(1,), in_specs=[full((2, CELLS, D))] + i...  8.43 us
    pallas_call x1, Pallas kernels, proj_grad(): pl.pallas_call(proj_kernel, out_shape=[shape, shape], compiler_params=plt...  4.17 us
    pallas_call x1, Pallas kernels, branch(): pl.pallas_call(branch_kernel, out_shape=[shape, shape, mask, mask], compi...  3.56 us
  transfers between devices with their start and end apart: 22, of which 5 were waited for; matrix products, arithmetic and copies ran while one was open for 2% of the time, Pallas kernels for 25%

profile of v2, /device:TPU:6, one launch (start us, length us, event | category | flops | bytes accessed | tf_op | source)
XLA Modules:
  0.0 103.2 jit_solution(1373506365648729266)
XLA Ops:
  0.6 1.0 slice_bitcast_fusion
  1.7 2.5 %collective-permute-start = (bf16[8,32,768]{2,1,0:T(8,128)(2,1)S(1)}, bf16[8,32,768]{2,1,0:T(8,128)(2,1)S(1)}, u32[]{:S(2)}, u32[]{:S(2)}) collective-permute-start(bf16[8,32,768]{2,1,0:T(8,128)(2,1)S(1)} %slice_bitcast_fusion), channel_id=1, source_target_pairs={{0,56},{8,0},{16,8},{24,16},{32,24},{40,32},{48,40},{56,48},{1,57}... | collective-permute-start | bytes 1179656 | tf_op jit(solution)/shard_map/ppermute | solution.py:325
  4.1 1.0 fusion.7
  5.1 5.9 %collective-permute-start.1 = (bf16[8,8,768]{2,1,0:T(8,128)(2,1)S(1)}, bf16[8,8,768]{2,1,0:T(8,128)(2,1)S(1)}, u32[]{:S(2)}, u32[]{:S(2)}) collective-permute-start(bf16[8,8,768]{2,1,0:T(8,128)(2,1)S(1)} %get-tuple-element.77), channel_id=1, source_target_pairs={{0,7},{1,0},{2,1},{3,2},{4,3},{5,4},{6,5},{7,6},{8,15},{9,8},{10,9... | collective-permute-start | bytes 294920 | tf_op jit(solution)/shard_map/ppermute | solution.py:325
  11.0 0.8 collective-permute-start.2
  11.9 3.6 %branch.1 = (bf16[2,256,768]{2,1,0:T(8,128)(2,1)}, bf16[2,256,768]{2,1,0:T(8,128)(2,1)}, bf16[2,256,128]{2,1,0:T(8,128)(2,1)}, bf16[2,256,128]{2,1,0:T(8,128)(2,1)}) custom-call(bf16[16,2,16,768]{3,2,1,0:T(8,128)(2,1)} %bitcast.39, s32[16,32]{1,0:T(8,128)} %bitcast.41, bf16[768,768]{1,0:T(8,128)(2,1)} %wp_ref.3), custom_call_target="tpu_custom_call" | custom-call | flops 600000000 | bytes 4000000 | tf_op jit(solution)/shard_map/branch/pallas_call | solution.py:62
  15.4 0.4 collective-permute-done.2.diag_ref
  16.1 0.4 copy-done.5
  16.6 13.8 %first_heads.1 = (bf16[384,1536]{1,0:T(8,128)(2,1)}, bf16[384,1536]{1,0:T(8,128)(2,1)}, bf16[2,256,512]{2,1,0:T(8,128)(2,1)}, bf16[2,2,256,768]{3,2,1,0:T(8,128)...) custom-call(bf16[16,32,768]{2,1,0:T(8,128)(2,1)} %bitcast.37, bf16[8,32,768]{2,1,0:T(8,128)(2,1)} %copy-done.3, ...), custom_call_target="tpu_custom_call" | custom-call | flops 6000000000 | bytes 10000000 | tf_op jit(solution)/shard_map/first_heads/pallas_call | solution.py:219
  30.7 8.4 %last_heads.1 = (bf16[384,768]{1,0:T(8,128)(2,1)}, bf16[384,768]{1,0:T(8,128)(2,1)}, bf16[2,256,256]{2,1,0:T(8,128)(2,1)}, bf16[1,2,256,768]{3,2,1,0:T(8,128)(2,1)}) custom-call(bf16[2,256,768]{2,1,0:T(8,128)(2,1)} %get-tuple-element.39.hid_ref, bf16[2,256,128]{2,1,0:T(8,128)(2,1)} %get-tuple-element.36.tis_ref, ...), custom_call_target="tpu_custom_call" | custom-call | flops 4000000000 | bytes 6000000 | tf_op jit(solution)/shard_map/last_heads/pallas_call | solution.py:234
  39.1 0.5 collective-permute-start.3
  39.9 4.2 %proj_grad.1 = (bf16[384,768]{1,0:T(8,128)(2,1)}, bf16[384,768]{1,0:T(8,128)(2,1)}) custom-call(bf16[2,256,512]{2,1,0:T(8,128)(2,1)} %get-tuple-element.42.att0_ref, bf16[2,256,256]{2,1,0:T(8,128)(2,1)} %get-tuple-element.46.att1_ref, bf16[2,256,768]{2,1,0:T(8,128)(2,1)} %get-tuple-element.47.db_ref), custom_call_target="tpu_custom_call" | custom-call | flops 2000000000 | bytes 4000000 | tf_op jit(solution)/shard_map/proj_grad/pallas_call | solution.py:255
  44.3 0.6 collective-permute-start.6
  44.9 1.5 %collective-permute-start.7 = (bf16[96,768]{1,0:T(8,128)(2,1)S(1)}, bf16[96,768]{1,0:T(8,128)(2,1)S(1)}, u32[]{:S(2)}, u32[]{:S(2)}) collective-permute-start(bf16[96,768]{1,0:T(8,128)(2,1)S(1)} %get-tuple-element.72), channel_id=1, source_target_pairs={{0,192},{64,0},{128,64},{192,128},{1,193},{65,1},{129,65},{193,129... | collective-permute-start | bytes 442376 | tf_op jit(solution)/shard_map/ppermute | solution.py:325
  46.5 4.1 %collective-permute-done.6 = bf16[96,768]{1,0:T(8,128)(2,1)S(1)} collective-permute-done((bf16[96,768]{1,0:T(8,128)(2,1)S(1)}, bf16[96,768]{1,0:T(8,128)(2,1)S(1)}, u32[]{:S(2)}, u32[]{:S(2)}) %collective-permute-start.6) | collective-permute-done | bytes 147488 | tf_op jit(solution)/shard_map/ppermute | solution.py:325
  50.6 1.4 %collective-permute-done.7 = bf16[96,768]{1,0:T(8,128)(2,1)S(1)} collective-permute-done((bf16[96,768]{1,0:T(8,128)(2,1)S(1)}, bf16[96,768]{1,0:T(8,128)(2,1)S(1)}, u32[]{:S(2)}, u32[]{:S(2)}) %collective-permute-start.7) | collective-permute-done | bytes 147488 | tf_op jit(solution)/shard_map/ppermute | solution.py:325
  52.2 3.3 %collective-permute-start.9 = (bf16[96,768]{1,0:T(8,128)(2,1)S(1)}, bf16[96,768]{1,0:T(8,128)(2,1)S(1)}, u32[]{:S(2)}, u32[]{:S(2)}) collective-permute-start(bf16[96,768]{1,0:T(8,128)(2,1)S(1)} %get-tuple-element.83), channel_id=1, source_target_pairs={{0,48},{8,56},{16,0},{24,8},{32,16},{40,24},{48,32},{56,40},{1,49}... | collective-permute-start | bytes 442376 | tf_op jit(solution)/shard_map/ppermute | solution.py:325
  55.6 0.6 collective-permute-start.11
  56.2 3.0 %collective-permute-start.10 = (bf16[96,1536]{1,0:T(8,128)(2,1)S(1)}, bf16[96,1536]{1,0:T(8,128)(2,1)S(1)}, u32[]{:S(2)}, u32[]{:S(2)}) collective-permute-start(bf16[96,1536]{1,0:T(8,128)(2,1)S(1)} %pad_maximum_fusion), channel_id=1, source_target_pairs={{0,64},{64,128},{128,192},{192,0},{1,65},{65,129},{129,193},{193,1... | collective-permute-start | bytes 884744 | tf_op jit(solution)/shard_map/ppermute | solution.py:325
  59.3 2.7 %collective-permute-start.13 = (bf16[96,1536]{1,0:T(8,128)(2,1)S(1)}, bf16[96,1536]{1,0:T(8,128)(2,1)S(1)}, u32[]{:S(2)}, u32[]{:S(2)}) collective-permute-start(bf16[96,1536]{1,0:T(8,128)(2,1)S(1)} %pad_maximum_fusion.3), channel_id=1, source_target_pairs={{0,48},{8,56},{16,0},{24,8},{32,16},{40,24},{48,32},{56,40},{1,49}... | collective-permute-start | bytes 884744 | tf_op jit(solution)/shard_map/ppermute | solution.py:325
  62.1 9.7 %outs.1 = (bf16[16,2,16,768]{3,2,1,0:T(8,128)(2,1)}, bf16[16,2,16,768]{3,2,1,0:T(8,128)(2,1)}) custom-call(bf16[2,256,768]{2,1,0:T(8,128)(2,1)} %get-tuple-element.54.xw_ref, bf16[16,2,16,768]{3,2,1,0:T(8,128)(2,1)} %bitcast.40, bf16[2,256,128]{2,1,0:T(8,128)(2,1)} %get-tuple-element.36.tis_ref, bf16[2,256,512]{2,1,0:T(8,128)(2,1)} %get-tuple-element.42.att0_ref, ...), custom_call_target="tpu_custom_call" | custom-call | flops 6000000000 | bytes 12000000 | tf_op jit(solution)/shard_map/outs/pallas_call | solution.py:303
  72.2 3.3 %collective-permute-start.16 = (bf16[24,768]{1,0:T(8,128)(2,1)S(1)}, bf16[24,768]{1,0:T(8,128)(2,1)S(1)}, u32[]{:S(2)}, u32[]{:S(2)}) collective-permute-start(bf16[24,768]{1,0:T(8,128)(2,1)S(1)} %get-tuple-element.89), channel_id=1, source_target_pairs={{0,48},{8,56},{16,0},{24,8},{32,16},{40,24},{48,32},{56,40},{1,49}... | collective-permute-start | bytes 110600 | tf_op jit(solution)/shard_map/ppermute | solution.py:325
  75.5 0.3 collective-permute-start.18
  75.8 1.7 %collective-permute-start.20 = (bf16[24,768]{1,0:T(8,128)(2,1)S(1)}, bf16[24,768]{1,0:T(8,128)(2,1)S(1)}, u32[]{:S(2)}, u32[]{:S(2)}) collective-permute-start(bf16[24,768]{1,0:T(8,128)(2,1)S(1)} %get-tuple-element.95), channel_id=1, source_target_pairs={{0,192},{64,0},{128,64},{192,128},{1,193},{65,1},{129,65},{193,129... | collective-permute-start | bytes 110600 | tf_op jit(solution)/shard_map/ppermute | solution.py:325
  77.7 3.3 %collective-permute-start.17 = (bf16[24,1536]{1,0:T(8,128)(2,1)S(1)}, bf16[24,1536]{1,0:T(8,128)(2,1)S(1)}, u32[]{:S(2)}, u32[]{:S(2)}) collective-permute-start(bf16[24,1536]{1,0:T(8,128)(2,1)S(1)} %pad_maximum_fusion.6), channel_id=1, source_target_pairs={{0,48},{8,56},{16,0},{24,8},{32,16},{40,24},{48,32},{56,40},{1,49}... | collective-permute-start | bytes 221192 | tf_op jit(solution)/shard_map/ppermute | solution.py:325
  81.0 1.6 %collective-permute-start.19 = (bf16[24,1536]{1,0:T(8,128)(2,1)S(1)}, bf16[24,1536]{1,0:T(8,128)(2,1)S(1)}, u32[]{:S(2)}, u32[]{:S(2)}) collective-permute-start(bf16[24,1536]{1,0:T(8,128)(2,1)S(1)} %pad_maximum_fusion.7), channel_id=1, source_target_pairs={{0,64},{64,128},{128,192},{192,0},{1,65},{65,129},{129,193},{193,1... | collective-permute-start | bytes 221192 | tf_op jit(solution)/shard_map/ppermute | solution.py:325
  82.6 0.6 collective-permute-start.21
  83.3 2.2 %collective-permute-done.19 = bf16[24,1536]{1,0:T(8,128)(2,1)S(1)} collective-permute-done((bf16[24,1536]{1,0:T(8,128)(2,1)S(1)}, bf16[24,1536]{1,0:T(8,128)(2,1)S(1)}, u32[]{:S(2)}, u32[]{:S(2)}) %collective-permute-start.19) | collective-permute-done | bytes 73760 | tf_op jit(solution)/shard_map/ppermute | solution.py:325
  85.4 2.9 %collective-permute-done.21 = bf16[24,1536]{1,0:T(8,128)(2,1)S(1)} collective-permute-done((bf16[24,1536]{1,0:T(8,128)(2,1)S(1)}, bf16[24,1536]{1,0:T(8,128)(2,1)S(1)}, u32[]{:S(2)}, u32[]{:S(2)}) %collective-permute-start.21) | collective-permute-done | bytes 73760 | tf_op jit(solution)/shard_map/ppermute | solution.py:325
  88.4 13.3 %all_to_all.5 = bf16[8,3,3072]{2,1,0:T(4,128)(2,1)S(1)} all-to-all(bf16[8,3,3072]{2,1,0:T(4,128)(2,1)S(1)} %reshape.100), channel_id=1, replica_groups=mesh['dp'=4,'gy'=8,'gx'=8] {'gx'}, dimensions={0} | all-to-all | bytes 294912 | tf_op jit(solution)/shard_map/all_to_all | solution.py:404
  101.9 0.6 slice.277
  102.5 0.6 reshape.102
  (69 shorter events, 2.6 us)
Async XLA Ops:
  1.7 14.1 %collective-permute-start = (bf16[8,32,768]{2,1,0:T(8,128)(2,1)S(1)}, bf16[8,32,768]{2,1,0:T(8,128)(2,1)S(1)}, u32[]{:S(2)}, u32[]{:S(2)}) collective-permute-start(bf16[8,32,768]{2,1,0:T(8,128)(2,1)S(1)} %slice_bitcast_fusion), channel_id=1, source_target_pairs={{0,56},{8,0},{16,8},{24,16},{32,24},{40,32},{48,40},{56,48},{1,57}... | collective-permute-start | bytes 1179656 | tf_op jit(solution)/shard_map/ppermute | solution.py:325
  5.1 10.3 %collective-permute-start.1 = (bf16[8,8,768]{2,1,0:T(8,128)(2,1)S(1)}, bf16[8,8,768]{2,1,0:T(8,128)(2,1)S(1)}, u32[]{:S(2)}, u32[]{:S(2)}) collective-permute-start(bf16[8,8,768]{2,1,0:T(8,128)(2,1)S(1)} %get-tuple-element.77), channel_id=1, source_target_pairs={{0,7},{1,0},{2,1},{3,2},{4,3},{5,4},{6,5},{7,6},{8,15},{9,8},{10,9... | collective-permute-start | bytes 294920 | tf_op jit(solution)/shard_map/ppermute | solution.py:325
  11.0 4.8 %collective-permute-start.2 = (bf16[8,8,768]{2,1,0:T(8,128)(2,1)S(1)}, bf16[8,8,768]{2,1,0:T(8,128)(2,1)S(1)}, u32[]{:S(2)}, u32[]{:S(2)}) collective-permute-start(bf16[8,8,768]{2,1,0:T(8,128)(2,1)S(1)} %get-tuple-element.76), channel_id=1, source_target_pairs={{0,63},{1,56},{2,57},{3,58},{4,59},{5,60},{6,61},{7,62},{8,7},{9,0... | collective-permute-start | bytes 294920 | tf_op jit(solution)/shard_map/ppermute | solution.py:366
  15.4 0.6 copy-start.4
  15.8 0.6 copy-start.5
  15.8 0.8 copy-start.3
  30.4 9.2 %collective-permute-start.4 = (bf16[384,1536]{1,0:T(8,128)(2,1)}, bf16[384,1536]{1,0:T(8,128)(2,1)S(1)}, u32[]{:S(2)}, u32[]{:S(2)}) collective-permute-start(bf16[384,1536]{1,0:T(8,128)(2,1)} %get-tuple-element.44), channel_id=1, source_target_pairs={{0,8},{8,0},{16,24},{24,16},{32,40},{40,32},{48,56},{56,48},{1,9},... | collective-permute-start | bytes 3538952 | tf_op jit(solution)/shard_map/ppermute | solution.py:325
  30.7 8.9 %copy-start = (bf16[384,1536]{1,0:T(8,128)(2,1)S(1)}, bf16[384,1536]{1,0:T(8,128)(2,1)}, u32[]{:S(2)}) copy-start(bf16[384,1536]{1,0:T(8,128)(2,1)} %get-tuple-element.43) | copy-start | bytes 3538948
  39.1 5.0 %collective-permute-start.3 = (bf16[384,768]{1,0:T(8,128)(2,1)}, bf16[384,768]{1,0:T(8,128)(2,1)S(1)}, u32[]{:S(2)}, u32[]{:S(2)}) collective-permute-start(bf16[384,768]{1,0:T(8,128)(2,1)} %get-tuple-element.41), channel_id=1, source_target_pairs={{0,8},{8,0},{16,24},{24,16},{32,40},{40,32},{48,56},{56,48},{1,9},... | collective-permute-start | bytes 1769480 | tf_op jit(solution)/shard_map/ppermute | solution.py:325
  39.9 4.2 %copy-start.1 = (bf16[384,768]{1,0:T(8,128)(2,1)S(1)}, bf16[384,768]{1,0:T(8,128)(2,1)}, u32[]{:S(2)}) copy-start(bf16[384,768]{1,0:T(8,128)(2,1)} %get-tuple-element.40) | copy-start | bytes 1769476
  44.1 2.3 %collective-permute-start.5 = (bf16[384,768]{1,0:T(8,128)(2,1)}, bf16[384,768]{1,0:T(8,128)(2,1)S(1)}, u32[]{:S(2)}, u32[]{:S(2)}) collective-permute-start(bf16[384,768]{1,0:T(8,128)(2,1)} %get-tuple-element.49), channel_id=1, source_target_pairs={{0,8},{8,0},{16,24},{24,16},{32,40},{40,32},{48,56},{56,48},{1,9},... | collective-permute-start | bytes 1769480 | tf_op jit(solution)/shard_map/ppermute | solution.py:325
  44.1 2.3 %copy-start.2 = (bf16[384,768]{1,0:T(8,128)(2,1)S(1)}, bf16[384,768]{1,0:T(8,128)(2,1)}, u32[]{:S(2)}) copy-start(bf16[384,768]{1,0:T(8,128)(2,1)} %get-tuple-element.48) | copy-start | bytes 1769476
  44.3 6.3 %collective-permute-start.6 = (bf16[96,768]{1,0:T(8,128)(2,1)S(1)}, bf16[96,768]{1,0:T(8,128)(2,1)S(1)}, u32[]{:S(2)}, u32[]{:S(2)}) collective-permute-start(bf16[96,768]{1,0:T(8,128)(2,1)S(1)} %get-tuple-element.73), channel_id=1, source_target_pairs={{0,64},{64,128},{128,192},{192,0},{1,65},{65,129},{129,193},{193,1... | collective-permute-start | bytes 442376 | tf_op jit(solution)/shard_map/ppermute | solution.py:325
  44.9 7.2 %collective-permute-start.7 = (bf16[96,768]{1,0:T(8,128)(2,1)S(1)}, bf16[96,768]{1,0:T(8,128)(2,1)S(1)}, u32[]{:S(2)}, u32[]{:S(2)}) collective-permute-start(bf16[96,768]{1,0:T(8,128)(2,1)S(1)} %get-tuple-element.72), channel_id=1, source_target_pairs={{0,192},{64,0},{128,64},{192,128},{1,193},{65,1},{129,65},{193,129... | collective-permute-start | bytes 442376 | tf_op jit(solution)/shard_map/ppermute | solution.py:325
  52.0 7.2 %collective-permute-start.8 = (bf16[96,768]{1,0:T(8,128)(2,1)S(1)}, bf16[96,768]{1,0:T(8,128)(2,1)S(1)}, u32[]{:S(2)}, u32[]{:S(2)}) collective-permute-start(bf16[96,768]{1,0:T(8,128)(2,1)S(1)} %get-tuple-element.81), channel_id=1, source_target_pairs={{0,16},{8,24},{16,32},{24,40},{32,48},{40,56},{48,0},{56,8},{1,17}... | collective-permute-start | bytes 442376 | tf_op jit(solution)/shard_map/ppermute | solution.py:325
  52.2 7.0 %collective-permute-start.9 = (bf16[96,768]{1,0:T(8,128)(2,1)S(1)}, bf16[96,768]{1,0:T(8,128)(2,1)S(1)}, u32[]{:S(2)}, u32[]{:S(2)}) collective-permute-start(bf16[96,768]{1,0:T(8,128)(2,1)S(1)} %get-tuple-element.83), channel_id=1, source_target_pairs={{0,48},{8,56},{16,0},{24,8},{32,16},{40,24},{48,32},{56,40},{1,49}... | collective-permute-start | bytes 442376 | tf_op jit(solution)/shard_map/ppermute | solution.py:325
  55.6 16.2 %collective-permute-start.11 = (bf16[96,1536]{1,0:T(8,128)(2,1)S(1)}, bf16[96,1536]{1,0:T(8,128)(2,1)S(1)}, u32[]{:S(2)}, u32[]{:S(2)}) collective-permute-start(bf16[96,1536]{1,0:T(8,128)(2,1)S(1)} %pad_maximum_fusion.1), channel_id=1, source_target_pairs={{0,192},{64,0},{128,64},{192,128},{1,193},{65,1},{129,65},{193,129... | collective-permute-start | bytes 884744 | tf_op jit(solution)/shard_map/ppermute | solution.py:325
  56.2 15.6 %collective-permute-start.10 = (bf16[96,1536]{1,0:T(8,128)(2,1)S(1)}, bf16[96,1536]{1,0:T(8,128)(2,1)S(1)}, u32[]{:S(2)}, u32[]{:S(2)}) collective-permute-start(bf16[96,1536]{1,0:T(8,128)(2,1)S(1)} %pad_maximum_fusion), channel_id=1, source_target_pairs={{0,64},{64,128},{128,192},{192,0},{1,65},{65,129},{129,193},{193,1... | collective-permute-start | bytes 884744 | tf_op jit(solution)/shard_map/ppermute | solution.py:325
  59.3 12.5 %collective-permute-start.13 = (bf16[96,1536]{1,0:T(8,128)(2,1)S(1)}, bf16[96,1536]{1,0:T(8,128)(2,1)S(1)}, u32[]{:S(2)}, u32[]{:S(2)}) collective-permute-start(bf16[96,1536]{1,0:T(8,128)(2,1)S(1)} %pad_maximum_fusion.3), channel_id=1, source_target_pairs={{0,48},{8,56},{16,0},{24,8},{32,16},{40,24},{48,32},{56,40},{1,49}... | collective-permute-start | bytes 884744 | tf_op jit(solution)/shard_map/ppermute | solution.py:325
  62.0 9.8 %collective-permute-start.12 = (bf16[96,1536]{1,0:T(8,128)(2,1)S(1)}, bf16[96,1536]{1,0:T(8,128)(2,1)S(1)}, u32[]{:S(2)}, u32[]{:S(2)}) collective-permute-start(bf16[96,1536]{1,0:T(8,128)(2,1)S(1)} %pad_maximum_fusion.2), channel_id=1, source_target_pairs={{0,16},{8,24},{16,32},{24,40},{32,48},{40,56},{48,0},{56,8},{1,17}... | collective-permute-start | bytes 884744 | tf_op jit(solution)/shard_map/ppermute | solution.py:325
  72.1 5.4 %collective-permute-start.14 = (bf16[24,768]{1,0:T(8,128)(2,1)S(1)}, bf16[24,768]{1,0:T(8,128)(2,1)S(1)}, u32[]{:S(2)}, u32[]{:S(2)}) collective-permute-start(bf16[24,768]{1,0:T(8,128)(2,1)S(1)} %get-tuple-element.86), channel_id=1, source_target_pairs={{0,16},{8,24},{16,32},{24,40},{32,48},{40,56},{48,0},{56,8},{1,17}... | collective-permute-start | bytes 110600 | tf_op jit(solution)/shard_map/ppermute | solution.py:325
  72.2 5.4 %collective-permute-start.16 = (bf16[24,768]{1,0:T(8,128)(2,1)S(1)}, bf16[24,768]{1,0:T(8,128)(2,1)S(1)}, u32[]{:S(2)}, u32[]{:S(2)}) collective-permute-start(bf16[24,768]{1,0:T(8,128)(2,1)S(1)} %get-tuple-element.89), channel_id=1, source_target_pairs={{0,48},{8,56},{16,0},{24,8},{32,16},{40,24},{48,32},{56,40},{1,49}... | collective-permute-start | bytes 110600 | tf_op jit(solution)/shard_map/ppermute | solution.py:325
  75.5 5.5 %collective-permute-start.18 = (bf16[24,768]{1,0:T(8,128)(2,1)S(1)}, bf16[24,768]{1,0:T(8,128)(2,1)S(1)}, u32[]{:S(2)}, u32[]{:S(2)}) collective-permute-start(bf16[24,768]{1,0:T(8,128)(2,1)S(1)} %get-tuple-element.92), channel_id=1, source_target_pairs={{0,64},{64,128},{128,192},{192,0},{1,65},{65,129},{129,193},{193,1... | collective-permute-start | bytes 110600 | tf_op jit(solution)/shard_map/ppermute | solution.py:325
  75.8 6.8 %collective-permute-start.20 = (bf16[24,768]{1,0:T(8,128)(2,1)S(1)}, bf16[24,768]{1,0:T(8,128)(2,1)S(1)}, u32[]{:S(2)}, u32[]{:S(2)}) collective-permute-start(bf16[24,768]{1,0:T(8,128)(2,1)S(1)} %get-tuple-element.95), channel_id=1, source_target_pairs={{0,192},{64,0},{128,64},{192,128},{1,193},{65,1},{129,65},{193,129... | collective-permute-start | bytes 110600 | tf_op jit(solution)/shard_map/ppermute | solution.py:325
  77.5 5.7 %collective-permute-start.15 = (bf16[24,1536]{1,0:T(8,128)(2,1)S(1)}, bf16[24,1536]{1,0:T(8,128)(2,1)S(1)}, u32[]{:S(2)}, u32[]{:S(2)}) collective-permute-start(bf16[24,1536]{1,0:T(8,128)(2,1)S(1)} %pad_maximum_fusion.5), channel_id=1, source_target_pairs={{0,16},{8,24},{16,32},{24,40},{32,48},{40,56},{48,0},{56,8},{1,17}... | collective-permute-start | bytes 221192 | tf_op jit(solution)/shard_map/ppermute | solution.py:325
  77.7 5.6 %collective-permute-start.17 = (bf16[24,1536]{1,0:T(8,128)(2,1)S(1)}, bf16[24,1536]{1,0:T(8,128)(2,1)S(1)}, u32[]{:S(2)}, u32[]{:S(2)}) collective-permute-start(bf16[24,1536]{1,0:T(8,128)(2,1)S(1)} %pad_maximum_fusion.6), channel_id=1, source_target_pairs={{0,48},{8,56},{16,0},{24,8},{32,16},{40,24},{48,32},{56,40},{1,49}... | collective-permute-start | bytes 221192 | tf_op jit(solution)/shard_map/ppermute | solution.py:325
  81.0 4.4 %collective-permute-start.19 = (bf16[24,1536]{1,0:T(8,128)(2,1)S(1)}, bf16[24,1536]{1,0:T(8,128)(2,1)S(1)}, u32[]{:S(2)}, u32[]{:S(2)}) collective-permute-start(bf16[24,1536]{1,0:T(8,128)(2,1)S(1)} %pad_maximum_fusion.7), channel_id=1, source_target_pairs={{0,64},{64,128},{128,192},{192,0},{1,65},{65,129},{129,193},{193,1... | collective-permute-start | bytes 221192 | tf_op jit(solution)/shard_map/ppermute | solution.py:325
  82.6 5.6 %collective-permute-start.21 = (bf16[24,1536]{1,0:T(8,128)(2,1)S(1)}, bf16[24,1536]{1,0:T(8,128)(2,1)S(1)}, u32[]{:S(2)}, u32[]{:S(2)}) collective-permute-start(bf16[24,1536]{1,0:T(8,128)(2,1)S(1)} %pad_maximum_fusion.8), channel_id=1, source_target_pairs={{0,192},{64,0},{128,64},{192,128},{1,193},{65,1},{129,65},{193,129... | collective-permute-start | bytes 221192 | tf_op jit(solution)/shard_map/ppermute | solution.py:325

commit v3 on v2

--- a/solution.py
+++ b/solution.py
@@ -15,7 +15,7 @@
 GROUPS = 3
 GW = D // GROUPS
 HEAD_SCALE = 0.125
-VMEM = 56 * 1024 * 1024
+VMEM = 32 * 1024 * 1024
 
 
 def nn(a, b):
@@ -70,16 +70,19 @@
 
 def row_order(first):
     gy = lax.axis_index("gy")
-    dp, y, core = lax.axis_index("dp"), gy >> 1, gy & 1
+    dp, y, core, gx = lax.axis_index("dp"), gy >> 1, gy & 1, lax.axis_index("gx")
     at = lax.broadcasted_iota(jnp.int32, (D, 1), 0)
-    block = ((at.astype(F32) + 0.5) * (1.0 / 24)).astype(jnp.int32)
-    outer, inner = (block >> 2) & 3, block & 3
+    third = ((at.astype(F32) + 0.5) * (1.0 / 3)).astype(jnp.int32)
+    bit = [(third >> i) & 1 for i in range(8)]
+    z_of = gx ^ (bit[0] * 4 + bit[1] * 2 + bit[2])
+    distance = bit[6] * 2 + bit[5]
+    partner = bit[4] ^ (bit[3] * 3)
     if first == "dp":
-        dp_of, y_of = (outer + dp) & 3, (inner + y) & 3
+        dp_of, y_of = (distance + dp) & 3, partner ^ y
     else:
-        dp_of, y_of = (inner + dp) & 3, (outer + y) & 3
-    core_of = ((block >> 4) + core) & 1
-    source = (dp_of * 8 + y_of * 2 + core_of) * 24 + at - block * 24
+        dp_of, y_of = partner ^ dp, (distance + y) & 3
+    core_of = bit[7] ^ core
+    source = ((dp_of * 8 + y_of * 2 + core_of) * 8 + z_of) * 3 + at - third * 3
     column = lax.broadcasted_iota(jnp.int32, (D, D), 1)
     return jnp.where(column == source, 1.0, 0.0).astype(BF)
 
@@ -158,10 +161,10 @@
         perm = row_order("dp")
         for w in range(2):
             if w == 0:
-                top, bottom = own[:, 8:24], low[:, 8:24]
+                top, bottom = own[:, 8:24], low[:, :16]
             else:
                 top = jnp.concatenate([own[:, 24:32], right], 1)
-                bottom = jnp.concatenate([low[:, 24:32], diag], 1)
+                bottom = jnp.concatenate([low[:, 16:24], diag], 1)
             x = jnp.concatenate([top, bottom], 0).reshape(CELLS, D)
             xw_ref[w] = x.astype(BF)
             normed, _ = moments(x)
@@ -176,16 +179,27 @@
 
 
 def last_kernel(
-    hid_ref, tis_ref, live_ref, wq_ref, wk_ref, wv_ref, da_ref,
-    keep_ref, send_ref, att_ref, dqkv_ref, hid_t_ref,
+    hid_ref, hid_t_ref, tis_ref, live_ref, wq_ref, wk_ref, wv_ref, da_ref,
+    keep_ref, send_ref, att_ref, dqkv_ref,
 ):
-    perm = row_order("gy")
-    for w in range(2):
-        hid_t_ref[:, w * CELLS : (w + 1) * CELLS] = nt(perm, hid_ref[w]).astype(BF)
     heads_group(
         hid_ref, hid_t_ref, tis_ref, live_ref, wq_ref, wk_ref, wv_ref, da_ref,
         keep_ref, send_ref, att_ref, dqkv_ref,
     )
+
+
+def turn_kernel(hid_ref, hid_t_ref):
+    hid_t_ref[...] = nt(row_order("gy"), hid_ref[...].reshape(2 * CELLS, D)).astype(BF)
+
+
+def turn(hid):
+    return pl.pallas_call(
+        turn_kernel,
+        out_shape=jax.ShapeDtypeStruct((D, 2 * CELLS), BF),
+        compiler_params=pltpu.CompilerParams(vmem_limit_bytes=VMEM),
+        cost_estimate=cost(2e9, 2e6),
+        name="turn",
+    )(hid)
 
 
 def columns(block, first):
@@ -219,7 +233,7 @@
     return pl.pallas_call(
         first_kernel,
         grid=(2,),
-        in_specs=[full((16, 32, D)), full((8, 32, D)), full((8, 8, D)), full((8, 8, D))] + inputs,
+        in_specs=[full((16, 32, D)), full((8, 24, D)), full((8, 8, D)), full((8, 8, D))] + inputs,
         out_specs=outputs + [full((2, CELLS, D))] * 2,
         out_shape=shapes + [rows, rows],
         scratch_shapes=[pltpu.VMEM((D, 2 * CELLS), BF)],
@@ -229,19 +243,18 @@
     )(tiles, below, right, diag, tis, live, w_qkv, w_qkv, w_qkv, da)
 
 
-def last_heads(hid, tis, live, w_qkv, da):
+def last_heads(hid, hid_t, tis, live, w_qkv, da):
     inputs, outputs, shapes = heads_specs(2, 1)
     return pl.pallas_call(
         last_kernel,
         grid=(1,),
-        in_specs=[full((2, CELLS, D))] + inputs,
+        in_specs=[full((2, CELLS, D)), full((D, 2 * CELLS))] + inputs,
         out_specs=outputs,
         out_shape=shapes,
-        scratch_shapes=[pltpu.VMEM((D, 2 * CELLS), BF)],
         compiler_params=pltpu.CompilerParams(vmem_limit_bytes=VMEM),
         cost_estimate=cost(4e9, 6e6),
         name="last_heads",
-    )(hid, tis, live, w_qkv, w_qkv, w_qkv, da)
+    )(hid, hid_t, tis, live, w_qkv, w_qkv, w_qkv, da)
 
 
 def proj_kernel(att0_ref, att1_ref, db_ref, keep_ref, send_ref):
@@ -261,34 +274,47 @@
     )(att0, att1, db)
 
 
-def outs_kernel(
-    xw_ref, cot_ref, tis_ref, att0_ref, att1_ref, dqkv0_ref, dqkv1_ref,
-    wq_ref, wk_ref, wv_ref, wp_ref, out_ref, grad_ref, acc_ref,
+def out_kernel(xw_ref, tis_ref, att0_ref, att1_ref, wp_ref, out_ref):
+    for w in range(2):
+        tis = jnp.tile(tis_ref[w].astype(F32), (1, D // 128))
+        attended = jnp.concatenate([att0_ref[w], att1_ref[w]], 1)
+        out = xw_ref[w].astype(F32) + tis * nn(attended, wp_ref[...])
+        out_ref[:, w] = out.astype(BF).reshape(WIN, WIN, D)
+
+
+def out_part(xw, tis, att0, att1, w_proj):
+    out = pl.pallas_call(
+        out_kernel,
+        out_shape=jax.ShapeDtypeStruct((WIN, 2, WIN, D), BF),
+        compiler_params=pltpu.CompilerParams(vmem_limit_bytes=VMEM),
+        cost_estimate=cost(3e9, 5e6),
+        name="out_part",
+    )(xw, tis, att0, att1, w_proj)
+    return out.reshape(1, WIN, 2 * WIN, D)
+
+
+def grad_kernel(
+    xw_ref, cot_ref, dqkv0_ref, dqkv1_ref, wq_ref, wk_ref, wv_ref, grad_ref, acc_ref
 ):
     step = pl.program_id(0)
     weights = jnp.concatenate([wq_ref[...], wk_ref[...], wv_ref[...]], 1)
-    for w in range(2):
-        dqkv = jnp.where(step < GROUPS - 1, dqkv0_ref[0, w], dqkv1_ref[0, w])
-        part = nt(dqkv, weights)
-
-        @pl.when(step == 0)
-        def _():
-            acc_ref[w] = part
-
-        @pl.when(step > 0)
-        def _():
-            acc_ref[w] += part
+    dqkv = jnp.where(step < GROUPS - 1, dqkv0_ref[0], dqkv1_ref[0])
+    part = nt(dqkv.reshape(2 * CELLS, D), weights)
+
+    @pl.when(step == 0)
+    def _():
+        acc_ref[...] = part
+
+    @pl.when((step > 0) & (step < GROUPS - 1))
+    def _():
+        acc_ref[...] += part
 
     @pl.when(step == GROUPS - 1)
     def _():
+        acc_ref[...] += part
         for w in range(2):
-            x = xw_ref[w].astype(F32)
-            tis = jnp.tile(tis_ref[w].astype(F32), (1, D // 128))
-            attended = jnp.concatenate([att0_ref[w], att1_ref[w]], 1)
-            out = x + tis * nn(attended, wp_ref[...])
-            out_ref[:, w] = out.astype(BF).reshape(WIN, WIN, D)
-            normed, inv = moments(x)
-            dh = acc_ref[w]
+            normed, inv = moments(xw_ref[w].astype(F32))
+            dh = acc_ref[w * CELLS : (w + 1) * CELLS]
             dnorm = inv * (
                 dh
                 - jnp.mean(dh, -1, keepdims=True)
@@ -298,26 +324,24 @@
             grad_ref[:, w] = grad.astype(BF).reshape(WIN, WIN, D)
 
 
-def outs(xw, cot, tis, att0, att1, dqkv0, dqkv1, w_qkv, w_proj):
-    shape = jax.ShapeDtypeStruct((WIN, 2, WIN, D), BF)
-    out, grad = pl.pallas_call(
-        outs_kernel,
+def grad_part(xw, cot, dqkv0, dqkv1, w_qkv):
+    grad = pl.pallas_call(
+        grad_kernel,
         grid=(GROUPS,),
         in_specs=[
-            full((2, CELLS, D)), full((WIN, 2, WIN, D)), full((2, CELLS, 128)),
-            full((2, CELLS, 2 * GW)), full((2, CELLS, GW)),
+            full((2, CELLS, D)), full((WIN, 2, WIN, D)),
             pl.BlockSpec((1, 2, CELLS, D), lambda g: (jnp.minimum(g, 1), 0, 0, 0)),
             full((1, 2, CELLS, D)),
-            columns(0, 0), columns(1, 0), columns(2, 0), full((D, D)),
+            columns(0, 0), columns(1, 0), columns(2, 0),
         ],
-        out_specs=[full((WIN, 2, WIN, D))] * 2,
-        out_shape=[shape, shape],
-        scratch_shapes=[pltpu.VMEM((2, CELLS, D), F32)],
-        compiler_params=pltpu.CompilerParams(vmem_limit_bytes=VMEM),
-        cost_estimate=cost(6e9, 12e6),
-        name="outs",
-    )(xw, cot, tis, att0, att1, dqkv0, dqkv1, w_qkv, w_qkv, w_qkv, w_proj)
-    return out.reshape(1, WIN, 2 * WIN, D), grad.reshape(1, WIN, 2 * WIN, D)
+        out_specs=full((WIN, 2, WIN, D)),
+        out_shape=jax.ShapeDtypeStruct((WIN, 2, WIN, D), BF),
+        scratch_shapes=[pltpu.VMEM((2 * CELLS, D), F32)],
+        compiler_params=pltpu.CompilerParams(vmem_limit_bytes=VMEM),
+        cost_estimate=cost(6e9, 10e6),
+        name="grad_part",
+    )(xw, cot, dqkv0, dqkv1, w_qkv, w_qkv, w_qkv)
+    return grad.reshape(1, WIN, 2 * WIN, D)
 
 
 def send(value, axis, move):
@@ -347,7 +371,17 @@
 def ring_end(low, high, came):
     n = low.shape[2]
     up, down = came
-    return add(low[0], up[:, :n], down[:, :n]), add(high[0], up[:, n:], down[:, n:])
+    low = add(low[0], up[:, :n], down[:, :n])
+    high = add(high[0], up[:, n:], down[:, n:])
+    return jnp.concatenate([low, high], 1)
+
+
+def halve_start(rows, axis, flip):
+    return send(rows[rows.shape[0] // 2 :], axis, lambda j: j ^ flip)
+
+
+def halve_end(rows, came):
+    return add(rows[: rows.shape[0] // 2], came)
 
 
 def tie(*values):
@@ -360,7 +394,7 @@
 
 def shards(tiles, cotangent, tissue, w_qkv, w_proj):
     mine = tiles[0]
-    below = send(mine[:8], "gy", lambda i: i - 1)
+    below = send(mine[:8, 8:], "gy", lambda i: i - 1)
     right = send(mine[8:, :8], "gx", lambda i: i - 1)
     ny, nx = lax.axis_size("gy"), lax.axis_size("gx")
     diag = lax.ppermute(
@@ -377,32 +411,41 @@
     keep0, send0, att0, dqkv0, xw, hid = first_heads(
         mine, below, right, diag, tis, live, w_qkv, da
     )
-    first = add(keep0, send(send0, "gy", lambda i: i ^ 1))
-    keep1, send1, att1, dqkv1 = last_heads(hid, tis, live, w_qkv, da)
-    low_b = add(keep1, send(send1, "gy", lambda i: i ^ 1))
-    first, att1 = tie(first, att1)
+    came = send(send0, "gy", lambda i: i ^ 1)
+    hid_t = turn(hid)
+    came, hid_t = tie(came, hid_t)
+    first = add(keep0, came)
     low_a, high_a = blocks(first[:, :D]), blocks(first[:, D:])
+    low_a, high_a, hid_t = tie(low_a, high_a, hid_t)
     came_a = ring_start(low_a, high_a, "dp", 1)
+    keep1, send1, att1, dqkv1 = last_heads(hid, hid_t, tis, live, w_qkv, da)
+    came_a, send1, att1 = tie(came_a, send1, att1)
+    came_a = ring_pass(low_a, high_a, came_a, "dp", 1)
+    came = send(send1, "gy", lambda i: i ^ 1)
     keep2, send2 = proj_grad(att0, att1, db)
+    came, send2, keep2 = tie(came, send2, keep2)
+    low_b = add(keep1, came)
     high_b = add(keep2, send(send2, "gy", lambda i: i ^ 1))
-    low_b, high_b, came_a = tie(blocks(low_b), blocks(high_b), came_a)
+    low_b, high_b, att1 = tie(blocks(low_b), blocks(high_b), att1)
     came_b = ring_start(low_b, high_b, "gy", 2)
-    came_a = ring_pass(low_a, high_a, came_a, "dp", 1)
-    came_b, xw = tie(came_b, xw)
+    out = out_part(xw, tis, att0, att1, w_proj)
+    came_a, came_b, out, xw = tie(came_a, came_b, out, xw)
+    rows_a = ring_end(low_a, high_a, came_a)
     came_b = ring_pass(low_b, high_b, came_b, "gy", 2)
-    out, grad = outs(xw, cot, tis, att0, att1, dqkv0, dqkv1, w_qkv, w_proj)
-    out, came_a, came_b = tie(out, came_a, came_b)
-    low_a, high_a = (blocks(v) for v in ring_end(low_a, high_a, came_a))
-    low_b, high_b = (blocks(v) for v in ring_end(low_b, high_b, came_b))
-    came_a = ring_start(low_a, high_a, "gy", 2)
-    came_b = ring_start(low_b, high_b, "dp", 1)
-    came_a = ring_pass(low_a, high_a, came_a, "gy", 2)
-    came_b = ring_pass(low_b, high_b, came_b, "dp", 1)
-    low_a, high_a = ring_end(low_a, high_a, came_a)
-    low_b, high_b = ring_end(low_b, high_b, came_b)
-    rows = jnp.concatenate([low_a, high_a, low_b, high_b], 1)
-    parts = lax.all_to_all(rows.reshape(8, 3, -1), "gx", 0, 0)
-    total = jnp.sum(parts.astype(F32), 0) * (1.0 / math.sqrt(512))
+    came_a = halve_start(rows_a, "gy", 2)
+    grad = grad_part(xw, cot, dqkv0, dqkv1, w_qkv)
+    came_a, came_b, grad = tie(came_a, came_b, grad)
+    rows_a = halve_end(rows_a, came_a)
+    rows_b = ring_end(low_b, high_b, came_b)
+    came_a = halve_start(rows_a, "gy", 6)
+    came_b = halve_start(rows_b, "dp", 1)
+    rows_b = halve_end(rows_b, came_b)
+    came_b = halve_start(rows_b, "dp", 3)
+    rows = jnp.concatenate([halve_end(rows_a, came_a), halve_end(rows_b, came_b)], 1)
+    for flip in (1, 2):
+        rows = halve_end(rows, halve_start(rows, "gx", flip))
+    came = halve_start(rows, "gx", 4)
+    total = (rows[:3].astype(F32) + came.astype(F32)) * (1.0 / math.sqrt(512))
     grad_qkv = total[:, : 3 * D].reshape(3, GROUPS, 3, GW).transpose(0, 2, 1, 3)
     return out, grad, grad_qkv.reshape(3, 3 * D), total[:, 3 * D :]
 

time: 103 us -> 97.5 us (0.947)
  the two profiles are of different devices: /device:TPU:6 before, /device:TPU:8 now
where the time goes in v3:
time: 97.5 us; the launch traced here: 97.2 us
  waiting for transfers between devices  32.4 us (33%)
  starting transfers between devices  27.8 us (29%)
  Pallas kernels  26.2 us (27%)
  local copies, waits for them, and re-layouts  8.58 us (9%)
  other arithmetic  1.22 us (1%)
  between operations  1.03 us (1%)
    ppermute x20, waiting for transfers between devices, send(): lax.ppermute(value, axis, [(i, move(i) % devices) for i in range(devices)])  32.4 us
    ppermute x20, starting transfers between devices, send(): lax.ppermute(value, axis, [(i, move(i) % devices) for i in range(devices)])  21.9 us
    pallas_call x1, Pallas kernels, first_heads(): pl.pallas_call(first_kernel, grid=(2,), in_specs=[full((16, 32, D)), full...  10.9 us
    ppermute x1, starting transfers between devices, shards(): lax.ppermute(mine[:8, :8], ('gy', 'gx'), [(a * nx + b, (a - 1) % ny * nx...  5.92 us
    unnamed x16, local copies, waits for them, and re-layouts  5.12 us
    pallas_call x1, Pallas kernels, grad_part(): pl.pallas_call(grad_kernel, grid=(GROUPS,), in_specs=[full((2, CELLS, D))...  4.94 us
    pallas_call x1, Pallas kernels, last_heads(): pl.pallas_call(last_kernel, grid=(1,), in_specs=[full((2, CELLS, D)), ful...  4.37 us
    pallas_call x1, Pallas kernels, proj_grad(): pl.pallas_call(proj_kernel, out_shape=[shape, shape], compiler_params=plt...  2.05 us
  transfers between devices with their start and end apart: 21, of which 10 were waited for; matrix products, arithmetic and copies ran while one was open for 2% of the time, Pallas kernels for 16%

profile of v3, /device:TPU:8, one launch (start us, length us, event | category | flops | bytes accessed | tf_op | source)
XLA Modules:
  0.0 97.2 jit_solution(13834245598450228536)
XLA Ops:
  0.6 1.0 %slice.180 = bf16[8,24,768]{2,1,0:T(8,128)(2,1)S(1)} slice(bf16[16,32,768]{2,1,0:T(8,128)(2,1)} %bitcast.50), slice={[0:8], [8:32], [0:768]} | slice | bytes 589824 | tf_op jit(solution)/shard_map/slice | solution.py:397
  2.6 5.9 %collective-permute-start.2 = (bf16[8,8,768]{2,1,0:T(8,128)(2,1)S(1)}, bf16[8,8,768]{2,1,0:T(8,128)(2,1)S(1)}, u32[]{:S(2)}, u32[]{:S(2)}) collective-permute-start(bf16[8,8,768]{2,1,0:T(8,128)(2,1)S(1)} %get-tuple-element.88), channel_id=1, source_target_pairs={{0,63},{1,56},{2,57},{3,58},{4,59},{5,60},{6,61},{7,62},{8,7},{9,0... | collective-permute-start | bytes 294920 | tf_op jit(solution)/shard_map/ppermute | solution.py:400
  8.5 1.0 %collective-permute-start.1 = (bf16[8,8,768]{2,1,0:T(8,128)(2,1)S(1)}, bf16[8,8,768]{2,1,0:T(8,128)(2,1)S(1)}, u32[]{:S(2)}, u32[]{:S(2)}) collective-permute-start(bf16[8,8,768]{2,1,0:T(8,128)(2,1)S(1)} %get-tuple-element.89), channel_id=1, source_target_pairs={{0,7},{1,0},{2,1},{3,2},{4,3},{5,4},{6,5},{7,6},{8,15},{9,8},{10,9... | collective-permute-start | bytes 294920 | tf_op jit(solution)/shard_map/ppermute | solution.py:349
  9.5 1.3 %copy-done.3 = bf16[768,768]{1,0:T(8,128)(2,1)S(1)} copy-done((bf16[768,768]{1,0:T(8,128)(2,1)S(1)}, bf16[768,768]{1,0:T(8,128)(2,1)}, u32[]{:S(2)}) %copy-start.3) | copy-done | bytes 1179672
  10.8 1.1 %copy-done.5 = bf16[1,16,32,768]{3,2,1,0:T(8,128)(2,1)S(1)} copy-done((bf16[1,16,32,768]{3,2,1,0:T(8,128)(2,1)S(1)}, bf16[1,16,32,768]{3,2,1,0:T(8,128)(2,1)}, u32[]{:S(2)}) %copy-start.5) | copy-done | bytes 786456
  12.6 1.1 %branch.1 = (bf16[2,256,768]{2,1,0:T(8,128)(2,1)S(1)}, bf16[2,256,768]{2,1,0:T(8,128)(2,1)S(1)}, bf16[2,256,128]{2,1,0:T(8,128)(2,1)S(1)}, bf16[2,256,128]{2,1,0:T(8,128)(2,1)S(1)}) custom-call(bf16[16,2,16,768]{3,2,1,0:T(8,128)(2,1)S(1)} %bitcast.53, s32[16,32]{1,0:T(8,128)S(1)} %bitcast.55, bf16[768,768]{1,0:T(8,128)(2,1)S(1)} %copy-done.3), custom_call_target="tpu_custom_call" | custom-call | flops 600000000 | bytes 4000000 | tf_op jit(solution)/shard_map/branch/pallas_call | solution.py:62
  13.8 2.0 %copy-done.1 = bf16[768,2304]{1,0:T(8,128)(2,1)S(1)} copy-done((bf16[768,2304]{1,0:T(8,128)(2,1)S(1)}, bf16[768,2304]{1,0:T(8,128)(2,1)}, u32[]{:S(2)}) %copy-start.1) | copy-done | bytes 3538968
  15.8 10.9 %first_heads.1 = (bf16[384,1536]{1,0:T(8,128)(2,1)S(1)}, bf16[384,1536]{1,0:T(8,128)(2,1)S(1)}, bf16[2,256,512]{2,1,0:T(8,128)(2,1)S(1)}, bf16[2,2,256,768]{3,2,...) custom-call(bf16[16,32,768]{2,1,0:T(8,128)(2,1)S(1)} %bitcast.52, ...), custom_call_target="tpu_custom_call" | custom-call | flops 6000000000 | bytes 10000000 | tf_op jit(solution)/shard_map/first_heads/pallas_call | solution.py:233
  26.8 1.2 %turn.1.hid_t_ref = bf16[768,512]{1,0:T(8,128)(2,1)S(1)} custom-call(bf16[2,256,768]{2,1,0:T(8,128)(2,1)S(1)} %get-tuple-element.50.hid_ref), custom_call_target="tpu_custom_call" | custom-call | flops 2000000000 | bytes 2000000 | tf_op jit(solution)/shard_map/turn/pallas_call | solution.py:196
  28.0 1.7 %collective-permute-done.3 = bf16[384,1536]{1,0:T(8,128)(2,1)S(1)} collective-permute-done((bf16[384,1536]{1,0:T(8,128)(2,1)S(1)}, bf16[384,1536]{1,0:T(8,128)(2,1)S(1)}, u32[]{:S(2)}, u32[]{:S(2)}) %collective-permute-start.3) | collective-permute-done | bytes 1179680 | tf_op jit(solution)/shard_map/ppermute | solution.py:349
  30.0 1.6 %collective-permute-start.4 = (bf16[96,768]{1,0:T(8,128)(2,1)S(1)}, bf16[96,768]{1,0:T(8,128)(2,1)S(1)}, u32[]{:S(2)}, u32[]{:S(2)}) collective-permute-start(bf16[96,768]{1,0:T(8,128)(2,1)S(1)} %get-tuple-element.99), channel_id=1, source_target_pairs={{0,64},{64,128},{128,192},{192,0},{1,65},{65,129},{129,193},{193,1... | collective-permute-start | bytes 442376 | tf_op jit(solution)/shard_map/ppermute | solution.py:349
  31.6 2.0 %collective-permute-start.5 = (bf16[96,768]{1,0:T(8,128)(2,1)S(1)}, bf16[96,768]{1,0:T(8,128)(2,1)S(1)}, u32[]{:S(2)}, u32[]{:S(2)}) collective-permute-start(bf16[96,768]{1,0:T(8,128)(2,1)S(1)} %get-tuple-element.100), channel_id=1, source_target_pairs={{0,192},{64,0},{128,64},{192,128},{1,193},{65,1},{129,65},{193,129... | collective-permute-start | bytes 442376 | tf_op jit(solution)/shard_map/ppermute | solution.py:349
  33.6 4.4 %last_heads.1 = (bf16[384,768]{1,0:T(8,128)(2,1)S(1)}, bf16[384,768]{1,0:T(8,128)(2,1)S(1)}, bf16[2,256,256]{2,1,0:T(8,128)(2,1)S(1)}, bf16[1,2,256,768]{3,2,1,0:T(8,128)(2,1)S(1)}) custom-call(bf16[2,256,768]{2,1,0:T(8,128)(2,1)S(1)} %get-tuple-element.50.hid_ref, bf16[768,512]{1,0:T(8,128)(2,1)S(1)} %turn.1.hid_t_ref, ...), custom_call_target="tpu_custom_call" | custom-call | flops 4000000000 | bytes 6000000 | tf_op jit(solution)/shard_map/last_heads/pallas_call | solution.py:248
  38.1 2.1 %proj_grad.1 = (bf16[384,768]{1,0:T(8,128)(2,1)S(1)}, bf16[384,768]{1,0:T(8,128)(2,1)S(1)}) custom-call(bf16[2,256,512]{2,1,0:T(8,128)(2,1)S(1)} %get-tuple-element.62.att0_ref, bf16[2,256,256]{2,1,0:T(8,128)(2,1)S(1)} %get-tuple-element.73.att1_ref, bf16[2,256,768]{2,1,0:T(8,128)(2,1)S(1)} %get-tuple-element.64.db_ref), custom_call_target="tpu_custom_call" | custom-call | flops 2000000000 | bytes 4000000 | tf_op jit(solution)/shard_map/proj_grad/pallas_call | solution.py:268
  40.9 2.4 %collective-permute-start.7 = (bf16[96,1536]{1,0:T(8,128)(2,1)S(1)}, bf16[96,1536]{1,0:T(8,128)(2,1)S(1)}, u32[]{:S(2)}, u32[]{:S(2)}) collective-permute-start(bf16[96,1536]{1,0:T(8,128)(2,1)S(1)} %pad_maximum_fusion.1), channel_id=1, source_target_pairs={{0,192},{64,0},{128,64},{192,128},{1,193},{65,1},{129,65},{193,129... | collective-permute-start | bytes 884744 | tf_op jit(solution)/shard_map/ppermute | solution.py:349
  43.8 1.6 %collective-permute-start.10 = (bf16[96,768]{1,0:T(8,128)(2,1)S(1)}, bf16[96,768]{1,0:T(8,128)(2,1)S(1)}, u32[]{:S(2)}, u32[]{:S(2)}) collective-permute-start(bf16[96,768]{1,0:T(8,128)(2,1)S(1)} %get-tuple-element.93), channel_id=1, source_target_pairs={{0,16},{8,24},{16,32},{24,40},{32,48},{40,56},{48,0},{56,8},{1,17}... | collective-permute-start | bytes 442376 | tf_op jit(solution)/shard_map/ppermute | solution.py:349
  45.4 1.5 %collective-permute-start.11 = (bf16[96,768]{1,0:T(8,128)(2,1)S(1)}, bf16[96,768]{1,0:T(8,128)(2,1)S(1)}, u32[]{:S(2)}, u32[]{:S(2)}) collective-permute-start(bf16[96,768]{1,0:T(8,128)(2,1)S(1)} %get-tuple-element.95), channel_id=1, source_target_pairs={{0,48},{8,56},{16,0},{24,8},{32,16},{40,24},{48,32},{56,40},{1,49}... | collective-permute-start | bytes 442376 | tf_op jit(solution)/shard_map/ppermute | solution.py:349
  47.0 1.7 %out_part.1 = bf16[16,2,16,768]{3,2,1,0:T(8,128)(2,1)} custom-call(bf16[2,256,768]{2,1,0:T(8,128)(2,1)S(1)} %get-tuple-element.79.xw_ref, bf16[2,256,128]{2,1,0:T(8,128)(2,1)S(1)} %get-tuple-element.45.tis_ref, bf16[2,256,512]{2,1,0:T(8,128)(2,1)S(1)} %get-tuple-element.62.att0_ref, bf16[2,256,256]{2,1,0:T(8,128)(2,1)S(1)} %get-tuple-element.73.att1_ref, ...), custom_call_target="tpu_custom_call" | custom-call | flops 3000000000 | bytes 5000000 | tf_op jit(solution)/shard_map/out_part/pallas_call | solution.py:286
  48.6 1.3 %collective-permute-done.7 = bf16[96,1536]{1,0:T(8,128)(2,1)S(1)} collective-permute-done((bf16[96,1536]{1,0:T(8,128)(2,1)S(1)}, bf16[96,1536]{1,0:T(8,128)(2,1)S(1)}, u32[]{:S(2)}, u32[]{:S(2)}) %collective-permute-start.7) | collective-permute-done | bytes 294944 | tf_op jit(solution)/shard_map/ppermute | solution.py:349
  49.9 3.4 %collective-permute-done.6 = bf16[96,1536]{1,0:T(8,128)(2,1)S(1)} collective-permute-done((bf16[96,1536]{1,0:T(8,128)(2,1)S(1)}, bf16[96,1536]{1,0:T(8,128)(2,1)S(1)}, u32[]{:S(2)}, u32[]{:S(2)}) %collective-permute-start.6) | collective-permute-done | bytes 294944 | tf_op jit(solution)/shard_map/ppermute | solution.py:349
  53.5 3.1 %collective-permute-start.12 = (bf16[48,1536]{1,0:T(8,128)(2,1)S(1)}, bf16[48,1536]{1,0:T(8,128)(2,1)S(1)}, u32[]{:S(2)}, u32[]{:S(2)}) collective-permute-start(bf16[48,1536]{1,0:T(8,128)(2,1)S(1)} %fusion.13), channel_id=1, source_target_pairs={{0,16},{8,24},{16,0},{24,8},{32,48},{40,56},{48,32},{56,40},{1,17}... | collective-permute-start | bytes 442376 | tf_op jit(solution)/shard_map/ppermute | solution.py:349
  57.0 2.1 %collective-permute-start.13 = (bf16[96,1536]{1,0:T(8,128)(2,1)S(1)}, bf16[96,1536]{1,0:T(8,128)(2,1)S(1)}, u32[]{:S(2)}, u32[]{:S(2)}) collective-permute-start(bf16[96,1536]{1,0:T(8,128)(2,1)S(1)} %pad_maximum_fusion.2), channel_id=1, source_target_pairs={{0,16},{8,24},{16,32},{24,40},{32,48},{40,56},{48,0},{56,8},{1,17}... | collective-permute-start | bytes 884744 | tf_op jit(solution)/shard_map/ppermute | solution.py:349
  59.1 4.9 %grad_part.1 = bf16[16,2,16,768]{3,2,1,0:T(8,128)(2,1)} custom-call(bf16[2,256,768]{2,1,0:T(8,128)(2,1)S(1)} %get-tuple-element.79.xw_ref, bf16[16,2,16,768]{3,2,1,0:T(8,128)(2,1)S(1)} %bitcast.54, bf16[2,2,256,768]{3,2,1,0:T(8,128)(2,1)S(1)} %get-tuple-element.80.dqkv0_ref, bf16[1,2,256,768]{3,2,1,0:T(8,128)(2,1)S(1)} %get-tuple-element.81.dqkv1_ref, ...), custom_call_target="tpu_custom_call" | custom-call | flops 6000000000 | bytes 10000000 | tf_op jit(solution)/shard_map/grad_part/pallas_call | solution.py:328
  64.0 1.0 %collective-permute-done.14 = bf16[96,1536]{1,0:T(8,128)(2,1)S(1)} collective-permute-done((bf16[96,1536]{1,0:T(8,128)(2,1)S(1)}, bf16[96,1536]{1,0:T(8,128)(2,1)S(1)}, u32[]{:S(2)}, u32[]{:S(2)}) %collective-permute-start.14) | collective-permute-done | bytes 294944 | tf_op jit(solution)/shard_map/ppermute | solution.py:349
  65.1 1.0 %collective-permute-done.13 = bf16[96,1536]{1,0:T(8,128)(2,1)S(1)} collective-permute-done((bf16[96,1536]{1,0:T(8,128)(2,1)S(1)}, bf16[96,1536]{1,0:T(8,128)(2,1)S(1)}, u32[]{:S(2)}, u32[]{:S(2)}) %collective-permute-start.13) | collective-permute-done | bytes 294944 | tf_op jit(solution)/shard_map/ppermute | solution.py:349
  66.7 4.8 %collective-permute-done.16 = bf16[48,1536]{1,0:T(8,128)(2,1)S(1)} collective-permute-done((bf16[48,1536]{1,0:T(8,128)(2,1)S(1)}, bf16[48,1536]{1,0:T(8,128)(2,1)S(1)}, u32[]{:S(2)}, u32[]{:S(2)}) %collective-permute-start.16) | collective-permute-done | bytes 147488 | tf_op jit(solution)/shard_map/ppermute | solution.py:349
  71.9 5.3 %collective-permute-done.17 = bf16[24,1536]{1,0:T(8,128)(2,1)S(1)} collective-permute-done((bf16[24,1536]{1,0:T(8,128)(2,1)S(1)}, bf16[24,1536]{1,0:T(8,128)(2,1)S(1)}, u32[]{:S(2)}, u32[]{:S(2)}) %collective-permute-start.17) | collective-permute-done | bytes 73760 | tf_op jit(solution)/shard_map/ppermute | solution.py:349
  77.2 1.1 %collective-permute-start.18 = (bf16[12,3072]{1,0:T(8,128)(2,1)S(1)}, bf16[12,3072]{1,0:T(8,128)(2,1)S(1)}, u32[]{:S(2)}, u32[]{:S(2)}) collective-permute-start(bf16[12,3072]{1,0:T(8,128)(2,1)S(1)} %pad_maximum_fusion.6), channel_id=1, source_target_pairs={{0,1},{1,0},{2,3},{3,2},{4,5},{5,4},{6,7},{7,6},{8,9},{9,8},{10,11... | collective-permute-start | bytes 221192 | tf_op jit(solution)/shard_map/ppermute | solution.py:349
  78.3 4.1 %collective-permute-done.18 = bf16[12,3072]{1,0:T(8,128)(2,1)S(1)} collective-permute-done((bf16[12,3072]{1,0:T(8,128)(2,1)S(1)}, bf16[12,3072]{1,0:T(8,128)(2,1)S(1)}, u32[]{:S(2)}, u32[]{:S(2)}) %collective-permute-start.18) | collective-permute-done | bytes 73760 | tf_op jit(solution)/shard_map/ppermute | solution.py:349
  82.7 5.3 %collective-permute-done.19 = bf16[6,3072]{1,0:T(8,128)(2,1)S(1)} collective-permute-done((bf16[6,3072]{1,0:T(8,128)(2,1)S(1)}, bf16[6,3072]{1,0:T(8,128)(2,1)S(1)}, u32[]{:S(2)}, u32[]{:S(2)}) %collective-permute-start.19) | collective-permute-done | bytes 36896 | tf_op jit(solution)/shard_map/ppermute | solution.py:349
  88.1 3.3 %collective-permute-start.20 = (bf16[3,3072]{1,0:T(4,128)(2,1)S(1)}, bf16[3,3072]{1,0:T(4,128)(2,1)S(1)}, u32[]{:S(2)}, u32[]{:S(2)}) collective-permute-start(bf16[3,3072]{1,0:T(4,128)(2,1)S(1)} %slice.198), channel_id=1, source_target_pairs={{0,4},{1,5},{2,6},{3,7},{4,0},{5,1},{6,2},{7,3},{8,12},{9,13},{10,... | collective-permute-start | bytes 55304 | tf_op jit(solution)/shard_map/ppermute | solution.py:349
  91.4 4.5 %collective-permute-done.20 = bf16[3,3072]{1,0:T(4,128)(2,1)S(1)} collective-permute-done((bf16[3,3072]{1,0:T(4,128)(2,1)S(1)}, bf16[3,3072]{1,0:T(4,128)(2,1)S(1)}, u32[]{:S(2)}, u32[]{:S(2)}) %collective-permute-start.20) | collective-permute-done | bytes 18464 | tf_op jit(solution)/shard_map/ppermute | solution.py:349
  (72 shorter events, 6.6 us)
Async XLA Ops:
  1.6 12.2 %collective-permute-start = (bf16[8,24,768]{2,1,0:T(8,128)(2,1)S(1)}, bf16[8,24,768]{2,1,0:T(8,128)(2,1)S(1)}, u32[]{:S(2)}, u32[]{:S(2)}) collective-permute-start(bf16[8,24,768]{2,1,0:T(8,128)(2,1)S(1)} %slice.180), channel_id=1, source_target_pairs={{0,56},{8,0},{16,8},{24,16},{32,24},{40,32},{48,40},{56,48},{1,57}... | collective-permute-start | bytes 884744 | tf_op jit(solution)/shard_map/ppermute | solution.py:349
  2.6 11.2 %copy-start = (bf16[1,16,32,768]{3,2,1,0:T(8,128)(2,1)S(1)}, bf16[1,16,32,768]{3,2,1,0:T(8,128)(2,1)}, u32[]{:S(2)}) copy-start(bf16[1,16,32,768]{3,2,1,0:T(8,128)(2,1)} %param.5) | copy-start | bytes 2359300
  2.6 11.2 %collective-permute-start.2 = (bf16[8,8,768]{2,1,0:T(8,128)(2,1)S(1)}, bf16[8,8,768]{2,1,0:T(8,128)(2,1)S(1)}, u32[]{:S(2)}, u32[]{:S(2)}) collective-permute-start(bf16[8,8,768]{2,1,0:T(8,128)(2,1)S(1)} %get-tuple-element.88), channel_id=1, source_target_pairs={{0,63},{1,56},{2,57},{3,58},{4,59},{5,60},{6,61},{7,62},{8,7},{9,0... | collective-permute-start | bytes 294920 | tf_op jit(solution)/shard_map/ppermute | solution.py:400
  8.5 5.3 %collective-permute-start.1 = (bf16[8,8,768]{2,1,0:T(8,128)(2,1)S(1)}, bf16[8,8,768]{2,1,0:T(8,128)(2,1)S(1)}, u32[]{:S(2)}, u32[]{:S(2)}) collective-permute-start(bf16[8,8,768]{2,1,0:T(8,128)(2,1)S(1)} %get-tuple-element.89), channel_id=1, source_target_pairs={{0,7},{1,0},{2,1},{3,2},{4,3},{5,4},{6,5},{7,6},{8,15},{9,8},{10,9... | collective-permute-start | bytes 294920 | tf_op jit(solution)/shard_map/ppermute | solution.py:349
  9.5 1.3 %copy-start.3 = (bf16[768,768]{1,0:T(8,128)(2,1)S(1)}, bf16[768,768]{1,0:T(8,128)(2,1)}, u32[]{:S(2)}) copy-start(bf16[768,768]{1,0:T(8,128)(2,1)} %wp_ref.3) | copy-start | bytes 3538948
  10.8 1.1 %copy-start.5 = (bf16[1,16,32,768]{3,2,1,0:T(8,128)(2,1)S(1)}, bf16[1,16,32,768]{3,2,1,0:T(8,128)(2,1)}, u32[]{:S(2)}) copy-start(bf16[1,16,32,768]{3,2,1,0:T(8,128)(2,1)} %param.6) | copy-start | bytes 2359300
  12.0 0.7 copy-start.7
  13.8 2.0 %copy-start.1 = (bf16[768,2304]{1,0:T(8,128)(2,1)S(1)}, bf16[768,2304]{1,0:T(8,128)(2,1)}, u32[]{:S(2)}) copy-start(bf16[768,2304]{1,0:T(8,128)(2,1)} %wv_ref.5) | copy-start | bytes 10616836
  26.7 2.9 %collective-permute-start.3 = (bf16[384,1536]{1,0:T(8,128)(2,1)S(1)}, bf16[384,1536]{1,0:T(8,128)(2,1)S(1)}, u32[]{:S(2)}, u32[]{:S(2)}) collective-permute-start(bf16[384,1536]{1,0:T(8,128)(2,1)S(1)} %get-tuple-element.49), channel_id=1, source_target_pairs={{0,8},{8,0},{16,24},{24,16},{32,40},{40,32},{48,56},{56,48},{1,9},... | collective-permute-start | bytes 3538952 | tf_op jit(solution)/shard_map/ppermute | solution.py:349
  29.9 3.7 %copy-start.2 = (bf16[768,2304]{1,0:T(8,128)(2,1)S(1)}, bf16[768,2304]{1,0:T(8,128)(2,1)}, u32[]{:S(2)}) copy-start(bf16[768,2304]{1,0:T(8,128)(2,1)} %wv_ref.5) | copy-start | bytes 10616836
  30.0 8.0 %collective-permute-start.4 = (bf16[96,768]{1,0:T(8,128)(2,1)S(1)}, bf16[96,768]{1,0:T(8,128)(2,1)S(1)}, u32[]{:S(2)}, u32[]{:S(2)}) collective-permute-start(bf16[96,768]{1,0:T(8,128)(2,1)S(1)} %get-tuple-element.99), channel_id=1, source_target_pairs={{0,64},{64,128},{128,192},{192,0},{1,65},{65,129},{129,193},{193,1... | collective-permute-start | bytes 442376 | tf_op jit(solution)/shard_map/ppermute | solution.py:349
  31.6 6.4 %collective-permute-start.5 = (bf16[96,768]{1,0:T(8,128)(2,1)S(1)}, bf16[96,768]{1,0:T(8,128)(2,1)S(1)}, u32[]{:S(2)}, u32[]{:S(2)}) collective-permute-start(bf16[96,768]{1,0:T(8,128)(2,1)S(1)} %get-tuple-element.100), channel_id=1, source_target_pairs={{0,192},{64,0},{128,64},{192,128},{1,193},{65,1},{129,65},{193,129... | collective-permute-start | bytes 442376 | tf_op jit(solution)/shard_map/ppermute | solution.py:349
  38.0 2.3 %collective-permute-start.8 = (bf16[384,768]{1,0:T(8,128)(2,1)S(1)}, bf16[384,768]{1,0:T(8,128)(2,1)S(1)}, u32[]{:S(2)}, u32[]{:S(2)}) collective-permute-start(bf16[384,768]{1,0:T(8,128)(2,1)S(1)} %get-tuple-element.61), channel_id=1, source_target_pairs={{0,8},{8,0},{16,24},{24,16},{32,40},{40,32},{48,56},{56,48},{1,9},... | collective-permute-start | bytes 1769480 | tf_op jit(solution)/shard_map/ppermute | solution.py:349
  40.3 3.3 %collective-permute-start.9 = (bf16[384,768]{1,0:T(8,128)(2,1)S(1)}, bf16[384,768]{1,0:T(8,128)(2,1)S(1)}, u32[]{:S(2)}, u32[]{:S(2)}) collective-permute-start(bf16[384,768]{1,0:T(8,128)(2,1)S(1)} %get-tuple-element.69), channel_id=1, source_target_pairs={{0,8},{8,0},{16,24},{24,16},{32,40},{40,32},{48,56},{56,48},{1,9},... | collective-permute-start | bytes 1769480 | tf_op jit(solution)/shard_map/ppermute | solution.py:349
  40.9 9.0 %collective-permute-start.7 = (bf16[96,1536]{1,0:T(8,128)(2,1)S(1)}, bf16[96,1536]{1,0:T(8,128)(2,1)S(1)}, u32[]{:S(2)}, u32[]{:S(2)}) collective-permute-start(bf16[96,1536]{1,0:T(8,128)(2,1)S(1)} %pad_maximum_fusion.1), channel_id=1, source_target_pairs={{0,192},{64,0},{128,64},{192,128},{1,193},{65,1},{129,65},{193,129... | collective-permute-start | bytes 884744 | tf_op jit(solution)/shard_map/ppermute | solution.py:349
  43.3 9.9 %collective-permute-start.6 = (bf16[96,1536]{1,0:T(8,128)(2,1)S(1)}, bf16[96,1536]{1,0:T(8,128)(2,1)S(1)}, u32[]{:S(2)}, u32[]{:S(2)}) collective-permute-start(bf16[96,1536]{1,0:T(8,128)(2,1)S(1)} %pad_maximum_fusion), channel_id=1, source_target_pairs={{0,64},{64,128},{128,192},{192,0},{1,65},{65,129},{129,193},{193,1... | collective-permute-start | bytes 884744 | tf_op jit(solution)/shard_map/ppermute | solution.py:349
  43.6 3.4 %copy-start.4 = (bf16[768,768]{1,0:T(8,128)(2,1)S(1)}, bf16[768,768]{1,0:T(8,128)(2,1)}, u32[]{:S(2)}) copy-start(bf16[768,768]{1,0:T(8,128)(2,1)} %wp_ref.3) | copy-start | bytes 3538948
  43.8 9.5 %collective-permute-start.10 = (bf16[96,768]{1,0:T(8,128)(2,1)S(1)}, bf16[96,768]{1,0:T(8,128)(2,1)S(1)}, u32[]{:S(2)}, u32[]{:S(2)}) collective-permute-start(bf16[96,768]{1,0:T(8,128)(2,1)S(1)} %get-tuple-element.93), channel_id=1, source_target_pairs={{0,16},{8,24},{16,32},{24,40},{32,48},{40,56},{48,0},{56,8},{1,17}... | collective-permute-start | bytes 442376 | tf_op jit(solution)/shard_map/ppermute | solution.py:349
  45.4 7.8 %collective-permute-start.11 = (bf16[96,768]{1,0:T(8,128)(2,1)S(1)}, bf16[96,768]{1,0:T(8,128)(2,1)S(1)}, u32[]{:S(2)}, u32[]{:S(2)}) collective-permute-start(bf16[96,768]{1,0:T(8,128)(2,1)S(1)} %get-tuple-element.95), channel_id=1, source_target_pairs={{0,48},{8,56},{16,0},{24,8},{32,16},{40,24},{48,32},{56,40},{1,49}... | collective-permute-start | bytes 442376 | tf_op jit(solution)/shard_map/ppermute | solution.py:349
  53.4 5.7 %copy-start.6 = (bf16[1,16,32,768]{3,2,1,0:T(8,128)(2,1)S(1)}, bf16[1,16,32,768]{3,2,1,0:T(8,128)(2,1)}, u32[]{:S(2)}) copy-start(bf16[1,16,32,768]{3,2,1,0:T(8,128)(2,1)} %param.6) | copy-start | bytes 2359300
  53.5 10.5 %collective-permute-start.12 = (bf16[48,1536]{1,0:T(8,128)(2,1)S(1)}, bf16[48,1536]{1,0:T(8,128)(2,1)S(1)}, u32[]{:S(2)}, u32[]{:S(2)}) collective-permute-start(bf16[48,1536]{1,0:T(8,128)(2,1)S(1)} %fusion.13), channel_id=1, source_target_pairs={{0,16},{8,24},{16,0},{24,8},{32,48},{40,56},{48,32},{56,40},{1,17}... | collective-permute-start | bytes 442376 | tf_op jit(solution)/shard_map/ppermute | solution.py:349
  56.6 8.4 %collective-permute-start.14 = (bf16[96,1536]{1,0:T(8,128)(2,1)S(1)}, bf16[96,1536]{1,0:T(8,128)(2,1)S(1)}, u32[]{:S(2)}, u32[]{:S(2)}) collective-permute-start(bf16[96,1536]{1,0:T(8,128)(2,1)S(1)} %pad_maximum_fusion.3), channel_id=1, source_target_pairs={{0,48},{8,56},{16,0},{24,8},{32,16},{40,24},{48,32},{56,40},{1,49}... | collective-permute-start | bytes 884744 | tf_op jit(solution)/shard_map/ppermute | solution.py:349
  57.0 9.1 %collective-permute-start.13 = (bf16[96,1536]{1,0:T(8,128)(2,1)S(1)}, bf16[96,1536]{1,0:T(8,128)(2,1)S(1)}, u32[]{:S(2)}, u32[]{:S(2)}) collective-permute-start(bf16[96,1536]{1,0:T(8,128)(2,1)S(1)} %pad_maximum_fusion.2), channel_id=1, source_target_pairs={{0,16},{8,24},{16,32},{24,40},{32,48},{40,56},{48,0},{56,8},{1,17}... | collective-permute-start | bytes 884744 | tf_op jit(solution)/shard_map/ppermute | solution.py:349
  66.2 5.2 %collective-permute-start.16 = (bf16[48,1536]{1,0:T(8,128)(2,1)S(1)}, bf16[48,1536]{1,0:T(8,128)(2,1)S(1)}, u32[]{:S(2)}, u32[]{:S(2)}) collective-permute-start(bf16[48,1536]{1,0:T(8,128)(2,1)S(1)} %pad_maximum_fusion.4), channel_id=1, source_target_pairs={{0,64},{64,0},{128,192},{192,128},{1,65},{65,1},{129,193},{193,129... | collective-permute-start | bytes 442376 | tf_op jit(solution)/shard_map/ppermute | solution.py:349
  66.4 5.5 %collective-permute-start.15 = (bf16[24,1536]{1,0:T(8,128)(2,1)S(1)}, bf16[24,1536]{1,0:T(8,128)(2,1)S(1)}, u32[]{:S(2)}, u32[]{:S(2)}) collective-permute-start(bf16[24,1536]{1,0:T(8,128)(2,1)S(1)} %slice.188), channel_id=1, source_target_pairs={{0,48},{8,56},{16,32},{24,40},{32,16},{40,24},{48,0},{56,8},{1,49}... | collective-permute-start | bytes 221192 | tf_op jit(solution)/shard_map/ppermute | solution.py:349
  71.5 5.7 %collective-permute-start.17 = (bf16[24,1536]{1,0:T(8,128)(2,1)S(1)}, bf16[24,1536]{1,0:T(8,128)(2,1)S(1)}, u32[]{:S(2)}, u32[]{:S(2)}) collective-permute-start(bf16[24,1536]{1,0:T(8,128)(2,1)S(1)} %slice.192), channel_id=1, source_target_pairs={{0,192},{64,128},{128,64},{192,0},{1,193},{65,129},{129,65},{193,1... | collective-permute-start | bytes 221192 | tf_op jit(solution)/shard_map/ppermute | solution.py:349
  77.2 5.2 %collective-permute-start.18 = (bf16[12,3072]{1,0:T(8,128)(2,1)S(1)}, bf16[12,3072]{1,0:T(8,128)(2,1)S(1)}, u32[]{:S(2)}, u32[]{:S(2)}) collective-permute-start(bf16[12,3072]{1,0:T(8,128)(2,1)S(1)} %pad_maximum_fusion.6), channel_id=1, source_target_pairs={{0,1},{1,0},{2,3},{3,2},{4,5},{5,4},{6,7},{7,6},{8,9},{9,8},{10,11... | collective-permute-start | bytes 221192 | tf_op jit(solution)/shard_map/ppermute | solution.py:349
  82.5 5.5 %collective-permute-start.19 = (bf16[6,3072]{1,0:T(8,128)(2,1)S(1)}, bf16[6,3072]{1,0:T(8,128)(2,1)S(1)}, u32[]{:S(2)}, u32[]{:S(2)}) collective-permute-start(bf16[6,3072]{1,0:T(8,128)(2,1)S(1)} %slice.196), channel_id=1, source_target_pairs={{0,2},{1,3},{2,0},{3,1},{4,6},{5,7},{6,4},{7,5},{8,10},{9,11},{10,... | collective-permute-start | bytes 110600 | tf_op jit(solution)/shard_map/ppermute | solution.py:349
  88.1 7.8 %collective-permute-start.20 = (bf16[3,3072]{1,0:T(4,128)(2,1)S(1)}, bf16[3,3072]{1,0:T(4,128)(2,1)S(1)}, u32[]{:S(2)}, u32[]{:S(2)}) collective-permute-start(bf16[3,3072]{1,0:T(4,128)(2,1)S(1)} %slice.198), channel_id=1, source_target_pairs={{0,4},{1,5},{2,6},{3,7},{4,0},{5,1},{6,2},{7,3},{8,12},{9,13},{10,... | collective-permute-start | bytes 55304 | tf_op jit(solution)/shard_map/ppermute | solution.py:349

commit v4 on v3

--- a/solution.py
+++ b/solution.py
@@ -38,13 +38,25 @@
     return pl.CostEstimate(flops=int(flops), bytes_accessed=int(size), transcendentals=0)
 
 
-def branch_kernel(cot_ref, tissue_ref, wp_ref, db_ref, da_ref, tis_ref, live_ref):
+def branch_kernel(
+    cot_hbm, tissue_hbm, wp_hbm, db_ref, da_ref, tis_ref, live_ref, cot_ref, tissue_ref, wp_ref, sem
+):
+    copies = [
+        pltpu.make_async_copy(tissue_hbm, tissue_ref, sem.at[0]),
+        pltpu.make_async_copy(cot_hbm, cot_ref, sem.at[1]),
+        pltpu.make_async_copy(wp_hbm, wp_ref, sem.at[2]),
+    ]
+    for copy in copies:
+        copy.start()
+    copies[0].wait()
     grid = tissue_ref[...].astype(F32).astype(BF)
     cell = lax.broadcasted_iota(jnp.int32, (CELLS, 1), 0)
     row_of = lax.broadcasted_iota(jnp.int32, (CELLS, WIN), 1) == (cell >> 4)
     rows = nn(row_of.astype(F32).astype(BF), grid)
     lane = lax.broadcasted_iota(jnp.int32, (CELLS, 2 * WIN), 1)
     ones = jnp.ones((2 * WIN, 128), BF)
+    copies[1].wait()
+    copies[2].wait()
     for w in range(2):
         own = jnp.where(lane == (cell & 15) + w * WIN, rows, 0.0).astype(BF)
         tis = nn(own, ones)
@@ -61,9 +73,16 @@
     mask = jax.ShapeDtypeStruct((2, CELLS, 128), BF)
     return pl.pallas_call(
         branch_kernel,
+        in_specs=[pl.BlockSpec(memory_space=pltpu.HBM)] * 3,
         out_shape=[shape, shape, mask, mask],
-        compiler_params=pltpu.CompilerParams(vmem_limit_bytes=VMEM),
-        cost_estimate=cost(6e8, 4e6),
+        scratch_shapes=[
+            pltpu.VMEM((WIN, 2, WIN, D), BF),
+            pltpu.VMEM((WIN, 2 * WIN), jnp.int32),
+            pltpu.VMEM((D, D), BF),
+            pltpu.SemaphoreType.DMA((3,)),
+        ],
+        compiler_params=pltpu.CompilerParams(vmem_limit_bytes=VMEM),
+        cost_estimate=cost(2e10, 4e6),
         name="branch",
     )(cot, tissue, w_proj)
 
@@ -73,15 +92,14 @@
     dp, y, core, gx = lax.axis_index("dp"), gy >> 1, gy & 1, lax.axis_index("gx")
     at = lax.broadcasted_iota(jnp.int32, (D, 1), 0)
     third = ((at.astype(F32) + 0.5) * (1.0 / 3)).astype(jnp.int32)
-    bit = [(third >> i) & 1 for i in range(8)]
-    z_of = gx ^ (bit[0] * 4 + bit[1] * 2 + bit[2])
-    distance = bit[6] * 2 + bit[5]
-    partner = bit[4] ^ (bit[3] * 3)
+    outer, inner, depth = (third >> 5) & 3, (third >> 3) & 3, third & 7
     if first == "dp":
-        dp_of, y_of = (distance + dp) & 3, partner ^ y
+        dp_of = (outer + dp) & 3
+        y_of = ((inner >> 1) ^ ((inner & 1) * 3)) ^ y
+        z_of = (depth + gx) & 7
     else:
-        dp_of, y_of = partner ^ dp, (distance + y) & 3
-    core_of = bit[7] ^ core
+        dp_of, y_of, z_of = inner, outer, depth
+    core_of = (third >> 7) ^ core
     source = ((dp_of * 8 + y_of * 2 + core_of) * 8 + z_of) * 3 + at - third * 3
     column = lax.broadcasted_iota(jnp.int32, (D, D), 1)
     return jnp.where(column == source, 1.0, 0.0).astype(BF)
@@ -287,7 +305,7 @@
         out_kernel,
         out_shape=jax.ShapeDtypeStruct((WIN, 2, WIN, D), BF),
         compiler_params=pltpu.CompilerParams(vmem_limit_bytes=VMEM),
-        cost_estimate=cost(3e9, 5e6),
+        cost_estimate=cost(1e3, 1e3),
         name="out_part",
     )(xw, tis, att0, att1, w_proj)
     return out.reshape(1, WIN, 2 * WIN, D)
@@ -338,7 +356,7 @@
         out_shape=jax.ShapeDtypeStruct((WIN, 2, WIN, D), BF),
         scratch_shapes=[pltpu.VMEM((2 * CELLS, D), F32)],
         compiler_params=pltpu.CompilerParams(vmem_limit_bytes=VMEM),
-        cost_estimate=cost(6e9, 10e6),
+        cost_estimate=cost(1e3, 1e3),
         name="grad_part",
     )(xw, cot, dqkv0, dqkv1, w_qkv, w_qkv, w_qkv)
     return grad.reshape(1, WIN, 2 * WIN, D)
@@ -382,6 +400,12 @@
 
 def halve_end(rows, came):
     return add(rows[: rows.shape[0] // 2], came)
+
+
+def exchange(rows, axis, groups=None):
+    parts = len(groups[0]) if groups else math.prod(lax.axis_size(a) for a in axis)
+    rows = rows.reshape(parts, rows.shape[0] // parts, rows.shape[1])
+    return lax.all_to_all(rows, axis, 0, 0, axis_index_groups=groups)
 
 
 def tie(*values):
@@ -424,30 +448,28 @@
     came = send(send1, "gy", lambda i: i ^ 1)
     keep2, send2 = proj_grad(att0, att1, db)
     came, send2, keep2 = tie(came, send2, keep2)
-    low_b = add(keep1, came)
-    high_b = add(keep2, send(send2, "gy", lambda i: i ^ 1))
-    low_b, high_b, att1 = tie(blocks(low_b), blocks(high_b), att1)
-    came_b = ring_start(low_b, high_b, "gy", 2)
+    rows_b = jnp.concatenate([add(keep1, came), add(keep2, send(send2, "gy", lambda i: i ^ 1))], 1)
+    rows_b, att1 = tie(rows_b, att1)
+    same_core = [[0, 2, 4, 6], [1, 3, 5, 7]]
+    parts_b = exchange(rows_b, "gy", same_core)
     out = out_part(xw, tis, att0, att1, w_proj)
-    came_a, came_b, out, xw = tie(came_a, came_b, out, xw)
     rows_a = ring_end(low_a, high_a, came_a)
-    came_b = ring_pass(low_b, high_b, came_b, "gy", 2)
     came_a = halve_start(rows_a, "gy", 2)
     grad = grad_part(xw, cot, dqkv0, dqkv1, w_qkv)
-    came_a, came_b, grad = tie(came_a, came_b, grad)
+    came_a, out, grad, parts_b = tie(came_a, out, grad, parts_b)
     rows_a = halve_end(rows_a, came_a)
-    rows_b = ring_end(low_b, high_b, came_b)
-    came_a = halve_start(rows_a, "gy", 6)
-    came_b = halve_start(rows_b, "dp", 1)
-    rows_b = halve_end(rows_b, came_b)
-    came_b = halve_start(rows_b, "dp", 3)
-    rows = jnp.concatenate([halve_end(rows_a, came_a), halve_end(rows_b, came_b)], 1)
-    for flip in (1, 2):
-        rows = halve_end(rows, halve_start(rows, "gx", flip))
-    came = halve_start(rows, "gx", 4)
-    total = (rows[:3].astype(F32) + came.astype(F32)) * (1.0 / math.sqrt(512))
-    grad_qkv = total[:, : 3 * D].reshape(3, GROUPS, 3, GW).transpose(0, 2, 1, 3)
-    return out, grad, grad_qkv.reshape(3, 3 * D), total[:, 3 * D :]
+    rows_a = halve_end(rows_a, halve_start(rows_a, "gy", 6))
+    rows_b, rows_a = tie(add(*parts_b), rows_a)
+    parts_b = exchange(rows_b, ("dp", "gx"))
+    rows_a = rows_a.reshape(8, 3, -1)
+    total_a = rows_a[0].astype(F32)
+    for d in range(1, 8):
+        total_a = total_a + send(rows_a[d], "gx", lambda j: j + d).astype(F32)
+    scale = 1.0 / math.sqrt(512)
+    total_b = jnp.sum(parts_b.astype(F32), 0) * scale
+    total = jnp.concatenate([total_a * scale, total_b[:, :D]], 1)
+    grad_qkv = total.reshape(3, GROUPS, 3, GW).transpose(0, 2, 1, 3)
+    return out, grad, grad_qkv.reshape(3, 3 * D), total_b[:, D:]
 
 
 def solution(mesh):

time: 97.5 us -> 105 us (1.077)
  the two profiles are of different devices: /device:TPU:8 before, /device:TPU:6 now
where the time goes in v4:
time: 105 us; the launch traced here: 104 us
  starting transfers between devices  45.9 us (44%)
  Pallas kernels  25.8 us (25%)
  local copies, waits for them, and re-layouts  12 us (11%)
  waiting for transfers between devices  11.7 us (11%)
  other arithmetic  7.16 us (7%)
  between operations  1.05 us (1%)
    ppermute x18, starting transfers between devices, send(): lax.ppermute(value, axis, [(i, move(i) % devices) for i in range(devices)])  28.2 us
    ppermute x18, waiting for transfers between devices, send(): lax.ppermute(value, axis, [(i, move(i) % devices) for i in range(devices)])  11.7 us
    pallas_call x1, Pallas kernels, first_heads(): pl.pallas_call(first_kernel, grid=(2,), in_specs=[full((16, 32, D)), full...  10.7 us
    all_to_all x2, starting transfers between devices, exchange(): return lax.all_to_all(rows, axis, 0, 0, axis_index_groups=groups)  9.88 us
    ppermute x1, starting transfers between devices, shards(): lax.ppermute(mine[:8, :8], ('gy', 'gx'), [(a * nx + b, (a - 1) % ny * nx...  7.82 us
    unnamed x50, local copies, waits for them, and re-layouts  7.65 us
    pallas_call x1, Pallas kernels, grad_part(): pl.pallas_call(grad_kernel, grid=(GROUPS,), in_specs=[full((2, CELLS, D))...  4.97 us
    pallas_call x1, Pallas kernels, last_heads(): pl.pallas_call(last_kernel, grid=(1,), in_specs=[full((2, CELLS, D)), ful...  4.36 us
  transfers between devices with their start and end apart: 21, of which 8 were waited for; matrix products, arithmetic and copies ran while one was open for 7% of the time, Pallas kernels for 15%

profile of v4, /device:TPU:6, one launch (start us, length us, event | category | flops | bytes accessed | tf_op | source)
XLA Modules:
  0.0 103.6 jit_solution(2371571055116419549)
XLA Ops:
  1.6 7.8 %collective-permute-start.2 = (bf16[8,8,768]{2,1,0:T(8,128)(2,1)S(1)}, bf16[8,8,768]{2,1,0:T(8,128)(2,1)S(1)}, u32[]{:S(2)}, u32[]{:S(2)}) collective-permute-start(bf16[8,8,768]{2,1,0:T(8,128)(2,1)S(1)} %get-tuple-element.78), channel_id=1, source_target_pairs={{0,63},{1,56},{2,57},{3,58},{4,59},{5,60},{6,61},{7,62},{8,7},{9,0... | collective-permute-start | bytes 294920 | tf_op jit(solution)/shard_map/ppermute | solution.py:424
  9.4 1.0 collective-permute-start.1
  12.0 1.3 %copy-done.5 = bf16[768,768]{1,0:T(8,128)(2,1)S(1)} copy-done((bf16[768,768]{1,0:T(8,128)(2,1)S(1)}, bf16[768,768]{1,0:T(8,128)(2,1)}, u32[]{:S(2)}) %copy-start.5) | copy-done | bytes 1179672
  13.3 1.1 %copy-done.7 = bf16[1,16,32,768]{3,2,1,0:T(8,128)(2,1)S(1)} copy-done((bf16[1,16,32,768]{3,2,1,0:T(8,128)(2,1)S(1)}, bf16[1,16,32,768]{3,2,1,0:T(8,128)(2,1)}, u32[]{:S(2)}) %copy-start.7) | copy-done | bytes 786456
  15.1 1.5 %branch.1 = (bf16[2,256,768]{2,1,0:T(8,128)(2,1)S(1)}, bf16[2,256,768]{2,1,0:T(8,128)(2,1)S(1)}, bf16[2,256,128]{2,1,0:T(8,128)(2,1)S(1)}, bf16[2,256,128]{2,1,0:T(8,128)(2,1)S(1)}) custom-call(bf16[16,2,16,768]{3,2,1,0:T(8,128)(2,1)S(1)} %bitcast.31, s32[16,32]{1,0:T(8,128)S(1)} %bitcast.36, bf16[768,768]{1,0:T(8,128)(2,1)S(1)} %copy-done.5), custom_call_target="tpu_custom_call" | custom-call | flops 20000000000 | bytes 4000000 | tf_op jit(solution)/shard_map/branch/pallas_call | solution.py:74
  17.3 10.7 %first_heads.1 = (bf16[384,1536]{1,0:T(8,128)(2,1)S(1)}, bf16[384,1536]{1,0:T(8,128)(2,1)S(1)}, bf16[2,256,512]{2,1,0:T(8,128)(2,1)S(1)}, bf16[2,2,256,768]{3,2,...) custom-call(bf16[16,32,768]{2,1,0:T(8,128)(2,1)S(1)} %bitcast.35, ...), custom_call_target="tpu_custom_call" | custom-call | flops 6000000000 | bytes 10000000 | tf_op jit(solution)/shard_map/first_heads/pallas_call | solution.py:251
  29.4 1.5 %collective-permute-done.3 = bf16[384,1536]{1,0:T(8,128)(2,1)S(1)} collective-permute-done((bf16[384,1536]{1,0:T(8,128)(2,1)S(1)}, bf16[384,1536]{1,0:T(8,128)(2,1)S(1)}, u32[]{:S(2)}, u32[]{:S(2)}) %collective-permute-start.3) | collective-permute-done | bytes 1179680 | tf_op jit(solution)/shard_map/ppermute | solution.py:367
  31.9 1.8 %collective-permute-start.5 = (bf16[96,768]{1,0:T(8,128)(2,1)S(1)}, bf16[96,768]{1,0:T(8,128)(2,1)S(1)}, u32[]{:S(2)}, u32[]{:S(2)}) collective-permute-start(bf16[96,768]{1,0:T(8,128)(2,1)S(1)} %get-tuple-element.83), channel_id=1, source_target_pairs={{0,192},{64,0},{128,64},{192,128},{1,193},{65,1},{129,65},{193,129... | collective-permute-start | bytes 442376 | tf_op jit(solution)/shard_map/ppermute | solution.py:367
  33.7 4.4 %last_heads.1 = (bf16[384,768]{1,0:T(8,128)(2,1)S(1)}, bf16[384,768]{1,0:T(8,128)(2,1)S(1)}, bf16[2,256,256]{2,1,0:T(8,128)(2,1)S(1)}, bf16[1,2,256,768]{3,2,1,0:T(8,128)(2,1)S(1)}) custom-call(bf16[2,256,768]{2,1,0:T(8,128)(2,1)S(1)} %get-tuple-element.45.hid_ref, bf16[768,512]{1,0:T(8,128)(2,1)S(1)} %turn.1.hid_t_ref, ...), custom_call_target="tpu_custom_call" | custom-call | flops 4000000000 | bytes 6000000 | tf_op jit(solution)/shard_map/last_heads/pallas_call | solution.py:266
  39.1 1.8 %proj_grad.1 = (bf16[384,768]{1,0:T(8,128)(2,1)S(1)}, bf16[384,768]{1,0:T(8,128)(2,1)S(1)}) custom-call(bf16[2,256,512]{2,1,0:T(8,128)(2,1)S(1)} %get-tuple-element.56.att0_ref, bf16[2,256,256]{2,1,0:T(8,128)(2,1)S(1)} %get-tuple-element.66.att1_ref, bf16[2,256,768]{2,1,0:T(8,128)(2,1)S(1)} %get-tuple-element.60.db_ref), custom_call_target="tpu_custom_call" | custom-call | flops 2000000000 | bytes 4000000 | tf_op jit(solution)/shard_map/proj_grad/pallas_call | solution.py:286
  43.9 2.4 %collective-permute-start.6 = (bf16[96,1536]{1,0:T(8,128)(2,1)}, bf16[96,1536]{1,0:T(8,128)(2,1)}, u32[]{:S(2)}, u32[]{:S(2)}) collective-permute-start(bf16[96,1536]{1,0:T(8,128)(2,1)} %pad_maximum_fusion.1), channel_id=1, source_target_pairs={{0,64},{64,128},{128,192},{192,0},{1,65},{65,129},{129,193},{193,1... | collective-permute-start | bytes 884744 | tf_op jit(solution)/shard_map/ppermute | solution.py:367
  46.6 1.1 %pad_maximum_fusion = bf16[384,1536]{1,0:T(8,128)(2,1)} fusion(bf16[384,768]{1,0:T(8,128)(2,1)S(1)} %add_convert_fusion.1, bf16[384,768]{1,0:T(8,128)(2,1)S(1)} %add_convert_fusion.2), kind=kLoop, calls=%fused_computation.1 | loop fusion | flops 2359296 | bytes 2359296 | tf_op jit(solution)/shard_map/concatenate | solution.py:451
  47.7 4.3 %all-to-all-start = ((bf16[4,96,1536]{2,1,0:T(8,128)(2,1)}), bf16[4,96,1536]{2,1,0:T(8,128)(2,1)}, u32[]{:S(2)}, u32[]{:S(2)}) async-start(bf16[4,96,1536]{2,1,0:T(8,128)(2,1)} %bitcast.37), calls=%async_computation | async-start | bytes 2359296 | tf_op jit(solution)/shard_map/all_to_all | solution.py:408
  52.9 1.4 %fusion.2 = (bf16[96,768]{1,0:T(8,128)(2,1)S(1)}, bf16[96,768]{1,0:T(8,128)(2,1)S(1)}) fusion(bf16[96,1536]{1,0:T(8,128)(2,1)} %collective-permute-done.7, bf16[96,1536]{1,0:T(8,128)(2,1)} %collective-permute-done.6, bf16[4,96,768]{2,1,0:T(8,128)(2,1)} %bitcast.40, bf16[4,96,768]{2,1,0:T(8,128)(2,1)} %bitcast.43), kind=kLoop, calls=%fused_computation.13 | loop fusion | flops 884736 | bytes 1179648 | tf_op jit(solution)/shard_map/convert_element_type | solution.py:374
  54.3 1.3 %collective-permute-start.8 = (bf16[48,1536]{1,0:T(8,128)(2,1)S(1)}, bf16[48,1536]{1,0:T(8,128)(2,1)}, u32[]{:S(2)}, u32[]{:S(2)}) collective-permute-start(bf16[48,1536]{1,0:T(8,128)(2,1)S(1)} %fusion.7), channel_id=1, source_target_pairs={{0,16},{8,24},{16,0},{24,8},{32,48},{40,56},{48,32},{56,40},{1,17}... | collective-permute-start | bytes 442376 | tf_op jit(solution)/shard_map/ppermute | solution.py:367
  55.6 1.4 %copy-done.4 = bf16[2,2,256,768]{3,2,1,0:T(8,128)(2,1)S(1)} copy-done((bf16[2,2,256,768]{3,2,1,0:T(8,128)(2,1)S(1)}, bf16[2,2,256,768]{3,2,1,0:T(8,128)(2,1)}, u32[]{:S(2)}) %copy-start.4) | copy-done | bytes 1572888
  57.0 1.1 %copy-done.10 = bf16[1,2,256,768]{3,2,1,0:T(8,128)(2,1)S(1)} copy-done((bf16[1,2,256,768]{3,2,1,0:T(8,128)(2,1)S(1)}, bf16[1,2,256,768]{3,2,1,0:T(8,128)(2,1)}, u32[]{:S(2)}) %copy-start.10) | copy-done | bytes 786456
  58.2 5.0 %grad_part.1 = bf16[16,2,16,768]{3,2,1,0:T(8,128)(2,1)} custom-call(bf16[2,256,768]{2,1,0:T(8,128)(2,1)S(1)} %copy-done.2, bf16[16,2,16,768]{3,2,1,0:T(8,128)(2,1)S(1)} %bitcast.32, bf16[2,2,256,768]{3,2,1,0:T(8,128)(2,1)S(1)} %copy-done.4, bf16[1,2,256,768]{3,2,1,0:T(8,128)(2,1)S(1)} %copy-done.10, bf16[768,2304]{1,0:T(8,128)(2,1)S(1)} %copy-done, ...), custom_call_target="tpu_custom_call" | custom-call | flops 1000 | bytes 1000 | tf_op jit(solution)/shard_map/grad_part/pallas_call | solution.py:346
  63.2 1.7 %out_part.1 = bf16[16,2,16,768]{3,2,1,0:T(8,128)(2,1)} custom-call(bf16[2,256,768]{2,1,0:T(8,128)(2,1)S(1)} %copy-done.2, bf16[2,256,128]{2,1,0:T(8,128)(2,1)S(1)} %copy-done.17, bf16[2,256,512]{2,1,0:T(8,128)(2,1)S(1)} %copy-done.12, bf16[2,256,256]{2,1,0:T(8,128)(2,1)S(1)} %copy-done.15, bf16[768,768]{1,0:T(8,128)(2,1)S(1)} %copy-done.6), custom_call_target="tpu_custom_call" | custom-call | flops 1000 | bytes 1000 | tf_op jit(solution)/shard_map/out_part/pallas_call | solution.py:304
  64.8 5.3 %collective-permute-done.8 = bf16[48,1536]{1,0:T(8,128)(2,1)} collective-permute-done((bf16[48,1536]{1,0:T(8,128)(2,1)S(1)}, bf16[48,1536]{1,0:T(8,128)(2,1)}, u32[]{:S(2)}, u32[]{:S(2)}) %collective-permute-start.8) | collective-permute-done | bytes 147488 | tf_op jit(solution)/shard_map/ppermute | solution.py:367
  71.1 2.4 %collective-permute-start.11 = (bf16[24,1536]{1,0:T(8,128)(2,1)S(1)}, bf16[24,1536]{1,0:T(8,128)(2,1)S(1)}, u32[]{:S(2)}, u32[]{:S(2)}) collective-permute-start(bf16[24,1536]{1,0:T(8,128)(2,1)S(1)} %slice.144), channel_id=1, source_target_pairs={{0,48},{8,56},{16,32},{24,40},{32,16},{40,24},{48,0},{56,8},{1,49}... | collective-permute-start | bytes 221192 | tf_op jit(solution)/shard_map/ppermute | solution.py:367
  73.5 1.4 %fusion = bf16[96,1536]{1,0:T(8,128)(2,1)S(1)} fusion(bf16[4,96,1536]{2,1,0:T(8,128)(2,1)} %all-to-all-done), kind=kLoop, calls=%fused_computation.6 | loop fusion | flops 1179648 | bytes 1474560 | tf_op jit(solution)/shard_map/add | solution.py:373
  74.9 2.1 %collective-permute-done.11 = bf16[24,1536]{1,0:T(8,128)(2,1)S(1)} collective-permute-done((bf16[24,1536]{1,0:T(8,128)(2,1)S(1)}, bf16[24,1536]{1,0:T(8,128)(2,1)S(1)}, u32[]{:S(2)}, u32[]{:S(2)}) %collective-permute-start.11) | collective-permute-done | bytes 73760 | tf_op jit(solution)/shard_map/ppermute | solution.py:367
  77.9 5.6 %all-to-all-start.1 = ((bf16[32,3,1536]{2,1,0:T(4,128)(2,1)}), bf16[32,3,1536]{2,1,0:T(4,128)(2,1)S(1)}, u32[]{:S(2)}, u32[]{:S(2)}) async-start(bf16[32,3,1536]{2,1,0:T(4,128)(2,1)} %reshape.74), calls=%async_computation.1 | async-start | bytes 786432 | tf_op jit(solution)/shard_map/all_to_all | solution.py:408
  83.6 1.5 %collective-permute-start.12 = (bf16[3,1536]{1,0:T(4,128)(2,1)S(1)}, bf16[3,1536]{1,0:T(4,128)(2,1)S(1)}, u32[]{:S(2)}, u32[]{:S(2)}) collective-permute-start(bf16[3,1536]{1,0:T(4,128)(2,1)S(1)} %get-tuple-element.86), channel_id=1, source_target_pairs={{0,1},{1,2},{2,3},{3,4},{4,5},{5,6},{6,7},{7,0},{8,9},{9,10},{10,1... | collective-permute-start | bytes 27656 | tf_op jit(solution)/shard_map/ppermute | solution.py:367
  85.1 1.8 %collective-permute-start.18 = (bf16[3,1536]{1,0:T(4,128)(2,1)S(1)}, bf16[3,1536]{1,0:T(4,128)(2,1)S(1)}, u32[]{:S(2)}, u32[]{:S(2)}) collective-permute-start(bf16[3,1536]{1,0:T(4,128)(2,1)S(1)} %get-tuple-element.87), channel_id=1, source_target_pairs={{0,7},{1,0},{2,1},{3,2},{4,3},{5,4},{6,5},{7,6},{8,15},{9,8},{10,9... | collective-permute-start | bytes 27656 | tf_op jit(solution)/shard_map/ppermute | solution.py:367
  86.9 2.4 %collective-permute-start.17 = (bf16[3,1536]{1,0:T(4,128)(2,1)S(1)}, bf16[3,1536]{1,0:T(4,128)(2,1)S(1)}, u32[]{:S(2)}, u32[]{:S(2)}) collective-permute-start(bf16[3,1536]{1,0:T(4,128)(2,1)S(1)} %get-tuple-element.88), channel_id=1, source_target_pairs={{0,6},{1,7},{2,0},{3,1},{4,2},{5,3},{6,4},{7,5},{8,14},{9,15},{10,... | collective-permute-start | bytes 27656 | tf_op jit(solution)/shard_map/ppermute | solution.py:367
  89.3 3.0 %collective-permute-start.16 = (bf16[3,1536]{1,0:T(4,128)(2,1)S(1)}, bf16[3,1536]{1,0:T(4,128)(2,1)S(1)}, u32[]{:S(2)}, u32[]{:S(2)}) collective-permute-start(bf16[3,1536]{1,0:T(4,128)(2,1)S(1)} %get-tuple-element.89), channel_id=1, source_target_pairs={{0,5},{1,6},{2,7},{3,0},{4,1},{5,2},{6,3},{7,4},{8,13},{9,14},{10,... | collective-permute-start | bytes 27656 | tf_op jit(solution)/shard_map/ppermute | solution.py:367
  92.3 2.0 %collective-permute-start.15 = (bf16[3,1536]{1,0:T(4,128)(2,1)S(1)}, bf16[3,1536]{1,0:T(4,128)(2,1)S(1)}, u32[]{:S(2)}, u32[]{:S(2)}) collective-permute-start(bf16[3,1536]{1,0:T(4,128)(2,1)S(1)} %get-tuple-element.90), channel_id=1, source_target_pairs={{0,4},{1,5},{2,6},{3,7},{4,0},{5,1},{6,2},{7,3},{8,12},{9,13},{10,... | collective-permute-start | bytes 27656 | tf_op jit(solution)/shard_map/ppermute | solution.py:367
  94.4 1.8 %collective-permute-start.14 = (bf16[3,1536]{1,0:T(4,128)(2,1)S(1)}, bf16[3,1536]{1,0:T(4,128)(2,1)S(1)}, u32[]{:S(2)}, u32[]{:S(2)}) collective-permute-start(bf16[3,1536]{1,0:T(4,128)(2,1)S(1)} %get-tuple-element.91), channel_id=1, source_target_pairs={{0,3},{1,4},{2,5},{3,6},{4,7},{5,0},{6,1},{7,2},{8,11},{9,12},{10,... | collective-permute-start | bytes 27656 | tf_op jit(solution)/shard_map/ppermute | solution.py:367
  96.1 4.1 %collective-permute-start.13 = (bf16[3,1536]{1,0:T(4,128)(2,1)S(1)}, bf16[3,1536]{1,0:T(4,128)(2,1)S(1)}, u32[]{:S(2)}, u32[]{:S(2)}) collective-permute-start(bf16[3,1536]{1,0:T(4,128)(2,1)S(1)} %get-tuple-element.92), channel_id=1, source_target_pairs={{0,2},{1,3},{2,4},{3,5},{4,6},{5,7},{6,0},{7,1},{8,10},{9,11},{10,... | collective-permute-start | bytes 27656 | tf_op jit(solution)/shard_map/ppermute | solution.py:367
  101.1 1.0 collective-permute-done.13
  (96 shorter events, 15.6 us)
Async XLA Ops:
  1.6 15.0 %collective-permute-start.2 = (bf16[8,8,768]{2,1,0:T(8,128)(2,1)S(1)}, bf16[8,8,768]{2,1,0:T(8,128)(2,1)S(1)}, u32[]{:S(2)}, u32[]{:S(2)}) collective-permute-start(bf16[8,8,768]{2,1,0:T(8,128)(2,1)S(1)} %get-tuple-element.78), channel_id=1, source_target_pairs={{0,63},{1,56},{2,57},{3,58},{4,59},{5,60},{6,61},{7,62},{8,7},{9,0... | collective-permute-start | bytes 294920 | tf_op jit(solution)/shard_map/ppermute | solution.py:424
  9.4 7.2 %collective-permute-start.1 = (bf16[8,8,768]{2,1,0:T(8,128)(2,1)S(1)}, bf16[8,8,768]{2,1,0:T(8,128)(2,1)S(1)}, u32[]{:S(2)}, u32[]{:S(2)}) collective-permute-start(bf16[8,8,768]{2,1,0:T(8,128)(2,1)S(1)} %get-tuple-element.79), channel_id=1, source_target_pairs={{0,7},{1,0},{2,1},{3,2},{4,3},{5,4},{6,5},{7,6},{8,15},{9,8},{10,9... | collective-permute-start | bytes 294920 | tf_op jit(solution)/shard_map/ppermute | solution.py:367
  11.4 5.2 %collective-permute-start = (bf16[8,24,768]{2,1,0:T(8,128)(2,1)S(1)}, bf16[8,24,768]{2,1,0:T(8,128)(2,1)S(1)}, u32[]{:S(2)}, u32[]{:S(2)}) collective-permute-start(bf16[8,24,768]{2,1,0:T(8,128)(2,1)S(1)} %slice.132), channel_id=1, source_target_pairs={{0,56},{8,0},{16,8},{24,16},{32,24},{40,32},{48,40},{56,48},{1,57}... | collective-permute-start | bytes 884744 | tf_op jit(solution)/shard_map/ppermute | solution.py:367
  16.6 17.2 %copy-start.16 = (bf16[2,256,128]{2,1,0:T(8,128)(2,1)}, bf16[2,256,128]{2,1,0:T(8,128)(2,1)S(1)}, u32[]{:S(2)}) copy-start(bf16[2,256,128]{2,1,0:T(8,128)(2,1)S(1)} %get-tuple-element.40.tis_ref) | copy-start | bytes 393220
  28.0 11.1 %copy-start.11 = (bf16[2,256,512]{2,1,0:T(8,128)(2,1)}, bf16[2,256,512]{2,1,0:T(8,128)(2,1)S(1)}, u32[]{:S(2)}) copy-start(bf16[2,256,512]{2,1,0:T(8,128)(2,1)S(1)} %get-tuple-element.56.att0_ref) | copy-start | bytes 1572868
  28.0 2.9 %collective-permute-start.3 = (bf16[384,1536]{1,0:T(8,128)(2,1)S(1)}, bf16[384,1536]{1,0:T(8,128)(2,1)S(1)}, u32[]{:S(2)}, u32[]{:S(2)}) collective-permute-start(bf16[384,1536]{1,0:T(8,128)(2,1)S(1)} %get-tuple-element.44), channel_id=1, source_target_pairs={{0,8},{8,0},{16,24},{24,16},{32,40},{40,32},{48,56},{56,48},{1,9},... | collective-permute-start | bytes 3538952 | tf_op jit(solution)/shard_map/ppermute | solution.py:367
  31.3 9.6 %copy-start.20 = (bf16[384,768]{1,0:T(8,128)(2,1)}, bf16[384,768]{1,0:T(8,128)(2,1)S(1)}, u32[]{:S(2)}) copy-start(bf16[384,768]{1,0:T(8,128)(2,1)S(1)} %get-tuple-element.77) | copy-start | bytes 1769476
  31.3 9.6 %copy-start.19 = (bf16[384,768]{1,0:T(8,128)(2,1)}, bf16[384,768]{1,0:T(8,128)(2,1)S(1)}, u32[]{:S(2)}) copy-start(bf16[384,768]{1,0:T(8,128)(2,1)S(1)} %get-tuple-element.76) | copy-start | bytes 1769476
  31.3 7.6 %collective-permute-start.4 = (bf16[96,768]{1,0:T(8,128)(2,1)S(1)}, bf16[96,768]{1,0:T(8,128)(2,1)S(1)}, u32[]{:S(2)}, u32[]{:S(2)}) collective-permute-start(bf16[96,768]{1,0:T(8,128)(2,1)S(1)} %get-tuple-element.85), channel_id=1, source_target_pairs={{0,64},{64,128},{128,192},{192,0},{1,65},{65,129},{129,193},{193,1... | collective-permute-start | bytes 442376 | tf_op jit(solution)/shard_map/ppermute | solution.py:367
  31.9 7.1 %collective-permute-start.5 = (bf16[96,768]{1,0:T(8,128)(2,1)S(1)}, bf16[96,768]{1,0:T(8,128)(2,1)S(1)}, u32[]{:S(2)}, u32[]{:S(2)}) collective-permute-start(bf16[96,768]{1,0:T(8,128)(2,1)S(1)} %get-tuple-element.83), channel_id=1, source_target_pairs={{0,192},{64,0},{128,64},{192,128},{1,193},{65,1},{129,65},{193,129... | collective-permute-start | bytes 442376 | tf_op jit(solution)/shard_map/ppermute | solution.py:367
  39.0 2.1 %collective-permute-start.9 = (bf16[384,768]{1,0:T(8,128)(2,1)S(1)}, bf16[384,768]{1,0:T(8,128)(2,1)S(1)}, u32[]{:S(2)}, u32[]{:S(2)}) collective-permute-start(bf16[384,768]{1,0:T(8,128)(2,1)S(1)} %get-tuple-element.58), channel_id=1, source_target_pairs={{0,8},{8,0},{16,24},{24,16},{32,40},{40,32},{48,56},{56,48},{1,9},... | collective-permute-start | bytes 1769480 | tf_op jit(solution)/shard_map/ppermute | solution.py:367
  41.1 5.4 %collective-permute-start.10 = (bf16[384,768]{1,0:T(8,128)(2,1)S(1)}, bf16[384,768]{1,0:T(8,128)(2,1)S(1)}, u32[]{:S(2)}, u32[]{:S(2)}) collective-permute-start(bf16[384,768]{1,0:T(8,128)(2,1)S(1)} %get-tuple-element.65), channel_id=1, source_target_pairs={{0,8},{8,0},{16,24},{24,16},{32,40},{40,32},{48,56},{56,48},{1,9},... | collective-permute-start | bytes 1769480 | tf_op jit(solution)/shard_map/ppermute | solution.py:367
  42.3 10.5 %collective-permute-start.7 = (bf16[96,1536]{1,0:T(8,128)(2,1)}, bf16[96,1536]{1,0:T(8,128)(2,1)}, u32[]{:S(2)}, u32[]{:S(2)}) collective-permute-start(bf16[96,1536]{1,0:T(8,128)(2,1)} %pad_maximum_fusion.2), channel_id=1, source_target_pairs={{0,192},{64,0},{128,64},{192,128},{1,193},{65,1},{129,65},{193,129... | collective-permute-start | bytes 884744 | tf_op jit(solution)/shard_map/ppermute | solution.py:367
  43.9 9.0 %collective-permute-start.6 = (bf16[96,1536]{1,0:T(8,128)(2,1)}, bf16[96,1536]{1,0:T(8,128)(2,1)}, u32[]{:S(2)}, u32[]{:S(2)}) collective-permute-start(bf16[96,1536]{1,0:T(8,128)(2,1)} %pad_maximum_fusion.1), channel_id=1, source_target_pairs={{0,64},{64,128},{128,192},{192,0},{1,65},{65,129},{129,193},{193,1... | collective-permute-start | bytes 884744 | tf_op jit(solution)/shard_map/ppermute | solution.py:367
  47.7 22.4 %all-to-all-start = ((bf16[4,96,1536]{2,1,0:T(8,128)(2,1)}), bf16[4,96,1536]{2,1,0:T(8,128)(2,1)}, u32[]{:S(2)}, u32[]{:S(2)}) async-start(bf16[4,96,1536]{2,1,0:T(8,128)(2,1)} %bitcast.37), calls=%async_computation | async-start | bytes 2359296 | tf_op jit(solution)/shard_map/all_to_all | solution.py:408
  52.0 3.6 %copy-start.2 = (bf16[2,256,768]{2,1,0:T(8,128)(2,1)S(1)}, bf16[2,256,768]{2,1,0:T(8,128)(2,1)}, u32[]{:S(2)}) copy-start(bf16[2,256,768]{2,1,0:T(8,128)(2,1)} %copy-done.1) | copy-start | bytes 2359300
  54.3 15.9 %collective-permute-start.8 = (bf16[48,1536]{1,0:T(8,128)(2,1)S(1)}, bf16[48,1536]{1,0:T(8,128)(2,1)}, u32[]{:S(2)}, u32[]{:S(2)}) collective-permute-start(bf16[48,1536]{1,0:T(8,128)(2,1)S(1)} %fusion.7), channel_id=1, source_target_pairs={{0,16},{8,24},{16,0},{24,8},{32,48},{40,56},{48,32},{56,40},{1,17}... | collective-permute-start | bytes 442376 | tf_op jit(solution)/shard_map/ppermute | solution.py:367
  58.2 5.0 %copy-start.6 = (bf16[768,768]{1,0:T(8,128)(2,1)S(1)}, bf16[768,768]{1,0:T(8,128)(2,1)}, u32[]{:S(2)}) copy-start(bf16[768,768]{1,0:T(8,128)(2,1)} %wp_ref.1) | copy-start | bytes 3538948
  58.2 5.0 %copy-start.12 = (bf16[2,256,512]{2,1,0:T(8,128)(2,1)S(1)}, bf16[2,256,512]{2,1,0:T(8,128)(2,1)}, u32[]{:S(2)}) copy-start(bf16[2,256,512]{2,1,0:T(8,128)(2,1)} %copy-done.11) | copy-start | bytes 1572868
  58.2 5.0 %copy-start.15 = (bf16[2,256,256]{2,1,0:T(8,128)(2,1)S(1)}, bf16[2,256,256]{2,1,0:T(8,128)(2,1)}, u32[]{:S(2)}) copy-start(bf16[2,256,256]{2,1,0:T(8,128)(2,1)} %copy-done.14) | copy-start | bytes 786436
  58.2 5.0 %copy-start.17 = (bf16[2,256,128]{2,1,0:T(8,128)(2,1)S(1)}, bf16[2,256,128]{2,1,0:T(8,128)(2,1)}, u32[]{:S(2)}) copy-start(bf16[2,256,128]{2,1,0:T(8,128)(2,1)} %copy-done.16) | copy-start | bytes 393220
  63.2 7.0 %copy-start.22 = (bf16[96,768]{1,0:T(8,128)(2,1)S(1)}, bf16[96,768]{1,0:T(8,128)(2,1)}, u32[]{:S(2)}) copy-start(bf16[96,768]{1,0:T(8,128)(2,1)} %copy-done.21) | copy-start | bytes 442372
  63.2 7.0 %copy-start.24 = (bf16[96,768]{1,0:T(8,128)(2,1)S(1)}, bf16[96,768]{1,0:T(8,128)(2,1)}, u32[]{:S(2)}) copy-start(bf16[96,768]{1,0:T(8,128)(2,1)} %copy-done.23) | copy-start | bytes 442372
  71.1 5.9 %collective-permute-start.11 = (bf16[24,1536]{1,0:T(8,128)(2,1)S(1)}, bf16[24,1536]{1,0:T(8,128)(2,1)S(1)}, u32[]{:S(2)}, u32[]{:S(2)}) collective-permute-start(bf16[24,1536]{1,0:T(8,128)(2,1)S(1)} %slice.144), channel_id=1, source_target_pairs={{0,48},{8,56},{16,32},{24,40},{32,16},{40,24},{48,0},{56,8},{1,49}... | collective-permute-start | bytes 221192 | tf_op jit(solution)/shard_map/ppermute | solution.py:367
  77.9 24.2 %all-to-all-start.1 = ((bf16[32,3,1536]{2,1,0:T(4,128)(2,1)}), bf16[32,3,1536]{2,1,0:T(4,128)(2,1)S(1)}, u32[]{:S(2)}, u32[]{:S(2)}) async-start(bf16[32,3,1536]{2,1,0:T(4,128)(2,1)} %reshape.74), calls=%async_computation.1 | async-start | bytes 786432 | tf_op jit(solution)/shard_map/all_to_all | solution.py:408
  83.6 10.8 %collective-permute-start.12 = (bf16[3,1536]{1,0:T(4,128)(2,1)S(1)}, bf16[3,1536]{1,0:T(4,128)(2,1)S(1)}, u32[]{:S(2)}, u32[]{:S(2)}) collective-permute-start(bf16[3,1536]{1,0:T(4,128)(2,1)S(1)} %get-tuple-element.86), channel_id=1, source_target_pairs={{0,1},{1,2},{2,3},{3,4},{4,5},{5,6},{6,7},{7,0},{8,9},{9,10},{10,1... | collective-permute-start | bytes 27656 | tf_op jit(solution)/shard_map/ppermute | solution.py:367
  85.1 11.0 %collective-permute-start.18 = (bf16[3,1536]{1,0:T(4,128)(2,1)S(1)}, bf16[3,1536]{1,0:T(4,128)(2,1)S(1)}, u32[]{:S(2)}, u32[]{:S(2)}) collective-permute-start(bf16[3,1536]{1,0:T(4,128)(2,1)S(1)} %get-tuple-element.87), channel_id=1, source_target_pairs={{0,7},{1,0},{2,1},{3,2},{4,3},{5,4},{6,5},{7,6},{8,15},{9,8},{10,9... | collective-permute-start | bytes 27656 | tf_op jit(solution)/shard_map/ppermute | solution.py:367
  86.9 13.4 %collective-permute-start.17 = (bf16[3,1536]{1,0:T(4,128)(2,1)S(1)}, bf16[3,1536]{1,0:T(4,128)(2,1)S(1)}, u32[]{:S(2)}, u32[]{:S(2)}) collective-permute-start(bf16[3,1536]{1,0:T(4,128)(2,1)S(1)} %get-tuple-element.88), channel_id=1, source_target_pairs={{0,6},{1,7},{2,0},{3,1},{4,2},{5,3},{6,4},{7,5},{8,14},{9,15},{10,... | collective-permute-start | bytes 27656 | tf_op jit(solution)/shard_map/ppermute | solution.py:367
  89.3 11.0 %collective-permute-start.16 = (bf16[3,1536]{1,0:T(4,128)(2,1)S(1)}, bf16[3,1536]{1,0:T(4,128)(2,1)S(1)}, u32[]{:S(2)}, u32[]{:S(2)}) collective-permute-start(bf16[3,1536]{1,0:T(4,128)(2,1)S(1)} %get-tuple-element.89), channel_id=1, source_target_pairs={{0,5},{1,6},{2,7},{3,0},{4,1},{5,2},{6,3},{7,4},{8,13},{9,14},{10,... | collective-permute-start | bytes 27656 | tf_op jit(solution)/shard_map/ppermute | solution.py:367
  92.3 8.0 %collective-permute-start.15 = (bf16[3,1536]{1,0:T(4,128)(2,1)S(1)}, bf16[3,1536]{1,0:T(4,128)(2,1)S(1)}, u32[]{:S(2)}, u32[]{:S(2)}) collective-permute-start(bf16[3,1536]{1,0:T(4,128)(2,1)S(1)} %get-tuple-element.90), channel_id=1, source_target_pairs={{0,4},{1,5},{2,6},{3,7},{4,0},{5,1},{6,2},{7,3},{8,12},{9,13},{10,... | collective-permute-start | bytes 27656 | tf_op jit(solution)/shard_map/ppermute | solution.py:367
  94.4 6.7 %collective-permute-start.14 = (bf16[3,1536]{1,0:T(4,128)(2,1)S(1)}, bf16[3,1536]{1,0:T(4,128)(2,1)S(1)}, u32[]{:S(2)}, u32[]{:S(2)}) collective-permute-start(bf16[3,1536]{1,0:T(4,128)(2,1)S(1)} %get-tuple-element.91), channel_id=1, source_target_pairs={{0,3},{1,4},{2,5},{3,6},{4,7},{5,0},{6,1},{7,2},{8,11},{9,12},{10,... | collective-permute-start | bytes 27656 | tf_op jit(solution)/shard_map/ppermute | solution.py:367
  96.1 5.9 %collective-permute-start.13 = (bf16[3,1536]{1,0:T(4,128)(2,1)S(1)}, bf16[3,1536]{1,0:T(4,128)(2,1)S(1)}, u32[]{:S(2)}, u32[]{:S(2)}) collective-permute-start(bf16[3,1536]{1,0:T(4,128)(2,1)S(1)} %get-tuple-element.92), channel_id=1, source_target_pairs={{0,2},{1,3},{2,4},{3,5},{4,6},{5,7},{6,0},{7,1},{8,10},{9,11},{10,... | collective-permute-start | bytes 27656 | tf_op jit(solution)/shard_map/ppermute | solution.py:367
  (14 other events, 21.4 us)

commit v5 on v4

--- a/solution.py
+++ b/solution.py
@@ -36,6 +36,32 @@
 
 def cost(flops, size):
     return pl.CostEstimate(flops=int(flops), bytes_accessed=int(size), transcendentals=0)
+
+
+def edges_kernel(tiles, above, left, corner, sem):
+    copies = [
+        pltpu.make_async_copy(tiles.at[0:8, 8:32], above, sem.at[0]),
+        pltpu.make_async_copy(tiles.at[8:16, 0:8], left, sem.at[1]),
+        pltpu.make_async_copy(tiles.at[0:8, 0:8], corner, sem.at[2]),
+    ]
+    for copy in copies:
+        copy.start()
+    for copy in copies:
+        copy.wait()
+
+
+def edges(tiles):
+    small = jax.ShapeDtypeStruct((8, 8, D), BF)
+    return pl.pallas_call(
+        edges_kernel,
+        in_specs=[pl.BlockSpec(memory_space=pl.ANY)],
+        out_specs=[pl.BlockSpec(memory_space=pl.ANY)] * 3,
+        out_shape=[jax.ShapeDtypeStruct((8, 24, D), BF), small, small],
+        scratch_shapes=[pltpu.SemaphoreType.DMA((3,))],
+        compiler_params=pltpu.CompilerParams(vmem_limit_bytes=VMEM),
+        cost_estimate=cost(3e10, 1e6),
+        name="edges",
+    )(tiles)
 
 
 def branch_kernel(
@@ -87,20 +113,19 @@
     )(cot, tissue, w_proj)
 
 
-def row_order(first):
+def row_order(permutes):
     gy = lax.axis_index("gy")
-    dp, y, core, gx = lax.axis_index("dp"), gy >> 1, gy & 1, lax.axis_index("gx")
+    dp, y, core = lax.axis_index("dp"), gy >> 1, gy & 1
     at = lax.broadcasted_iota(jnp.int32, (D, 1), 0)
     third = ((at.astype(F32) + 0.5) * (1.0 / 3)).astype(jnp.int32)
     outer, inner, depth = (third >> 5) & 3, (third >> 3) & 3, third & 7
-    if first == "dp":
+    if permutes:
         dp_of = (outer + dp) & 3
         y_of = ((inner >> 1) ^ ((inner & 1) * 3)) ^ y
-        z_of = (depth + gx) & 7
     else:
-        dp_of, y_of, z_of = inner, outer, depth
+        dp_of, y_of = outer, inner
     core_of = (third >> 7) ^ core
-    source = ((dp_of * 8 + y_of * 2 + core_of) * 8 + z_of) * 3 + at - third * 3
+    source = ((dp_of * 8 + y_of * 2 + core_of) * 8 + depth) * 3 + at - third * 3
     column = lax.broadcasted_iota(jnp.int32, (D, D), 1)
     return jnp.where(column == source, 1.0, 0.0).astype(BF)
 
@@ -176,7 +201,7 @@
         low = below_ref[...].astype(F32)
         right = right_ref[...].astype(F32)
         diag = diag_ref[...].astype(F32)
-        perm = row_order("dp")
+        perm = row_order(True)
         for w in range(2):
             if w == 0:
                 top, bottom = own[:, 8:24], low[:, :16]
@@ -207,7 +232,7 @@
 
 
 def turn_kernel(hid_ref, hid_t_ref):
-    hid_t_ref[...] = nt(row_order("gy"), hid_ref[...].reshape(2 * CELLS, D)).astype(BF)
+    hid_t_ref[...] = nt(row_order(False), hid_ref[...].reshape(2 * CELLS, D)).astype(BF)
 
 
 def turn(hid):
@@ -277,7 +302,7 @@
 
 def proj_kernel(att0_ref, att1_ref, db_ref, keep_ref, send_ref):
     attended = jnp.concatenate([att0_ref[...], att1_ref[...]], 2).reshape(2 * CELLS, D)
-    att_t = nt(row_order("gy"), attended).astype(BF)
+    att_t = nt(row_order(False), attended).astype(BF)
     put(nn(att_t, db_ref[...].reshape(2 * CELLS, D)), keep_ref, send_ref)
 
 
@@ -418,11 +443,12 @@
 
 def shards(tiles, cotangent, tissue, w_qkv, w_proj):
     mine = tiles[0]
-    below = send(mine[:8, 8:], "gy", lambda i: i - 1)
-    right = send(mine[8:, :8], "gx", lambda i: i - 1)
+    above, left, corner = edges(mine)
+    below = send(above, "gy", lambda i: i - 1)
+    right = send(left, "gx", lambda i: i - 1)
     ny, nx = lax.axis_size("gy"), lax.axis_size("gx")
     diag = lax.ppermute(
-        mine[:8, :8],
+        corner,
         ("gy", "gx"),
         [
             (a * nx + b, (a - 1) % ny * nx + (b - 1) % nx)
@@ -450,26 +476,21 @@
     came, send2, keep2 = tie(came, send2, keep2)
     rows_b = jnp.concatenate([add(keep1, came), add(keep2, send(send2, "gy", lambda i: i ^ 1))], 1)
     rows_b, att1 = tie(rows_b, att1)
-    same_core = [[0, 2, 4, 6], [1, 3, 5, 7]]
-    parts_b = exchange(rows_b, "gy", same_core)
+    same_core = [[d * 8 + y * 2 + c for d in range(4) for y in range(4)] for c in range(2)]
+    parts_b = exchange(rows_b, ("dp", "gy"), same_core)
+    rows_a, att1 = tie(ring_end(low_a, high_a, came_a), att1)
+    came_a = halve_start(rows_a, "gy", 2)
     out = out_part(xw, tis, att0, att1, w_proj)
-    rows_a = ring_end(low_a, high_a, came_a)
-    came_a = halve_start(rows_a, "gy", 2)
+    came_a, out, xw = tie(came_a, out, xw)
+    rows_a = halve_end(rows_a, came_a)
+    came_a = halve_start(rows_a, "gy", 6)
     grad = grad_part(xw, cot, dqkv0, dqkv1, w_qkv)
-    came_a, out, grad, parts_b = tie(came_a, out, grad, parts_b)
-    rows_a = halve_end(rows_a, came_a)
-    rows_a = halve_end(rows_a, halve_start(rows_a, "gy", 6))
-    rows_b, rows_a = tie(add(*parts_b), rows_a)
-    parts_b = exchange(rows_b, ("dp", "gx"))
-    rows_a = rows_a.reshape(8, 3, -1)
-    total_a = rows_a[0].astype(F32)
-    for d in range(1, 8):
-        total_a = total_a + send(rows_a[d], "gx", lambda j: j + d).astype(F32)
-    scale = 1.0 / math.sqrt(512)
-    total_b = jnp.sum(parts_b.astype(F32), 0) * scale
-    total = jnp.concatenate([total_a * scale, total_b[:, :D]], 1)
-    grad_qkv = total.reshape(3, GROUPS, 3, GW).transpose(0, 2, 1, 3)
-    return out, grad, grad_qkv.reshape(3, 3 * D), total_b[:, D:]
+    came_a, grad, parts_b = tie(came_a, grad, parts_b)
+    rows = jnp.concatenate([halve_end(rows_a, came_a), add(*parts_b)], 1)
+    parts = exchange(rows, ("gx",))
+    total = jnp.sum(parts.astype(F32), 0) * (1.0 / math.sqrt(512))
+    grad_qkv = total[:, : 3 * D].reshape(3, GROUPS, 3, GW).transpose(0, 2, 1, 3)
+    return out, grad, grad_qkv.reshape(3, 3 * D), total[:, 3 * D :]
 
 
 def solution(mesh):

time: 105 us -> 95.3 us (0.908)
  starting transfers between devices: 45.9 us -> 27.3 us
  blocking collectives: 0 us -> 13 us
  local copies, waits for them, and re-layouts: 12 us -> 6.89 us
  waiting for transfers between devices: 11.7 us -> 14.3 us
    all_to_all x0 -> x1, blocking collectives: none -> 13 us  [exchange(): return lax.all_to_all(rows, axis, 0, 0, axis_index_groups=groups)]
    ppermute x18 -> x11, starting transfers between devices: 28.2 us -> 17.4 us  [send(): lax.ppermute(value, axis, [(i, move(i) % devices) for i in range(devices)])]
    ppermute x1, starting transfers between devices: 7.82 us -> 2.62 us  [shards(): lax.ppermute(corner, ('gy', 'gx'), [(a * nx + b, (a - 1) % ny * nx + (b -...]
    ppermute x18 -> x11, waiting for transfers between devices: 11.7 us -> 14.3 us  [send(): lax.ppermute(value, axis, [(i, move(i) % devices) for i in range(devices)])]
    all_to_all x2 -> x1, starting transfers between devices: 9.88 us -> 7.26 us  [exchange(): return lax.all_to_all(rows, axis, 0, 0, axis_index_groups=groups)]
    unnamed x50 -> x44, local copies, waits for them, and re-layouts: 7.65 us -> 5.35 us
    slice x4 -> x2, local copies, waits for them, and re-layouts: 2.59 us -> 0.61 us  [the longest x1 0.6 us: shards(): return (out, grad, grad_qkv.reshape(3, 3 * D), total[:, 3 * D:])]
    add x1 -> x0, other arithmetic: 1.38 us -> none  [add(): total = total + term.astype(F32)]
  transfers between devices with their start and end apart: 21 -> 13, of which waited for: 8 -> 4; matrix products, arithmetic and copies ran while one was open for 7% -> 5% of each run, Pallas kernels for 15% -> 16%
where the time goes in v5:
time: 95.3 us; the launch traced here: 94.8 us
  starting transfers between devices  27.3 us (29%)
  Pallas kernels  25.9 us (27%)
  waiting for transfers between devices  14.3 us (15%)
  blocking collectives  13 us (14%)
  local copies, waits for them, and re-layouts  6.89 us (7%)
  other arithmetic  6.39 us (7%)
  between operations  1 us (1%)
    ppermute x11, starting transfers between devices, send(): lax.ppermute(value, axis, [(i, move(i) % devices) for i in range(devices)])  17.4 us
    ppermute x11, waiting for transfers between devices, send(): lax.ppermute(value, axis, [(i, move(i) % devices) for i in range(devices)])  14.3 us
    all_to_all x1, blocking collectives, exchange(): return lax.all_to_all(rows, axis, 0, 0, axis_index_groups=groups)  13 us
    pallas_call x1, Pallas kernels, first_heads(): pl.pallas_call(first_kernel, grid=(2,), in_specs=[full((16, 32, D)), full...  10.6 us
    all_to_all x1, starting transfers between devices, exchange(): return lax.all_to_all(rows, axis, 0, 0, axis_index_groups=groups)  7.26 us
    unnamed x44, local copies, waits for them, and re-layouts  5.35 us
    pallas_call x1, Pallas kernels, grad_part(): pl.pallas_call(grad_kernel, grid=(GROUPS,), in_specs=[full((2, CELLS, D))...  4.96 us
    pallas_call x1, Pallas kernels, last_heads(): pl.pallas_call(last_kernel, grid=(1,), in_specs=[full((2, CELLS, D)), ful...  4.36 us
  transfers between devices with their start and end apart: 13, of which 4 were waited for; matrix products, arithmetic and copies ran while one was open for 5% of the time, Pallas kernels for 16%

profile of v5, /device:TPU:6, one launch (start us, length us, event | category | flops | bytes accessed | tf_op | source)
XLA Modules:
  0.0 94.8 jit_solution(16229187468935279088)
XLA Ops:
  0.6 1.1 %copy-done.17 = bf16[1,16,32,768]{3,2,1,0:T(8,128)(2,1)S(1)} copy-done((bf16[1,16,32,768]{3,2,1,0:T(8,128)(2,1)S(1)}, bf16[1,16,32,768]{3,2,1,0:T(8,128)(2,1)}, u32[]{:S(2)}) %copy-start.17) | copy-done | bytes 786456
  1.9 5.9 %collective-permute-start.1 = (bf16[8,8,768]{2,1,0:T(8,128)(2,1)S(1)}, bf16[8,8,768]{2,1,0:T(8,128)(2,1)S(1)}, u32[]{:S(2)}, u32[]{:S(2)}) collective-permute-start(bf16[8,8,768]{2,1,0:T(8,128)(2,1)S(1)} %get-tuple-element.46), channel_id=1, source_target_pairs={{0,7},{1,0},{2,1},{3,2},{4,3},{5,4},{6,5},{7,6},{8,15},{9,8},{10,9... | collective-permute-start | bytes 294920 | tf_op jit(solution)/shard_map/ppermute | solution.py:392
  7.8 2.6 %collective-permute-start.2 = (bf16[8,8,768]{2,1,0:T(8,128)(2,1)S(1)}, bf16[8,8,768]{2,1,0:T(8,128)(2,1)S(1)}, u32[]{:S(2)}, u32[]{:S(2)}) collective-permute-start(bf16[8,8,768]{2,1,0:T(8,128)(2,1)S(1)} %get-tuple-element.47), channel_id=1, source_target_pairs={{0,63},{1,56},{2,57},{3,58},{4,59},{5,60},{6,61},{7,62},{8,7},{9,0... | collective-permute-start | bytes 294920 | tf_op jit(solution)/shard_map/ppermute | solution.py:450
  10.4 1.1 %collective-permute-start = (bf16[8,24,768]{2,1,0:T(8,128)(2,1)S(1)}, bf16[8,24,768]{2,1,0:T(8,128)(2,1)S(1)}, u32[]{:S(2)}, u32[]{:S(2)}) collective-permute-start(bf16[8,24,768]{2,1,0:T(8,128)(2,1)S(1)} %get-tuple-element.45), channel_id=1, source_target_pairs={{0,56},{8,0},{16,8},{24,16},{32,24},{40,32},{48,40},{56,48},{1,57}... | collective-permute-start | bytes 884744 | tf_op jit(solution)/shard_map/ppermute | solution.py:392
  11.6 1.5 %branch.1 = (bf16[2,256,768]{2,1,0:T(8,128)(2,1)S(1)}, bf16[2,256,768]{2,1,0:T(8,128)(2,1)S(1)}, bf16[2,256,128]{2,1,0:T(8,128)(2,1)S(1)}, bf16[2,256,128]{2,1,0:T(8,128)(2,1)S(1)}) custom-call(bf16[16,2,16,768]{3,2,1,0:T(8,128)(2,1)S(1)} %bitcast.34, s32[16,32]{1,0:T(8,128)S(1)} %bitcast.38, bf16[768,768]{1,0:T(8,128)(2,1)S(1)} %copy-done.5), custom_call_target="tpu_custom_call" | custom-call | flops 20000000000 | bytes 4000000 | tf_op jit(solution)/shard_map/branch/pallas_call | solution.py:100
  13.1 3.1 %collective-permute-done.below_ref = bf16[8,24,768]{2,1,0:T(8,128)(2,1)S(1)} collective-permute-done((bf16[8,24,768]{2,1,0:T(8,128)(2,1)S(1)}, bf16[8,24,768]{2,1,0:T(8,128)(2,1)S(1)}, u32[]{:S(2)}, u32[]{:S(2)}) %collective-permute-start) | collective-permute-done | bytes 294944 | tf_op jit(solution)/shard_map/ppermute | solution.py:392
  16.2 10.6 %first_heads.1 = (bf16[384,1536]{1,0:T(8,128)(2,1)S(1)}, bf16[384,1536]{1,0:T(8,128)(2,1)S(1)}, bf16[2,256,512]{2,1,0:T(8,128)(2,1)S(1)}, bf16[2,2,256,768]{3,2,...) custom-call(bf16[16,32,768]{2,1,0:T(8,128)(2,1)S(1)} %bitcast.37, ...), custom_call_target="tpu_custom_call" | custom-call | flops 6000000000 | bytes 10000000 | tf_op jit(solution)/shard_map/first_heads/pallas_call | solution.py:276
  27.0 0.9 turn.1.hid_t_ref
  28.3 1.5 %collective-permute-done.3 = bf16[384,1536]{1,0:T(8,128)(2,1)S(1)} collective-permute-done((bf16[384,1536]{1,0:T(8,128)(2,1)S(1)}, bf16[384,1536]{1,0:T(8,128)(2,1)S(1)}, u32[]{:S(2)}, u32[]{:S(2)}) %collective-permute-start.3) | collective-permute-done | bytes 1179680 | tf_op jit(solution)/shard_map/ppermute | solution.py:392
  30.8 1.8 %collective-permute-start.5 = (bf16[96,768]{1,0:T(8,128)(2,1)S(1)}, bf16[96,768]{1,0:T(8,128)(2,1)S(1)}, u32[]{:S(2)}, u32[]{:S(2)}) collective-permute-start(bf16[96,768]{1,0:T(8,128)(2,1)S(1)} %get-tuple-element.91), channel_id=1, source_target_pairs={{0,192},{64,0},{128,64},{192,128},{1,193},{65,1},{129,65},{193,129... | collective-permute-start | bytes 442376 | tf_op jit(solution)/shard_map/ppermute | solution.py:392
  32.6 4.4 %last_heads.1 = (bf16[384,768]{1,0:T(8,128)(2,1)S(1)}, bf16[384,768]{1,0:T(8,128)(2,1)S(1)}, bf16[2,256,256]{2,1,0:T(8,128)(2,1)S(1)}, bf16[1,2,256,768]{3,2,1,0:T(8,128)(2,1)S(1)}) custom-call(bf16[2,256,768]{2,1,0:T(8,128)(2,1)S(1)} %get-tuple-element.53.hid_ref, bf16[768,512]{1,0:T(8,128)(2,1)S(1)} %turn.1.hid_t_ref, ...), custom_call_target="tpu_custom_call" | custom-call | flops 4000000000 | bytes 6000000 | tf_op jit(solution)/shard_map/last_heads/pallas_call | solution.py:291
  37.0 0.9 copy-done.9
  38.0 1.8 %proj_grad.1 = (bf16[384,768]{1,0:T(8,128)(2,1)S(1)}, bf16[384,768]{1,0:T(8,128)(2,1)S(1)}) custom-call(bf16[2,256,512]{2,1,0:T(8,128)(2,1)S(1)} %get-tuple-element.65.att0_ref, bf16[2,256,256]{2,1,0:T(8,128)(2,1)S(1)} %get-tuple-element.76.att1_ref, bf16[2,256,768]{2,1,0:T(8,128)(2,1)S(1)} %get-tuple-element.67.db_ref), custom_call_target="tpu_custom_call" | custom-call | flops 2000000000 | bytes 4000000 | tf_op jit(solution)/shard_map/proj_grad/pallas_call | solution.py:311
  40.5 0.7 pad_maximum_fusion.2
  41.2 0.8 collective-permute-start.7
  42.0 0.7 pad_maximum_fusion.1
  42.7 2.4 %collective-permute-start.6 = (bf16[96,1536]{1,0:T(8,128)(2,1)}, bf16[96,1536]{1,0:T(8,128)(2,1)}, u32[]{:S(2)}, u32[]{:S(2)}) collective-permute-start(bf16[96,1536]{1,0:T(8,128)(2,1)} %pad_maximum_fusion.1), channel_id=1, source_target_pairs={{0,64},{64,128},{128,192},{192,0},{1,65},{65,129},{129,193},{193,1... | collective-permute-start | bytes 884744 | tf_op jit(solution)/shard_map/ppermute | solution.py:392
  45.4 1.1 %pad_maximum_fusion = bf16[384,1536]{1,0:T(8,128)(2,1)} fusion(bf16[384,768]{1,0:T(8,128)(2,1)S(1)} %add_convert_fusion.1, bf16[384,768]{1,0:T(8,128)(2,1)S(1)} %add_convert_fusion.2), kind=kLoop, calls=%fused_computation.1 | loop fusion | flops 2359296 | bytes 2359296 | tf_op jit(solution)/shard_map/concatenate | solution.py:477
  46.5 7.3 %all-to-all-start = ((bf16[16,24,1536]{2,1,0:T(8,128)(2,1)}), bf16[16,24,1536]{2,1,0:T(8,128)(2,1)}, u32[]{:S(2)}, u32[]{:S(2)}) async-start(bf16[16,24,1536]{2,1,0:T(8,128)(2,1)} %bitcast.39), calls=%async_computation | async-start | bytes 2359296 | tf_op jit(solution)/shard_map/all_to_all | solution.py:433
  53.8 1.5 %fusion.5 = (bf16[96,768]{1,0:T(8,128)(2,1)S(1)}, bf16[96,768]{1,0:T(8,128)(2,1)S(1)}) fusion(bf16[96,1536]{1,0:T(8,128)(2,1)} %collective-permute-done.7, bf16[96,1536]{1,0:T(8,128)(2,1)} %collective-permute-done.6, bf16[4,96,768]{2,1,0:T(8,128)(2,1)} %bitcast.45, bf16[4,96,768]{2,1,0:T(8,128)(2,1)} %bitcast.42), kind=kLoop, calls=%fused_computation.17 | loop fusion | flops 884736 | bytes 1179648 | tf_op jit(solution)/shard_map/convert_element_type | solution.py:399
  55.4 1.6 %collective-permute-start.10 = (bf16[48,1536]{1,0:T(8,128)(2,1)S(1)}, bf16[48,1536]{1,0:T(8,128)(2,1)S(1)}, u32[]{:S(2)}, u32[]{:S(2)}) collective-permute-start(bf16[48,1536]{1,0:T(8,128)(2,1)S(1)} %slice.74), channel_id=1, source_target_pairs={{0,16},{8,24},{16,0},{24,8},{32,48},{40,56},{48,32},{56,40},{1,17}... | collective-permute-start | bytes 442376 | tf_op jit(solution)/shard_map/ppermute | solution.py:392
  56.9 1.0 %copy-done.12 = bf16[2,256,512]{2,1,0:T(8,128)(2,1)S(1)} copy-done((bf16[2,256,512]{2,1,0:T(8,128)(2,1)S(1)}, bf16[2,256,512]{2,1,0:T(8,128)(2,1)}, u32[]{:S(2)}) %copy-start.12) | copy-done | bytes 524312
  58.0 0.9 copy-done.14
  58.9 0.9 copy-done.16
  59.8 1.7 %out_part.1 = bf16[16,2,16,768]{3,2,1,0:T(8,128)(2,1)} custom-call(bf16[2,256,768]{2,1,0:T(8,128)(2,1)S(1)} %copy-done.2, bf16[2,256,128]{2,1,0:T(8,128)(2,1)S(1)} %copy-done.16, bf16[2,256,512]{2,1,0:T(8,128)(2,1)S(1)} %copy-done.12, bf16[2,256,256]{2,1,0:T(8,128)(2,1)S(1)} %copy-done.14, bf16[768,768]{1,0:T(8,128)(2,1)S(1)} %copy-done.6), custom_call_target="tpu_custom_call" | custom-call | flops 1000 | bytes 1000 | tf_op jit(solution)/shard_map/out_part/pallas_call | solution.py:329
  61.5 9.6 %collective-permute-done.10 = bf16[48,1536]{1,0:T(8,128)(2,1)S(1)} collective-permute-done((bf16[48,1536]{1,0:T(8,128)(2,1)S(1)}, bf16[48,1536]{1,0:T(8,128)(2,1)S(1)}, u32[]{:S(2)}, u32[]{:S(2)}) %collective-permute-start.10) | collective-permute-done | bytes 147488 | tf_op jit(solution)/shard_map/ppermute | solution.py:392
  71.1 2.6 %collective-permute-start.11 = (bf16[24,1536]{1,0:T(8,128)(2,1)S(1)}, bf16[24,1536]{1,0:T(8,128)(2,1)}, u32[]{:S(2)}, u32[]{:S(2)}) collective-permute-start(bf16[24,1536]{1,0:T(8,128)(2,1)S(1)} %slice.86), channel_id=1, source_target_pairs={{0,48},{8,56},{16,32},{24,40},{32,16},{40,24},{48,0},{56,8},{1,49}... | collective-permute-start | bytes 221192 | tf_op jit(solution)/shard_map/ppermute | solution.py:392
  73.7 5.0 %grad_part.1 = bf16[16,2,16,768]{3,2,1,0:T(8,128)(2,1)} custom-call(bf16[2,256,768]{2,1,0:T(8,128)(2,1)S(1)} %copy-done.2, bf16[16,2,16,768]{3,2,1,0:T(8,128)(2,1)S(1)} %bitcast.35, bf16[2,2,256,768]{3,2,1,0:T(8,128)(2,1)S(1)} %copy-done.4, bf16[1,2,256,768]{3,2,1,0:T(8,128)(2,1)S(1)} %copy-done.10, bf16[768,2304]{1,0:T(8,128)(2,1)S(1)} %copy-done, ...), custom_call_target="tpu_custom_call" | custom-call | flops 1000 | bytes 1000 | tf_op jit(solution)/shard_map/grad_part/pallas_call | solution.py:371
  78.7 1.6 %fusion.6 = (bf16[24,1536]{1,0:T(8,128)(2,1)S(1)}, bf16[24,1536]{1,0:T(8,128)(2,1)S(1)}) fusion(bf16[16,24,1536]{2,1,0:T(8,128)(2,1)} %all-to-all-done, bf16[24,1536]{1,0:T(8,128)(2,1)} %collective-permute-done.11, bf16[48,1536]{1,0:T(8,128)(2,1)} %copy-done.21), kind=kLoop, calls=%fused_computation.21 | loop fusion | flops 1327104 | bytes 1474560 | tf_op jit(solution)/shard_map/convert_element_type | solution.py:399
  80.3 13.0 %all_to_all.10 = bf16[8,3,3072]{2,1,0:T(4,128)(2,1)S(1)} all-to-all(bf16[8,3,3072]{2,1,0:T(4,128)(2,1)S(1)} %reshape.80), channel_id=1, replica_groups=mesh['dp'=4,'gy'=8,'gx'=8] {'gx'}, dimensions={0} | all-to-all | bytes 294912 | tf_op jit(solution)/shard_map/all_to_all | solution.py:433
  93.5 0.6 slice.89
  94.2 0.6 reshape.82
  (73 shorter events, 3.0 us)
Async XLA Ops:
  0.6 1.1 %copy-start.17 = (bf16[1,16,32,768]{3,2,1,0:T(8,128)(2,1)S(1)}, bf16[1,16,32,768]{3,2,1,0:T(8,128)(2,1)}, u32[]{:S(2)}) copy-start(bf16[1,16,32,768]{3,2,1,0:T(8,128)(2,1)} %param.5) | copy-start | bytes 2359300
  1.8 9.8 %copy-start.5 = (bf16[768,768]{1,0:T(8,128)(2,1)S(1)}, bf16[768,768]{1,0:T(8,128)(2,1)}, u32[]{:S(2)}) copy-start(bf16[768,768]{1,0:T(8,128)(2,1)} %wp_ref.1) | copy-start | bytes 3538948
  1.8 9.8 %copy-start.7 = (bf16[1,16,32,768]{3,2,1,0:T(8,128)(2,1)S(1)}, bf16[1,16,32,768]{3,2,1,0:T(8,128)(2,1)}, u32[]{:S(2)}) copy-start(bf16[1,16,32,768]{3,2,1,0:T(8,128)(2,1)} %param.6) | copy-start | bytes 2359300
  1.8 9.8 %copy-start.18 = (s32[1,16,32]{2,1,0:T(8,128)S(1)}, s32[1,16,32]{2,1,0:T(8,128)}, u32[]{:S(2)}) copy-start(s32[1,16,32]{2,1,0:T(8,128)} %param.7) | copy-start | bytes 6148
  1.9 11.2 %collective-permute-start.1 = (bf16[8,8,768]{2,1,0:T(8,128)(2,1)S(1)}, bf16[8,8,768]{2,1,0:T(8,128)(2,1)S(1)}, u32[]{:S(2)}, u32[]{:S(2)}) collective-permute-start(bf16[8,8,768]{2,1,0:T(8,128)(2,1)S(1)} %get-tuple-element.46), channel_id=1, source_target_pairs={{0,7},{1,0},{2,1},{3,2},{4,3},{5,4},{6,5},{7,6},{8,15},{9,8},{10,9... | collective-permute-start | bytes 294920 | tf_op jit(solution)/shard_map/ppermute | solution.py:392
  7.8 5.3 %collective-permute-start.2 = (bf16[8,8,768]{2,1,0:T(8,128)(2,1)S(1)}, bf16[8,8,768]{2,1,0:T(8,128)(2,1)S(1)}, u32[]{:S(2)}, u32[]{:S(2)}) collective-permute-start(bf16[8,8,768]{2,1,0:T(8,128)(2,1)S(1)} %get-tuple-element.47), channel_id=1, source_target_pairs={{0,63},{1,56},{2,57},{3,58},{4,59},{5,60},{6,61},{7,62},{8,7},{9,0... | collective-permute-start | bytes 294920 | tf_op jit(solution)/shard_map/ppermute | solution.py:450
  10.4 5.7 %collective-permute-start = (bf16[8,24,768]{2,1,0:T(8,128)(2,1)S(1)}, bf16[8,24,768]{2,1,0:T(8,128)(2,1)S(1)}, u32[]{:S(2)}, u32[]{:S(2)}) collective-permute-start(bf16[8,24,768]{2,1,0:T(8,128)(2,1)S(1)} %get-tuple-element.45), channel_id=1, source_target_pairs={{0,56},{8,0},{16,8},{24,16},{32,24},{40,32},{48,40},{56,48},{1,57}... | collective-permute-start | bytes 884744 | tf_op jit(solution)/shard_map/ppermute | solution.py:392
  11.5 4.6 %copy-start = (bf16[768,2304]{1,0:T(8,128)(2,1)S(1)}, bf16[768,2304]{1,0:T(8,128)(2,1)}, u32[]{:S(2)}) copy-start(bf16[768,2304]{1,0:T(8,128)(2,1)} %wv_ref.5) | copy-start | bytes 10616836
  13.1 19.5 %copy-start.15 = (bf16[2,256,128]{2,1,0:T(8,128)(2,1)}, bf16[2,256,128]{2,1,0:T(8,128)(2,1)S(1)}, u32[]{:S(2)}) copy-start(bf16[2,256,128]{2,1,0:T(8,128)(2,1)S(1)} %get-tuple-element.48.tis_ref) | copy-start | bytes 393220
  26.8 1.1 %copy-start.1 = (bf16[2,256,768]{2,1,0:T(8,128)(2,1)}, bf16[2,256,768]{2,1,0:T(8,128)(2,1)S(1)}, u32[]{:S(2)}) copy-start(bf16[2,256,768]{2,1,0:T(8,128)(2,1)S(1)} %get-tuple-element.79.xw_ref) | copy-start | bytes 2359300
  26.8 1.4 %copy-start.3 = (bf16[2,2,256,768]{3,2,1,0:T(8,128)(2,1)}, bf16[2,2,256,768]{3,2,1,0:T(8,128)(2,1)S(1)}, u32[]{:S(2)}) copy-start(bf16[2,2,256,768]{3,2,1,0:T(8,128)(2,1)S(1)} %get-tuple-element.80.dqkv0_ref) | copy-start | bytes 4718596
  26.8 11.1 %copy-start.11 = (bf16[2,256,512]{2,1,0:T(8,128)(2,1)}, bf16[2,256,512]{2,1,0:T(8,128)(2,1)S(1)}, u32[]{:S(2)}) copy-start(bf16[2,256,512]{2,1,0:T(8,128)(2,1)S(1)} %get-tuple-element.65.att0_ref) | copy-start | bytes 1572868
  26.9 2.9 %collective-permute-start.3 = (bf16[384,1536]{1,0:T(8,128)(2,1)S(1)}, bf16[384,1536]{1,0:T(8,128)(2,1)S(1)}, u32[]{:S(2)}, u32[]{:S(2)}) collective-permute-start(bf16[384,1536]{1,0:T(8,128)(2,1)S(1)} %get-tuple-element.52), channel_id=1, source_target_pairs={{0,8},{8,0},{16,24},{24,16},{32,40},{40,32},{48,56},{56,48},{1,9},... | collective-permute-start | bytes 3538952 | tf_op jit(solution)/shard_map/ppermute | solution.py:392
  30.2 9.6 %copy-start.20 = (bf16[384,768]{1,0:T(8,128)(2,1)}, bf16[384,768]{1,0:T(8,128)(2,1)S(1)}, u32[]{:S(2)}) copy-start(bf16[384,768]{1,0:T(8,128)(2,1)S(1)} %get-tuple-element.87) | copy-start | bytes 1769476
  30.2 9.6 %copy-start.19 = (bf16[384,768]{1,0:T(8,128)(2,1)}, bf16[384,768]{1,0:T(8,128)(2,1)S(1)}, u32[]{:S(2)}) copy-start(bf16[384,768]{1,0:T(8,128)(2,1)S(1)} %get-tuple-element.86) | copy-start | bytes 1769476
  30.2 7.6 %collective-permute-start.4 = (bf16[96,768]{1,0:T(8,128)(2,1)S(1)}, bf16[96,768]{1,0:T(8,128)(2,1)S(1)}, u32[]{:S(2)}, u32[]{:S(2)}) collective-permute-start(bf16[96,768]{1,0:T(8,128)(2,1)S(1)} %get-tuple-element.93), channel_id=1, source_target_pairs={{0,64},{64,128},{128,192},{192,0},{1,65},{65,129},{129,193},{193,1... | collective-permute-start | bytes 442376 | tf_op jit(solution)/shard_map/ppermute | solution.py:392
  30.8 7.1 %collective-permute-start.5 = (bf16[96,768]{1,0:T(8,128)(2,1)S(1)}, bf16[96,768]{1,0:T(8,128)(2,1)S(1)}, u32[]{:S(2)}, u32[]{:S(2)}) collective-permute-start(bf16[96,768]{1,0:T(8,128)(2,1)S(1)} %get-tuple-element.91), channel_id=1, source_target_pairs={{0,192},{64,0},{128,64},{192,128},{1,193},{65,1},{129,65},{193,129... | collective-permute-start | bytes 442376 | tf_op jit(solution)/shard_map/ppermute | solution.py:392
  37.8 1.9 %copy-start.13 = (bf16[2,256,256]{2,1,0:T(8,128)(2,1)}, bf16[2,256,256]{2,1,0:T(8,128)(2,1)S(1)}, u32[]{:S(2)}) copy-start(bf16[2,256,256]{2,1,0:T(8,128)(2,1)S(1)} %get-tuple-element.76.att1_ref) | copy-start | bytes 786436
  37.9 2.1 %collective-permute-start.8 = (bf16[384,768]{1,0:T(8,128)(2,1)S(1)}, bf16[384,768]{1,0:T(8,128)(2,1)S(1)}, u32[]{:S(2)}, u32[]{:S(2)}) collective-permute-start(bf16[384,768]{1,0:T(8,128)(2,1)S(1)} %get-tuple-element.64), channel_id=1, source_target_pairs={{0,8},{8,0},{16,24},{24,16},{32,40},{40,32},{48,56},{56,48},{1,9},... | collective-permute-start | bytes 1769480 | tf_op jit(solution)/shard_map/ppermute | solution.py:392
  40.0 5.3 %collective-permute-start.9 = (bf16[384,768]{1,0:T(8,128)(2,1)S(1)}, bf16[384,768]{1,0:T(8,128)(2,1)S(1)}, u32[]{:S(2)}, u32[]{:S(2)}) collective-permute-start(bf16[384,768]{1,0:T(8,128)(2,1)S(1)} %get-tuple-element.72), channel_id=1, source_target_pairs={{0,8},{8,0},{16,24},{24,16},{32,40},{40,32},{48,56},{56,48},{1,9},... | collective-permute-start | bytes 1769480 | tf_op jit(solution)/shard_map/ppermute | solution.py:392
  41.2 12.6 %collective-permute-start.7 = (bf16[96,1536]{1,0:T(8,128)(2,1)}, bf16[96,1536]{1,0:T(8,128)(2,1)}, u32[]{:S(2)}, u32[]{:S(2)}) collective-permute-start(bf16[96,1536]{1,0:T(8,128)(2,1)} %pad_maximum_fusion.2), channel_id=1, source_target_pairs={{0,192},{64,0},{128,64},{192,128},{1,193},{65,1},{129,65},{193,129... | collective-permute-start | bytes 884744 | tf_op jit(solution)/shard_map/ppermute | solution.py:392
  42.7 11.1 %collective-permute-start.6 = (bf16[96,1536]{1,0:T(8,128)(2,1)}, bf16[96,1536]{1,0:T(8,128)(2,1)}, u32[]{:S(2)}, u32[]{:S(2)}) collective-permute-start(bf16[96,1536]{1,0:T(8,128)(2,1)} %pad_maximum_fusion.1), channel_id=1, source_target_pairs={{0,64},{64,128},{128,192},{192,0},{1,65},{65,129},{129,193},{193,1... | collective-permute-start | bytes 884744 | tf_op jit(solution)/shard_map/ppermute | solution.py:392
  46.5 32.1 %all-to-all-start = ((bf16[16,24,1536]{2,1,0:T(8,128)(2,1)}), bf16[16,24,1536]{2,1,0:T(8,128)(2,1)}, u32[]{:S(2)}, u32[]{:S(2)}) async-start(bf16[16,24,1536]{2,1,0:T(8,128)(2,1)} %bitcast.39), calls=%async_computation | async-start | bytes 2359296 | tf_op jit(solution)/shard_map/all_to_all | solution.py:433
  53.8 3.1 %copy-start.2 = (bf16[2,256,768]{2,1,0:T(8,128)(2,1)S(1)}, bf16[2,256,768]{2,1,0:T(8,128)(2,1)}, u32[]{:S(2)}) copy-start(bf16[2,256,768]{2,1,0:T(8,128)(2,1)} %copy-done.1) | copy-start | bytes 2359300
  53.8 3.1 %copy-start.6 = (bf16[768,768]{1,0:T(8,128)(2,1)S(1)}, bf16[768,768]{1,0:T(8,128)(2,1)}, u32[]{:S(2)}) copy-start(bf16[768,768]{1,0:T(8,128)(2,1)} %wp_ref.1) | copy-start | bytes 3538948
  55.4 15.7 %collective-permute-start.10 = (bf16[48,1536]{1,0:T(8,128)(2,1)S(1)}, bf16[48,1536]{1,0:T(8,128)(2,1)S(1)}, u32[]{:S(2)}, u32[]{:S(2)}) collective-permute-start(bf16[48,1536]{1,0:T(8,128)(2,1)S(1)} %slice.74), channel_id=1, source_target_pairs={{0,16},{8,24},{16,0},{24,8},{32,48},{40,56},{48,32},{56,40},{1,17}... | collective-permute-start | bytes 442376 | tf_op jit(solution)/shard_map/ppermute | solution.py:392
  56.9 1.0 %copy-start.12 = (bf16[2,256,512]{2,1,0:T(8,128)(2,1)S(1)}, bf16[2,256,512]{2,1,0:T(8,128)(2,1)}, u32[]{:S(2)}) copy-start(bf16[2,256,512]{2,1,0:T(8,128)(2,1)} %copy-done.11) | copy-start | bytes 1572868
  59.8 13.8 %copy-start.4 = (bf16[2,2,256,768]{3,2,1,0:T(8,128)(2,1)S(1)}, bf16[2,2,256,768]{3,2,1,0:T(8,128)(2,1)}, u32[]{:S(2)}) copy-start(bf16[2,2,256,768]{3,2,1,0:T(8,128)(2,1)} %copy-done.3) | copy-start | bytes 4718596
  59.8 13.8 %copy-start.8 = (bf16[1,16,32,768]{3,2,1,0:T(8,128)(2,1)S(1)}, bf16[1,16,32,768]{3,2,1,0:T(8,128)(2,1)}, u32[]{:S(2)}) copy-start(bf16[1,16,32,768]{3,2,1,0:T(8,128)(2,1)} %param.6) | copy-start | bytes 2359300
  59.8 13.8 %copy-start.10 = (bf16[1,2,256,768]{3,2,1,0:T(8,128)(2,1)S(1)}, bf16[1,2,256,768]{3,2,1,0:T(8,128)(2,1)}, u32[]{:S(2)}) copy-start(bf16[1,2,256,768]{3,2,1,0:T(8,128)(2,1)} %copy-done.9) | copy-start | bytes 2359300
  71.1 7.5 %copy-start.21 = (bf16[48,1536]{1,0:T(8,128)(2,1)}, bf16[48,1536]{1,0:T(8,128)(2,1)S(1)}, u32[]{:S(2)}) copy-start(bf16[48,1536]{1,0:T(8,128)(2,1)S(1)} %add_convert_fusion.3) | copy-start | bytes 442372
  71.1 7.5 %collective-permute-start.11 = (bf16[24,1536]{1,0:T(8,128)(2,1)S(1)}, bf16[24,1536]{1,0:T(8,128)(2,1)}, u32[]{:S(2)}, u32[]{:S(2)}) collective-permute-start(bf16[24,1536]{1,0:T(8,128)(2,1)S(1)} %slice.86), channel_id=1, source_target_pairs={{0,48},{8,56},{16,32},{24,40},{32,16},{40,24},{48,0},{56,8},{1,49}... | collective-permute-start | bytes 221192 | tf_op jit(solution)/shard_map/ppermute | solution.py:392
  (3 other events, 2.7 us)

commit v6 on v5

--- a/solution.py
+++ b/solution.py
@@ -113,17 +113,17 @@
     )(cot, tissue, w_proj)
 
 
-def row_order(permutes):
+def row_order(first):
     gy = lax.axis_index("gy")
     dp, y, core = lax.axis_index("dp"), gy >> 1, gy & 1
     at = lax.broadcasted_iota(jnp.int32, (D, 1), 0)
     third = ((at.astype(F32) + 0.5) * (1.0 / 3)).astype(jnp.int32)
-    outer, inner, depth = (third >> 5) & 3, (third >> 3) & 3, third & 7
-    if permutes:
-        dp_of = (outer + dp) & 3
-        y_of = ((inner >> 1) ^ ((inner & 1) * 3)) ^ y
+    distance, depth = (third >> 5) & 3, third & 7
+    partner = ((third >> 4) & 1) ^ (((third >> 3) & 1) * 3)
+    if first == "dp":
+        dp_of, y_of = (distance + dp) & 3, partner ^ y
     else:
-        dp_of, y_of = outer, inner
+        dp_of, y_of = partner ^ dp, (distance + y) & 3
     core_of = (third >> 7) ^ core
     source = ((dp_of * 8 + y_of * 2 + core_of) * 8 + depth) * 3 + at - third * 3
     column = lax.broadcasted_iota(jnp.int32, (D, D), 1)
@@ -201,7 +201,7 @@
         low = below_ref[...].astype(F32)
         right = right_ref[...].astype(F32)
         diag = diag_ref[...].astype(F32)
-        perm = row_order(True)
+        perm = row_order("dp")
         for w in range(2):
             if w == 0:
                 top, bottom = own[:, 8:24], low[:, :16]
@@ -232,7 +232,7 @@
 
 
 def turn_kernel(hid_ref, hid_t_ref):
-    hid_t_ref[...] = nt(row_order(False), hid_ref[...].reshape(2 * CELLS, D)).astype(BF)
+    hid_t_ref[...] = nt(row_order("gy"), hid_ref[...].reshape(2 * CELLS, D)).astype(BF)
 
 
 def turn(hid):
@@ -302,7 +302,7 @@
 
 def proj_kernel(att0_ref, att1_ref, db_ref, keep_ref, send_ref):
     attended = jnp.concatenate([att0_ref[...], att1_ref[...]], 2).reshape(2 * CELLS, D)
-    att_t = nt(row_order(False), attended).astype(BF)
+    att_t = nt(row_order("gy"), attended).astype(BF)
     put(nn(att_t, db_ref[...].reshape(2 * CELLS, D)), keep_ref, send_ref)
 
 
@@ -474,19 +474,24 @@
     came = send(send1, "gy", lambda i: i ^ 1)
     keep2, send2 = proj_grad(att0, att1, db)
     came, send2, keep2 = tie(came, send2, keep2)
-    rows_b = jnp.concatenate([add(keep1, came), add(keep2, send(send2, "gy", lambda i: i ^ 1))], 1)
-    rows_b, att1 = tie(rows_b, att1)
-    same_core = [[d * 8 + y * 2 + c for d in range(4) for y in range(4)] for c in range(2)]
-    parts_b = exchange(rows_b, ("dp", "gy"), same_core)
-    rows_a, att1 = tie(ring_end(low_a, high_a, came_a), att1)
+    low_b = add(keep1, came)
+    high_b = add(keep2, send(send2, "gy", lambda i: i ^ 1))
+    low_b, high_b, att1 = tie(blocks(low_b), blocks(high_b), att1)
+    came_b = ring_start(low_b, high_b, "gy", 2)
+    out = out_part(xw, tis, att0, att1, w_proj)
+    came_b, out, xw, low_a, high_a = tie(came_b, out, xw, low_a, high_a)
+    came_b = ring_pass(low_b, high_b, came_b, "gy", 2)
+    rows_a = ring_end(low_a, high_a, came_a)
     came_a = halve_start(rows_a, "gy", 2)
-    out = out_part(xw, tis, att0, att1, w_proj)
-    came_a, out, xw = tie(came_a, out, xw)
+    grad = grad_part(xw, cot, dqkv0, dqkv1, w_qkv)
+    came_a, came_b, grad = tie(came_a, came_b, grad)
     rows_a = halve_end(rows_a, came_a)
+    rows_b = ring_end(low_b, high_b, came_b)
     came_a = halve_start(rows_a, "gy", 6)
-    grad = grad_part(xw, cot, dqkv0, dqkv1, w_qkv)
-    came_a, grad, parts_b = tie(came_a, grad, parts_b)
-    rows = jnp.concatenate([halve_end(rows_a, came_a), add(*parts_b)], 1)
+    came_b = halve_start(rows_b, "dp", 1)
+    rows_b = halve_end(rows_b, came_b)
+    came_b = halve_start(rows_b, "dp", 3)
+    rows = jnp.concatenate([halve_end(rows_a, came_a), halve_end(rows_b, came_b)], 1)
     parts = exchange(rows, ("gx",))
     total = jnp.sum(parts.astype(F32), 0) * (1.0 / math.sqrt(512))
     grad_qkv = total[:, : 3 * D].reshape(3, GROUPS, 3, GW).transpose(0, 2, 1, 3)

time: 95.3 us -> 89.1 us (0.935)
  other arithmetic: 6.39 us -> 1.28 us
  waiting for transfers between devices: 14.3 us -> 19 us
  local copies, waits for them, and re-layouts: 6.89 us -> 2.72 us
  starting transfers between devices: 27.3 us -> 25.6 us
    all_to_all x1 -> x0, starting transfers between devices: 7.26 us -> none  [exchange(): return lax.all_to_all(rows, axis, 0, 0, axis_index_groups=groups)]
    ppermute x11 -> x17, starting transfers between devices: 17.4 us -> 22.9 us  [send(): lax.ppermute(value, axis, [(i, move(i) % devices) for i in range(devices)])]
    ppermute x11 -> x17, waiting for transfers between devices: 14.3 us -> 19 us  [send(): lax.ppermute(value, axis, [(i, move(i) % devices) for i in range(devices)])]
    unnamed x44 -> x10, local copies, waits for them, and re-layouts: 5.35 us -> 1.14 us
    convert_element_type x8 -> x13, other arithmetic: 3.7 us -> 1.06 us  [add(): return total.astype(BF)]
    concatenate x2 -> x1, other arithmetic: 1.11 us -> 0.01 us  [shards(): jnp.concatenate([halve_end(rows_a, came_a), halve_end(rows_b, came_b)], 1)]
  transfers between devices with their start and end apart: 13 -> 18, of which waited for: 4 -> 12; matrix products, arithmetic and copies ran while one was open for 5% -> 1% of each run, Pallas kernels for 16% -> 17%
where the time goes in v6:
time: 89.1 us; the launch traced here: 88.2 us
  Pallas kernels  26.1 us (29%)
  starting transfers between devices  25.6 us (29%)
  waiting for transfers between devices  19 us (21%)
  blocking collectives  12.5 us (14%)
  local copies, waits for them, and re-layouts  2.72 us (3%)
  other arithmetic  1.28 us (1%)
  between operations  0.93 us (1%)
    ppermute x17, starting transfers between devices, send(): lax.ppermute(value, axis, [(i, move(i) % devices) for i in range(devices)])  22.9 us
    ppermute x17, waiting for transfers between devices, send(): lax.ppermute(value, axis, [(i, move(i) % devices) for i in range(devices)])  19 us
    all_to_all x1, blocking collectives, exchange(): return lax.all_to_all(rows, axis, 0, 0, axis_index_groups=groups)  12.5 us
    pallas_call x1, Pallas kernels, first_heads(): pl.pallas_call(first_kernel, grid=(2,), in_specs=[full((16, 32, D)), full...  10.7 us
    pallas_call x1, Pallas kernels, grad_part(): pl.pallas_call(grad_kernel, grid=(GROUPS,), in_specs=[full((2, CELLS, D))...  4.97 us
    pallas_call x1, Pallas kernels, last_heads(): pl.pallas_call(last_kernel, grid=(1,), in_specs=[full((2, CELLS, D)), ful...  4.37 us
    ppermute x1, starting transfers between devices, shards(): lax.ppermute(corner, ('gy', 'gx'), [(a * nx + b, (a - 1) % ny * nx + (b -...  2.62 us
    pallas_call x1, Pallas kernels, proj_grad(): pl.pallas_call(proj_kernel, out_shape=[shape, shape], compiler_params=plt...  1.87 us
  transfers between devices with their start and end apart: 18, of which 12 were waited for; matrix products, arithmetic and copies ran while one was open for 1% of the time, Pallas kernels for 17%

profile of v6, /device:TPU:6, one launch (start us, length us, event | category | flops | bytes accessed | tf_op | source)
XLA Modules:
  0.0 88.2 jit_solution(6010158683549545018)
XLA Ops:
  0.6 1.1 %copy-done.3 = bf16[1,16,32,768]{3,2,1,0:T(8,128)(2,1)S(1)} copy-done((bf16[1,16,32,768]{3,2,1,0:T(8,128)(2,1)S(1)}, bf16[1,16,32,768]{3,2,1,0:T(8,128)(2,1)}, u32[]{:S(2)}) %copy-start.3) | copy-done | bytes 786456
  1.9 5.9 %collective-permute-start.1 = (bf16[8,8,768]{2,1,0:T(8,128)(2,1)S(1)}, bf16[8,8,768]{2,1,0:T(8,128)(2,1)S(1)}, u32[]{:S(2)}, u32[]{:S(2)}) collective-permute-start(bf16[8,8,768]{2,1,0:T(8,128)(2,1)S(1)} %get-tuple-element.49), channel_id=1, source_target_pairs={{0,7},{1,0},{2,1},{3,2},{4,3},{5,4},{6,5},{7,6},{8,15},{9,8},{10,9... | collective-permute-start | bytes 294920 | tf_op jit(solution)/shard_map/ppermute | solution.py:392
  7.8 2.6 %collective-permute-start.2 = (bf16[8,8,768]{2,1,0:T(8,128)(2,1)S(1)}, bf16[8,8,768]{2,1,0:T(8,128)(2,1)S(1)}, u32[]{:S(2)}, u32[]{:S(2)}) collective-permute-start(bf16[8,8,768]{2,1,0:T(8,128)(2,1)S(1)} %get-tuple-element.50), channel_id=1, source_target_pairs={{0,63},{1,56},{2,57},{3,58},{4,59},{5,60},{6,61},{7,62},{8,7},{9,0... | collective-permute-start | bytes 294920 | tf_op jit(solution)/shard_map/ppermute | solution.py:450
  10.4 1.1 %collective-permute-start = (bf16[8,24,768]{2,1,0:T(8,128)(2,1)S(1)}, bf16[8,24,768]{2,1,0:T(8,128)(2,1)S(1)}, u32[]{:S(2)}, u32[]{:S(2)}) collective-permute-start(bf16[8,24,768]{2,1,0:T(8,128)(2,1)S(1)} %get-tuple-element.48), channel_id=1, source_target_pairs={{0,56},{8,0},{16,8},{24,16},{32,24},{40,32},{48,40},{56,48},{1,57}... | collective-permute-start | bytes 884744 | tf_op jit(solution)/shard_map/ppermute | solution.py:392
  11.6 1.5 %branch.1 = (bf16[2,256,768]{2,1,0:T(8,128)(2,1)S(1)}, bf16[2,256,768]{2,1,0:T(8,128)(2,1)S(1)}, bf16[2,256,128]{2,1,0:T(8,128)(2,1)S(1)}, bf16[2,256,128]{2,1,0:T(8,128)(2,1)S(1)}) custom-call(bf16[16,2,16,768]{3,2,1,0:T(8,128)(2,1)S(1)} %bitcast.50, s32[16,32]{1,0:T(8,128)S(1)} %bitcast.54, bf16[768,768]{1,0:T(8,128)(2,1)S(1)} %copy-done.1), custom_call_target="tpu_custom_call" | custom-call | flops 20000000000 | bytes 4000000 | tf_op jit(solution)/shard_map/branch/pallas_call | solution.py:100
  13.1 3.1 %collective-permute-done.below_ref = bf16[8,24,768]{2,1,0:T(8,128)(2,1)S(1)} collective-permute-done((bf16[8,24,768]{2,1,0:T(8,128)(2,1)S(1)}, bf16[8,24,768]{2,1,0:T(8,128)(2,1)S(1)}, u32[]{:S(2)}, u32[]{:S(2)}) %collective-permute-start) | collective-permute-done | bytes 294944 | tf_op jit(solution)/shard_map/ppermute | solution.py:392
  16.2 10.7 %first_heads.1 = (bf16[384,1536]{1,0:T(8,128)(2,1)S(1)}, bf16[384,1536]{1,0:T(8,128)(2,1)S(1)}, bf16[2,256,512]{2,1,0:T(8,128)(2,1)S(1)}, bf16[2,2,256,768]{3,2,...) custom-call(bf16[16,32,768]{2,1,0:T(8,128)(2,1)S(1)} %bitcast.53, ...), custom_call_target="tpu_custom_call" | custom-call | flops 6000000000 | bytes 10000000 | tf_op jit(solution)/shard_map/first_heads/pallas_call | solution.py:276
  27.0 1.0 %turn.1.hid_t_ref = bf16[768,512]{1,0:T(8,128)(2,1)S(1)} custom-call(bf16[2,256,768]{2,1,0:T(8,128)(2,1)S(1)} %get-tuple-element.54.hid_ref), custom_call_target="tpu_custom_call" | custom-call | flops 2000000000 | bytes 2000000 | tf_op jit(solution)/shard_map/turn/pallas_call | solution.py:239
  28.0 1.8 %collective-permute-done.3 = bf16[384,1536]{1,0:T(8,128)(2,1)S(1)} collective-permute-done((bf16[384,1536]{1,0:T(8,128)(2,1)S(1)}, bf16[384,1536]{1,0:T(8,128)(2,1)S(1)}, u32[]{:S(2)}, u32[]{:S(2)}) %collective-permute-start.3) | collective-permute-done | bytes 1179680 | tf_op jit(solution)/shard_map/ppermute | solution.py:392
  30.2 0.6 collective-permute-start.4
  30.8 1.8 %collective-permute-start.5 = (bf16[96,768]{1,0:T(8,128)(2,1)S(1)}, bf16[96,768]{1,0:T(8,128)(2,1)S(1)}, u32[]{:S(2)}, u32[]{:S(2)}) collective-permute-start(bf16[96,768]{1,0:T(8,128)(2,1)S(1)} %get-tuple-element.103), channel_id=1, source_target_pairs={{0,192},{64,0},{128,64},{192,128},{1,193},{65,1},{129,65},{193,129... | collective-permute-start | bytes 442376 | tf_op jit(solution)/shard_map/ppermute | solution.py:392
  32.6 4.4 %last_heads.1 = (bf16[384,768]{1,0:T(8,128)(2,1)S(1)}, bf16[384,768]{1,0:T(8,128)(2,1)S(1)}, bf16[2,256,256]{2,1,0:T(8,128)(2,1)S(1)}, bf16[1,2,256,768]{3,2,1,0:T(8,128)(2,1)S(1)}) custom-call(bf16[2,256,768]{2,1,0:T(8,128)(2,1)S(1)} %get-tuple-element.54.hid_ref, bf16[768,512]{1,0:T(8,128)(2,1)S(1)} %turn.1.hid_t_ref, ...), custom_call_target="tpu_custom_call" | custom-call | flops 4000000000 | bytes 6000000 | tf_op jit(solution)/shard_map/last_heads/pallas_call | solution.py:291
  37.0 0.9 %collective-permute-done.5 = bf16[96,768]{1,0:T(8,128)(2,1)S(1)} collective-permute-done((bf16[96,768]{1,0:T(8,128)(2,1)S(1)}, bf16[96,768]{1,0:T(8,128)(2,1)S(1)}, u32[]{:S(2)}, u32[]{:S(2)}) %collective-permute-start.5) | collective-permute-done | bytes 147488 | tf_op jit(solution)/shard_map/ppermute | solution.py:392
  37.9 1.9 %proj_grad.1 = (bf16[384,768]{1,0:T(8,128)(2,1)S(1)}, bf16[384,768]{1,0:T(8,128)(2,1)S(1)}) custom-call(bf16[2,256,512]{2,1,0:T(8,128)(2,1)S(1)} %get-tuple-element.66.att0_ref, bf16[2,256,256]{2,1,0:T(8,128)(2,1)S(1)} %get-tuple-element.77.att1_ref, bf16[2,256,768]{2,1,0:T(8,128)(2,1)S(1)} %get-tuple-element.68.db_ref), custom_call_target="tpu_custom_call" | custom-call | flops 2000000000 | bytes 4000000 | tf_op jit(solution)/shard_map/proj_grad/pallas_call | solution.py:311
  39.9 0.5 collective-permute-start.7
  41.0 1.0 %collective-permute-done.7 = bf16[384,768]{1,0:T(8,128)(2,1)S(1)} collective-permute-done((bf16[384,768]{1,0:T(8,128)(2,1)S(1)}, bf16[384,768]{1,0:T(8,128)(2,1)S(1)}, u32[]{:S(2)}, u32[]{:S(2)}) %collective-permute-start.7) | collective-permute-done | bytes 589856 | tf_op jit(solution)/shard_map/ppermute | solution.py:392
  42.2 1.0 %collective-permute-start.8 = (bf16[96,768]{1,0:T(8,128)(2,1)S(1)}, bf16[96,768]{1,0:T(8,128)(2,1)S(1)}, u32[]{:S(2)}, u32[]{:S(2)}) collective-permute-start(bf16[96,768]{1,0:T(8,128)(2,1)S(1)} %get-tuple-element.97), channel_id=1, source_target_pairs={{0,16},{8,24},{16,32},{24,40},{32,48},{40,56},{48,0},{56,8},{1,17}... | collective-permute-start | bytes 442376 | tf_op jit(solution)/shard_map/ppermute | solution.py:392
  43.2 2.6 %collective-permute-start.9 = (bf16[96,768]{1,0:T(8,128)(2,1)S(1)}, bf16[96,768]{1,0:T(8,128)(2,1)S(1)}, u32[]{:S(2)}, u32[]{:S(2)}) collective-permute-start(bf16[96,768]{1,0:T(8,128)(2,1)S(1)} %get-tuple-element.99), channel_id=1, source_target_pairs={{0,48},{8,56},{16,0},{24,8},{32,16},{40,24},{48,32},{56,40},{1,49}... | collective-permute-start | bytes 442376 | tf_op jit(solution)/shard_map/ppermute | solution.py:392
  45.8 2.0 %collective-permute-start.10 = (bf16[96,1536]{1,0:T(8,128)(2,1)S(1)}, bf16[96,1536]{1,0:T(8,128)(2,1)S(1)}, u32[]{:S(2)}, u32[]{:S(2)}) collective-permute-start(bf16[96,1536]{1,0:T(8,128)(2,1)S(1)} %pad_maximum_fusion), channel_id=1, source_target_pairs={{0,64},{64,128},{128,192},{192,0},{1,65},{65,129},{129,193},{193,1... | collective-permute-start | bytes 884744 | tf_op jit(solution)/shard_map/ppermute | solution.py:392
  47.8 1.7 %out_part.1 = bf16[16,2,16,768]{3,2,1,0:T(8,128)(2,1)} custom-call(bf16[2,256,768]{2,1,0:T(8,128)(2,1)S(1)} %get-tuple-element.85.xw_ref, bf16[2,256,128]{2,1,0:T(8,128)(2,1)S(1)} %get-tuple-element.51.tis_ref, bf16[2,256,512]{2,1,0:T(8,128)(2,1)S(1)} %get-tuple-element.66.att0_ref, bf16[2,256,256]{2,1,0:T(8,128)(2,1)S(1)} %get-tuple-element.77.att1_ref, ...), custom_call_target="tpu_custom_call" | custom-call | flops 1000 | bytes 1000 | tf_op jit(solution)/shard_map/out_part/pallas_call | solution.py:329
  49.4 0.6 collective-permute-done.8
  50.2 3.1 %collective-permute-start.14 = (bf16[96,1536]{1,0:T(8,128)(2,1)S(1)}, bf16[96,1536]{1,0:T(8,128)(2,1)S(1)}, u32[]{:S(2)}, u32[]{:S(2)}) collective-permute-start(bf16[96,1536]{1,0:T(8,128)(2,1)S(1)} %pad_maximum_fusion.3), channel_id=1, source_target_pairs={{0,48},{8,56},{16,0},{24,8},{32,16},{40,24},{48,32},{56,40},{1,49}... | collective-permute-start | bytes 884744 | tf_op jit(solution)/shard_map/ppermute | solution.py:392
  53.6 1.2 %collective-permute-done.10 = bf16[96,1536]{1,0:T(8,128)(2,1)S(1)} collective-permute-done((bf16[96,1536]{1,0:T(8,128)(2,1)S(1)}, bf16[96,1536]{1,0:T(8,128)(2,1)S(1)}, u32[]{:S(2)}, u32[]{:S(2)}) %collective-permute-start.10) | collective-permute-done | bytes 294944 | tf_op jit(solution)/shard_map/ppermute | solution.py:392
  55.1 5.0 %grad_part.1 = bf16[16,2,16,768]{3,2,1,0:T(8,128)(2,1)} custom-call(bf16[2,256,768]{2,1,0:T(8,128)(2,1)S(1)} %get-tuple-element.85.xw_ref, bf16[16,2,16,768]{3,2,1,0:T(8,128)(2,1)S(1)} %bitcast.51, bf16[2,2,256,768]{3,2,1,0:T(8,128)(2,1)S(1)} %get-tuple-element.86.dqkv0_ref, bf16[1,2,256,768]{3,2,1,0:T(8,128)(2,1)S(1)} %get-tuple-element.87.dqkv1_ref, ...), custom_call_target="tpu_custom_call" | custom-call | flops 1000 | bytes 1000 | tf_op jit(solution)/shard_map/grad_part/pallas_call | solution.py:371
  60.1 2.7 %collective-permute-done.12 = bf16[48,1536]{1,0:T(8,128)(2,1)S(1)} collective-permute-done((bf16[48,1536]{1,0:T(8,128)(2,1)S(1)}, bf16[48,1536]{1,0:T(8,128)(2,1)S(1)}, u32[]{:S(2)}, u32[]{:S(2)}) %collective-permute-start.12) | collective-permute-done | bytes 147488 | tf_op jit(solution)/shard_map/ppermute | solution.py:392
  63.6 2.3 %collective-permute-start.15 = (bf16[24,1536]{1,0:T(8,128)(2,1)S(1)}, bf16[24,1536]{1,0:T(8,128)(2,1)S(1)}, u32[]{:S(2)}, u32[]{:S(2)}) collective-permute-start(bf16[24,1536]{1,0:T(8,128)(2,1)S(1)} %slice.153), channel_id=1, source_target_pairs={{0,48},{8,56},{16,32},{24,40},{32,16},{40,24},{48,0},{56,8},{1,49}... | collective-permute-start | bytes 221192 | tf_op jit(solution)/shard_map/ppermute | solution.py:392
  66.0 2.4 %collective-permute-done.16 = bf16[48,1536]{1,0:T(8,128)(2,1)S(1)} collective-permute-done((bf16[48,1536]{1,0:T(8,128)(2,1)S(1)}, bf16[48,1536]{1,0:T(8,128)(2,1)S(1)}, u32[]{:S(2)}, u32[]{:S(2)}) %collective-permute-start.16) | collective-permute-done | bytes 147488 | tf_op jit(solution)/shard_map/ppermute | solution.py:392
  68.4 0.7 collective-permute-start.17
  69.3 4.8 %collective-permute-done.17 = bf16[24,1536]{1,0:T(8,128)(2,1)S(1)} collective-permute-done((bf16[24,1536]{1,0:T(8,128)(2,1)S(1)}, bf16[24,1536]{1,0:T(8,128)(2,1)S(1)}, u32[]{:S(2)}, u32[]{:S(2)}) %collective-permute-start.17) | collective-permute-done | bytes 73760 | tf_op jit(solution)/shard_map/ppermute | solution.py:392
  74.2 12.5 %all_to_all.5 = bf16[8,3,3072]{2,1,0:T(4,128)(2,1)S(1)} all-to-all(bf16[8,3,3072]{2,1,0:T(4,128)(2,1)S(1)} %reshape.61), channel_id=1, replica_groups=mesh['dp'=4,'gy'=8,'gx'=8] {'gx'}, dimensions={0} | all-to-all | bytes 294912 | tf_op jit(solution)/shard_map/all_to_all | solution.py:433
  86.9 0.6 slice.159
  87.6 0.6 reshape.63
  (58 shorter events, 3.6 us)
Async XLA Ops:
  0.6 1.1 %copy-start.3 = (bf16[1,16,32,768]{3,2,1,0:T(8,128)(2,1)S(1)}, bf16[1,16,32,768]{3,2,1,0:T(8,128)(2,1)}, u32[]{:S(2)}) copy-start(bf16[1,16,32,768]{3,2,1,0:T(8,128)(2,1)} %param.5) | copy-start | bytes 2359300
  1.8 9.8 %copy-start.1 = (bf16[768,768]{1,0:T(8,128)(2,1)S(1)}, bf16[768,768]{1,0:T(8,128)(2,1)}, u32[]{:S(2)}) copy-start(bf16[768,768]{1,0:T(8,128)(2,1)} %wp_ref.1) | copy-start | bytes 3538948
  1.8 9.8 %copy-start.2 = (bf16[1,16,32,768]{3,2,1,0:T(8,128)(2,1)S(1)}, bf16[1,16,32,768]{3,2,1,0:T(8,128)(2,1)}, u32[]{:S(2)}) copy-start(bf16[1,16,32,768]{3,2,1,0:T(8,128)(2,1)} %param.6) | copy-start | bytes 2359300
  1.8 9.8 %copy-start.4 = (s32[1,16,32]{2,1,0:T(8,128)S(1)}, s32[1,16,32]{2,1,0:T(8,128)}, u32[]{:S(2)}) copy-start(s32[1,16,32]{2,1,0:T(8,128)} %param.7) | copy-start | bytes 6148
  1.9 11.2 %collective-permute-start.1 = (bf16[8,8,768]{2,1,0:T(8,128)(2,1)S(1)}, bf16[8,8,768]{2,1,0:T(8,128)(2,1)S(1)}, u32[]{:S(2)}, u32[]{:S(2)}) collective-permute-start(bf16[8,8,768]{2,1,0:T(8,128)(2,1)S(1)} %get-tuple-element.49), channel_id=1, source_target_pairs={{0,7},{1,0},{2,1},{3,2},{4,3},{5,4},{6,5},{7,6},{8,15},{9,8},{10,9... | collective-permute-start | bytes 294920 | tf_op jit(solution)/shard_map/ppermute | solution.py:392
  7.8 5.3 %collective-permute-start.2 = (bf16[8,8,768]{2,1,0:T(8,128)(2,1)S(1)}, bf16[8,8,768]{2,1,0:T(8,128)(2,1)S(1)}, u32[]{:S(2)}, u32[]{:S(2)}) collective-permute-start(bf16[8,8,768]{2,1,0:T(8,128)(2,1)S(1)} %get-tuple-element.50), channel_id=1, source_target_pairs={{0,63},{1,56},{2,57},{3,58},{4,59},{5,60},{6,61},{7,62},{8,7},{9,0... | collective-permute-start | bytes 294920 | tf_op jit(solution)/shard_map/ppermute | solution.py:450
  10.4 5.7 %collective-permute-start = (bf16[8,24,768]{2,1,0:T(8,128)(2,1)S(1)}, bf16[8,24,768]{2,1,0:T(8,128)(2,1)S(1)}, u32[]{:S(2)}, u32[]{:S(2)}) collective-permute-start(bf16[8,24,768]{2,1,0:T(8,128)(2,1)S(1)} %get-tuple-element.48), channel_id=1, source_target_pairs={{0,56},{8,0},{16,8},{24,16},{32,24},{40,32},{48,40},{56,48},{1,57}... | collective-permute-start | bytes 884744 | tf_op jit(solution)/shard_map/ppermute | solution.py:392
  11.5 4.6 %copy-start = (bf16[768,2304]{1,0:T(8,128)(2,1)S(1)}, bf16[768,2304]{1,0:T(8,128)(2,1)}, u32[]{:S(2)}) copy-start(bf16[768,2304]{1,0:T(8,128)(2,1)} %wv_ref.5) | copy-start | bytes 10616836
  26.9 2.9 %collective-permute-start.3 = (bf16[384,1536]{1,0:T(8,128)(2,1)S(1)}, bf16[384,1536]{1,0:T(8,128)(2,1)S(1)}, u32[]{:S(2)}, u32[]{:S(2)}) collective-permute-start(bf16[384,1536]{1,0:T(8,128)(2,1)S(1)} %get-tuple-element.56), channel_id=1, source_target_pairs={{0,8},{8,0},{16,24},{24,16},{32,40},{40,32},{48,56},{56,48},{1,9},... | collective-permute-start | bytes 3538952 | tf_op jit(solution)/shard_map/ppermute | solution.py:392
  30.2 6.8 %collective-permute-start.4 = (bf16[96,768]{1,0:T(8,128)(2,1)S(1)}, bf16[96,768]{1,0:T(8,128)(2,1)S(1)}, u32[]{:S(2)}, u32[]{:S(2)}) collective-permute-start(bf16[96,768]{1,0:T(8,128)(2,1)S(1)} %get-tuple-element.105), channel_id=1, source_target_pairs={{0,64},{64,128},{128,192},{192,0},{1,65},{65,129},{129,193},{193,1... | collective-permute-start | bytes 442376 | tf_op jit(solution)/shard_map/ppermute | solution.py:392
  30.8 7.1 %collective-permute-start.5 = (bf16[96,768]{1,0:T(8,128)(2,1)S(1)}, bf16[96,768]{1,0:T(8,128)(2,1)S(1)}, u32[]{:S(2)}, u32[]{:S(2)}) collective-permute-start(bf16[96,768]{1,0:T(8,128)(2,1)S(1)} %get-tuple-element.103), channel_id=1, source_target_pairs={{0,192},{64,0},{128,64},{192,128},{1,193},{65,1},{129,65},{193,129... | collective-permute-start | bytes 442376 | tf_op jit(solution)/shard_map/ppermute | solution.py:392
  37.9 2.0 %collective-permute-start.6 = (bf16[384,768]{1,0:T(8,128)(2,1)S(1)}, bf16[384,768]{1,0:T(8,128)(2,1)S(1)}, u32[]{:S(2)}, u32[]{:S(2)}) collective-permute-start(bf16[384,768]{1,0:T(8,128)(2,1)S(1)} %get-tuple-element.65), channel_id=1, source_target_pairs={{0,8},{8,0},{16,24},{24,16},{32,40},{40,32},{48,56},{56,48},{1,9},... | collective-permute-start | bytes 1769480 | tf_op jit(solution)/shard_map/ppermute | solution.py:392
  39.9 2.2 %collective-permute-start.7 = (bf16[384,768]{1,0:T(8,128)(2,1)S(1)}, bf16[384,768]{1,0:T(8,128)(2,1)S(1)}, u32[]{:S(2)}, u32[]{:S(2)}) collective-permute-start(bf16[384,768]{1,0:T(8,128)(2,1)S(1)} %get-tuple-element.73), channel_id=1, source_target_pairs={{0,8},{8,0},{16,24},{24,16},{32,40},{40,32},{48,56},{56,48},{1,9},... | collective-permute-start | bytes 1769480 | tf_op jit(solution)/shard_map/ppermute | solution.py:392
  40.4 13.2 %collective-permute-start.11 = (bf16[96,1536]{1,0:T(8,128)(2,1)S(1)}, bf16[96,1536]{1,0:T(8,128)(2,1)S(1)}, u32[]{:S(2)}, u32[]{:S(2)}) collective-permute-start(bf16[96,1536]{1,0:T(8,128)(2,1)S(1)} %pad_maximum_fusion.1), channel_id=1, source_target_pairs={{0,192},{64,0},{128,64},{192,128},{1,193},{65,1},{129,65},{193,129... | collective-permute-start | bytes 884744 | tf_op jit(solution)/shard_map/ppermute | solution.py:392
  42.2 7.8 %collective-permute-start.8 = (bf16[96,768]{1,0:T(8,128)(2,1)S(1)}, bf16[96,768]{1,0:T(8,128)(2,1)S(1)}, u32[]{:S(2)}, u32[]{:S(2)}) collective-permute-start(bf16[96,768]{1,0:T(8,128)(2,1)S(1)} %get-tuple-element.97), channel_id=1, source_target_pairs={{0,16},{8,24},{16,32},{24,40},{32,48},{40,56},{48,0},{56,8},{1,17}... | collective-permute-start | bytes 442376 | tf_op jit(solution)/shard_map/ppermute | solution.py:392
  43.2 6.8 %collective-permute-start.9 = (bf16[96,768]{1,0:T(8,128)(2,1)S(1)}, bf16[96,768]{1,0:T(8,128)(2,1)S(1)}, u32[]{:S(2)}, u32[]{:S(2)}) collective-permute-start(bf16[96,768]{1,0:T(8,128)(2,1)S(1)} %get-tuple-element.99), channel_id=1, source_target_pairs={{0,48},{8,56},{16,0},{24,8},{32,16},{40,24},{48,32},{56,40},{1,49}... | collective-permute-start | bytes 442376 | tf_op jit(solution)/shard_map/ppermute | solution.py:392
  45.8 9.1 %collective-permute-start.10 = (bf16[96,1536]{1,0:T(8,128)(2,1)S(1)}, bf16[96,1536]{1,0:T(8,128)(2,1)S(1)}, u32[]{:S(2)}, u32[]{:S(2)}) collective-permute-start(bf16[96,1536]{1,0:T(8,128)(2,1)S(1)} %pad_maximum_fusion), channel_id=1, source_target_pairs={{0,64},{64,128},{128,192},{192,0},{1,65},{65,129},{129,193},{193,1... | collective-permute-start | bytes 884744 | tf_op jit(solution)/shard_map/ppermute | solution.py:392
  50.2 12.6 %collective-permute-start.14 = (bf16[96,1536]{1,0:T(8,128)(2,1)S(1)}, bf16[96,1536]{1,0:T(8,128)(2,1)S(1)}, u32[]{:S(2)}, u32[]{:S(2)}) collective-permute-start(bf16[96,1536]{1,0:T(8,128)(2,1)S(1)} %pad_maximum_fusion.3), channel_id=1, source_target_pairs={{0,48},{8,56},{16,0},{24,8},{32,16},{40,24},{48,32},{56,40},{1,49}... | collective-permute-start | bytes 884744 | tf_op jit(solution)/shard_map/ppermute | solution.py:392
  53.3 9.7 %collective-permute-start.13 = (bf16[96,1536]{1,0:T(8,128)(2,1)S(1)}, bf16[96,1536]{1,0:T(8,128)(2,1)S(1)}, u32[]{:S(2)}, u32[]{:S(2)}) collective-permute-start(bf16[96,1536]{1,0:T(8,128)(2,1)S(1)} %pad_maximum_fusion.2), channel_id=1, source_target_pairs={{0,16},{8,24},{16,32},{24,40},{32,48},{40,56},{48,0},{56,8},{1,17}... | collective-permute-start | bytes 884744 | tf_op jit(solution)/shard_map/ppermute | solution.py:392
  55.0 7.8 %collective-permute-start.12 = (bf16[48,1536]{1,0:T(8,128)(2,1)S(1)}, bf16[48,1536]{1,0:T(8,128)(2,1)S(1)}, u32[]{:S(2)}, u32[]{:S(2)}) collective-permute-start(bf16[48,1536]{1,0:T(8,128)(2,1)S(1)} %fusion.13), channel_id=1, source_target_pairs={{0,16},{8,24},{16,0},{24,8},{32,48},{40,56},{48,32},{56,40},{1,17}... | collective-permute-start | bytes 442376 | tf_op jit(solution)/shard_map/ppermute | solution.py:392
  63.2 5.2 %collective-permute-start.16 = (bf16[48,1536]{1,0:T(8,128)(2,1)S(1)}, bf16[48,1536]{1,0:T(8,128)(2,1)S(1)}, u32[]{:S(2)}, u32[]{:S(2)}) collective-permute-start(bf16[48,1536]{1,0:T(8,128)(2,1)S(1)} %pad_maximum_fusion.4), channel_id=1, source_target_pairs={{0,64},{64,0},{128,192},{192,128},{1,65},{65,1},{129,193},{193,129... | collective-permute-start | bytes 442376 | tf_op jit(solution)/shard_map/ppermute | solution.py:392
  63.6 5.7 %collective-permute-start.15 = (bf16[24,1536]{1,0:T(8,128)(2,1)S(1)}, bf16[24,1536]{1,0:T(8,128)(2,1)S(1)}, u32[]{:S(2)}, u32[]{:S(2)}) collective-permute-start(bf16[24,1536]{1,0:T(8,128)(2,1)S(1)} %slice.153), channel_id=1, source_target_pairs={{0,48},{8,56},{16,32},{24,40},{32,16},{40,24},{48,0},{56,8},{1,49}... | collective-permute-start | bytes 221192 | tf_op jit(solution)/shard_map/ppermute | solution.py:392
  68.4 5.7 %collective-permute-start.17 = (bf16[24,1536]{1,0:T(8,128)(2,1)S(1)}, bf16[24,1536]{1,0:T(8,128)(2,1)S(1)}, u32[]{:S(2)}, u32[]{:S(2)}) collective-permute-start(bf16[24,1536]{1,0:T(8,128)(2,1)S(1)} %slice.157), channel_id=1, source_target_pairs={{0,192},{64,128},{128,64},{192,0},{1,193},{65,129},{129,65},{193,1... | collective-permute-start | bytes 221192 | tf_op jit(solution)/shard_map/ppermute | solution.py:392

commit v7 on v6

--- a/solution.py
+++ b/solution.py
@@ -38,30 +38,42 @@
     return pl.CostEstimate(flops=int(flops), bytes_accessed=int(size), transcendentals=0)
 
 
-def edges_kernel(tiles, above, left, corner, sem):
-    copies = [
-        pltpu.make_async_copy(tiles.at[0:8, 8:32], above, sem.at[0]),
-        pltpu.make_async_copy(tiles.at[8:16, 0:8], left, sem.at[1]),
-        pltpu.make_async_copy(tiles.at[0:8, 0:8], corner, sem.at[2]),
-    ]
-    for copy in copies:
-        copy.start()
-    for copy in copies:
-        copy.wait()
+def above_kernel(tiles_ref, above_ref):
+    above_ref[...] = tiles_ref[...].astype(F32)[:, 8:].astype(BF)
+
+
+def left_kernel(tiles_ref, after_ref, left_ref, corner_ref):
+    tiles = tiles_ref[...].astype(F32)[:, :8].astype(BF)
+    corner_ref[...] = tiles[:8]
+    left_ref[...] = tiles[8:]
 
 
 def edges(tiles):
     small = jax.ShapeDtypeStruct((8, 8, D), BF)
-    return pl.pallas_call(
-        edges_kernel,
-        in_specs=[pl.BlockSpec(memory_space=pl.ANY)],
-        out_specs=[pl.BlockSpec(memory_space=pl.ANY)] * 3,
-        out_shape=[jax.ShapeDtypeStruct((8, 24, D), BF), small, small],
-        scratch_shapes=[pltpu.SemaphoreType.DMA((3,))],
+    above = pl.pallas_call(
+        above_kernel,
+        grid=(1,),
+        in_specs=[pl.BlockSpec((8, 32, D), lambda g: (0, 0, 0))],
+        out_specs=full((8, 24, D)),
+        out_shape=jax.ShapeDtypeStruct((8, 24, D), BF),
         compiler_params=pltpu.CompilerParams(vmem_limit_bytes=VMEM),
         cost_estimate=cost(3e10, 1e6),
-        name="edges",
+        name="above",
     )(tiles)
+    left, corner = pl.pallas_call(
+        left_kernel,
+        grid=(1,),
+        in_specs=[
+            pl.BlockSpec((16, 16, D), lambda g: (0, 0, 0)),
+            pl.BlockSpec(memory_space=pl.ANY),
+        ],
+        out_specs=[full((8, 8, D))] * 2,
+        out_shape=[small, small],
+        compiler_params=pltpu.CompilerParams(vmem_limit_bytes=VMEM),
+        cost_estimate=cost(1e3, 1e3),
+        name="left",
+    )(tiles, above)
+    return above, left, corner
 
 
 def branch_kernel(
@@ -137,31 +149,6 @@
     return centred * inv, inv
 
 
-def head_pair(q2, k2, v2, da2, ones2):
-    lane = lax.broadcasted_iota(jnp.int32, (1, 128), 1)
-    sel_a = (lane < 64).astype(BF)
-    sel_b = (lane >= 64).astype(BF)
-    ka, kb, va, vb = k2 * sel_a, k2 * sel_b, v2 * sel_a, v2 * sel_b
-    wa = jnp.exp(nt(q2, ka)).astype(BF)
-    wb = jnp.exp(nt(q2, kb)).astype(BF)
-    both = nn(wa, jnp.concatenate([va, ones2 * sel_a], 1)) + nn(
-        wb, jnp.concatenate([vb, ones2 * sel_b], 1)
-    )
-    rinv = 1.0 / both[:, 128:]
-    attended = both[:, :128] * rinv
-    lhs = jnp.concatenate([da2, (da2.astype(F32) * attended).astype(BF)], 1)
-    minus_a = jnp.broadcast_to(-sel_a, (CELLS, 128))
-    minus_b = jnp.broadcast_to(-sel_b, (CELLS, 128))
-    dsa = (wa.astype(F32) * nt(lhs, jnp.concatenate([va, minus_a], 1))).astype(BF)
-    dsb = (wb.astype(F32) * nt(lhs, jnp.concatenate([vb, minus_b], 1))).astype(BF)
-    dq = (nn(dsa, ka) + nn(dsb, kb)) * (rinv * HEAD_SCALE)
-    dan = (da2.astype(F32) * rinv).astype(BF)
-    qn = (q2.astype(F32) * rinv).astype(BF)
-    dv = tn(wa, dan * sel_a) + tn(wb, dan * sel_b)
-    dk = tn(dsa, qn * sel_a) + tn(dsb, qn * sel_b)
-    return attended.astype(BF), dq.astype(BF), dk.astype(BF), dv.astype(BF)
-
-
 def put(grad, keep_ref, send_ref):
     keep_ref[...] = grad[: D // 2].astype(BF)
     send_ref[...] = grad[D // 2 :].astype(BF)
@@ -171,22 +158,48 @@
     hid_ref, hid_t_ref, tis_ref, live_ref, wq_ref, wk_ref, wv_ref, da_ref,
     keep_ref, send_ref, att_ref, dqkv_ref,
 ):
-    for w in range(2):
-        hidden = hid_ref[w]
-        query = nn(hidden, wq_ref[...]).astype(BF) * BF(HEAD_SCALE)
-        tis2 = tis_ref[w]
-        tis4 = jnp.concatenate([tis2, tis2], 1)
-        key = nn(hidden, wk_ref[...]).astype(BF) * tis4
-        value = nn(hidden, wv_ref[...]).astype(BF) * tis4
-        for p in range(2):
-            s = slice(p * 128, (p + 1) * 128)
-            att, dq, dk, dv = head_pair(
-                query[:, s], key[:, s], value[:, s], da_ref[w, :, s], live_ref[w]
-            )
-            att_ref[w, :, s] = att
-            dqkv_ref[0, w, :, s] = dq
-            dqkv_ref[0, w, :, slice(GW + p * 128, GW + (p + 1) * 128)] = dk * tis2
-            dqkv_ref[0, w, :, slice(2 * GW + p * 128, 2 * GW + (p + 1) * 128)] = dv * tis2
+    hidden = hid_ref[...].reshape(2 * CELLS, D)
+    query = nn(hidden, wq_ref[...]).astype(BF) * BF(HEAD_SCALE)
+    key = nn(hidden, wk_ref[...]).astype(BF)
+    value = nn(hidden, wv_ref[...]).astype(BF)
+    lane = lax.broadcasted_iota(jnp.int32, (1, 128), 1)
+    sel = [(lane < 64).astype(BF), (lane >= 64).astype(BF)]
+    units = [(w, p) for w in range(2) for p in range(2)]
+    q, k, v, da, weight, ds, rinv, att = {}, {}, {}, {}, {}, {}, {}, {}
+    for u in units:
+        w, p = u
+        rows, lanes = slice(w * CELLS, (w + 1) * CELLS), slice(p * 128, (p + 1) * 128)
+        q[u] = query[rows, lanes]
+        k[u] = key[rows, lanes] * tis_ref[w]
+        v[u] = value[rows, lanes] * tis_ref[w]
+        da[u] = da_ref[w, :, lanes]
+    for u in units:
+        for h in range(2):
+            weight[u, h] = jnp.exp(nt(q[u], k[u] * sel[h])).astype(BF)
+    for u in units:
+        live = live_ref[u[0]]
+        both = nn(weight[u, 0], jnp.concatenate([v[u] * sel[0], live * sel[0]], 1)) + nn(
+            weight[u, 1], jnp.concatenate([v[u] * sel[1], live * sel[1]], 1)
+        )
+        rinv[u] = 1.0 / both[:, 128:]
+        att[u] = both[:, :128] * rinv[u]
+        att_ref[u[0], :, u[1] * 128 : (u[1] + 1) * 128] = att[u].astype(BF)
+    for u in units:
+        terms = da[u].astype(F32) * att[u]
+        for h in range(2):
+            delta = jnp.sum(terms * sel[h].astype(F32), 1, keepdims=True)
+            dprobs = nt(da[u], v[u] * sel[h]) - delta
+            ds[u, h] = (weight[u, h].astype(F32) * dprobs).astype(BF)
+    for u in units:
+        w, p = u
+        dq = (nn(ds[u, 0], k[u] * sel[0]) + nn(ds[u, 1], k[u] * sel[1])) * (rinv[u] * HEAD_SCALE)
+        dan = (da[u].astype(F32) * rinv[u]).astype(BF)
+        qn = (q[u].astype(F32) * rinv[u]).astype(BF)
+        dv = tn(weight[u, 0], dan * sel[0]) + tn(weight[u, 1], dan * sel[1])
+        dk = tn(ds[u, 0], qn * sel[0]) + tn(ds[u, 1], qn * sel[1])
+        for i, grad in enumerate((dq, dk, dv)):
+            at = i * GW + p * 128
+            dqkv_ref[0, w, :, at : at + 128] = grad.astype(BF)
     put(nn(hid_t_ref[...], dqkv_ref[0].reshape(2 * CELLS, D)), keep_ref, send_ref)
 
 
@@ -213,7 +226,8 @@
             normed, _ = moments(x)
             hidden = normed.astype(BF)
             hid_ref[w] = hidden
-            hid_t_ref[:, w * CELLS : (w + 1) * CELLS] = nt(perm, hidden).astype(BF)
+            masked = hidden * jnp.tile(tis_ref[w], (1, D // 128))
+            hid_t_ref[:, w * CELLS : (w + 1) * CELLS] = nt(perm, masked).astype(BF)
 
     heads_group(
         hid_ref, hid_t_ref, tis_ref, live_ref, wq_ref, wk_ref, wv_ref, da_ref,
@@ -231,18 +245,21 @@
     )
 
 
-def turn_kernel(hid_ref, hid_t_ref):
-    hid_t_ref[...] = nt(row_order("gy"), hid_ref[...].reshape(2 * CELLS, D)).astype(BF)
-
-
-def turn(hid):
+def turn_kernel(hid_ref, tis_ref, hid_t_ref):
+    perm = row_order("gy")
+    for w in range(2):
+        masked = hid_ref[w] * jnp.tile(tis_ref[w], (1, D // 128))
+        hid_t_ref[:, w * CELLS : (w + 1) * CELLS] = nt(perm, masked).astype(BF)
+
+
+def turn(hid, tis):
     return pl.pallas_call(
         turn_kernel,
         out_shape=jax.ShapeDtypeStruct((D, 2 * CELLS), BF),
         compiler_params=pltpu.CompilerParams(vmem_limit_bytes=VMEM),
         cost_estimate=cost(2e9, 2e6),
         name="turn",
-    )(hid)
+    )(hid, tis)
 
 
 def columns(block, first):
@@ -337,7 +354,7 @@
 
 
 def grad_kernel(
-    xw_ref, cot_ref, dqkv0_ref, dqkv1_ref, wq_ref, wk_ref, wv_ref, grad_ref, acc_ref
+    xw_ref, cot_ref, tis_ref, dqkv0_ref, dqkv1_ref, wq_ref, wk_ref, wv_ref, grad_ref, acc_ref
 ):
     step = pl.program_id(0)
     weights = jnp.concatenate([wq_ref[...], wk_ref[...], wv_ref[...]], 1)
@@ -357,7 +374,8 @@
         acc_ref[...] += part
         for w in range(2):
             normed, inv = moments(xw_ref[w].astype(F32))
-            dh = acc_ref[w * CELLS : (w + 1) * CELLS]
+            tis = jnp.tile(tis_ref[w].astype(F32), (1, D // 128))
+            dh = acc_ref[w * CELLS : (w + 1) * CELLS] * tis
             dnorm = inv * (
                 dh
                 - jnp.mean(dh, -1, keepdims=True)
@@ -367,12 +385,12 @@
             grad_ref[:, w] = grad.astype(BF).reshape(WIN, WIN, D)
 
 
-def grad_part(xw, cot, dqkv0, dqkv1, w_qkv):
+def grad_part(xw, cot, tis, dqkv0, dqkv1, w_qkv):
     grad = pl.pallas_call(
         grad_kernel,
         grid=(GROUPS,),
         in_specs=[
-            full((2, CELLS, D)), full((WIN, 2, WIN, D)),
+            full((2, CELLS, D)), full((WIN, 2, WIN, D)), full((2, CELLS, 128)),
             pl.BlockSpec((1, 2, CELLS, D), lambda g: (jnp.minimum(g, 1), 0, 0, 0)),
             full((1, 2, CELLS, D)),
             columns(0, 0), columns(1, 0), columns(2, 0),
@@ -383,8 +401,33 @@
         compiler_params=pltpu.CompilerParams(vmem_limit_bytes=VMEM),
         cost_estimate=cost(1e3, 1e3),
         name="grad_part",
-    )(xw, cot, dqkv0, dqkv1, w_qkv, w_qkv, w_qkv)
+    )(xw, cot, tis, dqkv0, dqkv1, w_qkv, w_qkv, w_qkv)
     return grad.reshape(1, WIN, 2 * WIN, D)
+
+
+def finish_kernel(parts_ref, qkv_ref, proj_ref):
+    total = parts_ref[0].astype(F32)
+    for part in range(1, parts_ref.shape[0]):
+        total = total + parts_ref[part].astype(F32)
+    total = total * (1.0 / math.sqrt(512))
+    for i in range(3):
+        for g in range(GROUPS):
+            at = g * D + i * GW
+            qkv_ref[:, i * D + g * GW : i * D + (g + 1) * GW] = total[:, at : at + GW]
+    proj_ref[...] = total[:, 3 * D :]
+
+
+def finish(parts):
+    rows = parts.shape[1]
+    return pl.pallas_call(
+        finish_kernel,
+        out_shape=[
+            jax.ShapeDtypeStruct((rows, 3 * D), F32),
+            jax.ShapeDtypeStruct((rows, D), F32),
+        ],
+        compiler_params=pltpu.CompilerParams(vmem_limit_bytes=VMEM),
+        name="finish",
+    )(parts)
 
 
 def send(value, axis, move):
@@ -462,7 +505,7 @@
         mine, below, right, diag, tis, live, w_qkv, da
     )
     came = send(send0, "gy", lambda i: i ^ 1)
-    hid_t = turn(hid)
+    hid_t = turn(hid, tis)
     came, hid_t = tie(came, hid_t)
     first = add(keep0, came)
     low_a, high_a = blocks(first[:, :D]), blocks(first[:, D:])
@@ -483,7 +526,7 @@
     came_b = ring_pass(low_b, high_b, came_b, "gy", 2)
     rows_a = ring_end(low_a, high_a, came_a)
     came_a = halve_start(rows_a, "gy", 2)
-    grad = grad_part(xw, cot, dqkv0, dqkv1, w_qkv)
+    grad = grad_part(xw, cot, tis, dqkv0, dqkv1, w_qkv)
     came_a, came_b, grad = tie(came_a, came_b, grad)
     rows_a = halve_end(rows_a, came_a)
     rows_b = ring_end(low_b, high_b, came_b)
@@ -492,10 +535,8 @@
     rows_b = halve_end(rows_b, came_b)
     came_b = halve_start(rows_b, "dp", 3)
     rows = jnp.concatenate([halve_end(rows_a, came_a), halve_end(rows_b, came_b)], 1)
-    parts = exchange(rows, ("gx",))
-    total = jnp.sum(parts.astype(F32), 0) * (1.0 / math.sqrt(512))
-    grad_qkv = total[:, : 3 * D].reshape(3, GROUPS, 3, GW).transpose(0, 2, 1, 3)
-    return out, grad, grad_qkv.reshape(3, 3 * D), total[:, 3 * D :]
+    grad_qkv, grad_proj = finish(exchange(rows, ("gx",)))
+    return out, grad, grad_qkv, grad_proj
 
 
 def solution(mesh):

time: 89.1 us -> 84.9 us (0.953)
  Pallas kernels: 26.1 us -> 23.3 us
  local copies, waits for them, and re-layouts: 2.72 us -> 1.43 us
  blocking collectives: 12.5 us -> 13.6 us
    ppermute x17, waiting for transfers between devices: 19 us -> 16.7 us  [send(): lax.ppermute(value, axis, [(i, move(i) % devices) for i in range(devices)])]
    pallas_call x1, Pallas kernels: 10.7 us -> 8.34 us  [first_heads(): pl.pallas_call(first_kernel, grid=(2,), in_specs=[full((16, 32, D)), full...]
    ppermute x1, waiting for transfers between devices: 0.01 us -> 1.94 us  [shards(): lax.ppermute(corner, ('gy', 'gx'), [(a * nx + b, (a - 1) % ny * nx + (b -...]
    ppermute x1, starting transfers between devices: 2.62 us -> 0.84 us  [shards(): lax.ppermute(corner, ('gy', 'gx'), [(a * nx + b, (a - 1) % ny * nx + (b -...]
    pallas_call x1, Pallas kernels: 4.37 us -> 3.15 us  [last_heads(): pl.pallas_call(last_kernel, grid=(1,), in_specs=[full((2, CELLS, D)), ful...]
    ppermute x17, starting transfers between devices: 22.9 us -> 24.1 us  [send(): lax.ppermute(value, axis, [(i, move(i) % devices) for i in range(devices)])]
    all_to_all x1, blocking collectives: 12.5 us -> 13.6 us  [exchange(): return lax.all_to_all(rows, axis, 0, 0, axis_index_groups=groups)]
  transfers between devices with their start and end apart: 18 -> 18, of which waited for: 12 -> 14; matrix products, arithmetic and copies ran while one was open for 1% -> 1% of each run, Pallas kernels for 17% -> 17%
where the time goes in v7:
time: 84.9 us; the launch traced here: 83.9 us
  starting transfers between devices  24.9 us (29%)
  Pallas kernels  23.3 us (27%)
  waiting for transfers between devices  18.6 us (22%)
  blocking collectives  13.6 us (16%)
  local copies, waits for them, and re-layouts  1.43 us (2%)
  other arithmetic  1.18 us (1%)
  between operations  0.89 us (1%)
    ppermute x17, starting transfers between devices, send(): lax.ppermute(value, axis, [(i, move(i) % devices) for i in range(devices)])  24.1 us
    ppermute x17, waiting for transfers between devices, send(): lax.ppermute(value, axis, [(i, move(i) % devices) for i in range(devices)])  16.7 us
    all_to_all x1, blocking collectives, exchange(): return lax.all_to_all(rows, axis, 0, 0, axis_index_groups=groups)  13.6 us
    pallas_call x1, Pallas kernels, first_heads(): pl.pallas_call(first_kernel, grid=(2,), in_specs=[full((16, 32, D)), full...  8.34 us
    pallas_call x1, Pallas kernels, grad_part(): pl.pallas_call(grad_kernel, grid=(GROUPS,), in_specs=[full((2, CELLS, D))...  5.04 us
    pallas_call x1, Pallas kernels, last_heads(): pl.pallas_call(last_kernel, grid=(1,), in_specs=[full((2, CELLS, D)), ful...  3.15 us
    ppermute x1, waiting for transfers between devices, shards(): lax.ppermute(corner, ('gy', 'gx'), [(a * nx + b, (a - 1) % ny * nx + (b -...  1.94 us
    pallas_call x1, Pallas kernels, proj_grad(): pl.pallas_call(proj_kernel, out_shape=[shape, shape], compiler_params=plt...  1.86 us
  transfers between devices with their start and end apart: 18, of which 14 were waited for; matrix products, arithmetic and copies ran while one was open for 1% of the time, Pallas kernels for 17%

profile of v7, /device:TPU:6, one launch (start us, length us, event | category | flops | bytes accessed | tf_op | source)
XLA Modules:
  0.0 83.9 jit_solution(4106265557913818467)
XLA Ops:
  0.6 1.1 %copy-done.2 = bf16[1,16,32,768]{3,2,1,0:T(8,128)(2,1)S(1)} copy-done((bf16[1,16,32,768]{3,2,1,0:T(8,128)(2,1)S(1)}, bf16[1,16,32,768]{3,2,1,0:T(8,128)(2,1)}, u32[]{:S(2)}) %copy-start.2) | copy-done | bytes 786456
  1.8 2.5 %collective-permute-start = (bf16[8,24,768]{2,1,0:T(8,128)(2,1)S(1)}, bf16[8,24,768]{2,1,0:T(8,128)(2,1)S(1)}, u32[]{:S(2)}, u32[]{:S(2)}) collective-permute-start(bf16[8,24,768]{2,1,0:T(8,128)(2,1)S(1)} %above.1.after_ref), channel_id=1, source_target_pairs={{0,56},{8,0},{16,8},{24,16},{32,24},{40,32},{48,40},{56,48},{1,57}... | collective-permute-start | bytes 884744 | tf_op jit(solution)/shard_map/ppermute | solution.py:435
  4.3 5.9 %collective-permute-start.1 = (bf16[8,8,768]{2,1,0:T(8,128)(2,1)S(1)}, bf16[8,8,768]{2,1,0:T(8,128)(2,1)S(1)}, u32[]{:S(2)}, u32[]{:S(2)}) collective-permute-start(bf16[8,8,768]{2,1,0:T(8,128)(2,1)S(1)} %get-tuple-element.49), channel_id=1, source_target_pairs={{0,7},{1,0},{2,1},{3,2},{4,3},{5,4},{6,5},{7,6},{8,15},{9,8},{10,9... | collective-permute-start | bytes 294920 | tf_op jit(solution)/shard_map/ppermute | solution.py:435
  10.2 0.8 %collective-permute-start.2 = (bf16[8,8,768]{2,1,0:T(8,128)(2,1)S(1)}, bf16[8,8,768]{2,1,0:T(8,128)(2,1)S(1)}, u32[]{:S(2)}, u32[]{:S(2)}) collective-permute-start(bf16[8,8,768]{2,1,0:T(8,128)(2,1)S(1)} %get-tuple-element.50), channel_id=1, source_target_pairs={{0,63},{1,56},{2,57},{3,58},{4,59},{5,60},{6,61},{7,62},{8,7},{9,0... | collective-permute-start | bytes 294920 | tf_op jit(solution)/shard_map/ppermute | solution.py:493
  11.1 1.5 %branch.1 = (bf16[2,256,768]{2,1,0:T(8,128)(2,1)S(1)}, bf16[2,256,768]{2,1,0:T(8,128)(2,1)S(1)}, bf16[2,256,128]{2,1,0:T(8,128)(2,1)S(1)}, bf16[2,256,128]{2,1,0:T(8,128)(2,1)S(1)}) custom-call(bf16[16,2,16,768]{3,2,1,0:T(8,128)(2,1)S(1)} %bitcast.52, s32[16,32]{1,0:T(8,128)S(1)} %bitcast.54, bf16[768,768]{1,0:T(8,128)(2,1)S(1)} %copy-done.1), custom_call_target="tpu_custom_call" | custom-call | flops 20000000000 | bytes 4000000 | tf_op jit(solution)/shard_map/branch/pallas_call | solution.py:112
  12.6 0.5 collective-permute-done.1.right_ref
  13.0 1.9 %collective-permute-done.2.diag_ref = bf16[8,8,768]{2,1,0:T(8,128)(2,1)S(1)} collective-permute-done((bf16[8,8,768]{2,1,0:T(8,128)(2,1)S(1)}, bf16[8,8,768]{2,1,0:T(8,128)(2,1)S(1)}, u32[]{:S(2)}, u32[]{:S(2)}) %collective-permute-start.2) | collective-permute-done | bytes 98336 | tf_op jit(solution)/shard_map/ppermute | solution.py:493
  15.0 8.3 %first_heads.1 = (bf16[384,1536]{1,0:T(8,128)(2,1)S(1)}, bf16[384,1536]{1,0:T(8,128)(2,1)S(1)}, bf16[2,256,512]{2,1,0:T(8,128)(2,1)S(1)}, bf16[2,2,256,768]{3,2,...) custom-call(bf16[16,32,768]{2,1,0:T(8,128)(2,1)S(1)} %bitcast.51, ...), custom_call_target="tpu_custom_call" | custom-call | flops 6000000000 | bytes 10000000 | tf_op jit(solution)/shard_map/first_heads/pallas_call | solution.py:293
  23.4 1.1 %turn.1.hid_t_ref = bf16[768,512]{1,0:T(8,128)(2,1)S(1)} custom-call(bf16[2,256,768]{2,1,0:T(8,128)(2,1)S(1)} %get-tuple-element.54.hid_ref, bf16[2,256,128]{2,1,0:T(8,128)(2,1)S(1)} %get-tuple-element.51.tis_ref), custom_call_target="tpu_custom_call" | custom-call | flops 2000000000 | bytes 2000000 | tf_op jit(solution)/shard_map/turn/pallas_call | solution.py:256
  24.5 1.7 %collective-permute-done.3 = bf16[384,1536]{1,0:T(8,128)(2,1)S(1)} collective-permute-done((bf16[384,1536]{1,0:T(8,128)(2,1)S(1)}, bf16[384,1536]{1,0:T(8,128)(2,1)S(1)}, u32[]{:S(2)}, u32[]{:S(2)}) %collective-permute-start.3) | collective-permute-done | bytes 1179680 | tf_op jit(solution)/shard_map/ppermute | solution.py:435
  26.7 0.5 collective-permute-start.4
  27.2 1.8 %collective-permute-start.5 = (bf16[96,768]{1,0:T(8,128)(2,1)S(1)}, bf16[96,768]{1,0:T(8,128)(2,1)S(1)}, u32[]{:S(2)}, u32[]{:S(2)}) collective-permute-start(bf16[96,768]{1,0:T(8,128)(2,1)S(1)} %get-tuple-element.105), channel_id=1, source_target_pairs={{0,192},{64,0},{128,64},{192,128},{1,193},{65,1},{129,65},{193,129... | collective-permute-start | bytes 442376 | tf_op jit(solution)/shard_map/ppermute | solution.py:435
  29.1 3.2 %last_heads.1 = (bf16[384,768]{1,0:T(8,128)(2,1)S(1)}, bf16[384,768]{1,0:T(8,128)(2,1)S(1)}, bf16[2,256,256]{2,1,0:T(8,128)(2,1)S(1)}, bf16[1,2,256,768]{3,2,1,0:T(8,128)(2,1)S(1)}) custom-call(bf16[2,256,768]{2,1,0:T(8,128)(2,1)S(1)} %get-tuple-element.54.hid_ref, bf16[768,512]{1,0:T(8,128)(2,1)S(1)} %turn.1.hid_t_ref, ...), custom_call_target="tpu_custom_call" | custom-call | flops 4000000000 | bytes 6000000 | tf_op jit(solution)/shard_map/last_heads/pallas_call | solution.py:308
  32.6 1.7 %collective-permute-done.5 = bf16[96,768]{1,0:T(8,128)(2,1)S(1)} collective-permute-done((bf16[96,768]{1,0:T(8,128)(2,1)S(1)}, bf16[96,768]{1,0:T(8,128)(2,1)S(1)}, u32[]{:S(2)}, u32[]{:S(2)}) %collective-permute-start.5) | collective-permute-done | bytes 147488 | tf_op jit(solution)/shard_map/ppermute | solution.py:435
  34.3 1.9 %proj_grad.1 = (bf16[384,768]{1,0:T(8,128)(2,1)S(1)}, bf16[384,768]{1,0:T(8,128)(2,1)S(1)}) custom-call(bf16[2,256,512]{2,1,0:T(8,128)(2,1)S(1)} %get-tuple-element.66.att0_ref, bf16[2,256,256]{2,1,0:T(8,128)(2,1)S(1)} %get-tuple-element.77.att1_ref, bf16[2,256,768]{2,1,0:T(8,128)(2,1)S(1)} %get-tuple-element.68.db_ref), custom_call_target="tpu_custom_call" | custom-call | flops 2000000000 | bytes 4000000 | tf_op jit(solution)/shard_map/proj_grad/pallas_call | solution.py:328
  36.3 0.5 collective-permute-start.7
  36.9 0.4 collective-permute-start.11
  37.5 1.0 %collective-permute-done.7 = bf16[384,768]{1,0:T(8,128)(2,1)S(1)} collective-permute-done((bf16[384,768]{1,0:T(8,128)(2,1)S(1)}, bf16[384,768]{1,0:T(8,128)(2,1)S(1)}, u32[]{:S(2)}, u32[]{:S(2)}) %collective-permute-start.7) | collective-permute-done | bytes 589856 | tf_op jit(solution)/shard_map/ppermute | solution.py:435
  38.9 3.1 %collective-permute-start.9 = (bf16[96,768]{1,0:T(8,128)(2,1)S(1)}, bf16[96,768]{1,0:T(8,128)(2,1)S(1)}, u32[]{:S(2)}, u32[]{:S(2)}) collective-permute-start(bf16[96,768]{1,0:T(8,128)(2,1)S(1)} %get-tuple-element.101), channel_id=1, source_target_pairs={{0,48},{8,56},{16,0},{24,8},{32,16},{40,24},{48,32},{56,40},{1,49}... | collective-permute-start | bytes 442376 | tf_op jit(solution)/shard_map/ppermute | solution.py:435
  42.1 2.0 %collective-permute-start.10 = (bf16[96,1536]{1,0:T(8,128)(2,1)S(1)}, bf16[96,1536]{1,0:T(8,128)(2,1)S(1)}, u32[]{:S(2)}, u32[]{:S(2)}) collective-permute-start(bf16[96,1536]{1,0:T(8,128)(2,1)S(1)} %pad_maximum_fusion), channel_id=1, source_target_pairs={{0,64},{64,128},{128,192},{192,0},{1,65},{65,129},{129,193},{193,1... | collective-permute-start | bytes 884744 | tf_op jit(solution)/shard_map/ppermute | solution.py:435
  44.1 1.7 %out_part.1 = bf16[16,2,16,768]{3,2,1,0:T(8,128)(2,1)} custom-call(bf16[2,256,768]{2,1,0:T(8,128)(2,1)S(1)} %get-tuple-element.85.xw_ref, bf16[2,256,128]{2,1,0:T(8,128)(2,1)S(1)} %get-tuple-element.51.tis_ref, bf16[2,256,512]{2,1,0:T(8,128)(2,1)S(1)} %get-tuple-element.66.att0_ref, bf16[2,256,256]{2,1,0:T(8,128)(2,1)S(1)} %get-tuple-element.77.att1_ref, ...), custom_call_target="tpu_custom_call" | custom-call | flops 1000 | bytes 1000 | tf_op jit(solution)/shard_map/out_part/pallas_call | solution.py:346
  46.2 3.1 %collective-permute-start.14 = (bf16[96,1536]{1,0:T(8,128)(2,1)S(1)}, bf16[96,1536]{1,0:T(8,128)(2,1)S(1)}, u32[]{:S(2)}, u32[]{:S(2)}) collective-permute-start(bf16[96,1536]{1,0:T(8,128)(2,1)S(1)} %pad_maximum_fusion.3), channel_id=1, source_target_pairs={{0,48},{8,56},{16,0},{24,8},{32,16},{40,24},{48,32},{56,40},{1,49}... | collective-permute-start | bytes 884744 | tf_op jit(solution)/shard_map/ppermute | solution.py:435
  49.4 1.5 %collective-permute-done.10 = bf16[96,1536]{1,0:T(8,128)(2,1)S(1)} collective-permute-done((bf16[96,1536]{1,0:T(8,128)(2,1)S(1)}, bf16[96,1536]{1,0:T(8,128)(2,1)S(1)}, u32[]{:S(2)}, u32[]{:S(2)}) %collective-permute-start.10) | collective-permute-done | bytes 294944 | tf_op jit(solution)/shard_map/ppermute | solution.py:435
  51.3 5.0 %grad_part.1 = bf16[16,2,16,768]{3,2,1,0:T(8,128)(2,1)} custom-call(bf16[2,256,768]{2,1,0:T(8,128)(2,1)S(1)} %get-tuple-element.85.xw_ref, bf16[16,2,16,768]{3,2,1,0:T(8,128)(2,1)S(1)} %bitcast.53, bf16[2,256,128]{2,1,0:T(8,128)(2,1)S(1)} %get-tuple-element.51.tis_ref, bf16[2,2,256,768]{3,2,1,0:T(8,128)(2,1)S(1)} %get-tuple-element.86.dqkv0_ref, ...), custom_call_target="tpu_custom_call" | custom-call | flops 1000 | bytes 1000 | tf_op jit(solution)/shard_map/grad_part/pallas_call | solution.py:389
  56.4 1.9 %collective-permute-done.12 = bf16[48,1536]{1,0:T(8,128)(2,1)S(1)} collective-permute-done((bf16[48,1536]{1,0:T(8,128)(2,1)S(1)}, bf16[48,1536]{1,0:T(8,128)(2,1)S(1)}, u32[]{:S(2)}, u32[]{:S(2)}) %collective-permute-start.12) | collective-permute-done | bytes 147488 | tf_op jit(solution)/shard_map/ppermute | solution.py:435
  58.6 0.4 collective-permute-start.16
  59.1 2.3 %collective-permute-start.15 = (bf16[24,1536]{1,0:T(8,128)(2,1)S(1)}, bf16[24,1536]{1,0:T(8,128)(2,1)S(1)}, u32[]{:S(2)}, u32[]{:S(2)}) collective-permute-start(bf16[24,1536]{1,0:T(8,128)(2,1)S(1)} %slice.145), channel_id=1, source_target_pairs={{0,48},{8,56},{16,32},{24,40},{32,16},{40,24},{48,0},{56,8},{1,49}... | collective-permute-start | bytes 221192 | tf_op jit(solution)/shard_map/ppermute | solution.py:435
  61.5 2.4 %collective-permute-done.16 = bf16[48,1536]{1,0:T(8,128)(2,1)S(1)} collective-permute-done((bf16[48,1536]{1,0:T(8,128)(2,1)S(1)}, bf16[48,1536]{1,0:T(8,128)(2,1)S(1)}, u32[]{:S(2)}, u32[]{:S(2)}) %collective-permute-start.16) | collective-permute-done | bytes 147488 | tf_op jit(solution)/shard_map/ppermute | solution.py:435
  63.9 0.6 collective-permute-start.17
  64.8 4.8 %collective-permute-done.17 = bf16[24,1536]{1,0:T(8,128)(2,1)S(1)} collective-permute-done((bf16[24,1536]{1,0:T(8,128)(2,1)S(1)}, bf16[24,1536]{1,0:T(8,128)(2,1)S(1)}, u32[]{:S(2)}, u32[]{:S(2)}) %collective-permute-start.17) | collective-permute-done | bytes 73760 | tf_op jit(solution)/shard_map/ppermute | solution.py:435
  69.7 13.6 %all_to_all.5.parts_ref = bf16[8,3,3072]{2,1,0:T(4,128)(2,1)S(1)} all-to-all(bf16[8,3,3072]{2,1,0:T(4,128)(2,1)S(1)} %reshape.55), channel_id=1, replica_groups=mesh['dp'=4,'gy'=8,'gx'=8] {'gx'}, dimensions={0} | all-to-all | bytes 294912 | tf_op jit(solution)/shard_map/all_to_all | solution.py:476
  83.3 0.6 finish.1
  (55 shorter events, 3.6 us)
Async XLA Ops:
  0.6 1.1 %copy-start.2 = (bf16[1,16,32,768]{3,2,1,0:T(8,128)(2,1)S(1)}, bf16[1,16,32,768]{3,2,1,0:T(8,128)(2,1)}, u32[]{:S(2)}) copy-start(bf16[1,16,32,768]{3,2,1,0:T(8,128)(2,1)} %param.5) | copy-start | bytes 2359300
  1.8 9.3 %copy-start.1 = (bf16[768,768]{1,0:T(8,128)(2,1)S(1)}, bf16[768,768]{1,0:T(8,128)(2,1)}, u32[]{:S(2)}) copy-start(bf16[768,768]{1,0:T(8,128)(2,1)} %wp_ref.1) | copy-start | bytes 3538948
  1.8 9.3 %copy-start.4 = (bf16[1,16,32,768]{3,2,1,0:T(8,128)(2,1)S(1)}, bf16[1,16,32,768]{3,2,1,0:T(8,128)(2,1)}, u32[]{:S(2)}) copy-start(bf16[1,16,32,768]{3,2,1,0:T(8,128)(2,1)} %param.6) | copy-start | bytes 2359300
  1.8 9.3 %copy-start.5 = (s32[1,16,32]{2,1,0:T(8,128)S(1)}, s32[1,16,32]{2,1,0:T(8,128)}, u32[]{:S(2)}) copy-start(s32[1,16,32]{2,1,0:T(8,128)} %param.7) | copy-start | bytes 6148
  1.8 13.2 %collective-permute-start = (bf16[8,24,768]{2,1,0:T(8,128)(2,1)S(1)}, bf16[8,24,768]{2,1,0:T(8,128)(2,1)S(1)}, u32[]{:S(2)}, u32[]{:S(2)}) collective-permute-start(bf16[8,24,768]{2,1,0:T(8,128)(2,1)S(1)} %above.1.after_ref), channel_id=1, source_target_pairs={{0,56},{8,0},{16,8},{24,16},{32,24},{40,32},{48,40},{56,48},{1,57}... | collective-permute-start | bytes 884744 | tf_op jit(solution)/shard_map/ppermute | solution.py:435
  4.3 8.8 %collective-permute-start.1 = (bf16[8,8,768]{2,1,0:T(8,128)(2,1)S(1)}, bf16[8,8,768]{2,1,0:T(8,128)(2,1)S(1)}, u32[]{:S(2)}, u32[]{:S(2)}) collective-permute-start(bf16[8,8,768]{2,1,0:T(8,128)(2,1)S(1)} %get-tuple-element.49), channel_id=1, source_target_pairs={{0,7},{1,0},{2,1},{3,2},{4,3},{5,4},{6,5},{7,6},{8,15},{9,8},{10,9... | collective-permute-start | bytes 294920 | tf_op jit(solution)/shard_map/ppermute | solution.py:435
  10.2 4.8 %collective-permute-start.2 = (bf16[8,8,768]{2,1,0:T(8,128)(2,1)S(1)}, bf16[8,8,768]{2,1,0:T(8,128)(2,1)S(1)}, u32[]{:S(2)}, u32[]{:S(2)}) collective-permute-start(bf16[8,8,768]{2,1,0:T(8,128)(2,1)S(1)} %get-tuple-element.50), channel_id=1, source_target_pairs={{0,63},{1,56},{2,57},{3,58},{4,59},{5,60},{6,61},{7,62},{8,7},{9,0... | collective-permute-start | bytes 294920 | tf_op jit(solution)/shard_map/ppermute | solution.py:493
  11.1 3.9 %copy-start = (bf16[768,2304]{1,0:T(8,128)(2,1)S(1)}, bf16[768,2304]{1,0:T(8,128)(2,1)}, u32[]{:S(2)}) copy-start(bf16[768,2304]{1,0:T(8,128)(2,1)} %wv_ref.5) | copy-start | bytes 10616836
  11.1 3.9 %copy-start.3 = (bf16[1,16,32,768]{3,2,1,0:T(8,128)(2,1)S(1)}, bf16[1,16,32,768]{3,2,1,0:T(8,128)(2,1)}, u32[]{:S(2)}) copy-start(bf16[1,16,32,768]{3,2,1,0:T(8,128)(2,1)} %param.5) | copy-start | bytes 2359300
  23.3 2.9 %collective-permute-start.3 = (bf16[384,1536]{1,0:T(8,128)(2,1)S(1)}, bf16[384,1536]{1,0:T(8,128)(2,1)S(1)}, u32[]{:S(2)}, u32[]{:S(2)}) collective-permute-start(bf16[384,1536]{1,0:T(8,128)(2,1)S(1)} %get-tuple-element.56), channel_id=1, source_target_pairs={{0,8},{8,0},{16,24},{24,16},{32,40},{40,32},{48,56},{56,48},{1,9},... | collective-permute-start | bytes 3538952 | tf_op jit(solution)/shard_map/ppermute | solution.py:435
  26.7 6.0 %collective-permute-start.4 = (bf16[96,768]{1,0:T(8,128)(2,1)S(1)}, bf16[96,768]{1,0:T(8,128)(2,1)S(1)}, u32[]{:S(2)}, u32[]{:S(2)}) collective-permute-start(bf16[96,768]{1,0:T(8,128)(2,1)S(1)} %get-tuple-element.107), channel_id=1, source_target_pairs={{0,64},{64,128},{128,192},{192,0},{1,65},{65,129},{129,193},{193,1... | collective-permute-start | bytes 442376 | tf_op jit(solution)/shard_map/ppermute | solution.py:435
  27.2 7.1 %collective-permute-start.5 = (bf16[96,768]{1,0:T(8,128)(2,1)S(1)}, bf16[96,768]{1,0:T(8,128)(2,1)S(1)}, u32[]{:S(2)}, u32[]{:S(2)}) collective-permute-start(bf16[96,768]{1,0:T(8,128)(2,1)S(1)} %get-tuple-element.105), channel_id=1, source_target_pairs={{0,192},{64,0},{128,64},{192,128},{1,193},{65,1},{129,65},{193,129... | collective-permute-start | bytes 442376 | tf_op jit(solution)/shard_map/ppermute | solution.py:435
  34.3 2.0 %collective-permute-start.6 = (bf16[384,768]{1,0:T(8,128)(2,1)S(1)}, bf16[384,768]{1,0:T(8,128)(2,1)S(1)}, u32[]{:S(2)}, u32[]{:S(2)}) collective-permute-start(bf16[384,768]{1,0:T(8,128)(2,1)S(1)} %get-tuple-element.65), channel_id=1, source_target_pairs={{0,8},{8,0},{16,24},{24,16},{32,40},{40,32},{48,56},{56,48},{1,9},... | collective-permute-start | bytes 1769480 | tf_op jit(solution)/shard_map/ppermute | solution.py:435
  36.3 2.1 %collective-permute-start.7 = (bf16[384,768]{1,0:T(8,128)(2,1)S(1)}, bf16[384,768]{1,0:T(8,128)(2,1)S(1)}, u32[]{:S(2)}, u32[]{:S(2)}) collective-permute-start(bf16[384,768]{1,0:T(8,128)(2,1)S(1)} %get-tuple-element.73), channel_id=1, source_target_pairs={{0,8},{8,0},{16,24},{24,16},{32,40},{40,32},{48,56},{56,48},{1,9},... | collective-permute-start | bytes 1769480 | tf_op jit(solution)/shard_map/ppermute | solution.py:435
  36.9 12.6 %collective-permute-start.11 = (bf16[96,1536]{1,0:T(8,128)(2,1)S(1)}, bf16[96,1536]{1,0:T(8,128)(2,1)S(1)}, u32[]{:S(2)}, u32[]{:S(2)}) collective-permute-start(bf16[96,1536]{1,0:T(8,128)(2,1)S(1)} %pad_maximum_fusion.1), channel_id=1, source_target_pairs={{0,192},{64,0},{128,64},{192,128},{1,193},{65,1},{129,65},{193,129... | collective-permute-start | bytes 884744 | tf_op jit(solution)/shard_map/ppermute | solution.py:435
  38.6 7.4 %collective-permute-start.8 = (bf16[96,768]{1,0:T(8,128)(2,1)S(1)}, bf16[96,768]{1,0:T(8,128)(2,1)S(1)}, u32[]{:S(2)}, u32[]{:S(2)}) collective-permute-start(bf16[96,768]{1,0:T(8,128)(2,1)S(1)} %get-tuple-element.99), channel_id=1, source_target_pairs={{0,16},{8,24},{16,32},{24,40},{32,48},{40,56},{48,0},{56,8},{1,17}... | collective-permute-start | bytes 442376 | tf_op jit(solution)/shard_map/ppermute | solution.py:435
  38.9 7.1 %collective-permute-start.9 = (bf16[96,768]{1,0:T(8,128)(2,1)S(1)}, bf16[96,768]{1,0:T(8,128)(2,1)S(1)}, u32[]{:S(2)}, u32[]{:S(2)}) collective-permute-start(bf16[96,768]{1,0:T(8,128)(2,1)S(1)} %get-tuple-element.101), channel_id=1, source_target_pairs={{0,48},{8,56},{16,0},{24,8},{32,16},{40,24},{48,32},{56,40},{1,49}... | collective-permute-start | bytes 442376 | tf_op jit(solution)/shard_map/ppermute | solution.py:435
  42.1 8.8 %collective-permute-start.10 = (bf16[96,1536]{1,0:T(8,128)(2,1)S(1)}, bf16[96,1536]{1,0:T(8,128)(2,1)S(1)}, u32[]{:S(2)}, u32[]{:S(2)}) collective-permute-start(bf16[96,1536]{1,0:T(8,128)(2,1)S(1)} %pad_maximum_fusion), channel_id=1, source_target_pairs={{0,64},{64,128},{128,192},{192,0},{1,65},{65,129},{129,193},{193,1... | collective-permute-start | bytes 884744 | tf_op jit(solution)/shard_map/ppermute | solution.py:435
  46.2 12.1 %collective-permute-start.14 = (bf16[96,1536]{1,0:T(8,128)(2,1)S(1)}, bf16[96,1536]{1,0:T(8,128)(2,1)S(1)}, u32[]{:S(2)}, u32[]{:S(2)}) collective-permute-start(bf16[96,1536]{1,0:T(8,128)(2,1)S(1)} %pad_maximum_fusion.3), channel_id=1, source_target_pairs={{0,48},{8,56},{16,0},{24,8},{32,16},{40,24},{48,32},{56,40},{1,49}... | collective-permute-start | bytes 884744 | tf_op jit(solution)/shard_map/ppermute | solution.py:435
  49.3 9.2 %collective-permute-start.13 = (bf16[96,1536]{1,0:T(8,128)(2,1)S(1)}, bf16[96,1536]{1,0:T(8,128)(2,1)S(1)}, u32[]{:S(2)}, u32[]{:S(2)}) collective-permute-start(bf16[96,1536]{1,0:T(8,128)(2,1)S(1)} %pad_maximum_fusion.2), channel_id=1, source_target_pairs={{0,16},{8,24},{16,32},{24,40},{32,48},{40,56},{48,0},{56,8},{1,17}... | collective-permute-start | bytes 884744 | tf_op jit(solution)/shard_map/ppermute | solution.py:435
  51.0 7.2 %collective-permute-start.12 = (bf16[48,1536]{1,0:T(8,128)(2,1)S(1)}, bf16[48,1536]{1,0:T(8,128)(2,1)S(1)}, u32[]{:S(2)}, u32[]{:S(2)}) collective-permute-start(bf16[48,1536]{1,0:T(8,128)(2,1)S(1)} %fusion.13), channel_id=1, source_target_pairs={{0,16},{8,24},{16,0},{24,8},{32,48},{40,56},{48,32},{56,40},{1,17}... | collective-permute-start | bytes 442376 | tf_op jit(solution)/shard_map/ppermute | solution.py:435
  58.6 5.2 %collective-permute-start.16 = (bf16[48,1536]{1,0:T(8,128)(2,1)S(1)}, bf16[48,1536]{1,0:T(8,128)(2,1)S(1)}, u32[]{:S(2)}, u32[]{:S(2)}) collective-permute-start(bf16[48,1536]{1,0:T(8,128)(2,1)S(1)} %pad_maximum_fusion.4), channel_id=1, source_target_pairs={{0,64},{64,0},{128,192},{192,128},{1,65},{65,1},{129,193},{193,129... | collective-permute-start | bytes 442376 | tf_op jit(solution)/shard_map/ppermute | solution.py:435
  59.1 5.7 %collective-permute-start.15 = (bf16[24,1536]{1,0:T(8,128)(2,1)S(1)}, bf16[24,1536]{1,0:T(8,128)(2,1)S(1)}, u32[]{:S(2)}, u32[]{:S(2)}) collective-permute-start(bf16[24,1536]{1,0:T(8,128)(2,1)S(1)} %slice.145), channel_id=1, source_target_pairs={{0,48},{8,56},{16,32},{24,40},{32,16},{40,24},{48,0},{56,8},{1,49}... | collective-permute-start | bytes 221192 | tf_op jit(solution)/shard_map/ppermute | solution.py:435
  63.9 5.7 %collective-permute-start.17 = (bf16[24,1536]{1,0:T(8,128)(2,1)S(1)}, bf16[24,1536]{1,0:T(8,128)(2,1)S(1)}, u32[]{:S(2)}, u32[]{:S(2)}) collective-permute-start(bf16[24,1536]{1,0:T(8,128)(2,1)S(1)} %slice.149), channel_id=1, source_target_pairs={{0,192},{64,128},{128,64},{192,0},{1,193},{65,129},{129,65},{193,1... | collective-permute-start | bytes 221192 | tf_op jit(solution)/shard_map/ppermute | solution.py:435

commit v8 on v7

--- a/solution.py
+++ b/solution.py
@@ -125,19 +125,15 @@
     )(cot, tissue, w_proj)
 
 
-def row_order(first):
+def row_order():
     gy = lax.axis_index("gy")
     dp, y, core = lax.axis_index("dp"), gy >> 1, gy & 1
     at = lax.broadcasted_iota(jnp.int32, (D, 1), 0)
     third = ((at.astype(F32) + 0.5) * (1.0 / 3)).astype(jnp.int32)
-    distance, depth = (third >> 5) & 3, third & 7
-    partner = ((third >> 4) & 1) ^ (((third >> 3) & 1) * 3)
-    if first == "dp":
-        dp_of, y_of = (distance + dp) & 3, partner ^ y
-    else:
-        dp_of, y_of = partner ^ dp, (distance + y) & 3
+    dp_of = ((third >> 6) & 1) ^ (((third >> 5) & 1) * 3) ^ dp
+    y_of = ((third >> 4) & 1) ^ (((third >> 3) & 1) * 3) ^ y
     core_of = (third >> 7) ^ core
-    source = ((dp_of * 8 + y_of * 2 + core_of) * 8 + depth) * 3 + at - third * 3
+    source = ((dp_of * 8 + y_of * 2 + core_of) * 8 + (third & 7)) * 3 + at - third * 3
     column = lax.broadcasted_iota(jnp.int32, (D, D), 1)
     return jnp.where(column == source, 1.0, 0.0).astype(BF)
 
@@ -149,14 +145,18 @@
     return centred * inv, inv
 
 
-def put(grad, keep_ref, send_ref):
+def put(grad, keep_ref, send_ref, y_first):
+    if y_first:
+        size = D // 32
+        places = [(c * 4 + x) * 4 + y for c in range(2) for y in range(4) for x in range(4)]
+        grad = jnp.concatenate([grad[at * size : (at + 1) * size] for at in places], 0)
     keep_ref[...] = grad[: D // 2].astype(BF)
     send_ref[...] = grad[D // 2 :].astype(BF)
 
 
 def heads_group(
     hid_ref, hid_t_ref, tis_ref, live_ref, wq_ref, wk_ref, wv_ref, da_ref,
-    keep_ref, send_ref, att_ref, dqkv_ref,
+    keep_ref, send_ref, att_ref, dqkv_ref, y_first,
 ):
     hidden = hid_ref[...].reshape(2 * CELLS, D)
     query = nn(hidden, wq_ref[...]).astype(BF) * BF(HEAD_SCALE)
@@ -200,7 +200,8 @@
         for i, grad in enumerate((dq, dk, dv)):
             at = i * GW + p * 128
             dqkv_ref[0, w, :, at : at + 128] = grad.astype(BF)
-    put(nn(hid_t_ref[...], dqkv_ref[0].reshape(2 * CELLS, D)), keep_ref, send_ref)
+    grad = nn(hid_t_ref[...], dqkv_ref[0].reshape(2 * CELLS, D))
+    put(grad, keep_ref, send_ref, y_first)
 
 
 def first_kernel(
@@ -214,7 +215,7 @@
         low = below_ref[...].astype(F32)
         right = right_ref[...].astype(F32)
         diag = diag_ref[...].astype(F32)
-        perm = row_order("dp")
+        perm = row_order()
         for w in range(2):
             if w == 0:
                 top, bottom = own[:, 8:24], low[:, :16]
@@ -231,35 +232,12 @@
 
     heads_group(
         hid_ref, hid_t_ref, tis_ref, live_ref, wq_ref, wk_ref, wv_ref, da_ref,
-        keep_ref, send_ref, att_ref, dqkv_ref,
+        keep_ref, send_ref, att_ref, dqkv_ref, False,
     )
 
 
-def last_kernel(
-    hid_ref, hid_t_ref, tis_ref, live_ref, wq_ref, wk_ref, wv_ref, da_ref,
-    keep_ref, send_ref, att_ref, dqkv_ref,
-):
-    heads_group(
-        hid_ref, hid_t_ref, tis_ref, live_ref, wq_ref, wk_ref, wv_ref, da_ref,
-        keep_ref, send_ref, att_ref, dqkv_ref,
-    )
-
-
-def turn_kernel(hid_ref, tis_ref, hid_t_ref):
-    perm = row_order("gy")
-    for w in range(2):
-        masked = hid_ref[w] * jnp.tile(tis_ref[w], (1, D // 128))
-        hid_t_ref[:, w * CELLS : (w + 1) * CELLS] = nt(perm, masked).astype(BF)
-
-
-def turn(hid, tis):
-    return pl.pallas_call(
-        turn_kernel,
-        out_shape=jax.ShapeDtypeStruct((D, 2 * CELLS), BF),
-        compiler_params=pltpu.CompilerParams(vmem_limit_bytes=VMEM),
-        cost_estimate=cost(2e9, 2e6),
-        name="turn",
-    )(hid, tis)
+def last_kernel(*refs):
+    heads_group(*refs, True)
 
 
 def columns(block, first):
@@ -294,9 +272,8 @@
         first_kernel,
         grid=(2,),
         in_specs=[full((16, 32, D)), full((8, 24, D)), full((8, 8, D)), full((8, 8, D))] + inputs,
-        out_specs=outputs + [full((2, CELLS, D))] * 2,
-        out_shape=shapes + [rows, rows],
-        scratch_shapes=[pltpu.VMEM((D, 2 * CELLS), BF)],
+        out_specs=outputs + [full((2, CELLS, D))] * 2 + [full((D, 2 * CELLS))],
+        out_shape=shapes + [rows, rows, jax.ShapeDtypeStruct((D, 2 * CELLS), BF)],
         compiler_params=pltpu.CompilerParams(vmem_limit_bytes=VMEM),
         cost_estimate=cost(6e9, 10e6),
         name="first_heads",
@@ -319,8 +296,8 @@
 
 def proj_kernel(att0_ref, att1_ref, db_ref, keep_ref, send_ref):
     attended = jnp.concatenate([att0_ref[...], att1_ref[...]], 2).reshape(2 * CELLS, D)
-    att_t = nt(row_order("gy"), attended).astype(BF)
-    put(nn(att_t, db_ref[...].reshape(2 * CELLS, D)), keep_ref, send_ref)
+    att_t = nt(row_order(), attended).astype(BF)
+    put(nn(att_t, db_ref[...].reshape(2 * CELLS, D)), keep_ref, send_ref, True)
 
 
 def proj_grad(att0, att1, db):
@@ -442,16 +419,16 @@
     return total.astype(BF)
 
 
-def ring_start(low, high, axis, step):
-    from_low = send(low[2], axis, lambda j: j + step)
-    from_high = send(high[2], axis, lambda j: j - step)
-    return from_low, from_high
-
-
-def ring_pass(low, high, came, axis, step):
-    up = jnp.concatenate([add(low[1], came[0]), high[1]], 1)
-    down = jnp.concatenate([low[3], add(high[3], came[1])], 1)
-    return send(up, axis, lambda j: j + step), send(down, axis, lambda j: j - step)
+def ring_start(low, high, axis, flips):
+    one, three = flips
+    return send(low[3], axis, lambda j: j ^ one), send(high[3], axis, lambda j: j ^ three)
+
+
+def ring_pass(low, high, came, axis, flips):
+    one, three = flips
+    to_one = jnp.concatenate([low[2], add(high[2], came[1])], 1)
+    to_three = jnp.concatenate([add(low[1], came[0]), high[1]], 1)
+    return send(to_one, axis, lambda j: j ^ one), send(to_three, axis, lambda j: j ^ three)
 
 
 def ring_end(low, high, came):
@@ -501,29 +478,28 @@
     )
     cot = cotangent.reshape(WIN, 2, WIN, D)
     db, da, tis, live = branch(cot, tissue[0], w_proj)
-    keep0, send0, att0, dqkv0, xw, hid = first_heads(
+    along_x, along_y = ("dp", (1, 3)), ("gy", (2, 6))
+    keep0, send0, att0, dqkv0, xw, hid, hid_t = first_heads(
         mine, below, right, diag, tis, live, w_qkv, da
     )
     came = send(send0, "gy", lambda i: i ^ 1)
-    hid_t = turn(hid, tis)
-    came, hid_t = tie(came, hid_t)
+    keep1, send1, att1, dqkv1 = last_heads(hid, hid_t, tis, live, w_qkv, da)
+    came, send1, att1 = tie(came, send1, att1)
     first = add(keep0, came)
     low_a, high_a = blocks(first[:, :D]), blocks(first[:, D:])
-    low_a, high_a, hid_t = tie(low_a, high_a, hid_t)
-    came_a = ring_start(low_a, high_a, "dp", 1)
-    keep1, send1, att1, dqkv1 = last_heads(hid, hid_t, tis, live, w_qkv, da)
-    came_a, send1, att1 = tie(came_a, send1, att1)
-    came_a = ring_pass(low_a, high_a, came_a, "dp", 1)
+    low_a, high_a, att1 = tie(low_a, high_a, att1)
+    came_a = ring_start(low_a, high_a, *along_x)
     came = send(send1, "gy", lambda i: i ^ 1)
     keep2, send2 = proj_grad(att0, att1, db)
-    came, send2, keep2 = tie(came, send2, keep2)
+    came_a, came, send2, keep2 = tie(came_a, came, send2, keep2)
+    came_a = ring_pass(low_a, high_a, came_a, *along_x)
     low_b = add(keep1, came)
     high_b = add(keep2, send(send2, "gy", lambda i: i ^ 1))
     low_b, high_b, att1 = tie(blocks(low_b), blocks(high_b), att1)
-    came_b = ring_start(low_b, high_b, "gy", 2)
+    came_b = ring_start(low_b, high_b, *along_y)
     out = out_part(xw, tis, att0, att1, w_proj)
     came_b, out, xw, low_a, high_a = tie(came_b, out, xw, low_a, high_a)
-    came_b = ring_pass(low_b, high_b, came_b, "gy", 2)
+    came_b = ring_pass(low_b, high_b, came_b, *along_y)
     rows_a = ring_end(low_a, high_a, came_a)
     came_a = halve_start(rows_a, "gy", 2)
     grad = grad_part(xw, cot, tis, dqkv0, dqkv1, w_qkv)

time: 84.9 us -> 85 us (level)
  waiting for transfers between devices: 18.6 us -> 22.4 us
  starting transfers between devices: 24.9 us -> 23.1 us
  Pallas kernels: 23.3 us -> 22.2 us
    ppermute x17, waiting for transfers between devices: 16.7 us -> 20.4 us  [send(): lax.ppermute(value, axis, [(i, move(i) % devices) for i in range(devices)])]
    ppermute x17, starting transfers between devices: 24.1 us -> 22.3 us  [send(): lax.ppermute(value, axis, [(i, move(i) % devices) for i in range(devices)])]
    pallas_call x1 -> x0, Pallas kernels: 1.09 us -> none  [turn(): pl.pallas_call(turn_kernel, out_shape=jax.ShapeDtypeStruct((D, 2 * CELLS)...]
  transfers between devices with their start and end apart: 18 -> 18, of which waited for: 14 -> 11; matrix products, arithmetic and copies ran while one was open for 1% -> 1% of each run, Pallas kernels for 17% -> 16%
where the time goes in v8:
time: 85 us; the launch traced here: 84.9 us
  starting transfers between devices  23.1 us (27%)
  waiting for transfers between devices  22.4 us (26%)
  Pallas kernels  22.2 us (26%)
  blocking collectives  13.7 us (16%)
  local copies, waits for them, and re-layouts  1.42 us (2%)
  other arithmetic  1.15 us (1%)
  between operations  0.92 us (1%)
    ppermute x17, starting transfers between devices, send(): lax.ppermute(value, axis, [(i, move(i) % devices) for i in range(devices)])  22.3 us
    ppermute x17, waiting for transfers between devices, send(): lax.ppermute(value, axis, [(i, move(i) % devices) for i in range(devices)])  20.4 us
    all_to_all x1, blocking collectives, exchange(): return lax.all_to_all(rows, axis, 0, 0, axis_index_groups=groups)  13.7 us
    pallas_call x1, Pallas kernels, first_heads(): pl.pallas_call(first_kernel, grid=(2,), in_specs=[full((16, 32, D)), full...  8.33 us
    pallas_call x1, Pallas kernels, grad_part(): pl.pallas_call(grad_kernel, grid=(GROUPS,), in_specs=[full((2, CELLS, D))...  5.01 us
    pallas_call x1, Pallas kernels, last_heads(): pl.pallas_call(last_kernel, grid=(1,), in_specs=[full((2, CELLS, D)), ful...  3.15 us
    ppermute x1, waiting for transfers between devices, shards(): lax.ppermute(corner, ('gy', 'gx'), [(a * nx + b, (a - 1) % ny * nx + (b -...  1.94 us
    pallas_call x1, Pallas kernels, proj_grad(): pl.pallas_call(proj_kernel, out_shape=[shape, shape], compiler_params=plt...  1.9 us
  transfers between devices with their start and end apart: 18, of which 11 were waited for; matrix products, arithmetic and copies ran while one was open for 1% of the time, Pallas kernels for 16%

profile of v8, /device:TPU:6, one launch (start us, length us, event | category | flops | bytes accessed | tf_op | source)
XLA Modules:
  0.0 84.9 jit_solution(16024861575736642136)
XLA Ops:
  0.6 1.1 %copy-done.2 = bf16[1,16,32,768]{3,2,1,0:T(8,128)(2,1)S(1)} copy-done((bf16[1,16,32,768]{3,2,1,0:T(8,128)(2,1)S(1)}, bf16[1,16,32,768]{3,2,1,0:T(8,128)(2,1)}, u32[]{:S(2)}) %copy-start.2) | copy-done | bytes 786456
  1.8 2.5 %collective-permute-start = (bf16[8,24,768]{2,1,0:T(8,128)(2,1)S(1)}, bf16[8,24,768]{2,1,0:T(8,128)(2,1)S(1)}, u32[]{:S(2)}, u32[]{:S(2)}) collective-permute-start(bf16[8,24,768]{2,1,0:T(8,128)(2,1)S(1)} %above.1.after_ref), channel_id=1, source_target_pairs={{0,56},{8,0},{16,8},{24,16},{32,24},{40,32},{48,40},{56,48},{1,57}... | collective-permute-start | bytes 884744 | tf_op jit(solution)/shard_map/ppermute | solution.py:412
  4.3 5.9 %collective-permute-start.1 = (bf16[8,8,768]{2,1,0:T(8,128)(2,1)S(1)}, bf16[8,8,768]{2,1,0:T(8,128)(2,1)S(1)}, u32[]{:S(2)}, u32[]{:S(2)}) collective-permute-start(bf16[8,8,768]{2,1,0:T(8,128)(2,1)S(1)} %get-tuple-element.49), channel_id=1, source_target_pairs={{0,7},{1,0},{2,1},{3,2},{4,3},{5,4},{6,5},{7,6},{8,15},{9,8},{10,9... | collective-permute-start | bytes 294920 | tf_op jit(solution)/shard_map/ppermute | solution.py:412
  10.2 0.8 collective-permute-start.2
  11.1 1.5 %branch.1 = (bf16[2,256,768]{2,1,0:T(8,128)(2,1)S(1)}, bf16[2,256,768]{2,1,0:T(8,128)(2,1)S(1)}, bf16[2,256,128]{2,1,0:T(8,128)(2,1)S(1)}, bf16[2,256,128]{2,1,0:T(8,128)(2,1)S(1)}) custom-call(bf16[16,2,16,768]{3,2,1,0:T(8,128)(2,1)S(1)} %bitcast.52, s32[16,32]{1,0:T(8,128)S(1)} %bitcast.54, bf16[768,768]{1,0:T(8,128)(2,1)S(1)} %copy-done.1), custom_call_target="tpu_custom_call" | custom-call | flops 20000000000 | bytes 4000000 | tf_op jit(solution)/shard_map/branch/pallas_call | solution.py:112
  12.6 0.5 collective-permute-done.1.right_ref
  13.0 1.9 %collective-permute-done.2.diag_ref = bf16[8,8,768]{2,1,0:T(8,128)(2,1)S(1)} collective-permute-done((bf16[8,8,768]{2,1,0:T(8,128)(2,1)S(1)}, bf16[8,8,768]{2,1,0:T(8,128)(2,1)S(1)}, u32[]{:S(2)}, u32[]{:S(2)}) %collective-permute-start.2) | collective-permute-done | bytes 98336 | tf_op jit(solution)/shard_map/ppermute | solution.py:470
  15.0 8.3 %first_heads.1 = (bf16[384,1536]{1,0:T(8,128)(2,1)S(1)}, bf16[384,1536]{1,0:T(8,128)(2,1)S(1)}, bf16[2,256,512]{2,1,0:T(8,128)(2,1)S(1)}, bf16[2,2,256,768]{3,2,...) custom-call(bf16[16,32,768]{2,1,0:T(8,128)(2,1)S(1)} %bitcast.51, ...), custom_call_target="tpu_custom_call" | custom-call | flops 6000000000 | bytes 10000000 | tf_op jit(solution)/shard_map/first_heads/pallas_call | solution.py:271
  23.4 3.1 %last_heads.1 = (bf16[384,768]{1,0:T(8,128)(2,1)S(1)}, bf16[384,768]{1,0:T(8,128)(2,1)S(1)}, bf16[2,256,256]{2,1,0:T(8,128)(2,1)S(1)}, bf16[1,2,256,768]{3,2,1,0:T(8,128)(2,1)S(1)}) custom-call(bf16[2,256,768]{2,1,0:T(8,128)(2,1)S(1)} %get-tuple-element.54.refs_0_, bf16[768,512]{1,0:T(8,128)(2,1)S(1)} %get-tuple-element.55.refs_1_, ...), custom_call_target="tpu_custom_call" | custom-call | flops 4000000000 | bytes 6000000 | tf_op jit(solution)/shard_map/last_heads/pallas_call | solution.py:285
  27.0 0.6 collective-permute-start.6
  27.6 1.1 %collective-permute-start.4 = (bf16[96,768]{1,0:T(8,128)(2,1)S(1)}, bf16[96,768]{1,0:T(8,128)(2,1)S(1)}, u32[]{:S(2)}, u32[]{:S(2)}) collective-permute-start(bf16[96,768]{1,0:T(8,128)(2,1)S(1)} %get-tuple-element.105), channel_id=1, source_target_pairs={{0,64},{64,0},{128,192},{192,128},{1,65},{65,1},{129,193},{193,129... | collective-permute-start | bytes 442376 | tf_op jit(solution)/shard_map/ppermute | solution.py:412
  28.7 1.2 %collective-permute-start.5 = (bf16[96,768]{1,0:T(8,128)(2,1)S(1)}, bf16[96,768]{1,0:T(8,128)(2,1)S(1)}, u32[]{:S(2)}, u32[]{:S(2)}) collective-permute-start(bf16[96,768]{1,0:T(8,128)(2,1)S(1)} %get-tuple-element.107), channel_id=1, source_target_pairs={{0,192},{64,128},{128,64},{192,0},{1,193},{65,129},{129,65},{193,1... | collective-permute-start | bytes 442376 | tf_op jit(solution)/shard_map/ppermute | solution.py:412
  29.9 1.9 %proj_grad.1 = (bf16[384,768]{1,0:T(8,128)(2,1)S(1)}, bf16[384,768]{1,0:T(8,128)(2,1)S(1)}) custom-call(bf16[2,256,512]{2,1,0:T(8,128)(2,1)S(1)} %get-tuple-element.66.att0_ref, bf16[2,256,256]{2,1,0:T(8,128)(2,1)S(1)} %get-tuple-element.77.att1_ref, bf16[2,256,768]{2,1,0:T(8,128)(2,1)S(1)} %get-tuple-element.68.db_ref), custom_call_target="tpu_custom_call" | custom-call | flops 2000000000 | bytes 4000000 | tf_op jit(solution)/shard_map/proj_grad/pallas_call | solution.py:305
  31.8 1.8 %collective-permute-done.4 = bf16[96,768]{1,0:T(8,128)(2,1)S(1)} collective-permute-done((bf16[96,768]{1,0:T(8,128)(2,1)S(1)}, bf16[96,768]{1,0:T(8,128)(2,1)S(1)}, u32[]{:S(2)}, u32[]{:S(2)}) %collective-permute-start.4) | collective-permute-done | bytes 147488 | tf_op jit(solution)/shard_map/ppermute | solution.py:412
  33.6 1.9 %collective-permute-done.5 = bf16[96,768]{1,0:T(8,128)(2,1)S(1)} collective-permute-done((bf16[96,768]{1,0:T(8,128)(2,1)S(1)}, bf16[96,768]{1,0:T(8,128)(2,1)S(1)}, u32[]{:S(2)}, u32[]{:S(2)}) %collective-permute-start.5) | collective-permute-done | bytes 147488 | tf_op jit(solution)/shard_map/ppermute | solution.py:412
  35.6 1.2 %collective-permute-start.11 = (bf16[96,1536]{1,0:T(8,128)(2,1)S(1)}, bf16[96,1536]{1,0:T(8,128)(2,1)S(1)}, u32[]{:S(2)}, u32[]{:S(2)}) collective-permute-start(bf16[96,1536]{1,0:T(8,128)(2,1)S(1)} %pad_maximum_fusion.1), channel_id=1, source_target_pairs={{0,192},{64,128},{128,64},{192,0},{1,193},{65,129},{129,65},{193,1... | collective-permute-start | bytes 884744 | tf_op jit(solution)/shard_map/ppermute | solution.py:412
  37.1 0.6 collective-permute-done.7
  38.2 2.6 %collective-permute-start.9 = (bf16[96,768]{1,0:T(8,128)(2,1)S(1)}, bf16[96,768]{1,0:T(8,128)(2,1)S(1)}, u32[]{:S(2)}, u32[]{:S(2)}) collective-permute-start(bf16[96,768]{1,0:T(8,128)(2,1)S(1)} %get-tuple-element.99), channel_id=1, source_target_pairs={{0,48},{8,56},{16,32},{24,40},{32,16},{40,24},{48,0},{56,8},{1,49}... | collective-permute-start | bytes 442376 | tf_op jit(solution)/shard_map/ppermute | solution.py:412
  40.9 1.7 %out_part.1 = bf16[16,2,16,768]{3,2,1,0:T(8,128)(2,1)} custom-call(bf16[2,256,768]{2,1,0:T(8,128)(2,1)S(1)} %get-tuple-element.85.xw_ref, bf16[2,256,128]{2,1,0:T(8,128)(2,1)S(1)} %get-tuple-element.51.tis_ref.refs_2_, bf16[2,256,512]{2,1,0:T(8,128)(2,1)S(1)} %get-tuple-element.66.att0_ref, bf16[2,256,256]{2,1,0:T(8,128)(2,1)S(1)} %get-tuple-element.77.att1_ref, ...), custom_call_target="tpu_custom_call" | custom-call | flops 1000 | bytes 1000 | tf_op jit(solution)/shard_map/out_part/pallas_call | solution.py:323
  42.6 1.2 %collective-permute-done.8 = bf16[96,768]{1,0:T(8,128)(2,1)S(1)} collective-permute-done((bf16[96,768]{1,0:T(8,128)(2,1)S(1)}, bf16[96,768]{1,0:T(8,128)(2,1)S(1)}, u32[]{:S(2)}, u32[]{:S(2)}) %collective-permute-start.8) | collective-permute-done | bytes 147488 | tf_op jit(solution)/shard_map/ppermute | solution.py:412
  43.8 1.3 %collective-permute-done.9 = bf16[96,768]{1,0:T(8,128)(2,1)S(1)} collective-permute-done((bf16[96,768]{1,0:T(8,128)(2,1)S(1)}, bf16[96,768]{1,0:T(8,128)(2,1)S(1)}, u32[]{:S(2)}, u32[]{:S(2)}) %collective-permute-start.9) | collective-permute-done | bytes 147488 | tf_op jit(solution)/shard_map/ppermute | solution.py:412
  45.2 2.9 %collective-permute-start.14 = (bf16[96,1536]{1,0:T(8,128)(2,1)S(1)}, bf16[96,1536]{1,0:T(8,128)(2,1)S(1)}, u32[]{:S(2)}, u32[]{:S(2)}) collective-permute-start(bf16[96,1536]{1,0:T(8,128)(2,1)S(1)} %pad_maximum_fusion.3), channel_id=1, source_target_pairs={{0,48},{8,56},{16,32},{24,40},{32,16},{40,24},{48,0},{56,8},{1,49}... | collective-permute-start | bytes 884744 | tf_op jit(solution)/shard_map/ppermute | solution.py:412
  48.2 1.4 %collective-permute-done.10 = bf16[96,1536]{1,0:T(8,128)(2,1)S(1)} collective-permute-done((bf16[96,1536]{1,0:T(8,128)(2,1)S(1)}, bf16[96,1536]{1,0:T(8,128)(2,1)S(1)}, u32[]{:S(2)}, u32[]{:S(2)}) %collective-permute-start.10) | collective-permute-done | bytes 294944 | tf_op jit(solution)/shard_map/ppermute | solution.py:412
  49.8 1.2 %collective-permute-start.12 = (bf16[48,1536]{1,0:T(8,128)(2,1)S(1)}, bf16[48,1536]{1,0:T(8,128)(2,1)S(1)}, u32[]{:S(2)}, u32[]{:S(2)}) collective-permute-start(bf16[48,1536]{1,0:T(8,128)(2,1)S(1)} %fusion.13), channel_id=1, source_target_pairs={{0,16},{8,24},{16,0},{24,8},{32,48},{40,56},{48,32},{56,40},{1,17}... | collective-permute-start | bytes 442376 | tf_op jit(solution)/shard_map/ppermute | solution.py:412
  51.0 5.0 %grad_part.1 = bf16[16,2,16,768]{3,2,1,0:T(8,128)(2,1)} custom-call(bf16[2,256,768]{2,1,0:T(8,128)(2,1)S(1)} %get-tuple-element.85.xw_ref, bf16[16,2,16,768]{3,2,1,0:T(8,128)(2,1)S(1)} %bitcast.53, bf16[2,256,128]{2,1,0:T(8,128)(2,1)S(1)} %get-tuple-element.51.tis_ref.refs_2_, bf16[2,2,256,768]{3,2,1,0:T(8,128)(2,1)S(1)} %get-tuple-element.86.dqkv0_ref, ...), custom_call_target="tpu_custom_call" | custom-call | flops 1000 | bytes 1000 | tf_op jit(solution)/shard_map/grad_part/pallas_call | solution.py:366
  56.0 3.3 %collective-permute-done.12 = bf16[48,1536]{1,0:T(8,128)(2,1)S(1)} collective-permute-done((bf16[48,1536]{1,0:T(8,128)(2,1)S(1)}, bf16[48,1536]{1,0:T(8,128)(2,1)S(1)}, u32[]{:S(2)}, u32[]{:S(2)}) %collective-permute-start.12) | collective-permute-done | bytes 147488 | tf_op jit(solution)/shard_map/ppermute | solution.py:412
  59.6 0.4 collective-permute-start.15
  60.0 4.7 %collective-permute-done.16 = bf16[48,1536]{1,0:T(8,128)(2,1)S(1)} collective-permute-done((bf16[48,1536]{1,0:T(8,128)(2,1)S(1)}, bf16[48,1536]{1,0:T(8,128)(2,1)S(1)}, u32[]{:S(2)}, u32[]{:S(2)}) %collective-permute-start.16) | collective-permute-done | bytes 147488 | tf_op jit(solution)/shard_map/ppermute | solution.py:412
  64.7 1.8 %collective-permute-start.17 = (bf16[24,1536]{1,0:T(8,128)(2,1)S(1)}, bf16[24,1536]{1,0:T(8,128)(2,1)S(1)}, u32[]{:S(2)}, u32[]{:S(2)}) collective-permute-start(bf16[24,1536]{1,0:T(8,128)(2,1)S(1)} %slice.149), channel_id=1, source_target_pairs={{0,192},{64,128},{128,64},{192,0},{1,193},{65,129},{129,65},{193,1... | collective-permute-start | bytes 221192 | tf_op jit(solution)/shard_map/ppermute | solution.py:412
  66.6 3.8 %collective-permute-done.17 = bf16[24,1536]{1,0:T(8,128)(2,1)S(1)} collective-permute-done((bf16[24,1536]{1,0:T(8,128)(2,1)S(1)}, bf16[24,1536]{1,0:T(8,128)(2,1)S(1)}, u32[]{:S(2)}, u32[]{:S(2)}) %collective-permute-start.17) | collective-permute-done | bytes 73760 | tf_op jit(solution)/shard_map/ppermute | solution.py:412
  70.5 13.7 %all_to_all.5.parts_ref = bf16[8,3,3072]{2,1,0:T(4,128)(2,1)S(1)} all-to-all(bf16[8,3,3072]{2,1,0:T(4,128)(2,1)S(1)} %reshape.55), channel_id=1, replica_groups=mesh['dp'=4,'gy'=8,'gx'=8] {'gx'}, dimensions={0} | all-to-all | bytes 294912 | tf_op jit(solution)/shard_map/all_to_all | solution.py:453
  84.2 0.6 finish.1
  (54 shorter events, 2.3 us)
Async XLA Ops:
  0.6 1.1 %copy-start.2 = (bf16[1,16,32,768]{3,2,1,0:T(8,128)(2,1)S(1)}, bf16[1,16,32,768]{3,2,1,0:T(8,128)(2,1)}, u32[]{:S(2)}) copy-start(bf16[1,16,32,768]{3,2,1,0:T(8,128)(2,1)} %param.5) | copy-start | bytes 2359300
  1.8 9.3 %copy-start.1 = (bf16[768,768]{1,0:T(8,128)(2,1)S(1)}, bf16[768,768]{1,0:T(8,128)(2,1)}, u32[]{:S(2)}) copy-start(bf16[768,768]{1,0:T(8,128)(2,1)} %wp_ref.1) | copy-start | bytes 3538948
  1.8 9.3 %copy-start.4 = (bf16[1,16,32,768]{3,2,1,0:T(8,128)(2,1)S(1)}, bf16[1,16,32,768]{3,2,1,0:T(8,128)(2,1)}, u32[]{:S(2)}) copy-start(bf16[1,16,32,768]{3,2,1,0:T(8,128)(2,1)} %param.6) | copy-start | bytes 2359300
  1.8 9.3 %copy-start.5 = (s32[1,16,32]{2,1,0:T(8,128)S(1)}, s32[1,16,32]{2,1,0:T(8,128)}, u32[]{:S(2)}) copy-start(s32[1,16,32]{2,1,0:T(8,128)} %param.7) | copy-start | bytes 6148
  1.8 13.2 %collective-permute-start = (bf16[8,24,768]{2,1,0:T(8,128)(2,1)S(1)}, bf16[8,24,768]{2,1,0:T(8,128)(2,1)S(1)}, u32[]{:S(2)}, u32[]{:S(2)}) collective-permute-start(bf16[8,24,768]{2,1,0:T(8,128)(2,1)S(1)} %above.1.after_ref), channel_id=1, source_target_pairs={{0,56},{8,0},{16,8},{24,16},{32,24},{40,32},{48,40},{56,48},{1,57}... | collective-permute-start | bytes 884744 | tf_op jit(solution)/shard_map/ppermute | solution.py:412
  4.3 8.8 %collective-permute-start.1 = (bf16[8,8,768]{2,1,0:T(8,128)(2,1)S(1)}, bf16[8,8,768]{2,1,0:T(8,128)(2,1)S(1)}, u32[]{:S(2)}, u32[]{:S(2)}) collective-permute-start(bf16[8,8,768]{2,1,0:T(8,128)(2,1)S(1)} %get-tuple-element.49), channel_id=1, source_target_pairs={{0,7},{1,0},{2,1},{3,2},{4,3},{5,4},{6,5},{7,6},{8,15},{9,8},{10,9... | collective-permute-start | bytes 294920 | tf_op jit(solution)/shard_map/ppermute | solution.py:412
  10.2 4.8 %collective-permute-start.2 = (bf16[8,8,768]{2,1,0:T(8,128)(2,1)S(1)}, bf16[8,8,768]{2,1,0:T(8,128)(2,1)S(1)}, u32[]{:S(2)}, u32[]{:S(2)}) collective-permute-start(bf16[8,8,768]{2,1,0:T(8,128)(2,1)S(1)} %get-tuple-element.50), channel_id=1, source_target_pairs={{0,63},{1,56},{2,57},{3,58},{4,59},{5,60},{6,61},{7,62},{8,7},{9,0... | collective-permute-start | bytes 294920 | tf_op jit(solution)/shard_map/ppermute | solution.py:470
  11.1 3.9 %copy-start = (bf16[768,2304]{1,0:T(8,128)(2,1)S(1)}, bf16[768,2304]{1,0:T(8,128)(2,1)}, u32[]{:S(2)}) copy-start(bf16[768,2304]{1,0:T(8,128)(2,1)} %wv_ref.3) | copy-start | bytes 10616836
  11.1 3.9 %copy-start.3 = (bf16[1,16,32,768]{3,2,1,0:T(8,128)(2,1)S(1)}, bf16[1,16,32,768]{3,2,1,0:T(8,128)(2,1)}, u32[]{:S(2)}) copy-start(bf16[1,16,32,768]{3,2,1,0:T(8,128)(2,1)} %param.5) | copy-start | bytes 2359300
  23.3 3.3 %collective-permute-start.3 = (bf16[384,1536]{1,0:T(8,128)(2,1)S(1)}, bf16[384,1536]{1,0:T(8,128)(2,1)S(1)}, u32[]{:S(2)}, u32[]{:S(2)}) collective-permute-start(bf16[384,1536]{1,0:T(8,128)(2,1)S(1)} %get-tuple-element.58), channel_id=1, source_target_pairs={{0,8},{8,0},{16,24},{24,16},{32,40},{40,32},{48,56},{56,48},{1,9},... | collective-permute-start | bytes 3538952 | tf_op jit(solution)/shard_map/ppermute | solution.py:412
  27.0 8.5 %collective-permute-start.6 = (bf16[384,768]{1,0:T(8,128)(2,1)S(1)}, bf16[384,768]{1,0:T(8,128)(2,1)S(1)}, u32[]{:S(2)}, u32[]{:S(2)}) collective-permute-start(bf16[384,768]{1,0:T(8,128)(2,1)S(1)} %get-tuple-element.65), channel_id=1, source_target_pairs={{0,8},{8,0},{16,24},{24,16},{32,40},{40,32},{48,56},{56,48},{1,9},... | collective-permute-start | bytes 1769480 | tf_op jit(solution)/shard_map/ppermute | solution.py:412
  27.6 6.0 %collective-permute-start.4 = (bf16[96,768]{1,0:T(8,128)(2,1)S(1)}, bf16[96,768]{1,0:T(8,128)(2,1)S(1)}, u32[]{:S(2)}, u32[]{:S(2)}) collective-permute-start(bf16[96,768]{1,0:T(8,128)(2,1)S(1)} %get-tuple-element.105), channel_id=1, source_target_pairs={{0,64},{64,0},{128,192},{192,128},{1,65},{65,1},{129,193},{193,129... | collective-permute-start | bytes 442376 | tf_op jit(solution)/shard_map/ppermute | solution.py:412
  28.7 6.8 %collective-permute-start.5 = (bf16[96,768]{1,0:T(8,128)(2,1)S(1)}, bf16[96,768]{1,0:T(8,128)(2,1)S(1)}, u32[]{:S(2)}, u32[]{:S(2)}) collective-permute-start(bf16[96,768]{1,0:T(8,128)(2,1)S(1)} %get-tuple-element.107), channel_id=1, source_target_pairs={{0,192},{64,128},{128,64},{192,0},{1,193},{65,129},{129,65},{193,1... | collective-permute-start | bytes 442376 | tf_op jit(solution)/shard_map/ppermute | solution.py:412
  35.5 2.1 %collective-permute-start.7 = (bf16[384,768]{1,0:T(8,128)(2,1)S(1)}, bf16[384,768]{1,0:T(8,128)(2,1)S(1)}, u32[]{:S(2)}, u32[]{:S(2)}) collective-permute-start(bf16[384,768]{1,0:T(8,128)(2,1)S(1)} %get-tuple-element.73), channel_id=1, source_target_pairs={{0,8},{8,0},{16,24},{24,16},{32,40},{40,32},{48,56},{56,48},{1,9},... | collective-permute-start | bytes 1769480 | tf_op jit(solution)/shard_map/ppermute | solution.py:412
  35.6 12.6 %collective-permute-start.11 = (bf16[96,1536]{1,0:T(8,128)(2,1)S(1)}, bf16[96,1536]{1,0:T(8,128)(2,1)S(1)}, u32[]{:S(2)}, u32[]{:S(2)}) collective-permute-start(bf16[96,1536]{1,0:T(8,128)(2,1)S(1)} %pad_maximum_fusion.1), channel_id=1, source_target_pairs={{0,192},{64,128},{128,64},{192,0},{1,193},{65,129},{129,65},{193,1... | collective-permute-start | bytes 884744 | tf_op jit(solution)/shard_map/ppermute | solution.py:412
  37.8 6.0 %collective-permute-start.8 = (bf16[96,768]{1,0:T(8,128)(2,1)S(1)}, bf16[96,768]{1,0:T(8,128)(2,1)S(1)}, u32[]{:S(2)}, u32[]{:S(2)}) collective-permute-start(bf16[96,768]{1,0:T(8,128)(2,1)S(1)} %get-tuple-element.101), channel_id=1, source_target_pairs={{0,16},{8,24},{16,0},{24,8},{32,48},{40,56},{48,32},{56,40},{1,17}... | collective-permute-start | bytes 442376 | tf_op jit(solution)/shard_map/ppermute | solution.py:412
  38.2 6.9 %collective-permute-start.9 = (bf16[96,768]{1,0:T(8,128)(2,1)S(1)}, bf16[96,768]{1,0:T(8,128)(2,1)S(1)}, u32[]{:S(2)}, u32[]{:S(2)}) collective-permute-start(bf16[96,768]{1,0:T(8,128)(2,1)S(1)} %get-tuple-element.99), channel_id=1, source_target_pairs={{0,48},{8,56},{16,32},{24,40},{32,16},{40,24},{48,0},{56,8},{1,49}... | collective-permute-start | bytes 442376 | tf_op jit(solution)/shard_map/ppermute | solution.py:412
  40.8 8.9 %collective-permute-start.10 = (bf16[96,1536]{1,0:T(8,128)(2,1)S(1)}, bf16[96,1536]{1,0:T(8,128)(2,1)S(1)}, u32[]{:S(2)}, u32[]{:S(2)}) collective-permute-start(bf16[96,1536]{1,0:T(8,128)(2,1)S(1)} %pad_maximum_fusion), channel_id=1, source_target_pairs={{0,64},{64,0},{128,192},{192,128},{1,65},{65,1},{129,193},{193,129... | collective-permute-start | bytes 884744 | tf_op jit(solution)/shard_map/ppermute | solution.py:412
  45.2 14.1 %collective-permute-start.14 = (bf16[96,1536]{1,0:T(8,128)(2,1)S(1)}, bf16[96,1536]{1,0:T(8,128)(2,1)S(1)}, u32[]{:S(2)}, u32[]{:S(2)}) collective-permute-start(bf16[96,1536]{1,0:T(8,128)(2,1)S(1)} %pad_maximum_fusion.3), channel_id=1, source_target_pairs={{0,48},{8,56},{16,32},{24,40},{32,16},{40,24},{48,0},{56,8},{1,49}... | collective-permute-start | bytes 884744 | tf_op jit(solution)/shard_map/ppermute | solution.py:412
  48.1 11.2 %collective-permute-start.13 = (bf16[96,1536]{1,0:T(8,128)(2,1)S(1)}, bf16[96,1536]{1,0:T(8,128)(2,1)S(1)}, u32[]{:S(2)}, u32[]{:S(2)}) collective-permute-start(bf16[96,1536]{1,0:T(8,128)(2,1)S(1)} %pad_maximum_fusion.2), channel_id=1, source_target_pairs={{0,16},{8,24},{16,0},{24,8},{32,48},{40,56},{48,32},{56,40},{1,17}... | collective-permute-start | bytes 884744 | tf_op jit(solution)/shard_map/ppermute | solution.py:412
  49.8 9.5 %collective-permute-start.12 = (bf16[48,1536]{1,0:T(8,128)(2,1)S(1)}, bf16[48,1536]{1,0:T(8,128)(2,1)S(1)}, u32[]{:S(2)}, u32[]{:S(2)}) collective-permute-start(bf16[48,1536]{1,0:T(8,128)(2,1)S(1)} %fusion.13), channel_id=1, source_target_pairs={{0,16},{8,24},{16,0},{24,8},{32,48},{40,56},{48,32},{56,40},{1,17}... | collective-permute-start | bytes 442376 | tf_op jit(solution)/shard_map/ppermute | solution.py:412
  59.5 5.2 %collective-permute-start.16 = (bf16[48,1536]{1,0:T(8,128)(2,1)S(1)}, bf16[48,1536]{1,0:T(8,128)(2,1)S(1)}, u32[]{:S(2)}, u32[]{:S(2)}) collective-permute-start(bf16[48,1536]{1,0:T(8,128)(2,1)S(1)} %pad_maximum_fusion.4), channel_id=1, source_target_pairs={{0,64},{64,0},{128,192},{192,128},{1,65},{65,1},{129,193},{193,129... | collective-permute-start | bytes 442376 | tf_op jit(solution)/shard_map/ppermute | solution.py:412
  59.6 6.9 %collective-permute-start.15 = (bf16[24,1536]{1,0:T(8,128)(2,1)S(1)}, bf16[24,1536]{1,0:T(8,128)(2,1)S(1)}, u32[]{:S(2)}, u32[]{:S(2)}) collective-permute-start(bf16[24,1536]{1,0:T(8,128)(2,1)S(1)} %slice.145), channel_id=1, source_target_pairs={{0,48},{8,56},{16,32},{24,40},{32,16},{40,24},{48,0},{56,8},{1,49}... | collective-permute-start | bytes 221192 | tf_op jit(solution)/shard_map/ppermute | solution.py:412
  64.7 5.7 %collective-permute-start.17 = (bf16[24,1536]{1,0:T(8,128)(2,1)S(1)}, bf16[24,1536]{1,0:T(8,128)(2,1)S(1)}, u32[]{:S(2)}, u32[]{:S(2)}) collective-permute-start(bf16[24,1536]{1,0:T(8,128)(2,1)S(1)} %slice.149), channel_id=1, source_target_pairs={{0,192},{64,128},{128,64},{192,0},{1,193},{65,129},{129,65},{193,1... | collective-permute-start | bytes 221192 | tf_op jit(solution)/shard_map/ppermute | solution.py:412

commit v9 on v8

--- a/solution.py
+++ b/solution.py
@@ -236,8 +236,18 @@
     )
 
 
-def last_kernel(*refs):
-    heads_group(*refs, True)
+def last_kernel(
+    hid_ref, hid_t_ref, tis_ref, live_ref, wq_ref, wk_ref, wv_ref, da_ref, att0_ref, db_ref,
+    keep_ref, send_ref, att_ref, dqkv_ref,
+):
+    heads_group(
+        hid_ref, hid_t_ref, tis_ref, live_ref, wq_ref, wk_ref, wv_ref, da_ref,
+        keep_ref.at[:, :D], send_ref.at[:, :D], att_ref, dqkv_ref, True,
+    )
+    attended = jnp.concatenate([att0_ref[...], att_ref[...]], 2).reshape(2 * CELLS, D)
+    att_t = nt(row_order(), attended).astype(BF)
+    grad = nn(att_t, db_ref[...].reshape(2 * CELLS, D))
+    put(grad, keep_ref.at[:, D:], send_ref.at[:, D:], True)
 
 
 def columns(block, first):
@@ -280,35 +290,20 @@
     )(tiles, below, right, diag, tis, live, w_qkv, w_qkv, w_qkv, da)
 
 
-def last_heads(hid, hid_t, tis, live, w_qkv, da):
+def last_heads(hid, hid_t, tis, live, w_qkv, da, att0, db):
     inputs, outputs, shapes = heads_specs(2, 1)
+    half = jax.ShapeDtypeStruct((D // 2, 2 * D), BF)
+    rows = full((2, CELLS, D))
     return pl.pallas_call(
         last_kernel,
         grid=(1,),
-        in_specs=[full((2, CELLS, D)), full((D, 2 * CELLS))] + inputs,
-        out_specs=outputs,
-        out_shape=shapes,
+        in_specs=[rows, full((D, 2 * CELLS))] + inputs + [full((2, CELLS, 2 * GW)), rows],
+        out_specs=[full((D // 2, 2 * D))] * 2 + outputs[2:],
+        out_shape=[half, half] + shapes[2:],
         compiler_params=pltpu.CompilerParams(vmem_limit_bytes=VMEM),
         cost_estimate=cost(4e9, 6e6),
         name="last_heads",
-    )(hid, hid_t, tis, live, w_qkv, w_qkv, w_qkv, da)
-
-
-def proj_kernel(att0_ref, att1_ref, db_ref, keep_ref, send_ref):
-    attended = jnp.concatenate([att0_ref[...], att1_ref[...]], 2).reshape(2 * CELLS, D)
-    att_t = nt(row_order(), attended).astype(BF)
-    put(nn(att_t, db_ref[...].reshape(2 * CELLS, D)), keep_ref, send_ref, True)
-
-
-def proj_grad(att0, att1, db):
-    shape = jax.ShapeDtypeStruct((D // 2, D), BF)
-    return pl.pallas_call(
-        proj_kernel,
-        out_shape=[shape, shape],
-        compiler_params=pltpu.CompilerParams(vmem_limit_bytes=VMEM),
-        cost_estimate=cost(2e9, 4e6),
-        name="proj_grad",
-    )(att0, att1, db)
+    )(hid, hid_t, tis, live, w_qkv, w_qkv, w_qkv, da, att0, db)
 
 
 def out_kernel(xw_ref, tis_ref, att0_ref, att1_ref, wp_ref, out_ref):
@@ -483,32 +478,29 @@
         mine, below, right, diag, tis, live, w_qkv, da
     )
     came = send(send0, "gy", lambda i: i ^ 1)
-    keep1, send1, att1, dqkv1 = last_heads(hid, hid_t, tis, live, w_qkv, da)
-    came, send1, att1 = tie(came, send1, att1)
+    keep1, send1, att1, dqkv1 = last_heads(hid, hid_t, tis, live, w_qkv, da, att0, db)
+    came, send1 = tie(came, send1)
     first = add(keep0, came)
     low_a, high_a = blocks(first[:, :D]), blocks(first[:, D:])
-    low_a, high_a, att1 = tie(low_a, high_a, att1)
     came_a = ring_start(low_a, high_a, *along_x)
-    came = send(send1, "gy", lambda i: i ^ 1)
-    keep2, send2 = proj_grad(att0, att1, db)
-    came_a, came, send2, keep2 = tie(came_a, came, send2, keep2)
-    came_a = ring_pass(low_a, high_a, came_a, *along_x)
-    low_b = add(keep1, came)
-    high_b = add(keep2, send(send2, "gy", lambda i: i ^ 1))
-    low_b, high_b, att1 = tie(blocks(low_b), blocks(high_b), att1)
+    second = add(keep1, send(send1, "gy", lambda i: i ^ 1))
+    second, att1 = tie(second, att1)
+    low_b, high_b = blocks(second[:, :D]), blocks(second[:, D:])
     came_b = ring_start(low_b, high_b, *along_y)
     out = out_part(xw, tis, att0, att1, w_proj)
     came_b, out, xw, low_a, high_a = tie(came_b, out, xw, low_a, high_a)
     came_b = ring_pass(low_b, high_b, came_b, *along_y)
-    rows_a = ring_end(low_a, high_a, came_a)
-    came_a = halve_start(rows_a, "gy", 2)
+    came_a = ring_pass(low_a, high_a, came_a, *along_x)
     grad = grad_part(xw, cot, tis, dqkv0, dqkv1, w_qkv)
     came_a, came_b, grad = tie(came_a, came_b, grad)
+    rows_a = ring_end(low_a, high_a, came_a)
+    rows_b = ring_end(low_b, high_b, came_b)
+    came_a = halve_start(rows_a, "gy", 2)
+    came_b = halve_start(rows_b, "dp", 1)
+    came_a, came_b = tie(came_a, came_b)
     rows_a = halve_end(rows_a, came_a)
-    rows_b = ring_end(low_b, high_b, came_b)
+    rows_b = halve_end(rows_b, came_b)
     came_a = halve_start(rows_a, "gy", 6)
-    came_b = halve_start(rows_b, "dp", 1)
-    rows_b = halve_end(rows_b, came_b)
     came_b = halve_start(rows_b, "dp", 3)
     rows = jnp.concatenate([halve_end(rows_a, came_a), halve_end(rows_b, came_b)], 1)
     grad_qkv, grad_proj = finish(exchange(rows, ("gx",)))

time: 85 us -> 80.1 us (0.942)
  waiting for transfers between devices: 22.4 us -> 16.6 us
  starting transfers between devices: 23.1 us -> 24 us
    ppermute x17 -> x16, waiting for transfers between devices: 20.4 us -> 14.7 us  [send(): lax.ppermute(value, axis, [(i, move(i) % devices) for i in range(devices)])]
    ppermute x17 -> x16, starting transfers between devices: 22.3 us -> 23.1 us  [send(): lax.ppermute(value, axis, [(i, move(i) % devices) for i in range(devices)])]
    pallas_call x2 -> x1, Pallas kernels: 5.05 us -> 4.65 us  [last_heads(): pl.pallas_call(last_kernel, grid=(1,), in_specs=[rows, full((D, 2 * CELLS...]
  transfers between devices with their start and end apart: 18 -> 17, of which waited for: 11 -> 12; matrix products, arithmetic and copies ran while one was open for 1% -> 1% of each run, Pallas kernels for 16% -> 16%
where the time goes in v9:
time: 80.1 us; the launch traced here: 79.5 us
  starting transfers between devices  24 us (30%)
  Pallas kernels  21.8 us (27%)
  waiting for transfers between devices  16.6 us (21%)
  blocking collectives  13.7 us (17%)
  local copies, waits for them, and re-layouts  1.43 us (2%)
  other arithmetic  1.14 us (1%)
  between operations  0.89 us (1%)
    ppermute x16, starting transfers between devices, send(): lax.ppermute(value, axis, [(i, move(i) % devices) for i in range(devices)])  23.1 us
    ppermute x16, waiting for transfers between devices, send(): lax.ppermute(value, axis, [(i, move(i) % devices) for i in range(devices)])  14.7 us
    all_to_all x1, blocking collectives, exchange(): return lax.all_to_all(rows, axis, 0, 0, axis_index_groups=groups)  13.7 us
    pallas_call x1, Pallas kernels, first_heads(): pl.pallas_call(first_kernel, grid=(2,), in_specs=[full((16, 32, D)), full...  8.33 us
    pallas_call x1, Pallas kernels, grad_part(): pl.pallas_call(grad_kernel, grid=(GROUPS,), in_specs=[full((2, CELLS, D))...  5.04 us
    pallas_call x1, Pallas kernels, last_heads(): pl.pallas_call(last_kernel, grid=(1,), in_specs=[rows, full((D, 2 * CELLS...  4.65 us
    ppermute x1, waiting for transfers between devices, shards(): lax.ppermute(corner, ('gy', 'gx'), [(a * nx + b, (a - 1) % ny * nx + (b -...  1.94 us
    pallas_call x1, Pallas kernels, out_part(): pl.pallas_call(out_kernel, out_shape=jax.ShapeDtypeStruct((WIN, 2, WIN, D...  1.66 us
  transfers between devices with their start and end apart: 17, of which 12 were waited for; matrix products, arithmetic and copies ran while one was open for 1% of the time, Pallas kernels for 16%

profile of v9, /device:TPU:6, one launch (start us, length us, event | category | flops | bytes accessed | tf_op | source)
XLA Modules:
  0.0 79.5 jit_solution(13409696601118007029)
XLA Ops:
  0.6 1.1 %copy-done.2 = bf16[1,16,32,768]{3,2,1,0:T(8,128)(2,1)S(1)} copy-done((bf16[1,16,32,768]{3,2,1,0:T(8,128)(2,1)S(1)}, bf16[1,16,32,768]{3,2,1,0:T(8,128)(2,1)}, u32[]{:S(2)}) %copy-start.2) | copy-done | bytes 786456
  1.8 2.5 %collective-permute-start = (bf16[8,24,768]{2,1,0:T(8,128)(2,1)S(1)}, bf16[8,24,768]{2,1,0:T(8,128)(2,1)S(1)}, u32[]{:S(2)}, u32[]{:S(2)}) collective-permute-start(bf16[8,24,768]{2,1,0:T(8,128)(2,1)S(1)} %above.1.after_ref), channel_id=1, source_target_pairs={{0,56},{8,0},{16,8},{24,16},{32,24},{40,32},{48,40},{56,48},{1,57}... | collective-permute-start | bytes 884744 | tf_op jit(solution)/shard_map/ppermute | solution.py:407
  4.3 5.9 %collective-permute-start.1 = (bf16[8,8,768]{2,1,0:T(8,128)(2,1)S(1)}, bf16[8,8,768]{2,1,0:T(8,128)(2,1)S(1)}, u32[]{:S(2)}, u32[]{:S(2)}) collective-permute-start(bf16[8,8,768]{2,1,0:T(8,128)(2,1)S(1)} %get-tuple-element.40), channel_id=1, source_target_pairs={{0,7},{1,0},{2,1},{3,2},{4,3},{5,4},{6,5},{7,6},{8,15},{9,8},{10,9... | collective-permute-start | bytes 294920 | tf_op jit(solution)/shard_map/ppermute | solution.py:407
  10.2 0.8 %collective-permute-start.2 = (bf16[8,8,768]{2,1,0:T(8,128)(2,1)S(1)}, bf16[8,8,768]{2,1,0:T(8,128)(2,1)S(1)}, u32[]{:S(2)}, u32[]{:S(2)}) collective-permute-start(bf16[8,8,768]{2,1,0:T(8,128)(2,1)S(1)} %get-tuple-element.41), channel_id=1, source_target_pairs={{0,63},{1,56},{2,57},{3,58},{4,59},{5,60},{6,61},{7,62},{8,7},{9,0... | collective-permute-start | bytes 294920 | tf_op jit(solution)/shard_map/ppermute | solution.py:465
  11.1 1.5 %branch.1 = (bf16[2,256,768]{2,1,0:T(8,128)(2,1)S(1)}, bf16[2,256,768]{2,1,0:T(8,128)(2,1)S(1)}, bf16[2,256,128]{2,1,0:T(8,128)(2,1)S(1)}, bf16[2,256,128]{2,1,0:T(8,128)(2,1)S(1)}) custom-call(bf16[16,2,16,768]{3,2,1,0:T(8,128)(2,1)S(1)} %bitcast.26, s32[16,32]{1,0:T(8,128)S(1)} %bitcast.28, bf16[768,768]{1,0:T(8,128)(2,1)S(1)} %copy-done.1), custom_call_target="tpu_custom_call" | custom-call | flops 20000000000 | bytes 4000000 | tf_op jit(solution)/shard_map/branch/pallas_call | solution.py:112
  12.6 0.5 collective-permute-done.1.right_ref
  13.0 1.9 %collective-permute-done.2.diag_ref = bf16[8,8,768]{2,1,0:T(8,128)(2,1)S(1)} collective-permute-done((bf16[8,8,768]{2,1,0:T(8,128)(2,1)S(1)}, bf16[8,8,768]{2,1,0:T(8,128)(2,1)S(1)}, u32[]{:S(2)}, u32[]{:S(2)}) %collective-permute-start.2) | collective-permute-done | bytes 98336 | tf_op jit(solution)/shard_map/ppermute | solution.py:465
  15.0 8.3 %first_heads.1 = (bf16[384,1536]{1,0:T(8,128)(2,1)S(1)}, bf16[384,1536]{1,0:T(8,128)(2,1)S(1)}, bf16[2,256,512]{2,1,0:T(8,128)(2,1)S(1)}, bf16[2,2,256,768]{3,2,...) custom-call(bf16[16,32,768]{2,1,0:T(8,128)(2,1)S(1)} %bitcast.25, ...), custom_call_target="tpu_custom_call" | custom-call | flops 6000000000 | bytes 10000000 | tf_op jit(solution)/shard_map/first_heads/pallas_call | solution.py:281
  23.6 4.6 %last_heads.1 = (bf16[384,1536]{1,0:T(8,128)(2,1)S(1)}, bf16[384,1536]{1,0:T(8,128)(2,1)S(1)}, bf16[2,256,256]{2,1,0:T(8,128)(2,1)S(1)}, bf16[1,2,256,768]{3,2,1,0:T(8,128)(2,1)S(1)}) custom-call(bf16[2,256,768]{2,1,0:T(8,128)(2,1)S(1)} %get-tuple-element.45.hid_ref, bf16[768,512]{1,0:T(8,128)(2,1)S(1)} %get-tuple-element.46.hid_t_ref, ...), custom_call_target="tpu_custom_call" | custom-call | flops 4000000000 | bytes 6000000 | tf_op jit(solution)/shard_map/last_heads/pallas_call | solution.py:297
  28.3 0.6 collective-permute-start.4
  29.2 0.9 %collective-permute-start.9 = (bf16[96,768]{1,0:T(8,128)(2,1)S(1)}, bf16[96,768]{1,0:T(8,128)(2,1)S(1)}, u32[]{:S(2)}, u32[]{:S(2)}) collective-permute-start(bf16[96,768]{1,0:T(8,128)(2,1)S(1)} %get-tuple-element.84), channel_id=1, source_target_pairs={{0,64},{64,0},{128,192},{192,128},{1,65},{65,1},{129,193},{193,129... | collective-permute-start | bytes 442376 | tf_op jit(solution)/shard_map/ppermute | solution.py:407
  30.1 1.1 %collective-permute-start.7 = (bf16[96,768]{1,0:T(8,128)(2,1)S(1)}, bf16[96,768]{1,0:T(8,128)(2,1)S(1)}, u32[]{:S(2)}, u32[]{:S(2)}) collective-permute-start(bf16[96,768]{1,0:T(8,128)(2,1)S(1)} %get-tuple-element.85), channel_id=1, source_target_pairs={{0,192},{64,128},{128,64},{192,0},{1,193},{65,129},{129,65},{193,1... | collective-permute-start | bytes 442376 | tf_op jit(solution)/shard_map/ppermute | solution.py:407
  31.7 2.8 %collective-permute-start.6 = (bf16[96,768]{1,0:T(8,128)(2,1)S(1)}, bf16[96,768]{1,0:T(8,128)(2,1)S(1)}, u32[]{:S(2)}, u32[]{:S(2)}) collective-permute-start(bf16[96,768]{1,0:T(8,128)(2,1)S(1)} %get-tuple-element.82), channel_id=1, source_target_pairs={{0,48},{8,56},{16,32},{24,40},{32,16},{40,24},{48,0},{56,8},{1,49}... | collective-permute-start | bytes 442376 | tf_op jit(solution)/shard_map/ppermute | solution.py:407
  34.5 1.7 %out_part.1 = bf16[16,2,16,768]{3,2,1,0:T(8,128)(2,1)} custom-call(bf16[2,256,768]{2,1,0:T(8,128)(2,1)S(1)} %get-tuple-element.64.xw_ref, bf16[2,256,128]{2,1,0:T(8,128)(2,1)S(1)} %get-tuple-element.42.tis_ref, bf16[2,256,512]{2,1,0:T(8,128)(2,1)S(1)} %get-tuple-element.47.att0_ref, bf16[2,256,256]{2,1,0:T(8,128)(2,1)S(1)} %get-tuple-element.56.att1_ref, ...), custom_call_target="tpu_custom_call" | custom-call | flops 1000 | bytes 1000 | tf_op jit(solution)/shard_map/out_part/pallas_call | solution.py:318
  36.2 2.9 %collective-permute-done.6 = bf16[96,768]{1,0:T(8,128)(2,1)S(1)} collective-permute-done((bf16[96,768]{1,0:T(8,128)(2,1)S(1)}, bf16[96,768]{1,0:T(8,128)(2,1)S(1)}, u32[]{:S(2)}, u32[]{:S(2)}) %collective-permute-start.6) | collective-permute-done | bytes 147488 | tf_op jit(solution)/shard_map/ppermute | solution.py:407
  39.1 0.9 %collective-permute-done.5 = bf16[96,768]{1,0:T(8,128)(2,1)S(1)} collective-permute-done((bf16[96,768]{1,0:T(8,128)(2,1)S(1)}, bf16[96,768]{1,0:T(8,128)(2,1)S(1)}, u32[]{:S(2)}, u32[]{:S(2)}) %collective-permute-start.5) | collective-permute-done | bytes 147488 | tf_op jit(solution)/shard_map/ppermute | solution.py:407
  40.1 0.4 collective-permute-start.11
  40.5 1.3 %collective-permute-start.12 = (bf16[96,1536]{1,0:T(8,128)(2,1)S(1)}, bf16[96,1536]{1,0:T(8,128)(2,1)S(1)}, u32[]{:S(2)}, u32[]{:S(2)}) collective-permute-start(bf16[96,1536]{1,0:T(8,128)(2,1)S(1)} %pad_maximum_fusion.3), channel_id=1, source_target_pairs={{0,48},{8,56},{16,32},{24,40},{32,16},{40,24},{48,0},{56,8},{1,49}... | collective-permute-start | bytes 884744 | tf_op jit(solution)/shard_map/ppermute | solution.py:407
  41.9 1.5 %collective-permute-start.10 = (bf16[96,1536]{1,0:T(8,128)(2,1)S(1)}, bf16[96,1536]{1,0:T(8,128)(2,1)S(1)}, u32[]{:S(2)}, u32[]{:S(2)}) collective-permute-start(bf16[96,1536]{1,0:T(8,128)(2,1)S(1)} %pad_maximum_fusion.1), channel_id=1, source_target_pairs={{0,192},{64,128},{128,64},{192,0},{1,193},{65,129},{129,65},{193,1... | collective-permute-start | bytes 884744 | tf_op jit(solution)/shard_map/ppermute | solution.py:407
  43.9 5.0 %grad_part.1 = bf16[16,2,16,768]{3,2,1,0:T(8,128)(2,1)} custom-call(bf16[2,256,768]{2,1,0:T(8,128)(2,1)S(1)} %get-tuple-element.64.xw_ref, bf16[16,2,16,768]{3,2,1,0:T(8,128)(2,1)S(1)} %bitcast.27, bf16[2,256,128]{2,1,0:T(8,128)(2,1)S(1)} %get-tuple-element.42.tis_ref, bf16[2,2,256,768]{3,2,1,0:T(8,128)(2,1)S(1)} %get-tuple-element.65.dqkv0_ref, ...), custom_call_target="tpu_custom_call" | custom-call | flops 1000 | bytes 1000 | tf_op jit(solution)/shard_map/grad_part/pallas_call | solution.py:361
  48.9 0.8 %collective-permute-done.12 = bf16[96,1536]{1,0:T(8,128)(2,1)S(1)} collective-permute-done((bf16[96,1536]{1,0:T(8,128)(2,1)S(1)}, bf16[96,1536]{1,0:T(8,128)(2,1)S(1)}, u32[]{:S(2)}, u32[]{:S(2)}) %collective-permute-start.12) | collective-permute-done | bytes 294944 | tf_op jit(solution)/shard_map/ppermute | solution.py:407
  49.8 1.4 %collective-permute-done.10 = bf16[96,1536]{1,0:T(8,128)(2,1)S(1)} collective-permute-done((bf16[96,1536]{1,0:T(8,128)(2,1)S(1)}, bf16[96,1536]{1,0:T(8,128)(2,1)S(1)}, u32[]{:S(2)}, u32[]{:S(2)}) %collective-permute-start.10) | collective-permute-done | bytes 294944 | tf_op jit(solution)/shard_map/ppermute | solution.py:407
  51.4 0.4 collective-permute-start.14
  51.9 1.2 %collective-permute-start.13 = (bf16[48,1536]{1,0:T(8,128)(2,1)S(1)}, bf16[48,1536]{1,0:T(8,128)(2,1)S(1)}, u32[]{:S(2)}, u32[]{:S(2)}) collective-permute-start(bf16[48,1536]{1,0:T(8,128)(2,1)S(1)} %pad_maximum_fusion.5), channel_id=1, source_target_pairs={{0,16},{8,24},{16,0},{24,8},{32,48},{40,56},{48,32},{56,40},{1,17}... | collective-permute-start | bytes 442376 | tf_op jit(solution)/shard_map/ppermute | solution.py:407
  53.1 3.5 %collective-permute-done.14 = bf16[48,1536]{1,0:T(8,128)(2,1)S(1)} collective-permute-done((bf16[48,1536]{1,0:T(8,128)(2,1)S(1)}, bf16[48,1536]{1,0:T(8,128)(2,1)S(1)}, u32[]{:S(2)}, u32[]{:S(2)}) %collective-permute-start.14) | collective-permute-done | bytes 147488 | tf_op jit(solution)/shard_map/ppermute | solution.py:407
  56.6 0.5 collective-permute-done.13
  57.2 2.1 %collective-permute-start.16 = (bf16[24,1536]{1,0:T(8,128)(2,1)S(1)}, bf16[24,1536]{1,0:T(8,128)(2,1)S(1)}, u32[]{:S(2)}, u32[]{:S(2)}) collective-permute-start(bf16[24,1536]{1,0:T(8,128)(2,1)S(1)} %slice.169), channel_id=1, source_target_pairs={{0,192},{64,128},{128,64},{192,0},{1,193},{65,129},{129,65},{193,1... | collective-permute-start | bytes 221192 | tf_op jit(solution)/shard_map/ppermute | solution.py:407
  59.4 1.8 %collective-permute-start.15 = (bf16[24,1536]{1,0:T(8,128)(2,1)S(1)}, bf16[24,1536]{1,0:T(8,128)(2,1)S(1)}, u32[]{:S(2)}, u32[]{:S(2)}) collective-permute-start(bf16[24,1536]{1,0:T(8,128)(2,1)S(1)} %slice.167), channel_id=1, source_target_pairs={{0,48},{8,56},{16,32},{24,40},{32,16},{40,24},{48,0},{56,8},{1,49}... | collective-permute-start | bytes 221192 | tf_op jit(solution)/shard_map/ppermute | solution.py:407
  61.2 1.6 %collective-permute-done.16 = bf16[24,1536]{1,0:T(8,128)(2,1)S(1)} collective-permute-done((bf16[24,1536]{1,0:T(8,128)(2,1)S(1)}, bf16[24,1536]{1,0:T(8,128)(2,1)S(1)}, u32[]{:S(2)}, u32[]{:S(2)}) %collective-permute-start.16) | collective-permute-done | bytes 73760 | tf_op jit(solution)/shard_map/ppermute | solution.py:407
  62.9 2.2 %collective-permute-done.15 = bf16[24,1536]{1,0:T(8,128)(2,1)S(1)} collective-permute-done((bf16[24,1536]{1,0:T(8,128)(2,1)S(1)}, bf16[24,1536]{1,0:T(8,128)(2,1)S(1)}, u32[]{:S(2)}, u32[]{:S(2)}) %collective-permute-start.15) | collective-permute-done | bytes 73760 | tf_op jit(solution)/shard_map/ppermute | solution.py:407
  65.2 13.7 %all_to_all.5.parts_ref = bf16[8,3,3072]{2,1,0:T(4,128)(2,1)S(1)} all-to-all(bf16[8,3,3072]{2,1,0:T(4,128)(2,1)S(1)} %reshape.61), channel_id=1, replica_groups=mesh['dp'=4,'gy'=8,'gx'=8] {'gx'}, dimensions={0} | all-to-all | bytes 294912 | tf_op jit(solution)/shard_map/all_to_all | solution.py:448
  78.9 0.6 finish.1
  (49 shorter events, 2.3 us)
Async XLA Ops:
  0.6 1.1 %copy-start.2 = (bf16[1,16,32,768]{3,2,1,0:T(8,128)(2,1)S(1)}, bf16[1,16,32,768]{3,2,1,0:T(8,128)(2,1)}, u32[]{:S(2)}) copy-start(bf16[1,16,32,768]{3,2,1,0:T(8,128)(2,1)} %param.5) | copy-start | bytes 2359300
  1.8 9.3 %copy-start.1 = (bf16[768,768]{1,0:T(8,128)(2,1)S(1)}, bf16[768,768]{1,0:T(8,128)(2,1)}, u32[]{:S(2)}) copy-start(bf16[768,768]{1,0:T(8,128)(2,1)} %wp_ref.1) | copy-start | bytes 3538948
  1.8 9.3 %copy-start.4 = (bf16[1,16,32,768]{3,2,1,0:T(8,128)(2,1)S(1)}, bf16[1,16,32,768]{3,2,1,0:T(8,128)(2,1)}, u32[]{:S(2)}) copy-start(bf16[1,16,32,768]{3,2,1,0:T(8,128)(2,1)} %param.6) | copy-start | bytes 2359300
  1.8 9.3 %copy-start.5 = (s32[1,16,32]{2,1,0:T(8,128)S(1)}, s32[1,16,32]{2,1,0:T(8,128)}, u32[]{:S(2)}) copy-start(s32[1,16,32]{2,1,0:T(8,128)} %param.7) | copy-start | bytes 6148
  1.8 13.2 %collective-permute-start = (bf16[8,24,768]{2,1,0:T(8,128)(2,1)S(1)}, bf16[8,24,768]{2,1,0:T(8,128)(2,1)S(1)}, u32[]{:S(2)}, u32[]{:S(2)}) collective-permute-start(bf16[8,24,768]{2,1,0:T(8,128)(2,1)S(1)} %above.1.after_ref), channel_id=1, source_target_pairs={{0,56},{8,0},{16,8},{24,16},{32,24},{40,32},{48,40},{56,48},{1,57}... | collective-permute-start | bytes 884744 | tf_op jit(solution)/shard_map/ppermute | solution.py:407
  4.3 8.8 %collective-permute-start.1 = (bf16[8,8,768]{2,1,0:T(8,128)(2,1)S(1)}, bf16[8,8,768]{2,1,0:T(8,128)(2,1)S(1)}, u32[]{:S(2)}, u32[]{:S(2)}) collective-permute-start(bf16[8,8,768]{2,1,0:T(8,128)(2,1)S(1)} %get-tuple-element.40), channel_id=1, source_target_pairs={{0,7},{1,0},{2,1},{3,2},{4,3},{5,4},{6,5},{7,6},{8,15},{9,8},{10,9... | collective-permute-start | bytes 294920 | tf_op jit(solution)/shard_map/ppermute | solution.py:407
  10.2 4.8 %collective-permute-start.2 = (bf16[8,8,768]{2,1,0:T(8,128)(2,1)S(1)}, bf16[8,8,768]{2,1,0:T(8,128)(2,1)S(1)}, u32[]{:S(2)}, u32[]{:S(2)}) collective-permute-start(bf16[8,8,768]{2,1,0:T(8,128)(2,1)S(1)} %get-tuple-element.41), channel_id=1, source_target_pairs={{0,63},{1,56},{2,57},{3,58},{4,59},{5,60},{6,61},{7,62},{8,7},{9,0... | collective-permute-start | bytes 294920 | tf_op jit(solution)/shard_map/ppermute | solution.py:465
  11.1 3.9 %copy-start = (bf16[768,2304]{1,0:T(8,128)(2,1)S(1)}, bf16[768,2304]{1,0:T(8,128)(2,1)}, u32[]{:S(2)}) copy-start(bf16[768,2304]{1,0:T(8,128)(2,1)} %wv_ref.5) | copy-start | bytes 10616836
  11.1 3.9 %copy-start.3 = (bf16[1,16,32,768]{3,2,1,0:T(8,128)(2,1)S(1)}, bf16[1,16,32,768]{3,2,1,0:T(8,128)(2,1)}, u32[]{:S(2)}) copy-start(bf16[1,16,32,768]{3,2,1,0:T(8,128)(2,1)} %param.5) | copy-start | bytes 2359300
  23.3 4.9 %collective-permute-start.3 = (bf16[384,1536]{1,0:T(8,128)(2,1)S(1)}, bf16[384,1536]{1,0:T(8,128)(2,1)S(1)}, u32[]{:S(2)}, u32[]{:S(2)}) collective-permute-start(bf16[384,1536]{1,0:T(8,128)(2,1)S(1)} %get-tuple-element.50), channel_id=1, source_target_pairs={{0,8},{8,0},{16,24},{24,16},{32,40},{40,32},{48,56},{56,48},{1,9},... | collective-permute-start | bytes 3538952 | tf_op jit(solution)/shard_map/ppermute | solution.py:407
  28.3 3.1 %collective-permute-start.4 = (bf16[384,1536]{1,0:T(8,128)(2,1)S(1)}, bf16[384,1536]{1,0:T(8,128)(2,1)S(1)}, u32[]{:S(2)}, u32[]{:S(2)}) collective-permute-start(bf16[384,1536]{1,0:T(8,128)(2,1)S(1)} %get-tuple-element.52), channel_id=1, source_target_pairs={{0,8},{8,0},{16,24},{24,16},{32,40},{40,32},{48,56},{56,48},{1,9},... | collective-permute-start | bytes 3538952 | tf_op jit(solution)/shard_map/ppermute | solution.py:407
  29.2 12.7 %collective-permute-start.9 = (bf16[96,768]{1,0:T(8,128)(2,1)S(1)}, bf16[96,768]{1,0:T(8,128)(2,1)S(1)}, u32[]{:S(2)}, u32[]{:S(2)}) collective-permute-start(bf16[96,768]{1,0:T(8,128)(2,1)S(1)} %get-tuple-element.84), channel_id=1, source_target_pairs={{0,64},{64,0},{128,192},{192,128},{1,65},{65,1},{129,193},{193,129... | collective-permute-start | bytes 442376 | tf_op jit(solution)/shard_map/ppermute | solution.py:407
  30.1 13.4 %collective-permute-start.7 = (bf16[96,768]{1,0:T(8,128)(2,1)S(1)}, bf16[96,768]{1,0:T(8,128)(2,1)S(1)}, u32[]{:S(2)}, u32[]{:S(2)}) collective-permute-start(bf16[96,768]{1,0:T(8,128)(2,1)S(1)} %get-tuple-element.85), channel_id=1, source_target_pairs={{0,192},{64,128},{128,64},{192,0},{1,193},{65,129},{129,65},{193,1... | collective-permute-start | bytes 442376 | tf_op jit(solution)/shard_map/ppermute | solution.py:407
  31.7 7.4 %collective-permute-start.6 = (bf16[96,768]{1,0:T(8,128)(2,1)S(1)}, bf16[96,768]{1,0:T(8,128)(2,1)S(1)}, u32[]{:S(2)}, u32[]{:S(2)}) collective-permute-start(bf16[96,768]{1,0:T(8,128)(2,1)S(1)} %get-tuple-element.82), channel_id=1, source_target_pairs={{0,48},{8,56},{16,32},{24,40},{32,16},{40,24},{48,0},{56,8},{1,49}... | collective-permute-start | bytes 442376 | tf_op jit(solution)/shard_map/ppermute | solution.py:407
  34.4 5.6 %collective-permute-start.5 = (bf16[96,768]{1,0:T(8,128)(2,1)S(1)}, bf16[96,768]{1,0:T(8,128)(2,1)S(1)}, u32[]{:S(2)}, u32[]{:S(2)}) collective-permute-start(bf16[96,768]{1,0:T(8,128)(2,1)S(1)} %get-tuple-element.83), channel_id=1, source_target_pairs={{0,16},{8,24},{16,0},{24,8},{32,48},{40,56},{48,32},{56,40},{1,17}... | collective-permute-start | bytes 442376 | tf_op jit(solution)/shard_map/ppermute | solution.py:407
  40.1 8.8 %collective-permute-start.11 = (bf16[96,1536]{1,0:T(8,128)(2,1)S(1)}, bf16[96,1536]{1,0:T(8,128)(2,1)S(1)}, u32[]{:S(2)}, u32[]{:S(2)}) collective-permute-start(bf16[96,1536]{1,0:T(8,128)(2,1)S(1)} %pad_maximum_fusion.2), channel_id=1, source_target_pairs={{0,16},{8,24},{16,0},{24,8},{32,48},{40,56},{48,32},{56,40},{1,17}... | collective-permute-start | bytes 884744 | tf_op jit(solution)/shard_map/ppermute | solution.py:407
  40.5 9.2 %collective-permute-start.12 = (bf16[96,1536]{1,0:T(8,128)(2,1)S(1)}, bf16[96,1536]{1,0:T(8,128)(2,1)S(1)}, u32[]{:S(2)}, u32[]{:S(2)}) collective-permute-start(bf16[96,1536]{1,0:T(8,128)(2,1)S(1)} %pad_maximum_fusion.3), channel_id=1, source_target_pairs={{0,48},{8,56},{16,32},{24,40},{32,16},{40,24},{48,0},{56,8},{1,49}... | collective-permute-start | bytes 884744 | tf_op jit(solution)/shard_map/ppermute | solution.py:407
  41.9 9.2 %collective-permute-start.10 = (bf16[96,1536]{1,0:T(8,128)(2,1)S(1)}, bf16[96,1536]{1,0:T(8,128)(2,1)S(1)}, u32[]{:S(2)}, u32[]{:S(2)}) collective-permute-start(bf16[96,1536]{1,0:T(8,128)(2,1)S(1)} %pad_maximum_fusion.1), channel_id=1, source_target_pairs={{0,192},{64,128},{128,64},{192,0},{1,193},{65,129},{129,65},{193,1... | collective-permute-start | bytes 884744 | tf_op jit(solution)/shard_map/ppermute | solution.py:407
  43.6 7.7 %collective-permute-start.8 = (bf16[96,1536]{1,0:T(8,128)(2,1)S(1)}, bf16[96,1536]{1,0:T(8,128)(2,1)S(1)}, u32[]{:S(2)}, u32[]{:S(2)}) collective-permute-start(bf16[96,1536]{1,0:T(8,128)(2,1)S(1)} %pad_maximum_fusion), channel_id=1, source_target_pairs={{0,64},{64,0},{128,192},{192,128},{1,65},{65,1},{129,193},{193,129... | collective-permute-start | bytes 884744 | tf_op jit(solution)/shard_map/ppermute | solution.py:407
  51.4 5.2 %collective-permute-start.14 = (bf16[48,1536]{1,0:T(8,128)(2,1)S(1)}, bf16[48,1536]{1,0:T(8,128)(2,1)S(1)}, u32[]{:S(2)}, u32[]{:S(2)}) collective-permute-start(bf16[48,1536]{1,0:T(8,128)(2,1)S(1)} %fusion.6), channel_id=1, source_target_pairs={{0,64},{64,0},{128,192},{192,128},{1,65},{65,1},{129,193},{193,129... | collective-permute-start | bytes 442376 | tf_op jit(solution)/shard_map/ppermute | solution.py:407
  51.9 5.2 %collective-permute-start.13 = (bf16[48,1536]{1,0:T(8,128)(2,1)S(1)}, bf16[48,1536]{1,0:T(8,128)(2,1)S(1)}, u32[]{:S(2)}, u32[]{:S(2)}) collective-permute-start(bf16[48,1536]{1,0:T(8,128)(2,1)S(1)} %pad_maximum_fusion.5), channel_id=1, source_target_pairs={{0,16},{8,24},{16,0},{24,8},{32,48},{40,56},{48,32},{56,40},{1,17}... | collective-permute-start | bytes 442376 | tf_op jit(solution)/shard_map/ppermute | solution.py:407
  57.2 5.7 %collective-permute-start.16 = (bf16[24,1536]{1,0:T(8,128)(2,1)S(1)}, bf16[24,1536]{1,0:T(8,128)(2,1)S(1)}, u32[]{:S(2)}, u32[]{:S(2)}) collective-permute-start(bf16[24,1536]{1,0:T(8,128)(2,1)S(1)} %slice.169), channel_id=1, source_target_pairs={{0,192},{64,128},{128,64},{192,0},{1,193},{65,129},{129,65},{193,1... | collective-permute-start | bytes 221192 | tf_op jit(solution)/shard_map/ppermute | solution.py:407
  59.4 5.7 %collective-permute-start.15 = (bf16[24,1536]{1,0:T(8,128)(2,1)S(1)}, bf16[24,1536]{1,0:T(8,128)(2,1)S(1)}, u32[]{:S(2)}, u32[]{:S(2)}) collective-permute-start(bf16[24,1536]{1,0:T(8,128)(2,1)S(1)} %slice.167), channel_id=1, source_target_pairs={{0,48},{8,56},{16,32},{24,40},{32,16},{40,24},{48,0},{56,8},{1,49}... | collective-permute-start | bytes 221192 | tf_op jit(solution)/shard_map/ppermute | solution.py:407

commit v10 on v9

--- a/solution.py
+++ b/solution.py
@@ -16,6 +16,7 @@
 GW = D // GROUPS
 HEAD_SCALE = 0.125
 VMEM = 32 * 1024 * 1024
+EDGE_VMEM = 60 * 1024 * 1024
 
 
 def nn(a, b):
@@ -56,7 +57,7 @@
         in_specs=[pl.BlockSpec((8, 32, D), lambda g: (0, 0, 0))],
         out_specs=full((8, 24, D)),
         out_shape=jax.ShapeDtypeStruct((8, 24, D), BF),
-        compiler_params=pltpu.CompilerParams(vmem_limit_bytes=VMEM),
+        compiler_params=pltpu.CompilerParams(vmem_limit_bytes=EDGE_VMEM),
         cost_estimate=cost(3e10, 1e6),
         name="above",
     )(tiles)
@@ -69,7 +70,7 @@
         ],
         out_specs=[full((8, 8, D))] * 2,
         out_shape=[small, small],
-        compiler_params=pltpu.CompilerParams(vmem_limit_bytes=VMEM),
+        compiler_params=pltpu.CompilerParams(vmem_limit_bytes=EDGE_VMEM),
         cost_estimate=cost(1e3, 1e3),
         name="left",
     )(tiles, above)
@@ -434,12 +435,17 @@
     return jnp.concatenate([low, high], 1)
 
 
-def halve_start(rows, axis, flip):
-    return send(rows[rows.shape[0] // 2 :], axis, lambda j: j ^ flip)
-
-
-def halve_end(rows, came):
-    return add(rows[: rows.shape[0] // 2], came)
+def direct_start(rows, axis, flips):
+    one, three = flips
+    part = blocks(rows)
+    return [
+        send(part[at], axis, lambda j, flip=flip: j ^ flip)
+        for at, flip in ((3, one ^ three), (1, three), (2, one))
+    ]
+
+
+def direct_end(rows, came):
+    return add(blocks(rows)[0], *came)
 
 
 def exchange(rows, axis, groups=None):
@@ -495,14 +501,9 @@
     came_a, came_b, grad = tie(came_a, came_b, grad)
     rows_a = ring_end(low_a, high_a, came_a)
     rows_b = ring_end(low_b, high_b, came_b)
-    came_a = halve_start(rows_a, "gy", 2)
-    came_b = halve_start(rows_b, "dp", 1)
-    came_a, came_b = tie(came_a, came_b)
-    rows_a = halve_end(rows_a, came_a)
-    rows_b = halve_end(rows_b, came_b)
-    came_a = halve_start(rows_a, "gy", 6)
-    came_b = halve_start(rows_b, "dp", 3)
-    rows = jnp.concatenate([halve_end(rows_a, came_a), halve_end(rows_b, came_b)], 1)
+    came_a = direct_start(rows_a, *along_y)
+    came_b = direct_start(rows_b, *along_x)
+    rows = jnp.concatenate([direct_end(rows_a, came_a), direct_end(rows_b, came_b)], 1)
     grad_qkv, grad_proj = finish(exchange(rows, ("gx",)))
     return out, grad, grad_qkv, grad_proj
 

time: 80.1 us -> 81.7 us (1.020)
  Pallas kernels: 21.8 us -> 25.4 us
  waiting for transfers between devices: 16.6 us -> 13.3 us
  starting transfers between devices: 24 us -> 26.7 us
  local copies, waits for them, and re-layouts: 1.43 us -> 0.28 us
    ppermute x16 -> x18, waiting for transfers between devices: 14.7 us -> 11.4 us  [send(): lax.ppermute(value, axis, [(i, move(i) % devices) for i in range(devices)])]
    ppermute x16 -> x18, starting transfers between devices: 23.1 us -> 25.9 us  [send(): lax.ppermute(value, axis, [(i, move(i) % devices) for i in range(devices)])]
    pallas_call x1, Pallas kernels: 0.02 us -> 1.87 us  [edges(): pl.pallas_call(above_kernel, grid=(1,), in_specs=[pl.BlockSpec((8, 32, D)...]
    pallas_call x1, Pallas kernels: 0.01 us -> 1.68 us  [edges(): pl.pallas_call(left_kernel, grid=(1,), in_specs=[pl.BlockSpec((16, 16, D)...]
    unnamed x12 -> x10, local copies, waits for them, and re-layouts: 1.15 us -> 0.02 us
  transfers between devices with their start and end apart: 17 -> 19, of which waited for: 12 -> 11; matrix products, arithmetic and copies ran while one was open for 1% -> 1% of each run, Pallas kernels for 16% -> 18%
where the time goes in v10:
time: 81.7 us; the launch traced here: 81.3 us
  starting transfers between devices  26.7 us (33%)
  Pallas kernels  25.4 us (31%)
  blocking collectives  13.7 us (17%)
  waiting for transfers between devices  13.3 us (16%)
  other arithmetic  1.12 us (1%)
  between operations  0.87 us (1%)
    ppermute x18, starting transfers between devices, send(): lax.ppermute(value, axis, [(i, move(i) % devices) for i in range(devices)])  25.9 us
    all_to_all x1, blocking collectives, exchange(): return lax.all_to_all(rows, axis, 0, 0, axis_index_groups=groups)  13.7 us
    ppermute x18, waiting for transfers between devices, send(): lax.ppermute(value, axis, [(i, move(i) % devices) for i in range(devices)])  11.4 us
    pallas_call x1, Pallas kernels, first_heads(): pl.pallas_call(first_kernel, grid=(2,), in_specs=[full((16, 32, D)), full...  8.32 us
    pallas_call x1, Pallas kernels, grad_part(): pl.pallas_call(grad_kernel, grid=(GROUPS,), in_specs=[full((2, CELLS, D))...  5.04 us
    pallas_call x1, Pallas kernels, last_heads(): pl.pallas_call(last_kernel, grid=(1,), in_specs=[rows, full((D, 2 * CELLS...  4.65 us
    pallas_call x1, Pallas kernels, edges(): pl.pallas_call(above_kernel, grid=(1,), in_specs=[pl.BlockSpec((8, 32, D)...  1.87 us
    ppermute x1, waiting for transfers between devices, shards(): lax.ppermute(corner, ('gy', 'gx'), [(a * nx + b, (a - 1) % ny * nx + (b -...  1.83 us
  transfers between devices with their start and end apart: 19, of which 11 were waited for; matrix products, arithmetic and copies ran while one was open for 1% of the time, Pallas kernels for 18%

profile of v10, /device:TPU:6, one launch (start us, length us, event | category | flops | bytes accessed | tf_op | source)
XLA Modules:
  0.0 81.3 jit_solution(17856065452597725460)
XLA Ops:
  0.7 1.9 %above.1.after_ref = bf16[8,24,768]{2,1,0:T(8,128)(2,1)} custom-call(bf16[16,32,768]{2,1,0:T(8,128)(2,1)} %bitcast.23), custom_call_target="tpu_custom_call" | custom-call | flops 30000001024 | bytes 1000000 | tf_op jit(solution)/shard_map/above/pallas_call | solution.py:54
  2.5 2.5 %collective-permute-start = (bf16[8,24,768]{2,1,0:T(8,128)(2,1)}, bf16[8,24,768]{2,1,0:T(8,128)(2,1)S(1)}, u32[]{:S(2)}, u32[]{:S(2)}) collective-permute-start(bf16[8,24,768]{2,1,0:T(8,128)(2,1)} %above.1.after_ref), channel_id=1, source_target_pairs={{0,56},{8,0},{16,8},{24,16},{32,24},{40,32},{48,40},{56,48},{1,57}... | collective-permute-start | bytes 884744 | tf_op jit(solution)/shard_map/ppermute | solution.py:408
  5.0 1.7 %left.1 = (bf16[8,8,768]{2,1,0:T(8,128)(2,1)}, bf16[8,8,768]{2,1,0:T(8,128)(2,1)}) custom-call(bf16[16,32,768]{2,1,0:T(8,128)(2,1)} %bitcast.24, bf16[8,24,768]{2,1,0:T(8,128)(2,1)} %above.1.after_ref), custom_call_target="tpu_custom_call" | custom-call | flops 1000 | bytes 1000 | tf_op jit(solution)/shard_map/left/pallas_call | solution.py:64
  6.7 5.9 %collective-permute-start.1 = (bf16[8,8,768]{2,1,0:T(8,128)(2,1)}, bf16[8,8,768]{2,1,0:T(8,128)(2,1)S(1)}, u32[]{:S(2)}, u32[]{:S(2)}) collective-permute-start(bf16[8,8,768]{2,1,0:T(8,128)(2,1)} %get-tuple-element.38), channel_id=1, source_target_pairs={{0,7},{1,0},{2,1},{3,2},{4,3},{5,4},{6,5},{7,6},{8,15},{9,8},{10,9... | collective-permute-start | bytes 294920 | tf_op jit(solution)/shard_map/ppermute | solution.py:408
  12.5 0.8 %collective-permute-start.2 = (bf16[8,8,768]{2,1,0:T(8,128)(2,1)}, bf16[8,8,768]{2,1,0:T(8,128)(2,1)S(1)}, u32[]{:S(2)}, u32[]{:S(2)}) collective-permute-start(bf16[8,8,768]{2,1,0:T(8,128)(2,1)} %get-tuple-element.39), channel_id=1, source_target_pairs={{0,63},{1,56},{2,57},{3,58},{4,59},{5,60},{6,61},{7,62},{8,7},{9,0... | collective-permute-start | bytes 294920 | tf_op jit(solution)/shard_map/ppermute | solution.py:471
  13.4 1.5 %branch.1 = (bf16[2,256,768]{2,1,0:T(8,128)(2,1)S(1)}, bf16[2,256,768]{2,1,0:T(8,128)(2,1)S(1)}, bf16[2,256,128]{2,1,0:T(8,128)(2,1)S(1)}, bf16[2,256,128]{2,1,0:T(8,128)(2,1)S(1)}) custom-call(bf16[16,2,16,768]{3,2,1,0:T(8,128)(2,1)S(1)} %bitcast.26, s32[16,32]{1,0:T(8,128)S(1)} %bitcast.28, bf16[768,768]{1,0:T(8,128)(2,1)S(1)} %copy-done.1), custom_call_target="tpu_custom_call" | custom-call | flops 20000000000 | bytes 4000000 | tf_op jit(solution)/shard_map/branch/pallas_call | solution.py:113
  14.9 0.8 collective-permute-done.1.right_ref
  15.7 1.8 %collective-permute-done.2.diag_ref = bf16[8,8,768]{2,1,0:T(8,128)(2,1)S(1)} collective-permute-done((bf16[8,8,768]{2,1,0:T(8,128)(2,1)}, bf16[8,8,768]{2,1,0:T(8,128)(2,1)S(1)}, u32[]{:S(2)}, u32[]{:S(2)}) %collective-permute-start.2) | collective-permute-done | bytes 98336 | tf_op jit(solution)/shard_map/ppermute | solution.py:471
  17.5 8.3 %first_heads.1 = (bf16[384,1536]{1,0:T(8,128)(2,1)S(1)}, bf16[384,1536]{1,0:T(8,128)(2,1)S(1)}, bf16[2,256,512]{2,1,0:T(8,128)(2,1)S(1)}, bf16[2,2,256,768]{3,2,...) custom-call(bf16[16,32,768]{2,1,0:T(8,128)(2,1)S(1)} %bitcast.25, ...), custom_call_target="tpu_custom_call" | custom-call | flops 6000000000 | bytes 10000000 | tf_op jit(solution)/shard_map/first_heads/pallas_call | solution.py:282
  26.1 4.6 %last_heads.1 = (bf16[384,1536]{1,0:T(8,128)(2,1)S(1)}, bf16[384,1536]{1,0:T(8,128)(2,1)S(1)}, bf16[2,256,256]{2,1,0:T(8,128)(2,1)S(1)}, bf16[1,2,256,768]{3,2,1,0:T(8,128)(2,1)S(1)}) custom-call(bf16[2,256,768]{2,1,0:T(8,128)(2,1)S(1)} %get-tuple-element.43.hid_ref, bf16[768,512]{1,0:T(8,128)(2,1)S(1)} %get-tuple-element.44.hid_t_ref, ...), custom_call_target="tpu_custom_call" | custom-call | flops 4000000000 | bytes 6000000 | tf_op jit(solution)/shard_map/last_heads/pallas_call | solution.py:298
  30.8 0.6 collective-permute-start.4
  31.7 0.9 %collective-permute-start.9 = (bf16[96,768]{1,0:T(8,128)(2,1)S(1)}, bf16[96,768]{1,0:T(8,128)(2,1)S(1)}, u32[]{:S(2)}, u32[]{:S(2)}) collective-permute-start(bf16[96,768]{1,0:T(8,128)(2,1)S(1)} %get-tuple-element.80), channel_id=1, source_target_pairs={{0,64},{64,0},{128,192},{192,128},{1,65},{65,1},{129,193},{193,129... | collective-permute-start | bytes 442376 | tf_op jit(solution)/shard_map/ppermute | solution.py:408
  32.6 1.1 %collective-permute-start.7 = (bf16[96,768]{1,0:T(8,128)(2,1)S(1)}, bf16[96,768]{1,0:T(8,128)(2,1)S(1)}, u32[]{:S(2)}, u32[]{:S(2)}) collective-permute-start(bf16[96,768]{1,0:T(8,128)(2,1)S(1)} %get-tuple-element.81), channel_id=1, source_target_pairs={{0,192},{64,128},{128,64},{192,0},{1,193},{65,129},{129,65},{193,1... | collective-permute-start | bytes 442376 | tf_op jit(solution)/shard_map/ppermute | solution.py:408
  34.2 2.8 %collective-permute-start.6 = (bf16[96,768]{1,0:T(8,128)(2,1)S(1)}, bf16[96,768]{1,0:T(8,128)(2,1)S(1)}, u32[]{:S(2)}, u32[]{:S(2)}) collective-permute-start(bf16[96,768]{1,0:T(8,128)(2,1)S(1)} %get-tuple-element.78), channel_id=1, source_target_pairs={{0,48},{8,56},{16,32},{24,40},{32,16},{40,24},{48,0},{56,8},{1,49}... | collective-permute-start | bytes 442376 | tf_op jit(solution)/shard_map/ppermute | solution.py:408
  37.0 1.7 %out_part.1 = bf16[16,2,16,768]{3,2,1,0:T(8,128)(2,1)} custom-call(bf16[2,256,768]{2,1,0:T(8,128)(2,1)S(1)} %get-tuple-element.62.xw_ref, bf16[2,256,128]{2,1,0:T(8,128)(2,1)S(1)} %get-tuple-element.40.tis_ref, bf16[2,256,512]{2,1,0:T(8,128)(2,1)S(1)} %get-tuple-element.45.att0_ref, bf16[2,256,256]{2,1,0:T(8,128)(2,1)S(1)} %get-tuple-element.54.att1_ref, ...), custom_call_target="tpu_custom_call" | custom-call | flops 1000 | bytes 1000 | tf_op jit(solution)/shard_map/out_part/pallas_call | solution.py:319
  38.7 2.9 %collective-permute-done.6 = bf16[96,768]{1,0:T(8,128)(2,1)S(1)} collective-permute-done((bf16[96,768]{1,0:T(8,128)(2,1)S(1)}, bf16[96,768]{1,0:T(8,128)(2,1)S(1)}, u32[]{:S(2)}, u32[]{:S(2)}) %collective-permute-start.6) | collective-permute-done | bytes 147488 | tf_op jit(solution)/shard_map/ppermute | solution.py:408
  41.6 1.0 %collective-permute-done.5 = bf16[96,768]{1,0:T(8,128)(2,1)S(1)} collective-permute-done((bf16[96,768]{1,0:T(8,128)(2,1)S(1)}, bf16[96,768]{1,0:T(8,128)(2,1)S(1)}, u32[]{:S(2)}, u32[]{:S(2)}) %collective-permute-start.5) | collective-permute-done | bytes 147488 | tf_op jit(solution)/shard_map/ppermute | solution.py:408
  43.0 1.3 %collective-permute-start.12 = (bf16[96,1536]{1,0:T(8,128)(2,1)S(1)}, bf16[96,1536]{1,0:T(8,128)(2,1)S(1)}, u32[]{:S(2)}, u32[]{:S(2)}) collective-permute-start(bf16[96,1536]{1,0:T(8,128)(2,1)S(1)} %pad_maximum_fusion.3), channel_id=1, source_target_pairs={{0,48},{8,56},{16,32},{24,40},{32,16},{40,24},{48,0},{56,8},{1,49}... | collective-permute-start | bytes 884744 | tf_op jit(solution)/shard_map/ppermute | solution.py:408
  44.5 1.5 %collective-permute-start.10 = (bf16[96,1536]{1,0:T(8,128)(2,1)S(1)}, bf16[96,1536]{1,0:T(8,128)(2,1)S(1)}, u32[]{:S(2)}, u32[]{:S(2)}) collective-permute-start(bf16[96,1536]{1,0:T(8,128)(2,1)S(1)} %pad_maximum_fusion.1), channel_id=1, source_target_pairs={{0,192},{64,128},{128,64},{192,0},{1,193},{65,129},{129,65},{193,1... | collective-permute-start | bytes 884744 | tf_op jit(solution)/shard_map/ppermute | solution.py:408
  46.4 5.0 %grad_part.1 = bf16[16,2,16,768]{3,2,1,0:T(8,128)(2,1)} custom-call(bf16[2,256,768]{2,1,0:T(8,128)(2,1)S(1)} %get-tuple-element.62.xw_ref, bf16[16,2,16,768]{3,2,1,0:T(8,128)(2,1)S(1)} %bitcast.27, bf16[2,256,128]{2,1,0:T(8,128)(2,1)S(1)} %get-tuple-element.40.tis_ref, bf16[2,2,256,768]{3,2,1,0:T(8,128)(2,1)S(1)} %get-tuple-element.63.dqkv0_ref, ...), custom_call_target="tpu_custom_call" | custom-call | flops 1000 | bytes 1000 | tf_op jit(solution)/shard_map/grad_part/pallas_call | solution.py:362
  51.4 0.8 %collective-permute-done.12 = bf16[96,1536]{1,0:T(8,128)(2,1)S(1)} collective-permute-done((bf16[96,1536]{1,0:T(8,128)(2,1)S(1)}, bf16[96,1536]{1,0:T(8,128)(2,1)S(1)}, u32[]{:S(2)}, u32[]{:S(2)}) %collective-permute-start.12) | collective-permute-done | bytes 294944 | tf_op jit(solution)/shard_map/ppermute | solution.py:408
  52.3 1.4 %collective-permute-done.10 = bf16[96,1536]{1,0:T(8,128)(2,1)S(1)} collective-permute-done((bf16[96,1536]{1,0:T(8,128)(2,1)S(1)}, bf16[96,1536]{1,0:T(8,128)(2,1)S(1)}, u32[]{:S(2)}, u32[]{:S(2)}) %collective-permute-start.10) | collective-permute-done | bytes 294944 | tf_op jit(solution)/shard_map/ppermute | solution.py:408
  54.0 2.1 %collective-permute-start.13 = (bf16[24,1536]{1,0:T(8,128)(2,1)S(1)}, bf16[24,1536]{1,0:T(8,128)(2,1)S(1)}, u32[]{:S(2)}, u32[]{:S(2)}) collective-permute-start(bf16[24,1536]{1,0:T(8,128)(2,1)S(1)} %get-tuple-element.86), channel_id=1, source_target_pairs={{0,32},{8,40},{16,48},{24,56},{32,0},{40,8},{48,16},{56,24},{1,33}... | collective-permute-start | bytes 221192 | tf_op jit(solution)/shard_map/ppermute | solution.py:408
  56.1 0.6 collective-permute-start.15
  56.7 1.5 %collective-permute-start.14 = (bf16[24,1536]{1,0:T(8,128)(2,1)S(1)}, bf16[24,1536]{1,0:T(8,128)(2,1)S(1)}, u32[]{:S(2)}, u32[]{:S(2)}) collective-permute-start(bf16[24,1536]{1,0:T(8,128)(2,1)S(1)} %get-tuple-element.88), channel_id=1, source_target_pairs={{0,48},{8,56},{16,32},{24,40},{32,16},{40,24},{48,0},{56,8},{1,49}... | collective-permute-start | bytes 221192 | tf_op jit(solution)/shard_map/ppermute | solution.py:408
  58.2 1.9 %collective-permute-start.16 = (bf16[24,1536]{1,0:T(8,128)(2,1)S(1)}, bf16[24,1536]{1,0:T(8,128)(2,1)S(1)}, u32[]{:S(2)}, u32[]{:S(2)}) collective-permute-start(bf16[24,1536]{1,0:T(8,128)(2,1)S(1)} %get-tuple-element.89), channel_id=1, source_target_pairs={{0,128},{64,192},{128,0},{192,64},{1,129},{65,193},{129,1},{193,65... | collective-permute-start | bytes 221192 | tf_op jit(solution)/shard_map/ppermute | solution.py:408
  60.1 1.1 %collective-permute-start.18 = (bf16[24,1536]{1,0:T(8,128)(2,1)S(1)}, bf16[24,1536]{1,0:T(8,128)(2,1)S(1)}, u32[]{:S(2)}, u32[]{:S(2)}) collective-permute-start(bf16[24,1536]{1,0:T(8,128)(2,1)S(1)} %get-tuple-element.90), channel_id=1, source_target_pairs={{0,64},{64,0},{128,192},{192,128},{1,65},{65,1},{129,193},{193,129... | collective-permute-start | bytes 221192 | tf_op jit(solution)/shard_map/ppermute | solution.py:408
  61.2 1.2 %collective-permute-start.17 = (bf16[24,1536]{1,0:T(8,128)(2,1)S(1)}, bf16[24,1536]{1,0:T(8,128)(2,1)S(1)}, u32[]{:S(2)}, u32[]{:S(2)}) collective-permute-start(bf16[24,1536]{1,0:T(8,128)(2,1)S(1)} %get-tuple-element.91), channel_id=1, source_target_pairs={{0,192},{64,128},{128,64},{192,0},{1,193},{65,129},{129,65},{193,1... | collective-permute-start | bytes 221192 | tf_op jit(solution)/shard_map/ppermute | solution.py:408
  62.5 1.7 %collective-permute-done.16 = bf16[24,1536]{1,0:T(8,128)(2,1)S(1)} collective-permute-done((bf16[24,1536]{1,0:T(8,128)(2,1)S(1)}, bf16[24,1536]{1,0:T(8,128)(2,1)S(1)}, u32[]{:S(2)}, u32[]{:S(2)}) %collective-permute-start.16) | collective-permute-done | bytes 73760 | tf_op jit(solution)/shard_map/ppermute | solution.py:408
  64.5 2.3 %collective-permute-done.17 = bf16[24,1536]{1,0:T(8,128)(2,1)S(1)} collective-permute-done((bf16[24,1536]{1,0:T(8,128)(2,1)S(1)}, bf16[24,1536]{1,0:T(8,128)(2,1)S(1)}, u32[]{:S(2)}, u32[]{:S(2)}) %collective-permute-start.17) | collective-permute-done | bytes 73760 | tf_op jit(solution)/shard_map/ppermute | solution.py:408
  67.0 13.7 %all_to_all.5.parts_ref = bf16[8,3,3072]{2,1,0:T(4,128)(2,1)S(1)} all-to-all(bf16[8,3,3072]{2,1,0:T(4,128)(2,1)S(1)} %reshape.81), channel_id=1, replica_groups=mesh['dp'=4,'gy'=8,'gx'=8] {'gx'}, dimensions={0} | all-to-all | bytes 294912 | tf_op jit(solution)/shard_map/all_to_all | solution.py:454
  80.7 0.6 finish.1
  (46 shorter events, 2.9 us)
Async XLA Ops:
  0.6 12.7 %copy-start.1 = (bf16[768,768]{1,0:T(8,128)(2,1)S(1)}, bf16[768,768]{1,0:T(8,128)(2,1)}, u32[]{:S(2)}) copy-start(bf16[768,768]{1,0:T(8,128)(2,1)} %wp_ref.1) | copy-start | bytes 3538948
  0.6 12.7 %copy-start.3 = (bf16[1,16,32,768]{3,2,1,0:T(8,128)(2,1)S(1)}, bf16[1,16,32,768]{3,2,1,0:T(8,128)(2,1)}, u32[]{:S(2)}) copy-start(bf16[1,16,32,768]{3,2,1,0:T(8,128)(2,1)} %param.6) | copy-start | bytes 2359300
  0.7 12.7 %copy-start.4 = (s32[1,16,32]{2,1,0:T(8,128)S(1)}, s32[1,16,32]{2,1,0:T(8,128)}, u32[]{:S(2)}) copy-start(s32[1,16,32]{2,1,0:T(8,128)} %param.7) | copy-start | bytes 6148
  2.5 15.0 %collective-permute-start = (bf16[8,24,768]{2,1,0:T(8,128)(2,1)}, bf16[8,24,768]{2,1,0:T(8,128)(2,1)S(1)}, u32[]{:S(2)}, u32[]{:S(2)}) collective-permute-start(bf16[8,24,768]{2,1,0:T(8,128)(2,1)} %above.1.after_ref), channel_id=1, source_target_pairs={{0,56},{8,0},{16,8},{24,16},{32,24},{40,32},{48,40},{56,48},{1,57}... | collective-permute-start | bytes 884744 | tf_op jit(solution)/shard_map/ppermute | solution.py:408
  6.7 9.0 %collective-permute-start.1 = (bf16[8,8,768]{2,1,0:T(8,128)(2,1)}, bf16[8,8,768]{2,1,0:T(8,128)(2,1)S(1)}, u32[]{:S(2)}, u32[]{:S(2)}) collective-permute-start(bf16[8,8,768]{2,1,0:T(8,128)(2,1)} %get-tuple-element.38), channel_id=1, source_target_pairs={{0,7},{1,0},{2,1},{3,2},{4,3},{5,4},{6,5},{7,6},{8,15},{9,8},{10,9... | collective-permute-start | bytes 294920 | tf_op jit(solution)/shard_map/ppermute | solution.py:408
  12.5 5.0 %collective-permute-start.2 = (bf16[8,8,768]{2,1,0:T(8,128)(2,1)}, bf16[8,8,768]{2,1,0:T(8,128)(2,1)S(1)}, u32[]{:S(2)}, u32[]{:S(2)}) collective-permute-start(bf16[8,8,768]{2,1,0:T(8,128)(2,1)} %get-tuple-element.39), channel_id=1, source_target_pairs={{0,63},{1,56},{2,57},{3,58},{4,59},{5,60},{6,61},{7,62},{8,7},{9,0... | collective-permute-start | bytes 294920 | tf_op jit(solution)/shard_map/ppermute | solution.py:471
  13.4 4.1 %copy-start = (bf16[768,2304]{1,0:T(8,128)(2,1)S(1)}, bf16[768,2304]{1,0:T(8,128)(2,1)}, u32[]{:S(2)}) copy-start(bf16[768,2304]{1,0:T(8,128)(2,1)} %wv_ref.5) | copy-start | bytes 10616836
  13.4 4.1 %copy-start.2 = (bf16[1,16,32,768]{3,2,1,0:T(8,128)(2,1)S(1)}, bf16[1,16,32,768]{3,2,1,0:T(8,128)(2,1)}, u32[]{:S(2)}) copy-start(bf16[1,16,32,768]{3,2,1,0:T(8,128)(2,1)} %param.5) | copy-start | bytes 2359300
  25.8 4.9 %collective-permute-start.3 = (bf16[384,1536]{1,0:T(8,128)(2,1)S(1)}, bf16[384,1536]{1,0:T(8,128)(2,1)S(1)}, u32[]{:S(2)}, u32[]{:S(2)}) collective-permute-start(bf16[384,1536]{1,0:T(8,128)(2,1)S(1)} %get-tuple-element.48), channel_id=1, source_target_pairs={{0,8},{8,0},{16,24},{24,16},{32,40},{40,32},{48,56},{56,48},{1,9},... | collective-permute-start | bytes 3538952 | tf_op jit(solution)/shard_map/ppermute | solution.py:408
  30.8 3.1 %collective-permute-start.4 = (bf16[384,1536]{1,0:T(8,128)(2,1)S(1)}, bf16[384,1536]{1,0:T(8,128)(2,1)S(1)}, u32[]{:S(2)}, u32[]{:S(2)}) collective-permute-start(bf16[384,1536]{1,0:T(8,128)(2,1)S(1)} %get-tuple-element.50), channel_id=1, source_target_pairs={{0,8},{8,0},{16,24},{24,16},{32,40},{40,32},{48,56},{56,48},{1,9},... | collective-permute-start | bytes 3538952 | tf_op jit(solution)/shard_map/ppermute | solution.py:408
  31.7 12.7 %collective-permute-start.9 = (bf16[96,768]{1,0:T(8,128)(2,1)S(1)}, bf16[96,768]{1,0:T(8,128)(2,1)S(1)}, u32[]{:S(2)}, u32[]{:S(2)}) collective-permute-start(bf16[96,768]{1,0:T(8,128)(2,1)S(1)} %get-tuple-element.80), channel_id=1, source_target_pairs={{0,64},{64,0},{128,192},{192,128},{1,65},{65,1},{129,193},{193,129... | collective-permute-start | bytes 442376 | tf_op jit(solution)/shard_map/ppermute | solution.py:408
  32.6 13.4 %collective-permute-start.7 = (bf16[96,768]{1,0:T(8,128)(2,1)S(1)}, bf16[96,768]{1,0:T(8,128)(2,1)S(1)}, u32[]{:S(2)}, u32[]{:S(2)}) collective-permute-start(bf16[96,768]{1,0:T(8,128)(2,1)S(1)} %get-tuple-element.81), channel_id=1, source_target_pairs={{0,192},{64,128},{128,64},{192,0},{1,193},{65,129},{129,65},{193,1... | collective-permute-start | bytes 442376 | tf_op jit(solution)/shard_map/ppermute | solution.py:408
  34.2 7.4 %collective-permute-start.6 = (bf16[96,768]{1,0:T(8,128)(2,1)S(1)}, bf16[96,768]{1,0:T(8,128)(2,1)S(1)}, u32[]{:S(2)}, u32[]{:S(2)}) collective-permute-start(bf16[96,768]{1,0:T(8,128)(2,1)S(1)} %get-tuple-element.78), channel_id=1, source_target_pairs={{0,48},{8,56},{16,32},{24,40},{32,16},{40,24},{48,0},{56,8},{1,49}... | collective-permute-start | bytes 442376 | tf_op jit(solution)/shard_map/ppermute | solution.py:408
  36.9 5.6 %collective-permute-start.5 = (bf16[96,768]{1,0:T(8,128)(2,1)S(1)}, bf16[96,768]{1,0:T(8,128)(2,1)S(1)}, u32[]{:S(2)}, u32[]{:S(2)}) collective-permute-start(bf16[96,768]{1,0:T(8,128)(2,1)S(1)} %get-tuple-element.79), channel_id=1, source_target_pairs={{0,16},{8,24},{16,0},{24,8},{32,48},{40,56},{48,32},{56,40},{1,17}... | collective-permute-start | bytes 442376 | tf_op jit(solution)/shard_map/ppermute | solution.py:408
  42.6 8.8 %collective-permute-start.11 = (bf16[96,1536]{1,0:T(8,128)(2,1)S(1)}, bf16[96,1536]{1,0:T(8,128)(2,1)S(1)}, u32[]{:S(2)}, u32[]{:S(2)}) collective-permute-start(bf16[96,1536]{1,0:T(8,128)(2,1)S(1)} %pad_maximum_fusion.2), channel_id=1, source_target_pairs={{0,16},{8,24},{16,0},{24,8},{32,48},{40,56},{48,32},{56,40},{1,17}... | collective-permute-start | bytes 884744 | tf_op jit(solution)/shard_map/ppermute | solution.py:408
  43.0 9.2 %collective-permute-start.12 = (bf16[96,1536]{1,0:T(8,128)(2,1)S(1)}, bf16[96,1536]{1,0:T(8,128)(2,1)S(1)}, u32[]{:S(2)}, u32[]{:S(2)}) collective-permute-start(bf16[96,1536]{1,0:T(8,128)(2,1)S(1)} %pad_maximum_fusion.3), channel_id=1, source_target_pairs={{0,48},{8,56},{16,32},{24,40},{32,16},{40,24},{48,0},{56,8},{1,49}... | collective-permute-start | bytes 884744 | tf_op jit(solution)/shard_map/ppermute | solution.py:408
  44.5 9.2 %collective-permute-start.10 = (bf16[96,1536]{1,0:T(8,128)(2,1)S(1)}, bf16[96,1536]{1,0:T(8,128)(2,1)S(1)}, u32[]{:S(2)}, u32[]{:S(2)}) collective-permute-start(bf16[96,1536]{1,0:T(8,128)(2,1)S(1)} %pad_maximum_fusion.1), channel_id=1, source_target_pairs={{0,192},{64,128},{128,64},{192,0},{1,193},{65,129},{129,65},{193,1... | collective-permute-start | bytes 884744 | tf_op jit(solution)/shard_map/ppermute | solution.py:408
  46.1 7.7 %collective-permute-start.8 = (bf16[96,1536]{1,0:T(8,128)(2,1)S(1)}, bf16[96,1536]{1,0:T(8,128)(2,1)S(1)}, u32[]{:S(2)}, u32[]{:S(2)}) collective-permute-start(bf16[96,1536]{1,0:T(8,128)(2,1)S(1)} %pad_maximum_fusion), channel_id=1, source_target_pairs={{0,64},{64,0},{128,192},{192,128},{1,65},{65,1},{129,193},{193,129... | collective-permute-start | bytes 884744 | tf_op jit(solution)/shard_map/ppermute | solution.py:408
  54.0 7.2 %collective-permute-start.13 = (bf16[24,1536]{1,0:T(8,128)(2,1)S(1)}, bf16[24,1536]{1,0:T(8,128)(2,1)S(1)}, u32[]{:S(2)}, u32[]{:S(2)}) collective-permute-start(bf16[24,1536]{1,0:T(8,128)(2,1)S(1)} %get-tuple-element.86), channel_id=1, source_target_pairs={{0,32},{8,40},{16,48},{24,56},{32,0},{40,8},{48,16},{56,24},{1,33}... | collective-permute-start | bytes 221192 | tf_op jit(solution)/shard_map/ppermute | solution.py:408
  56.1 6.3 %collective-permute-start.15 = (bf16[24,1536]{1,0:T(8,128)(2,1)S(1)}, bf16[24,1536]{1,0:T(8,128)(2,1)S(1)}, u32[]{:S(2)}, u32[]{:S(2)}) collective-permute-start(bf16[24,1536]{1,0:T(8,128)(2,1)S(1)} %get-tuple-element.87), channel_id=1, source_target_pairs={{0,16},{8,24},{16,0},{24,8},{32,48},{40,56},{48,32},{56,40},{1,17}... | collective-permute-start | bytes 221192 | tf_op jit(solution)/shard_map/ppermute | solution.py:408
  56.7 5.7 %collective-permute-start.14 = (bf16[24,1536]{1,0:T(8,128)(2,1)S(1)}, bf16[24,1536]{1,0:T(8,128)(2,1)S(1)}, u32[]{:S(2)}, u32[]{:S(2)}) collective-permute-start(bf16[24,1536]{1,0:T(8,128)(2,1)S(1)} %get-tuple-element.88), channel_id=1, source_target_pairs={{0,48},{8,56},{16,32},{24,40},{32,16},{40,24},{48,0},{56,8},{1,49}... | collective-permute-start | bytes 221192 | tf_op jit(solution)/shard_map/ppermute | solution.py:408
  58.2 5.9 %collective-permute-start.16 = (bf16[24,1536]{1,0:T(8,128)(2,1)S(1)}, bf16[24,1536]{1,0:T(8,128)(2,1)S(1)}, u32[]{:S(2)}, u32[]{:S(2)}) collective-permute-start(bf16[24,1536]{1,0:T(8,128)(2,1)S(1)} %get-tuple-element.89), channel_id=1, source_target_pairs={{0,128},{64,192},{128,0},{192,64},{1,129},{65,193},{129,1},{193,65... | collective-permute-start | bytes 221192 | tf_op jit(solution)/shard_map/ppermute | solution.py:408
  60.1 4.4 %collective-permute-start.18 = (bf16[24,1536]{1,0:T(8,128)(2,1)S(1)}, bf16[24,1536]{1,0:T(8,128)(2,1)S(1)}, u32[]{:S(2)}, u32[]{:S(2)}) collective-permute-start(bf16[24,1536]{1,0:T(8,128)(2,1)S(1)} %get-tuple-element.90), channel_id=1, source_target_pairs={{0,64},{64,0},{128,192},{192,128},{1,65},{65,1},{129,193},{193,129... | collective-permute-start | bytes 221192 | tf_op jit(solution)/shard_map/ppermute | solution.py:408
  61.2 5.6 %collective-permute-start.17 = (bf16[24,1536]{1,0:T(8,128)(2,1)S(1)}, bf16[24,1536]{1,0:T(8,128)(2,1)S(1)}, u32[]{:S(2)}, u32[]{:S(2)}) collective-permute-start(bf16[24,1536]{1,0:T(8,128)(2,1)S(1)} %get-tuple-element.91), channel_id=1, source_target_pairs={{0,192},{64,128},{128,64},{192,0},{1,193},{65,129},{129,65},{193,1... | collective-permute-start | bytes 221192 | tf_op jit(solution)/shard_map/ppermute | solution.py:408

commit v11 on v10

--- a/solution.py
+++ b/solution.py
@@ -16,7 +16,6 @@
 GW = D // GROUPS
 HEAD_SCALE = 0.125
 VMEM = 32 * 1024 * 1024
-EDGE_VMEM = 60 * 1024 * 1024
 
 
 def nn(a, b):
@@ -39,41 +38,36 @@
     return pl.CostEstimate(flops=int(flops), bytes_accessed=int(size), transcendentals=0)
 
 
-def above_kernel(tiles_ref, above_ref):
+def corner_kernel(tiles_ref, corner_ref):
+    corner_ref[...] = tiles_ref[...].astype(F32)[:, :8].astype(BF)
+
+
+def above_kernel(tiles_ref, after_ref, above_ref):
     above_ref[...] = tiles_ref[...].astype(F32)[:, 8:].astype(BF)
 
 
-def left_kernel(tiles_ref, after_ref, left_ref, corner_ref):
-    tiles = tiles_ref[...].astype(F32)[:, :8].astype(BF)
-    corner_ref[...] = tiles[:8]
-    left_ref[...] = tiles[8:]
+def left_kernel(tiles_ref, after_ref, left_ref):
+    left_ref[...] = tiles_ref[...].astype(F32)[:, :8].astype(BF)
+
+
+def cut(kernel, name, flops, tiles, after, block, first, columns):
+    place = pl.BlockSpec(memory_space=pl.ANY)
+    return pl.pallas_call(
+        kernel,
+        grid=(1,),
+        in_specs=[pl.BlockSpec(block + (D,), lambda g: (first, 0, 0))] + [place] * len(after),
+        out_specs=full((8, columns, D)),
+        out_shape=jax.ShapeDtypeStruct((8, columns, D), BF),
+        compiler_params=pltpu.CompilerParams(vmem_limit_bytes=VMEM),
+        cost_estimate=cost(flops, 1e3),
+        name=name,
+    )(tiles, *after)
 
 
 def edges(tiles):
-    small = jax.ShapeDtypeStruct((8, 8, D), BF)
-    above = pl.pallas_call(
-        above_kernel,
-        grid=(1,),
-        in_specs=[pl.BlockSpec((8, 32, D), lambda g: (0, 0, 0))],
-        out_specs=full((8, 24, D)),
-        out_shape=jax.ShapeDtypeStruct((8, 24, D), BF),
-        compiler_params=pltpu.CompilerParams(vmem_limit_bytes=EDGE_VMEM),
-        cost_estimate=cost(3e10, 1e6),
-        name="above",
-    )(tiles)
-    left, corner = pl.pallas_call(
-        left_kernel,
-        grid=(1,),
-        in_specs=[
-            pl.BlockSpec((16, 16, D), lambda g: (0, 0, 0)),
-            pl.BlockSpec(memory_space=pl.ANY),
-        ],
-        out_specs=[full((8, 8, D))] * 2,
-        out_shape=[small, small],
-        compiler_params=pltpu.CompilerParams(vmem_limit_bytes=EDGE_VMEM),
-        cost_estimate=cost(1e3, 1e3),
-        name="left",
-    )(tiles, above)
+    corner = cut(corner_kernel, "corner", 3e10, tiles, [], (8, 16), 0, 8)
+    above = cut(above_kernel, "above", 1e3, tiles, [corner], (8, 32), 0, 24)
+    left = cut(left_kernel, "left", 1e3, tiles, [above], (8, 16), 1, 8)
     return above, left, corner
 
 

time: 81.7 us -> 79.4 us (0.972)
  Pallas kernels: 25.4 us -> 21.9 us
  local copies, waits for them, and re-layouts: 0.28 us -> 1.42 us
    ppermute x1, starting transfers between devices: 0.84 us -> 7.82 us  [shards(): lax.ppermute(corner, ('gy', 'gx'), [(a * nx + b, (a - 1) % ny * nx + (b -...]
    ppermute x18, starting transfers between devices: 25.9 us -> 19.7 us  [send(): lax.ppermute(value, axis, [(i, move(i) % devices) for i in range(devices)])]
    pallas_call x2 -> x3, Pallas kernels: 3.54 us -> 0.03 us  [cut(): pl.pallas_call(kernel, grid=(1,), in_specs=[pl.BlockSpec(block + (D,), la...]
    ppermute x1, waiting for transfers between devices: 1.83 us -> 0.01 us  [shards(): lax.ppermute(corner, ('gy', 'gx'), [(a * nx + b, (a - 1) % ny * nx + (b -...]
    ppermute x18, waiting for transfers between devices: 11.4 us -> 12.7 us  [send(): lax.ppermute(value, axis, [(i, move(i) % devices) for i in range(devices)])]
    unnamed x10 -> x12, local copies, waits for them, and re-layouts: 0.02 us -> 1.15 us
  transfers between devices with their start and end apart: 19 -> 19, of which waited for: 11 -> 10; matrix products, arithmetic and copies ran while one was open for 1% -> 1% of each run, Pallas kernels for 18% -> 16%
where the time goes in v11:
time: 79.4 us; the launch traced here: 79 us
  starting transfers between devices  27.5 us (35%)
  Pallas kernels  21.9 us (28%)
  blocking collectives  13.4 us (17%)
  waiting for transfers between devices  12.7 us (16%)
  local copies, waits for them, and re-layouts  1.42 us (2%)
  other arithmetic  1.14 us (1%)
  between operations  0.89 us (1%)
    ppermute x18, starting transfers between devices, send(): lax.ppermute(value, axis, [(i, move(i) % devices) for i in range(devices)])  19.7 us
    all_to_all x1, blocking collectives, exchange(): return lax.all_to_all(rows, axis, 0, 0, axis_index_groups=groups)  13.4 us
    ppermute x18, waiting for transfers between devices, send(): lax.ppermute(value, axis, [(i, move(i) % devices) for i in range(devices)])  12.7 us
    pallas_call x1, Pallas kernels, first_heads(): pl.pallas_call(first_kernel, grid=(2,), in_specs=[full((16, 32, D)), full...  8.36 us
    ppermute x1, starting transfers between devices, shards(): lax.ppermute(corner, ('gy', 'gx'), [(a * nx + b, (a - 1) % ny * nx + (b -...  7.82 us
    pallas_call x1, Pallas kernels, grad_part(): pl.pallas_call(grad_kernel, grid=(GROUPS,), in_specs=[full((2, CELLS, D))...  5.04 us
    pallas_call x1, Pallas kernels, last_heads(): pl.pallas_call(last_kernel, grid=(1,), in_specs=[rows, full((D, 2 * CELLS...  4.66 us
    pallas_call x1, Pallas kernels, out_part(): pl.pallas_call(out_kernel, out_shape=jax.ShapeDtypeStruct((WIN, 2, WIN, D...  1.67 us
  transfers between devices with their start and end apart: 19, of which 10 were waited for; matrix products, arithmetic and copies ran while one was open for 1% of the time, Pallas kernels for 16%

profile of v11, /device:TPU:6, one launch (start us, length us, event | category | flops | bytes accessed | tf_op | source)
XLA Modules:
  0.0 79.0 jit_solution(16856521705276989949)
XLA Ops:
  0.6 1.1 %copy-done.1 = bf16[1,16,32,768]{3,2,1,0:T(8,128)(2,1)S(1)} copy-done((bf16[1,16,32,768]{3,2,1,0:T(8,128)(2,1)S(1)}, bf16[1,16,32,768]{3,2,1,0:T(8,128)(2,1)}, u32[]{:S(2)}) %copy-start.1) | copy-done | bytes 786456
  1.8 7.8 %collective-permute-start.2 = (bf16[8,8,768]{2,1,0:T(8,128)(2,1)S(1)}, bf16[8,8,768]{2,1,0:T(8,128)(2,1)S(1)}, u32[]{:S(2)}, u32[]{:S(2)}) collective-permute-start(bf16[8,8,768]{2,1,0:T(8,128)(2,1)S(1)} %corner.1.after_ref), channel_id=1, source_target_pairs={{0,63},{1,56},{2,57},{3,58},{4,59},{5,60},{6,61},{7,62},{8,7},{9,0... | collective-permute-start | bytes 294920 | tf_op jit(solution)/shard_map/ppermute | solution.py:465
  9.7 0.9 %collective-permute-start = (bf16[8,24,768]{2,1,0:T(8,128)(2,1)S(1)}, bf16[8,24,768]{2,1,0:T(8,128)(2,1)S(1)}, u32[]{:S(2)}, u32[]{:S(2)}) collective-permute-start(bf16[8,24,768]{2,1,0:T(8,128)(2,1)S(1)} %above.1.after_ref), channel_id=1, source_target_pairs={{0,56},{8,0},{16,8},{24,16},{32,24},{40,32},{48,40},{56,48},{1,57}... | collective-permute-start | bytes 884744 | tf_op jit(solution)/shard_map/ppermute | solution.py:402
  10.5 1.1 %collective-permute-start.1 = (bf16[8,8,768]{2,1,0:T(8,128)(2,1)S(1)}, bf16[8,8,768]{2,1,0:T(8,128)(2,1)S(1)}, u32[]{:S(2)}, u32[]{:S(2)}) collective-permute-start(bf16[8,8,768]{2,1,0:T(8,128)(2,1)S(1)} %left.1), channel_id=1, source_target_pairs={{0,7},{1,0},{2,1},{3,2},{4,3},{5,4},{6,5},{7,6},{8,15},{9,8},{10,9... | collective-permute-start | bytes 294920 | tf_op jit(solution)/shard_map/ppermute | solution.py:402
  11.6 1.5 %branch.1 = (bf16[2,256,768]{2,1,0:T(8,128)(2,1)S(1)}, bf16[2,256,768]{2,1,0:T(8,128)(2,1)S(1)}, bf16[2,256,128]{2,1,0:T(8,128)(2,1)S(1)}, bf16[2,256,128]{2,1,0:T(8,128)(2,1)S(1)}) custom-call(bf16[16,2,16,768]{3,2,1,0:T(8,128)(2,1)S(1)} %bitcast.27, s32[16,32]{1,0:T(8,128)S(1)} %bitcast.29, bf16[768,768]{1,0:T(8,128)(2,1)S(1)} %copy-done.3), custom_call_target="tpu_custom_call" | custom-call | flops 20000000000 | bytes 4000000 | tf_op jit(solution)/shard_map/branch/pallas_call | solution.py:107
  13.1 2.1 %collective-permute-done.1.right_ref = bf16[8,8,768]{2,1,0:T(8,128)(2,1)S(1)} collective-permute-done((bf16[8,8,768]{2,1,0:T(8,128)(2,1)S(1)}, bf16[8,8,768]{2,1,0:T(8,128)(2,1)S(1)}, u32[]{:S(2)}, u32[]{:S(2)}) %collective-permute-start.1) | collective-permute-done | bytes 98336 | tf_op jit(solution)/shard_map/ppermute | solution.py:402
  15.2 8.4 %first_heads.1 = (bf16[384,1536]{1,0:T(8,128)(2,1)S(1)}, bf16[384,1536]{1,0:T(8,128)(2,1)S(1)}, bf16[2,256,512]{2,1,0:T(8,128)(2,1)S(1)}, bf16[2,2,256,768]{3,2,...) custom-call(bf16[16,32,768]{2,1,0:T(8,128)(2,1)S(1)} %bitcast.26, ...), custom_call_target="tpu_custom_call" | custom-call | flops 6000000000 | bytes 10000000 | tf_op jit(solution)/shard_map/first_heads/pallas_call | solution.py:276
  23.9 4.7 %last_heads.1 = (bf16[384,1536]{1,0:T(8,128)(2,1)S(1)}, bf16[384,1536]{1,0:T(8,128)(2,1)S(1)}, bf16[2,256,256]{2,1,0:T(8,128)(2,1)S(1)}, bf16[1,2,256,768]{3,2,1,0:T(8,128)(2,1)S(1)}) custom-call(bf16[2,256,768]{2,1,0:T(8,128)(2,1)S(1)} %get-tuple-element.39.hid_ref, bf16[768,512]{1,0:T(8,128)(2,1)S(1)} %get-tuple-element.40.hid_t_ref, ...), custom_call_target="tpu_custom_call" | custom-call | flops 4000000000 | bytes 6000000 | tf_op jit(solution)/shard_map/last_heads/pallas_call | solution.py:292
  28.5 0.6 collective-permute-start.4
  29.4 0.9 %collective-permute-start.9 = (bf16[96,768]{1,0:T(8,128)(2,1)S(1)}, bf16[96,768]{1,0:T(8,128)(2,1)S(1)}, u32[]{:S(2)}, u32[]{:S(2)}) collective-permute-start(bf16[96,768]{1,0:T(8,128)(2,1)S(1)} %get-tuple-element.76), channel_id=1, source_target_pairs={{0,64},{64,0},{128,192},{192,128},{1,65},{65,1},{129,193},{193,129... | collective-permute-start | bytes 442376 | tf_op jit(solution)/shard_map/ppermute | solution.py:402
  30.4 1.1 %collective-permute-start.7 = (bf16[96,768]{1,0:T(8,128)(2,1)S(1)}, bf16[96,768]{1,0:T(8,128)(2,1)S(1)}, u32[]{:S(2)}, u32[]{:S(2)}) collective-permute-start(bf16[96,768]{1,0:T(8,128)(2,1)S(1)} %get-tuple-element.77), channel_id=1, source_target_pairs={{0,192},{64,128},{128,64},{192,0},{1,193},{65,129},{129,65},{193,1... | collective-permute-start | bytes 442376 | tf_op jit(solution)/shard_map/ppermute | solution.py:402
  31.9 3.0 %collective-permute-start.6 = (bf16[96,768]{1,0:T(8,128)(2,1)S(1)}, bf16[96,768]{1,0:T(8,128)(2,1)S(1)}, u32[]{:S(2)}, u32[]{:S(2)}) collective-permute-start(bf16[96,768]{1,0:T(8,128)(2,1)S(1)} %get-tuple-element.74), channel_id=1, source_target_pairs={{0,48},{8,56},{16,32},{24,40},{32,16},{40,24},{48,0},{56,8},{1,49}... | collective-permute-start | bytes 442376 | tf_op jit(solution)/shard_map/ppermute | solution.py:402
  35.0 1.7 %out_part.1 = bf16[16,2,16,768]{3,2,1,0:T(8,128)(2,1)} custom-call(bf16[2,256,768]{2,1,0:T(8,128)(2,1)S(1)} %get-tuple-element.58.xw_ref, bf16[2,256,128]{2,1,0:T(8,128)(2,1)S(1)} %get-tuple-element.36.tis_ref, bf16[2,256,512]{2,1,0:T(8,128)(2,1)S(1)} %get-tuple-element.41.att0_ref, bf16[2,256,256]{2,1,0:T(8,128)(2,1)S(1)} %get-tuple-element.50.att1_ref, ...), custom_call_target="tpu_custom_call" | custom-call | flops 1000 | bytes 1000 | tf_op jit(solution)/shard_map/out_part/pallas_call | solution.py:313
  36.7 2.7 %collective-permute-done.6 = bf16[96,768]{1,0:T(8,128)(2,1)S(1)} collective-permute-done((bf16[96,768]{1,0:T(8,128)(2,1)S(1)}, bf16[96,768]{1,0:T(8,128)(2,1)S(1)}, u32[]{:S(2)}, u32[]{:S(2)}) %collective-permute-start.6) | collective-permute-done | bytes 147488 | tf_op jit(solution)/shard_map/ppermute | solution.py:402
  39.4 1.2 %collective-permute-done.5 = bf16[96,768]{1,0:T(8,128)(2,1)S(1)} collective-permute-done((bf16[96,768]{1,0:T(8,128)(2,1)S(1)}, bf16[96,768]{1,0:T(8,128)(2,1)S(1)}, u32[]{:S(2)}, u32[]{:S(2)}) %collective-permute-start.5) | collective-permute-done | bytes 147488 | tf_op jit(solution)/shard_map/ppermute | solution.py:402
  40.6 0.4 collective-permute-start.11
  41.0 1.3 %collective-permute-start.12 = (bf16[96,1536]{1,0:T(8,128)(2,1)S(1)}, bf16[96,1536]{1,0:T(8,128)(2,1)S(1)}, u32[]{:S(2)}, u32[]{:S(2)}) collective-permute-start(bf16[96,1536]{1,0:T(8,128)(2,1)S(1)} %pad_maximum_fusion.3), channel_id=1, source_target_pairs={{0,48},{8,56},{16,32},{24,40},{32,16},{40,24},{48,0},{56,8},{1,49}... | collective-permute-start | bytes 884744 | tf_op jit(solution)/shard_map/ppermute | solution.py:402
  42.4 1.5 %collective-permute-start.10 = (bf16[96,1536]{1,0:T(8,128)(2,1)S(1)}, bf16[96,1536]{1,0:T(8,128)(2,1)S(1)}, u32[]{:S(2)}, u32[]{:S(2)}) collective-permute-start(bf16[96,1536]{1,0:T(8,128)(2,1)S(1)} %pad_maximum_fusion.1), channel_id=1, source_target_pairs={{0,192},{64,128},{128,64},{192,0},{1,193},{65,129},{129,65},{193,1... | collective-permute-start | bytes 884744 | tf_op jit(solution)/shard_map/ppermute | solution.py:402
  44.1 0.3 collective-permute-start.8
  44.4 5.0 %grad_part.1 = bf16[16,2,16,768]{3,2,1,0:T(8,128)(2,1)} custom-call(bf16[2,256,768]{2,1,0:T(8,128)(2,1)S(1)} %get-tuple-element.58.xw_ref, bf16[16,2,16,768]{3,2,1,0:T(8,128)(2,1)S(1)} %bitcast.28, bf16[2,256,128]{2,1,0:T(8,128)(2,1)S(1)} %get-tuple-element.36.tis_ref, bf16[2,2,256,768]{3,2,1,0:T(8,128)(2,1)S(1)} %get-tuple-element.59.dqkv0_ref, ...), custom_call_target="tpu_custom_call" | custom-call | flops 1000 | bytes 1000 | tf_op jit(solution)/shard_map/grad_part/pallas_call | solution.py:356
  49.4 0.8 %collective-permute-done.12 = bf16[96,1536]{1,0:T(8,128)(2,1)S(1)} collective-permute-done((bf16[96,1536]{1,0:T(8,128)(2,1)S(1)}, bf16[96,1536]{1,0:T(8,128)(2,1)S(1)}, u32[]{:S(2)}, u32[]{:S(2)}) %collective-permute-start.12) | collective-permute-done | bytes 294944 | tf_op jit(solution)/shard_map/ppermute | solution.py:402
  50.2 1.4 %collective-permute-done.10 = bf16[96,1536]{1,0:T(8,128)(2,1)S(1)} collective-permute-done((bf16[96,1536]{1,0:T(8,128)(2,1)S(1)}, bf16[96,1536]{1,0:T(8,128)(2,1)S(1)}, u32[]{:S(2)}, u32[]{:S(2)}) %collective-permute-start.10) | collective-permute-done | bytes 294944 | tf_op jit(solution)/shard_map/ppermute | solution.py:402
  52.0 2.1 %collective-permute-start.13 = (bf16[24,1536]{1,0:T(8,128)(2,1)S(1)}, bf16[24,1536]{1,0:T(8,128)(2,1)S(1)}, u32[]{:S(2)}, u32[]{:S(2)}) collective-permute-start(bf16[24,1536]{1,0:T(8,128)(2,1)S(1)} %get-tuple-element.82), channel_id=1, source_target_pairs={{0,32},{8,40},{16,48},{24,56},{32,0},{40,8},{48,16},{56,24},{1,33}... | collective-permute-start | bytes 221192 | tf_op jit(solution)/shard_map/ppermute | solution.py:402
  54.1 0.6 collective-permute-start.15
  54.7 1.5 %collective-permute-start.14 = (bf16[24,1536]{1,0:T(8,128)(2,1)S(1)}, bf16[24,1536]{1,0:T(8,128)(2,1)S(1)}, u32[]{:S(2)}, u32[]{:S(2)}) collective-permute-start(bf16[24,1536]{1,0:T(8,128)(2,1)S(1)} %get-tuple-element.84), channel_id=1, source_target_pairs={{0,48},{8,56},{16,32},{24,40},{32,16},{40,24},{48,0},{56,8},{1,49}... | collective-permute-start | bytes 221192 | tf_op jit(solution)/shard_map/ppermute | solution.py:402
  56.2 1.8 %collective-permute-start.16 = (bf16[24,1536]{1,0:T(8,128)(2,1)S(1)}, bf16[24,1536]{1,0:T(8,128)(2,1)S(1)}, u32[]{:S(2)}, u32[]{:S(2)}) collective-permute-start(bf16[24,1536]{1,0:T(8,128)(2,1)S(1)} %get-tuple-element.85), channel_id=1, source_target_pairs={{0,128},{64,192},{128,0},{192,64},{1,129},{65,193},{129,1},{193,65... | collective-permute-start | bytes 221192 | tf_op jit(solution)/shard_map/ppermute | solution.py:402
  58.1 1.1 %collective-permute-start.18 = (bf16[24,1536]{1,0:T(8,128)(2,1)S(1)}, bf16[24,1536]{1,0:T(8,128)(2,1)S(1)}, u32[]{:S(2)}, u32[]{:S(2)}) collective-permute-start(bf16[24,1536]{1,0:T(8,128)(2,1)S(1)} %get-tuple-element.86), channel_id=1, source_target_pairs={{0,64},{64,0},{128,192},{192,128},{1,65},{65,1},{129,193},{193,129... | collective-permute-start | bytes 221192 | tf_op jit(solution)/shard_map/ppermute | solution.py:402
  59.2 1.2 %collective-permute-start.17 = (bf16[24,1536]{1,0:T(8,128)(2,1)S(1)}, bf16[24,1536]{1,0:T(8,128)(2,1)S(1)}, u32[]{:S(2)}, u32[]{:S(2)}) collective-permute-start(bf16[24,1536]{1,0:T(8,128)(2,1)S(1)} %get-tuple-element.87), channel_id=1, source_target_pairs={{0,192},{64,128},{128,64},{192,0},{1,193},{65,129},{129,65},{193,1... | collective-permute-start | bytes 221192 | tf_op jit(solution)/shard_map/ppermute | solution.py:402
  60.5 1.7 %collective-permute-done.16 = bf16[24,1536]{1,0:T(8,128)(2,1)S(1)} collective-permute-done((bf16[24,1536]{1,0:T(8,128)(2,1)S(1)}, bf16[24,1536]{1,0:T(8,128)(2,1)S(1)}, u32[]{:S(2)}, u32[]{:S(2)}) %collective-permute-start.16) | collective-permute-done | bytes 73760 | tf_op jit(solution)/shard_map/ppermute | solution.py:402
  62.4 2.3 %collective-permute-done.17 = bf16[24,1536]{1,0:T(8,128)(2,1)S(1)} collective-permute-done((bf16[24,1536]{1,0:T(8,128)(2,1)S(1)}, bf16[24,1536]{1,0:T(8,128)(2,1)S(1)}, u32[]{:S(2)}, u32[]{:S(2)}) %collective-permute-start.17) | collective-permute-done | bytes 73760 | tf_op jit(solution)/shard_map/ppermute | solution.py:402
  64.9 13.4 %all_to_all.5.parts_ref = bf16[8,3,3072]{2,1,0:T(4,128)(2,1)S(1)} all-to-all(bf16[8,3,3072]{2,1,0:T(4,128)(2,1)S(1)} %reshape.81), channel_id=1, replica_groups=mesh['dp'=4,'gy'=8,'gx'=8] {'gx'}, dimensions={0} | all-to-all | bytes 294912 | tf_op jit(solution)/shard_map/all_to_all | solution.py:448
  78.3 0.6 finish.1
  (49 shorter events, 2.2 us)
Async XLA Ops:
  0.6 1.1 %copy-start.1 = (bf16[1,16,32,768]{3,2,1,0:T(8,128)(2,1)S(1)}, bf16[1,16,32,768]{3,2,1,0:T(8,128)(2,1)}, u32[]{:S(2)}) copy-start(bf16[1,16,32,768]{3,2,1,0:T(8,128)(2,1)} %param.5) | copy-start | bytes 2359300
  1.8 9.8 %copy-start.3 = (bf16[768,768]{1,0:T(8,128)(2,1)S(1)}, bf16[768,768]{1,0:T(8,128)(2,1)}, u32[]{:S(2)}) copy-start(bf16[768,768]{1,0:T(8,128)(2,1)} %wp_ref.1) | copy-start | bytes 3538948
  1.8 9.8 %copy-start.4 = (bf16[1,16,32,768]{3,2,1,0:T(8,128)(2,1)S(1)}, bf16[1,16,32,768]{3,2,1,0:T(8,128)(2,1)}, u32[]{:S(2)}) copy-start(bf16[1,16,32,768]{3,2,1,0:T(8,128)(2,1)} %param.6) | copy-start | bytes 2359300
  1.8 9.8 %copy-start.5 = (s32[1,16,32]{2,1,0:T(8,128)S(1)}, s32[1,16,32]{2,1,0:T(8,128)}, u32[]{:S(2)}) copy-start(s32[1,16,32]{2,1,0:T(8,128)} %param.7) | copy-start | bytes 6148
  1.8 11.3 %collective-permute-start.2 = (bf16[8,8,768]{2,1,0:T(8,128)(2,1)S(1)}, bf16[8,8,768]{2,1,0:T(8,128)(2,1)S(1)}, u32[]{:S(2)}, u32[]{:S(2)}) collective-permute-start(bf16[8,8,768]{2,1,0:T(8,128)(2,1)S(1)} %corner.1.after_ref), channel_id=1, source_target_pairs={{0,63},{1,56},{2,57},{3,58},{4,59},{5,60},{6,61},{7,62},{8,7},{9,0... | collective-permute-start | bytes 294920 | tf_op jit(solution)/shard_map/ppermute | solution.py:465
  9.7 5.6 %collective-permute-start = (bf16[8,24,768]{2,1,0:T(8,128)(2,1)S(1)}, bf16[8,24,768]{2,1,0:T(8,128)(2,1)S(1)}, u32[]{:S(2)}, u32[]{:S(2)}) collective-permute-start(bf16[8,24,768]{2,1,0:T(8,128)(2,1)S(1)} %above.1.after_ref), channel_id=1, source_target_pairs={{0,56},{8,0},{16,8},{24,16},{32,24},{40,32},{48,40},{56,48},{1,57}... | collective-permute-start | bytes 884744 | tf_op jit(solution)/shard_map/ppermute | solution.py:402
  10.5 4.7 %collective-permute-start.1 = (bf16[8,8,768]{2,1,0:T(8,128)(2,1)S(1)}, bf16[8,8,768]{2,1,0:T(8,128)(2,1)S(1)}, u32[]{:S(2)}, u32[]{:S(2)}) collective-permute-start(bf16[8,8,768]{2,1,0:T(8,128)(2,1)S(1)} %left.1), channel_id=1, source_target_pairs={{0,7},{1,0},{2,1},{3,2},{4,3},{5,4},{6,5},{7,6},{8,15},{9,8},{10,9... | collective-permute-start | bytes 294920 | tf_op jit(solution)/shard_map/ppermute | solution.py:402
  11.6 3.6 %copy-start = (bf16[768,2304]{1,0:T(8,128)(2,1)S(1)}, bf16[768,2304]{1,0:T(8,128)(2,1)}, u32[]{:S(2)}) copy-start(bf16[768,2304]{1,0:T(8,128)(2,1)} %wv_ref.5) | copy-start | bytes 10616836
  11.6 3.6 %copy-start.2 = (bf16[1,16,32,768]{3,2,1,0:T(8,128)(2,1)S(1)}, bf16[1,16,32,768]{3,2,1,0:T(8,128)(2,1)}, u32[]{:S(2)}) copy-start(bf16[1,16,32,768]{3,2,1,0:T(8,128)(2,1)} %param.5) | copy-start | bytes 2359300
  23.6 5.0 %collective-permute-start.3 = (bf16[384,1536]{1,0:T(8,128)(2,1)S(1)}, bf16[384,1536]{1,0:T(8,128)(2,1)S(1)}, u32[]{:S(2)}, u32[]{:S(2)}) collective-permute-start(bf16[384,1536]{1,0:T(8,128)(2,1)S(1)} %get-tuple-element.44), channel_id=1, source_target_pairs={{0,8},{8,0},{16,24},{24,16},{32,40},{40,32},{48,56},{56,48},{1,9},... | collective-permute-start | bytes 3538952 | tf_op jit(solution)/shard_map/ppermute | solution.py:402
  28.5 3.1 %collective-permute-start.4 = (bf16[384,1536]{1,0:T(8,128)(2,1)S(1)}, bf16[384,1536]{1,0:T(8,128)(2,1)S(1)}, u32[]{:S(2)}, u32[]{:S(2)}) collective-permute-start(bf16[384,1536]{1,0:T(8,128)(2,1)S(1)} %get-tuple-element.46), channel_id=1, source_target_pairs={{0,8},{8,0},{16,24},{24,16},{32,40},{40,32},{48,56},{56,48},{1,9},... | collective-permute-start | bytes 3538952 | tf_op jit(solution)/shard_map/ppermute | solution.py:402
  29.4 12.9 %collective-permute-start.9 = (bf16[96,768]{1,0:T(8,128)(2,1)S(1)}, bf16[96,768]{1,0:T(8,128)(2,1)S(1)}, u32[]{:S(2)}, u32[]{:S(2)}) collective-permute-start(bf16[96,768]{1,0:T(8,128)(2,1)S(1)} %get-tuple-element.76), channel_id=1, source_target_pairs={{0,64},{64,0},{128,192},{192,128},{1,65},{65,1},{129,193},{193,129... | collective-permute-start | bytes 442376 | tf_op jit(solution)/shard_map/ppermute | solution.py:402
  30.4 13.6 %collective-permute-start.7 = (bf16[96,768]{1,0:T(8,128)(2,1)S(1)}, bf16[96,768]{1,0:T(8,128)(2,1)S(1)}, u32[]{:S(2)}, u32[]{:S(2)}) collective-permute-start(bf16[96,768]{1,0:T(8,128)(2,1)S(1)} %get-tuple-element.77), channel_id=1, source_target_pairs={{0,192},{64,128},{128,64},{192,0},{1,193},{65,129},{129,65},{193,1... | collective-permute-start | bytes 442376 | tf_op jit(solution)/shard_map/ppermute | solution.py:402
  31.9 7.4 %collective-permute-start.6 = (bf16[96,768]{1,0:T(8,128)(2,1)S(1)}, bf16[96,768]{1,0:T(8,128)(2,1)S(1)}, u32[]{:S(2)}, u32[]{:S(2)}) collective-permute-start(bf16[96,768]{1,0:T(8,128)(2,1)S(1)} %get-tuple-element.74), channel_id=1, source_target_pairs={{0,48},{8,56},{16,32},{24,40},{32,16},{40,24},{48,0},{56,8},{1,49}... | collective-permute-start | bytes 442376 | tf_op jit(solution)/shard_map/ppermute | solution.py:402
  34.9 5.6 %collective-permute-start.5 = (bf16[96,768]{1,0:T(8,128)(2,1)S(1)}, bf16[96,768]{1,0:T(8,128)(2,1)S(1)}, u32[]{:S(2)}, u32[]{:S(2)}) collective-permute-start(bf16[96,768]{1,0:T(8,128)(2,1)S(1)} %get-tuple-element.75), channel_id=1, source_target_pairs={{0,16},{8,24},{16,0},{24,8},{32,48},{40,56},{48,32},{56,40},{1,17}... | collective-permute-start | bytes 442376 | tf_op jit(solution)/shard_map/ppermute | solution.py:402
  40.6 8.8 %collective-permute-start.11 = (bf16[96,1536]{1,0:T(8,128)(2,1)S(1)}, bf16[96,1536]{1,0:T(8,128)(2,1)S(1)}, u32[]{:S(2)}, u32[]{:S(2)}) collective-permute-start(bf16[96,1536]{1,0:T(8,128)(2,1)S(1)} %pad_maximum_fusion.2), channel_id=1, source_target_pairs={{0,16},{8,24},{16,0},{24,8},{32,48},{40,56},{48,32},{56,40},{1,17}... | collective-permute-start | bytes 884744 | tf_op jit(solution)/shard_map/ppermute | solution.py:402
  41.0 9.2 %collective-permute-start.12 = (bf16[96,1536]{1,0:T(8,128)(2,1)S(1)}, bf16[96,1536]{1,0:T(8,128)(2,1)S(1)}, u32[]{:S(2)}, u32[]{:S(2)}) collective-permute-start(bf16[96,1536]{1,0:T(8,128)(2,1)S(1)} %pad_maximum_fusion.3), channel_id=1, source_target_pairs={{0,48},{8,56},{16,32},{24,40},{32,16},{40,24},{48,0},{56,8},{1,49}... | collective-permute-start | bytes 884744 | tf_op jit(solution)/shard_map/ppermute | solution.py:402
  42.4 9.2 %collective-permute-start.10 = (bf16[96,1536]{1,0:T(8,128)(2,1)S(1)}, bf16[96,1536]{1,0:T(8,128)(2,1)S(1)}, u32[]{:S(2)}, u32[]{:S(2)}) collective-permute-start(bf16[96,1536]{1,0:T(8,128)(2,1)S(1)} %pad_maximum_fusion.1), channel_id=1, source_target_pairs={{0,192},{64,128},{128,64},{192,0},{1,193},{65,129},{129,65},{193,1... | collective-permute-start | bytes 884744 | tf_op jit(solution)/shard_map/ppermute | solution.py:402
  44.1 7.7 %collective-permute-start.8 = (bf16[96,1536]{1,0:T(8,128)(2,1)S(1)}, bf16[96,1536]{1,0:T(8,128)(2,1)S(1)}, u32[]{:S(2)}, u32[]{:S(2)}) collective-permute-start(bf16[96,1536]{1,0:T(8,128)(2,1)S(1)} %pad_maximum_fusion), channel_id=1, source_target_pairs={{0,64},{64,0},{128,192},{192,128},{1,65},{65,1},{129,193},{193,129... | collective-permute-start | bytes 884744 | tf_op jit(solution)/shard_map/ppermute | solution.py:402
  52.0 7.2 %collective-permute-start.13 = (bf16[24,1536]{1,0:T(8,128)(2,1)S(1)}, bf16[24,1536]{1,0:T(8,128)(2,1)S(1)}, u32[]{:S(2)}, u32[]{:S(2)}) collective-permute-start(bf16[24,1536]{1,0:T(8,128)(2,1)S(1)} %get-tuple-element.82), channel_id=1, source_target_pairs={{0,32},{8,40},{16,48},{24,56},{32,0},{40,8},{48,16},{56,24},{1,33}... | collective-permute-start | bytes 221192 | tf_op jit(solution)/shard_map/ppermute | solution.py:402
  54.1 6.3 %collective-permute-start.15 = (bf16[24,1536]{1,0:T(8,128)(2,1)S(1)}, bf16[24,1536]{1,0:T(8,128)(2,1)S(1)}, u32[]{:S(2)}, u32[]{:S(2)}) collective-permute-start(bf16[24,1536]{1,0:T(8,128)(2,1)S(1)} %get-tuple-element.83), channel_id=1, source_target_pairs={{0,16},{8,24},{16,0},{24,8},{32,48},{40,56},{48,32},{56,40},{1,17}... | collective-permute-start | bytes 221192 | tf_op jit(solution)/shard_map/ppermute | solution.py:402
  54.7 5.7 %collective-permute-start.14 = (bf16[24,1536]{1,0:T(8,128)(2,1)S(1)}, bf16[24,1536]{1,0:T(8,128)(2,1)S(1)}, u32[]{:S(2)}, u32[]{:S(2)}) collective-permute-start(bf16[24,1536]{1,0:T(8,128)(2,1)S(1)} %get-tuple-element.84), channel_id=1, source_target_pairs={{0,48},{8,56},{16,32},{24,40},{32,16},{40,24},{48,0},{56,8},{1,49}... | collective-permute-start | bytes 221192 | tf_op jit(solution)/shard_map/ppermute | solution.py:402
  56.2 5.9 %collective-permute-start.16 = (bf16[24,1536]{1,0:T(8,128)(2,1)S(1)}, bf16[24,1536]{1,0:T(8,128)(2,1)S(1)}, u32[]{:S(2)}, u32[]{:S(2)}) collective-permute-start(bf16[24,1536]{1,0:T(8,128)(2,1)S(1)} %get-tuple-element.85), channel_id=1, source_target_pairs={{0,128},{64,192},{128,0},{192,64},{1,129},{65,193},{129,1},{193,65... | collective-permute-start | bytes 221192 | tf_op jit(solution)/shard_map/ppermute | solution.py:402
  58.1 4.4 %collective-permute-start.18 = (bf16[24,1536]{1,0:T(8,128)(2,1)S(1)}, bf16[24,1536]{1,0:T(8,128)(2,1)S(1)}, u32[]{:S(2)}, u32[]{:S(2)}) collective-permute-start(bf16[24,1536]{1,0:T(8,128)(2,1)S(1)} %get-tuple-element.86), channel_id=1, source_target_pairs={{0,64},{64,0},{128,192},{192,128},{1,65},{65,1},{129,193},{193,129... | collective-permute-start | bytes 221192 | tf_op jit(solution)/shard_map/ppermute | solution.py:402
  59.2 5.6 %collective-permute-start.17 = (bf16[24,1536]{1,0:T(8,128)(2,1)S(1)}, bf16[24,1536]{1,0:T(8,128)(2,1)S(1)}, u32[]{:S(2)}, u32[]{:S(2)}) collective-permute-start(bf16[24,1536]{1,0:T(8,128)(2,1)S(1)} %get-tuple-element.87), channel_id=1, source_target_pairs={{0,192},{64,128},{128,64},{192,0},{1,193},{65,129},{129,65},{193,1... | collective-permute-start | bytes 221192 | tf_op jit(solution)/shard_map/ppermute | solution.py:402

commit v12 on v11

--- a/solution.py
+++ b/solution.py
@@ -38,11 +38,11 @@
     return pl.CostEstimate(flops=int(flops), bytes_accessed=int(size), transcendentals=0)
 
 
-def corner_kernel(tiles_ref, corner_ref):
+def corner_kernel(tiles_ref, after_ref, corner_ref):
     corner_ref[...] = tiles_ref[...].astype(F32)[:, :8].astype(BF)
 
 
-def above_kernel(tiles_ref, after_ref, above_ref):
+def above_kernel(tiles_ref, above_ref):
     above_ref[...] = tiles_ref[...].astype(F32)[:, 8:].astype(BF)
 
 
@@ -65,9 +65,9 @@
 
 
 def edges(tiles):
-    corner = cut(corner_kernel, "corner", 3e10, tiles, [], (8, 16), 0, 8)
-    above = cut(above_kernel, "above", 1e3, tiles, [corner], (8, 32), 0, 24)
-    left = cut(left_kernel, "left", 1e3, tiles, [above], (8, 16), 1, 8)
+    above = cut(above_kernel, "above", 3e10, tiles, [], (8, 32), 0, 24)
+    corner = cut(corner_kernel, "corner", 1e3, tiles, [above], (8, 16), 0, 8)
+    left = cut(left_kernel, "left", 1e3, tiles, [corner], (8, 16), 1, 8)
     return above, left, corner
 
 
@@ -149,18 +149,99 @@
     send_ref[...] = grad[D // 2 :].astype(BF)
 
 
-def heads_group(
-    hid_ref, hid_t_ref, tis_ref, live_ref, wq_ref, wk_ref, wv_ref, da_ref,
-    keep_ref, send_ref, att_ref, dqkv_ref, y_first,
+def attention(units, q, k, v, da, live, store):
+    lane = lax.broadcasted_iota(jnp.int32, (1, 128), 1)
+    sel = [(lane < 64).astype(BF), (lane >= 64).astype(BF)]
+    weight, ds, rinv, att = {}, {}, {}, {}
+    for u in units:
+        for h in range(2):
+            weight[u, h] = jnp.exp(nt(q[u], k[u] * sel[h])).astype(BF)
+    for u in units:
+        both = nn(weight[u, 0], jnp.concatenate([v[u] * sel[0], live[u] * sel[0]], 1)) + nn(
+            weight[u, 1], jnp.concatenate([v[u] * sel[1], live[u] * sel[1]], 1)
+        )
+        rinv[u] = 1.0 / both[:, 128:]
+        att[u] = both[:, :128] * rinv[u]
+    for u in units:
+        terms = da[u].astype(F32) * att[u]
+        for h in range(2):
+            delta = jnp.sum(terms * sel[h].astype(F32), 1, keepdims=True)
+            dprobs = nt(da[u], v[u] * sel[h]) - delta
+            ds[u, h] = (weight[u, h].astype(F32) * dprobs).astype(BF)
+    for u in units:
+        dq = (nn(ds[u, 0], k[u] * sel[0]) + nn(ds[u, 1], k[u] * sel[1])) * (rinv[u] * HEAD_SCALE)
+        dan = (da[u].astype(F32) * rinv[u]).astype(BF)
+        qn = (q[u].astype(F32) * rinv[u]).astype(BF)
+        dv = tn(weight[u, 0], dan * sel[0]) + tn(weight[u, 1], dan * sel[1])
+        dk = tn(ds[u, 0], qn * sel[0]) + tn(ds[u, 1], qn * sel[1])
+        store(u, att[u].astype(BF), (dq.astype(BF), dk.astype(BF), dv.astype(BF)))
+
+
+def window_heads(w, x, tis_ref, live_ref, weights, da_ref, outs):
+    att_ref, dqkv_ref, xw_ref, hid_ref, hid_t_ref = outs
+    tis = tis_ref[w]
+    xw_ref[...] = x.astype(BF)
+    normed, _ = moments(x)
+    hidden = normed.astype(BF)
+    hid_ref[...] = hidden
+    hid_t_ref[...] = nt(row_order(), hidden * jnp.tile(tis, (1, D // 128))).astype(BF)
+    units = [(g, p) for g in range(2) for p in range(2)]
+    q, k, v, da = {}, {}, {}, {}
+    for g in range(2):
+        query = nn(hidden, weights[g][...]).astype(BF) * BF(HEAD_SCALE)
+        key = nn(hidden, weights[2 + g][...]).astype(BF)
+        value = nn(hidden, weights[4 + g][...]).astype(BF)
+        for p in range(2):
+            lanes = slice(p * 128, (p + 1) * 128)
+            q[g, p] = query[:, lanes]
+            k[g, p] = key[:, lanes] * tis
+            v[g, p] = value[:, lanes] * tis
+            da[g, p] = da_ref[w, :, g * GW + p * 128 : g * GW + (p + 1) * 128]
+
+    def store(u, att, grads):
+        g, p = u
+        att_ref[:, g * GW + p * 128 : g * GW + (p + 1) * 128] = att
+        for i, grad in enumerate(grads):
+            dqkv_ref[g, :, i * GW + p * 128 : i * GW + (p + 1) * 128] = grad
+
+    attention(units, q, k, v, da, {u: live_ref[w] for u in units}, store)
+
+
+def left_window_kernel(
+    tiles_ref, below_ref, tis_ref, live_ref, w0, w1, w2, w3, w4, w5, da_ref, *outs
 ):
-    hidden = hid_ref[...].reshape(2 * CELLS, D)
+    own = tiles_ref[8:16].astype(F32)
+    low = below_ref[...].astype(F32)
+    x = jnp.concatenate([own[:, 8:24], low[:, :16]], 0).reshape(CELLS, D)
+    window_heads(0, x, tis_ref, live_ref, (w0, w1, w2, w3, w4, w5), da_ref, outs)
+
+
+def right_window_kernel(
+    tiles_ref, below_ref, right_ref, diag_ref, hid_t0_ref, dqkv0_ref,
+    tis_ref, live_ref, w0, w1, w2, w3, w4, w5, da_ref, keep_ref, send_ref, *outs
+):
+    own = tiles_ref[8:16].astype(F32)
+    low = below_ref[...].astype(F32)
+    top = jnp.concatenate([own[:, 24:32], right_ref[...].astype(F32)], 1)
+    bottom = jnp.concatenate([low[:, 16:24], diag_ref[...].astype(F32)], 1)
+    x = jnp.concatenate([top, bottom], 0).reshape(CELLS, D)
+    window_heads(1, x, tis_ref, live_ref, (w0, w1, w2, w3, w4, w5), da_ref, outs)
+    dqkv_ref, hid_t_ref = outs[1], outs[4]
+    for g in range(2):
+        grad = nn(hid_t0_ref[...], dqkv0_ref[g]) + nn(hid_t_ref[...], dqkv_ref[g])
+        put(grad, keep_ref.at[:, g * D : (g + 1) * D], send_ref.at[:, g * D : (g + 1) * D], False)
+
+
+def last_kernel(
+    hid0_ref, hid1_ref, hid_t0_ref, hid_t1_ref, tis_ref, live_ref, wq_ref, wk_ref, wv_ref, da_ref,
+    att0_ref, att1_ref, db_ref, keep_ref, send_ref, att_ref, dqkv_ref,
+):
+    hidden = jnp.concatenate([hid0_ref[...], hid1_ref[...]], 0)
     query = nn(hidden, wq_ref[...]).astype(BF) * BF(HEAD_SCALE)
     key = nn(hidden, wk_ref[...]).astype(BF)
     value = nn(hidden, wv_ref[...]).astype(BF)
-    lane = lax.broadcasted_iota(jnp.int32, (1, 128), 1)
-    sel = [(lane < 64).astype(BF), (lane >= 64).astype(BF)]
     units = [(w, p) for w in range(2) for p in range(2)]
-    q, k, v, da, weight, ds, rinv, att = {}, {}, {}, {}, {}, {}, {}, {}
+    q, k, v, da, live = {}, {}, {}, {}, {}
     for u in units:
         w, p = u
         rows, lanes = slice(w * CELLS, (w + 1) * CELLS), slice(p * 128, (p + 1) * 128)
@@ -168,78 +249,19 @@
         k[u] = key[rows, lanes] * tis_ref[w]
         v[u] = value[rows, lanes] * tis_ref[w]
         da[u] = da_ref[w, :, lanes]
-    for u in units:
-        for h in range(2):
-            weight[u, h] = jnp.exp(nt(q[u], k[u] * sel[h])).astype(BF)
-    for u in units:
-        live = live_ref[u[0]]
-        both = nn(weight[u, 0], jnp.concatenate([v[u] * sel[0], live * sel[0]], 1)) + nn(
-            weight[u, 1], jnp.concatenate([v[u] * sel[1], live * sel[1]], 1)
-        )
-        rinv[u] = 1.0 / both[:, 128:]
-        att[u] = both[:, :128] * rinv[u]
-        att_ref[u[0], :, u[1] * 128 : (u[1] + 1) * 128] = att[u].astype(BF)
-    for u in units:
-        terms = da[u].astype(F32) * att[u]
-        for h in range(2):
-            delta = jnp.sum(terms * sel[h].astype(F32), 1, keepdims=True)
-            dprobs = nt(da[u], v[u] * sel[h]) - delta
-            ds[u, h] = (weight[u, h].astype(F32) * dprobs).astype(BF)
-    for u in units:
+        live[u] = live_ref[w]
+
+    def store(u, att, grads):
         w, p = u
-        dq = (nn(ds[u, 0], k[u] * sel[0]) + nn(ds[u, 1], k[u] * sel[1])) * (rinv[u] * HEAD_SCALE)
-        dan = (da[u].astype(F32) * rinv[u]).astype(BF)
-        qn = (q[u].astype(F32) * rinv[u]).astype(BF)
-        dv = tn(weight[u, 0], dan * sel[0]) + tn(weight[u, 1], dan * sel[1])
-        dk = tn(ds[u, 0], qn * sel[0]) + tn(ds[u, 1], qn * sel[1])
-        for i, grad in enumerate((dq, dk, dv)):
-            at = i * GW + p * 128
-            dqkv_ref[0, w, :, at : at + 128] = grad.astype(BF)
-    grad = nn(hid_t_ref[...], dqkv_ref[0].reshape(2 * CELLS, D))
-    put(grad, keep_ref, send_ref, y_first)
-
-
-def first_kernel(
-    tiles_ref, below_ref, right_ref, diag_ref, tis_ref, live_ref,
-    wq_ref, wk_ref, wv_ref, da_ref,
-    keep_ref, send_ref, att_ref, dqkv_ref, xw_ref, hid_ref, hid_t_ref,
-):
-    @pl.when(pl.program_id(0) == 0)
-    def _():
-        own = tiles_ref[8:16].astype(F32)
-        low = below_ref[...].astype(F32)
-        right = right_ref[...].astype(F32)
-        diag = diag_ref[...].astype(F32)
-        perm = row_order()
-        for w in range(2):
-            if w == 0:
-                top, bottom = own[:, 8:24], low[:, :16]
-            else:
-                top = jnp.concatenate([own[:, 24:32], right], 1)
-                bottom = jnp.concatenate([low[:, 16:24], diag], 1)
-            x = jnp.concatenate([top, bottom], 0).reshape(CELLS, D)
-            xw_ref[w] = x.astype(BF)
-            normed, _ = moments(x)
-            hidden = normed.astype(BF)
-            hid_ref[w] = hidden
-            masked = hidden * jnp.tile(tis_ref[w], (1, D // 128))
-            hid_t_ref[:, w * CELLS : (w + 1) * CELLS] = nt(perm, masked).astype(BF)
-
-    heads_group(
-        hid_ref, hid_t_ref, tis_ref, live_ref, wq_ref, wk_ref, wv_ref, da_ref,
-        keep_ref, send_ref, att_ref, dqkv_ref, False,
-    )
-
-
-def last_kernel(
-    hid_ref, hid_t_ref, tis_ref, live_ref, wq_ref, wk_ref, wv_ref, da_ref, att0_ref, db_ref,
-    keep_ref, send_ref, att_ref, dqkv_ref,
-):
-    heads_group(
-        hid_ref, hid_t_ref, tis_ref, live_ref, wq_ref, wk_ref, wv_ref, da_ref,
-        keep_ref.at[:, :D], send_ref.at[:, :D], att_ref, dqkv_ref, True,
-    )
-    attended = jnp.concatenate([att0_ref[...], att_ref[...]], 2).reshape(2 * CELLS, D)
+        att_ref[w, :, p * 128 : (p + 1) * 128] = att
+        for i, grad in enumerate(grads):
+            dqkv_ref[w, :, i * GW + p * 128 : i * GW + (p + 1) * 128] = grad
+
+    attention(units, q, k, v, da, live, store)
+    grad = nn(hid_t0_ref[...], dqkv_ref[0]) + nn(hid_t1_ref[...], dqkv_ref[1])
+    put(grad, keep_ref.at[:, :D], send_ref.at[:, :D], True)
+    first = jnp.concatenate([att0_ref[...], att1_ref[...]], 0)
+    attended = jnp.concatenate([first, att_ref[...].reshape(2 * CELLS, GW)], 1)
     att_t = nt(row_order(), attended).astype(BF)
     grad = nn(att_t, db_ref[...].reshape(2 * CELLS, D))
     put(grad, keep_ref.at[:, D:], send_ref.at[:, D:], True)
@@ -249,98 +271,107 @@
     return pl.BlockSpec((D, GW), lambda g: (0, block * GROUPS + first + g))
 
 
-def heads_specs(first, groups):
-    inputs = [
-        full((2, CELLS, 128)), full((2, CELLS, 128)),
-        columns(0, first), columns(1, first), columns(2, first),
-        pl.BlockSpec((2, CELLS, GW), lambda g: (0, 0, first + g)),
-    ]
-    half = pl.BlockSpec((D // 2, D), lambda g: (0, g))
-    outputs = [
-        half, half,
-        pl.BlockSpec((2, CELLS, GW), lambda g: (0, 0, g)),
-        pl.BlockSpec((1, 2, CELLS, D), lambda g: (g, 0, 0, 0)),
-    ]
-    shapes = [
-        jax.ShapeDtypeStruct((D // 2, groups * D), BF),
-        jax.ShapeDtypeStruct((D // 2, groups * D), BF),
-        jax.ShapeDtypeStruct((2, CELLS, groups * GW), BF),
-        jax.ShapeDtypeStruct((groups, 2, CELLS, D), BF),
-    ]
-    return inputs, outputs, shapes
-
-
-def first_heads(tiles, below, right, diag, tis, live, w_qkv, da):
-    inputs, outputs, shapes = heads_specs(0, 2)
-    rows = jax.ShapeDtypeStruct((2, CELLS, D), BF)
+def window_specs():
+    shapes = [(CELLS, 2 * GW), (2, CELLS, D), (CELLS, D), (CELLS, D), (D, CELLS)]
+    masks = [full((2, CELLS, 128))] * 2
+    weights = [columns(block, g) for block in range(3) for g in range(2)]
+    inputs = masks + weights + [full((2, CELLS, D))]
+    return inputs, [full(s) for s in shapes], [jax.ShapeDtypeStruct(s, BF) for s in shapes]
+
+
+def left_window(tiles, below, tis, live, w_qkv, da):
+    inputs, outputs, shapes = window_specs()
     return pl.pallas_call(
-        first_kernel,
-        grid=(2,),
-        in_specs=[full((16, 32, D)), full((8, 24, D)), full((8, 8, D)), full((8, 8, D))] + inputs,
-        out_specs=outputs + [full((2, CELLS, D))] * 2 + [full((D, 2 * CELLS))],
-        out_shape=shapes + [rows, rows, jax.ShapeDtypeStruct((D, 2 * CELLS), BF)],
-        compiler_params=pltpu.CompilerParams(vmem_limit_bytes=VMEM),
-        cost_estimate=cost(6e9, 10e6),
-        name="first_heads",
-    )(tiles, below, right, diag, tis, live, w_qkv, w_qkv, w_qkv, da)
-
-
-def last_heads(hid, hid_t, tis, live, w_qkv, da, att0, db):
-    inputs, outputs, shapes = heads_specs(2, 1)
-    half = jax.ShapeDtypeStruct((D // 2, 2 * D), BF)
-    rows = full((2, CELLS, D))
+        left_window_kernel,
+        grid=(1,),
+        in_specs=[full((16, 32, D)), full((8, 24, D))] + inputs,
+        out_specs=outputs,
+        out_shape=shapes,
+        compiler_params=pltpu.CompilerParams(vmem_limit_bytes=VMEM),
+        cost_estimate=cost(3e9, 5e6),
+        name="left_window",
+    )(tiles, below, tis, live, *[w_qkv] * 6, da)
+
+
+def right_window(tiles, below, right, diag, hid_t0, dqkv0, tis, live, w_qkv, da):
+    inputs, outputs, shapes = window_specs()
+    half = full((D // 2, 2 * D))
+    half_shape = jax.ShapeDtypeStruct((D // 2, 2 * D), BF)
+    return pl.pallas_call(
+        right_window_kernel,
+        grid=(1,),
+        in_specs=[
+            full((16, 32, D)), full((8, 24, D)), full((8, 8, D)), full((8, 8, D)),
+            full((D, CELLS)), full((2, CELLS, D)),
+        ] + inputs,
+        out_specs=[half, half] + outputs,
+        out_shape=[half_shape, half_shape] + shapes,
+        compiler_params=pltpu.CompilerParams(vmem_limit_bytes=VMEM),
+        cost_estimate=cost(4e9, 6e6),
+        name="right_window",
+    )(tiles, below, right, diag, hid_t0, dqkv0, tis, live, *[w_qkv] * 6, da)
+
+
+def last_heads(hids, hid_ts, tis, live, w_qkv, da, atts, db):
+    rows, turned, masks = full((CELLS, D)), full((D, CELLS)), full((2, CELLS, 128))
+    part = full((CELLS, 2 * GW))
+    shapes = [(D // 2, 2 * D), (D // 2, 2 * D), (2, CELLS, GW), (2, CELLS, D)]
     return pl.pallas_call(
         last_kernel,
         grid=(1,),
-        in_specs=[rows, full((D, 2 * CELLS))] + inputs + [full((2, CELLS, 2 * GW)), rows],
-        out_specs=[full((D // 2, 2 * D))] * 2 + outputs[2:],
-        out_shape=[half, half] + shapes[2:],
+        in_specs=[
+            rows, rows, turned, turned, masks, masks, columns(0, 2), columns(1, 2), columns(2, 2),
+            pl.BlockSpec((2, CELLS, GW), lambda g: (0, 0, 2)), part, part, full((2, CELLS, D)),
+        ],
+        out_specs=[full(s) for s in shapes],
+        out_shape=[jax.ShapeDtypeStruct(s, BF) for s in shapes],
         compiler_params=pltpu.CompilerParams(vmem_limit_bytes=VMEM),
         cost_estimate=cost(4e9, 6e6),
         name="last_heads",
-    )(hid, hid_t, tis, live, w_qkv, w_qkv, w_qkv, da, att0, db)
-
-
-def out_kernel(xw_ref, tis_ref, att0_ref, att1_ref, wp_ref, out_ref):
-    for w in range(2):
+    )(*hids, *hid_ts, tis, live, w_qkv, w_qkv, w_qkv, da, *atts, db)
+
+
+def out_kernel(xw0_ref, xw1_ref, tis_ref, att0_ref, att1_ref, att2_ref, wp_ref, out_ref):
+    for w, (xw_ref, att_ref) in enumerate(((xw0_ref, att0_ref), (xw1_ref, att1_ref))):
         tis = jnp.tile(tis_ref[w].astype(F32), (1, D // 128))
-        attended = jnp.concatenate([att0_ref[w], att1_ref[w]], 1)
-        out = xw_ref[w].astype(F32) + tis * nn(attended, wp_ref[...])
+        attended = jnp.concatenate([att_ref[...], att2_ref[w]], 1)
+        out = xw_ref[...].astype(F32) + tis * nn(attended, wp_ref[...])
         out_ref[:, w] = out.astype(BF).reshape(WIN, WIN, D)
 
 
-def out_part(xw, tis, att0, att1, w_proj):
+def out_part(xws, tis, atts, att2, w_proj):
     out = pl.pallas_call(
         out_kernel,
         out_shape=jax.ShapeDtypeStruct((WIN, 2, WIN, D), BF),
         compiler_params=pltpu.CompilerParams(vmem_limit_bytes=VMEM),
         cost_estimate=cost(1e3, 1e3),
         name="out_part",
-    )(xw, tis, att0, att1, w_proj)
+    )(*xws, tis, *atts, att2, w_proj)
     return out.reshape(1, WIN, 2 * WIN, D)
 
 
 def grad_kernel(
-    xw_ref, cot_ref, tis_ref, dqkv0_ref, dqkv1_ref, wq_ref, wk_ref, wv_ref, grad_ref, acc_ref
+    xw0_ref, xw1_ref, cot_ref, tis_ref, dqkv0_ref, dqkv1_ref, dqkv2_ref,
+    wq_ref, wk_ref, wv_ref, grad_ref, acc_ref,
 ):
     step = pl.program_id(0)
     weights = jnp.concatenate([wq_ref[...], wk_ref[...], wv_ref[...]], 1)
-    dqkv = jnp.where(step < GROUPS - 1, dqkv0_ref[0], dqkv1_ref[0])
-    part = nt(dqkv.reshape(2 * CELLS, D), weights)
+    first = jnp.concatenate([dqkv0_ref[0], dqkv1_ref[0]], 0)
+    last = dqkv2_ref[...].reshape(2 * CELLS, D)
+    part = nt(jnp.where(step < GROUPS - 1, first, last), weights)
 
     @pl.when(step == 0)
     def _():
         acc_ref[...] = part
 
-    @pl.when((step > 0) & (step < GROUPS - 1))
+    @pl.when(step > 0)
     def _():
         acc_ref[...] += part
 
     @pl.when(step == GROUPS - 1)
     def _():
-        acc_ref[...] += part
-        for w in range(2):
-            normed, inv = moments(xw_ref[w].astype(F32))
+        for w, xw_ref in enumerate((xw0_ref, xw1_ref)):
+            normed, inv = moments(xw_ref[...].astype(F32))
             tis = jnp.tile(tis_ref[w].astype(F32), (1, D // 128))
             dh = acc_ref[w * CELLS : (w + 1) * CELLS] * tis
             dnorm = inv * (
@@ -352,15 +383,15 @@
             grad_ref[:, w] = grad.astype(BF).reshape(WIN, WIN, D)
 
 
-def grad_part(xw, cot, tis, dqkv0, dqkv1, w_qkv):
+def grad_part(xws, cot, tis, dqkvs, dqkv2, w_qkv):
+    part = pl.BlockSpec((1, CELLS, D), lambda g: (jnp.minimum(g, 1), 0, 0))
+    rows = full((CELLS, D))
     grad = pl.pallas_call(
         grad_kernel,
         grid=(GROUPS,),
         in_specs=[
-            full((2, CELLS, D)), full((WIN, 2, WIN, D)), full((2, CELLS, 128)),
-            pl.BlockSpec((1, 2, CELLS, D), lambda g: (jnp.minimum(g, 1), 0, 0, 0)),
-            full((1, 2, CELLS, D)),
-            columns(0, 0), columns(1, 0), columns(2, 0),
+            rows, rows, full((WIN, 2, WIN, D)), full((2, CELLS, 128)), part, part,
+            full((2, CELLS, D)), columns(0, 0), columns(1, 0), columns(2, 0),
         ],
         out_specs=full((WIN, 2, WIN, D)),
         out_shape=jax.ShapeDtypeStruct((WIN, 2, WIN, D), BF),
@@ -368,7 +399,7 @@
         compiler_params=pltpu.CompilerParams(vmem_limit_bytes=VMEM),
         cost_estimate=cost(1e3, 1e3),
         name="grad_part",
-    )(xw, cot, tis, dqkv0, dqkv1, w_qkv, w_qkv, w_qkv)
+    )(*xws, cot, tis, *dqkvs, dqkv2, w_qkv, w_qkv, w_qkv)
     return grad.reshape(1, WIN, 2 * WIN, D)
 
 
@@ -474,24 +505,27 @@
     cot = cotangent.reshape(WIN, 2, WIN, D)
     db, da, tis, live = branch(cot, tissue[0], w_proj)
     along_x, along_y = ("dp", (1, 3)), ("gy", (2, 6))
-    keep0, send0, att0, dqkv0, xw, hid, hid_t = first_heads(
-        mine, below, right, diag, tis, live, w_qkv, da
+    att0, dqkv0, xw0, hid0, hid_t0 = left_window(mine, below, tis, live, w_qkv, da)
+    keep0, send0, att1, dqkv1, xw1, hid1, hid_t1 = right_window(
+        mine, below, right, diag, hid_t0, dqkv0, tis, live, w_qkv, da
     )
     came = send(send0, "gy", lambda i: i ^ 1)
-    keep1, send1, att1, dqkv1 = last_heads(hid, hid_t, tis, live, w_qkv, da, att0, db)
+    keep1, send1, att2, dqkv2 = last_heads(
+        (hid0, hid1), (hid_t0, hid_t1), tis, live, w_qkv, da, (att0, att1), db
+    )
     came, send1 = tie(came, send1)
     first = add(keep0, came)
     low_a, high_a = blocks(first[:, :D]), blocks(first[:, D:])
     came_a = ring_start(low_a, high_a, *along_x)
     second = add(keep1, send(send1, "gy", lambda i: i ^ 1))
-    second, att1 = tie(second, att1)
+    second, att2 = tie(second, att2)
     low_b, high_b = blocks(second[:, :D]), blocks(second[:, D:])
     came_b = ring_start(low_b, high_b, *along_y)
-    out = out_part(xw, tis, att0, att1, w_proj)
-    came_b, out, xw, low_a, high_a = tie(came_b, out, xw, low_a, high_a)
+    out = out_part((xw0, xw1), tis, (att0, att1), att2, w_proj)
+    came_b, out, xw0, low_a, high_a = tie(came_b, out, xw0, low_a, high_a)
     came_b = ring_pass(low_b, high_b, came_b, *along_y)
     came_a = ring_pass(low_a, high_a, came_a, *along_x)
-    grad = grad_part(xw, cot, tis, dqkv0, dqkv1, w_qkv)
+    grad = grad_part((xw0, xw1), cot, tis, (dqkv0, dqkv1), dqkv2, w_qkv)
     came_a, came_b, grad = tie(came_a, came_b, grad)
     rows_a = ring_end(low_a, high_a, came_a)
     rows_b = ring_end(low_b, high_b, came_b)

time: 79.4 us -> 78.8 us (level)
  starting transfers between devices: 27.5 us -> 25.6 us
  blocking collectives: 13.4 us -> 15.2 us
  waiting for transfers between devices: 12.7 us -> 11.6 us
    all_to_all x1, blocking collectives: 13.4 us -> 15.2 us  [exchange(): return lax.all_to_all(rows, axis, 0, 0, axis_index_groups=groups)]
    ppermute x1, starting transfers between devices: 7.82 us -> 6.04 us  [shards(): lax.ppermute(corner, ('gy', 'gx'), [(a * nx + b, (a - 1) % ny * nx + (b -...]
    ppermute x18, waiting for transfers between devices: 12.7 us -> 11.6 us  [send(): lax.ppermute(value, axis, [(i, move(i) % devices) for i in range(devices)])]
    pallas_call x3 -> x4, Pallas kernels: 18.1 us -> 18 us  [the longest x1 5.11 us: grad_part(): pl.pallas_call(grad_kernel, grid=(GROUPS,), in_specs=[rows, rows, full((W...]
  transfers between devices with their start and end apart: 19 -> 19, of which waited for: 10 -> 7; matrix products, arithmetic and copies ran while one was open for 1% -> 1% of each run, Pallas kernels for 16% -> 21%
where the time goes in v12:
time: 78.8 us; the launch traced here: 78.4 us
  starting transfers between devices  25.6 us (32%)
  Pallas kernels  21.8 us (28%)
  blocking collectives  15.2 us (19%)
  waiting for transfers between devices  11.6 us (15%)
  local copies, waits for them, and re-layouts  2.07 us (3%)
  other arithmetic  1.15 us (1%)
  between operations  0.91 us (1%)
    ppermute x18, starting transfers between devices, send(): lax.ppermute(value, axis, [(i, move(i) % devices) for i in range(devices)])  19.6 us
    all_to_all x1, blocking collectives, exchange(): return lax.all_to_all(rows, axis, 0, 0, axis_index_groups=groups)  15.2 us
    ppermute x18, waiting for transfers between devices, send(): lax.ppermute(value, axis, [(i, move(i) % devices) for i in range(devices)])  11.6 us
    ppermute x1, starting transfers between devices, shards(): lax.ppermute(corner, ('gy', 'gx'), [(a * nx + b, (a - 1) % ny * nx + (b -...  6.04 us
    pallas_call x1, Pallas kernels, grad_part(): pl.pallas_call(grad_kernel, grid=(GROUPS,), in_specs=[rows, rows, full((W...  5.11 us
    pallas_call x1, Pallas kernels, last_heads(): pl.pallas_call(last_kernel, grid=(1,), in_specs=[rows, rows, turned, turn...  4.86 us
    pallas_call x1, Pallas kernels, right_window(): pl.pallas_call(right_window_kernel, grid=(1,), in_specs=[full((16, 32, D)...  4.63 us
    pallas_call x1, Pallas kernels, left_window(): pl.pallas_call(left_window_kernel, grid=(1,), in_specs=[full((16, 32, D))...  3.38 us
  transfers between devices with their start and end apart: 19, of which 7 were waited for; matrix products, arithmetic and copies ran while one was open for 1% of the time, Pallas kernels for 21%

profile of v12, /device:TPU:6, one launch (start us, length us, event | category | flops | bytes accessed | tf_op | source)
XLA Modules:
  0.0 78.4 jit_solution(6115517664632739272)
XLA Ops:
  0.6 1.1 %copy-done.1 = bf16[1,16,32,768]{3,2,1,0:T(8,128)(2,1)S(1)} copy-done((bf16[1,16,32,768]{3,2,1,0:T(8,128)(2,1)S(1)}, bf16[1,16,32,768]{3,2,1,0:T(8,128)(2,1)}, u32[]{:S(2)}) %copy-start.1) | copy-done | bytes 786456
  1.8 2.5 %collective-permute-start = (bf16[8,24,768]{2,1,0:T(8,128)(2,1)S(1)}, bf16[8,24,768]{2,1,0:T(8,128)(2,1)S(1)}, u32[]{:S(2)}, u32[]{:S(2)}) collective-permute-start(bf16[8,24,768]{2,1,0:T(8,128)(2,1)S(1)} %above.1.after_ref), channel_id=1, source_target_pairs={{0,56},{8,0},{16,8},{24,16},{32,24},{40,32},{48,40},{56,48},{1,57}... | collective-permute-start | bytes 884744 | tf_op jit(solution)/shard_map/ppermute | solution.py:433
  4.3 6.0 %collective-permute-start.2 = (bf16[8,8,768]{2,1,0:T(8,128)(2,1)S(1)}, bf16[8,8,768]{2,1,0:T(8,128)(2,1)S(1)}, u32[]{:S(2)}, u32[]{:S(2)}) collective-permute-start(bf16[8,8,768]{2,1,0:T(8,128)(2,1)S(1)} %corner.1.after_ref), channel_id=1, source_target_pairs={{0,63},{1,56},{2,57},{3,58},{4,59},{5,60},{6,61},{7,62},{8,7},{9,0... | collective-permute-start | bytes 294920 | tf_op jit(solution)/shard_map/ppermute | solution.py:496
  10.3 1.1 %collective-permute-start.1 = (bf16[8,8,768]{2,1,0:T(8,128)(2,1)S(1)}, bf16[8,8,768]{2,1,0:T(8,128)(2,1)S(1)}, u32[]{:S(2)}, u32[]{:S(2)}) collective-permute-start(bf16[8,8,768]{2,1,0:T(8,128)(2,1)S(1)} %left.1), channel_id=1, source_target_pairs={{0,7},{1,0},{2,1},{3,2},{4,3},{5,4},{6,5},{7,6},{8,15},{9,8},{10,9... | collective-permute-start | bytes 294920 | tf_op jit(solution)/shard_map/ppermute | solution.py:433
  11.5 1.5 %branch.1 = (bf16[2,256,768]{2,1,0:T(8,128)(2,1)S(1)}, bf16[2,256,768]{2,1,0:T(8,128)(2,1)S(1)}, bf16[2,256,128]{2,1,0:T(8,128)(2,1)S(1)}, bf16[2,256,128]{2,1,0:T(8,128)(2,1)S(1)}) custom-call(bf16[16,2,16,768]{3,2,1,0:T(8,128)(2,1)S(1)} %bitcast.28, s32[16,32]{1,0:T(8,128)S(1)} %bitcast.30, bf16[768,768]{1,0:T(8,128)(2,1)S(1)} %copy-done.3), custom_call_target="tpu_custom_call" | custom-call | flops 20000000000 | bytes 4000000 | tf_op jit(solution)/shard_map/branch/pallas_call | solution.py:107
  13.0 0.5 copy-done
  13.6 3.4 %left_window.1 = (bf16[256,512]{1,0:T(8,128)(2,1)S(1)}, bf16[2,256,768]{2,1,0:T(8,128)(2,1)S(1)}, bf16[256,768]{1,0:T(8,128)(2,1)S(1)}, bf16[256,768]{1,0:T(8,128)(2,1)S(1)}, bf16[768,256]{1,0:T(8,128)(2,1)S(1)}) custom-call(bf16[16,32,768]{2,1,0:T(8,128)(2,1)S(1)} %bitcast.26, bf16[8,24,768]{2,1,0:T(8,128)(2,1)S(1)} %collective-permute-done.below_ref, ...), custom_call_target="tpu_custom_call" | custom-call | flops 3000000000 | bytes 5000000 | tf_op jit(solution)/shard_map/left_window/pallas_call | solution.py:284
  17.0 4.6 %right_window.1 = (bf16[384,1536]{1,0:T(8,128)(2,1)S(1)}, bf16[384,1536]{1,0:T(8,128)(2,1)S(1)}, bf16[256,512]{1,0:T(8,128)(2,1)S(1)}, bf16[2,256,768]{2,1,0:T(8...) custom-call(bf16[16,32,768]{2,1,0:T(8,128)(2,1)S(1)} %bitcast.27, ...), custom_call_target="tpu_custom_call" | custom-call | flops 4000000000 | bytes 6000000 | tf_op jit(solution)/shard_map/right_window/pallas_call | solution.py:300
  21.9 4.9 %last_heads.1 = (bf16[384,1536]{1,0:T(8,128)(2,1)S(1)}, bf16[384,1536]{1,0:T(8,128)(2,1)S(1)}, bf16[2,256,256]{2,1,0:T(8,128)(2,1)S(1)}, bf16[2,256,768]{2,1,0:T(8,128)(2,1)S(1)}) custom-call(bf16[256,768]{1,0:T(8,128)(2,1)S(1)} %get-tuple-element.44.hid0_ref, bf16[256,768]{1,0:T(8,128)(2,1)S(1)} %get-tuple-element.47.hid1_ref, ...), custom_call_target="tpu_custom_call" | custom-call | flops 4000000000 | bytes 6000000 | tf_op jit(solution)/shard_map/last_heads/pallas_call | solution.py:319
  26.8 0.6 collective-permute-start.4
  27.7 0.9 %collective-permute-start.9 = (bf16[96,768]{1,0:T(8,128)(2,1)S(1)}, bf16[96,768]{1,0:T(8,128)(2,1)S(1)}, u32[]{:S(2)}, u32[]{:S(2)}) collective-permute-start(bf16[96,768]{1,0:T(8,128)(2,1)S(1)} %get-tuple-element.86), channel_id=1, source_target_pairs={{0,64},{64,0},{128,192},{192,128},{1,65},{65,1},{129,193},{193,129... | collective-permute-start | bytes 442376 | tf_op jit(solution)/shard_map/ppermute | solution.py:433
  28.6 1.1 %collective-permute-start.7 = (bf16[96,768]{1,0:T(8,128)(2,1)S(1)}, bf16[96,768]{1,0:T(8,128)(2,1)S(1)}, u32[]{:S(2)}, u32[]{:S(2)}) collective-permute-start(bf16[96,768]{1,0:T(8,128)(2,1)S(1)} %get-tuple-element.87), channel_id=1, source_target_pairs={{0,192},{64,128},{128,64},{192,0},{1,193},{65,129},{129,65},{193,1... | collective-permute-start | bytes 442376 | tf_op jit(solution)/shard_map/ppermute | solution.py:433
  30.2 0.8 %collective-permute-start.6 = (bf16[96,768]{1,0:T(8,128)(2,1)S(1)}, bf16[96,768]{1,0:T(8,128)(2,1)S(1)}, u32[]{:S(2)}, u32[]{:S(2)}) collective-permute-start(bf16[96,768]{1,0:T(8,128)(2,1)S(1)} %get-tuple-element.84), channel_id=1, source_target_pairs={{0,48},{8,56},{16,32},{24,40},{32,16},{40,24},{48,0},{56,8},{1,49}... | collective-permute-start | bytes 442376 | tf_op jit(solution)/shard_map/ppermute | solution.py:433
  31.1 1.7 %out_part.1 = bf16[16,2,16,768]{3,2,1,0:T(8,128)(2,1)} custom-call(bf16[256,768]{1,0:T(8,128)(2,1)S(1)} %get-tuple-element.68.xw0_ref, bf16[256,768]{1,0:T(8,128)(2,1)S(1)} %get-tuple-element.59.xw1_ref, bf16[2,256,128]{2,1,0:T(8,128)(2,1)S(1)} %get-tuple-element.41.tis_ref, bf16[256,512]{1,0:T(8,128)(2,1)S(1)} %get-tuple-element.49.att0_ref, ...), custom_call_target="tpu_custom_call" | custom-call | flops 1000 | bytes 1000 | tf_op jit(solution)/shard_map/out_part/pallas_call | solution.py:343
  32.8 4.8 %collective-permute-done.6 = bf16[96,768]{1,0:T(8,128)(2,1)S(1)} collective-permute-done((bf16[96,768]{1,0:T(8,128)(2,1)S(1)}, bf16[96,768]{1,0:T(8,128)(2,1)S(1)}, u32[]{:S(2)}, u32[]{:S(2)}) %collective-permute-start.6) | collective-permute-done | bytes 147488 | tf_op jit(solution)/shard_map/ppermute | solution.py:433
  37.9 2.1 %collective-permute-start.12 = (bf16[96,1536]{1,0:T(8,128)(2,1)S(1)}, bf16[96,1536]{1,0:T(8,128)(2,1)S(1)}, u32[]{:S(2)}, u32[]{:S(2)}) collective-permute-start(bf16[96,1536]{1,0:T(8,128)(2,1)S(1)} %pad_maximum_fusion.3), channel_id=1, source_target_pairs={{0,48},{8,56},{16,32},{24,40},{32,16},{40,24},{48,0},{56,8},{1,49}... | collective-permute-start | bytes 884744 | tf_op jit(solution)/shard_map/ppermute | solution.py:433
  40.1 1.2 %collective-permute-start.10 = (bf16[96,1536]{1,0:T(8,128)(2,1)S(1)}, bf16[96,1536]{1,0:T(8,128)(2,1)S(1)}, u32[]{:S(2)}, u32[]{:S(2)}) collective-permute-start(bf16[96,1536]{1,0:T(8,128)(2,1)S(1)} %pad_maximum_fusion.1), channel_id=1, source_target_pairs={{0,192},{64,128},{128,64},{192,0},{1,193},{65,129},{129,65},{193,1... | collective-permute-start | bytes 884744 | tf_op jit(solution)/shard_map/ppermute | solution.py:433
  41.3 0.6 collective-permute-start.8
  41.9 5.1 %grad_part.1 = bf16[16,2,16,768]{3,2,1,0:T(8,128)(2,1)} custom-call(bf16[256,768]{1,0:T(8,128)(2,1)S(1)} %get-tuple-element.68.xw0_ref, bf16[256,768]{1,0:T(8,128)(2,1)S(1)} %get-tuple-element.59.xw1_ref, bf16[16,2,16,768]{3,2,1,0:T(8,128)(2,1)S(1)} %bitcast.29, bf16[2,256,128]{2,1,0:T(8,128)(2,1)S(1)} %get-tuple-element.41.tis_ref, ...), custom_call_target="tpu_custom_call" | custom-call | flops 1000 | bytes 1000 | tf_op jit(solution)/shard_map/grad_part/pallas_call | solution.py:389
  47.0 0.6 collective-permute-done.12
  47.6 1.6 %collective-permute-done.10 = bf16[96,1536]{1,0:T(8,128)(2,1)S(1)} collective-permute-done((bf16[96,1536]{1,0:T(8,128)(2,1)S(1)}, bf16[96,1536]{1,0:T(8,128)(2,1)S(1)}, u32[]{:S(2)}, u32[]{:S(2)}) %collective-permute-start.10) | collective-permute-done | bytes 294944 | tf_op jit(solution)/shard_map/ppermute | solution.py:433
  49.5 2.2 %collective-permute-start.13 = (bf16[24,1536]{1,0:T(8,128)(2,1)S(1)}, bf16[24,1536]{1,0:T(8,128)(2,1)S(1)}, u32[]{:S(2)}, u32[]{:S(2)}) collective-permute-start(bf16[24,1536]{1,0:T(8,128)(2,1)S(1)} %get-tuple-element.92), channel_id=1, source_target_pairs={{0,32},{8,40},{16,48},{24,56},{32,0},{40,8},{48,16},{56,24},{1,33}... | collective-permute-start | bytes 221192 | tf_op jit(solution)/shard_map/ppermute | solution.py:433
  51.7 0.3 collective-permute-start.15
  52.0 1.7 %collective-permute-start.14 = (bf16[24,1536]{1,0:T(8,128)(2,1)S(1)}, bf16[24,1536]{1,0:T(8,128)(2,1)S(1)}, u32[]{:S(2)}, u32[]{:S(2)}) collective-permute-start(bf16[24,1536]{1,0:T(8,128)(2,1)S(1)} %get-tuple-element.94), channel_id=1, source_target_pairs={{0,48},{8,56},{16,32},{24,40},{32,16},{40,24},{48,0},{56,8},{1,49}... | collective-permute-start | bytes 221192 | tf_op jit(solution)/shard_map/ppermute | solution.py:433
  53.7 2.0 %collective-permute-start.16 = (bf16[24,1536]{1,0:T(8,128)(2,1)S(1)}, bf16[24,1536]{1,0:T(8,128)(2,1)S(1)}, u32[]{:S(2)}, u32[]{:S(2)}) collective-permute-start(bf16[24,1536]{1,0:T(8,128)(2,1)S(1)} %get-tuple-element.95), channel_id=1, source_target_pairs={{0,128},{64,192},{128,0},{192,64},{1,129},{65,193},{129,1},{193,65... | collective-permute-start | bytes 221192 | tf_op jit(solution)/shard_map/ppermute | solution.py:433
  55.7 1.1 %collective-permute-start.18 = (bf16[24,1536]{1,0:T(8,128)(2,1)S(1)}, bf16[24,1536]{1,0:T(8,128)(2,1)S(1)}, u32[]{:S(2)}, u32[]{:S(2)}) collective-permute-start(bf16[24,1536]{1,0:T(8,128)(2,1)S(1)} %get-tuple-element.96), channel_id=1, source_target_pairs={{0,64},{64,0},{128,192},{192,128},{1,65},{65,1},{129,193},{193,129... | collective-permute-start | bytes 221192 | tf_op jit(solution)/shard_map/ppermute | solution.py:433
  56.8 1.1 %collective-permute-start.17 = (bf16[24,1536]{1,0:T(8,128)(2,1)S(1)}, bf16[24,1536]{1,0:T(8,128)(2,1)S(1)}, u32[]{:S(2)}, u32[]{:S(2)}) collective-permute-start(bf16[24,1536]{1,0:T(8,128)(2,1)S(1)} %get-tuple-element.97), channel_id=1, source_target_pairs={{0,192},{64,128},{128,64},{192,0},{1,193},{65,129},{129,65},{193,1... | collective-permute-start | bytes 221192 | tf_op jit(solution)/shard_map/ppermute | solution.py:433
  58.0 1.7 %collective-permute-done.16 = bf16[24,1536]{1,0:T(8,128)(2,1)S(1)} collective-permute-done((bf16[24,1536]{1,0:T(8,128)(2,1)S(1)}, bf16[24,1536]{1,0:T(8,128)(2,1)S(1)}, u32[]{:S(2)}, u32[]{:S(2)}) %collective-permute-start.16) | collective-permute-done | bytes 73760 | tf_op jit(solution)/shard_map/ppermute | solution.py:433
  59.7 0.4 collective-permute-done.18
  60.0 2.3 %collective-permute-done.17 = bf16[24,1536]{1,0:T(8,128)(2,1)S(1)} collective-permute-done((bf16[24,1536]{1,0:T(8,128)(2,1)S(1)}, bf16[24,1536]{1,0:T(8,128)(2,1)S(1)}, u32[]{:S(2)}, u32[]{:S(2)}) %collective-permute-start.17) | collective-permute-done | bytes 73760 | tf_op jit(solution)/shard_map/ppermute | solution.py:433
  62.6 15.2 %all_to_all.5.parts_ref = bf16[8,3,3072]{2,1,0:T(4,128)(2,1)S(1)} all-to-all(bf16[8,3,3072]{2,1,0:T(4,128)(2,1)S(1)} %reshape.81), channel_id=1, replica_groups=mesh['dp'=4,'gy'=8,'gx'=8] {'gx'}, dimensions={0} | all-to-all | bytes 294912 | tf_op jit(solution)/shard_map/all_to_all | solution.py:479
  77.7 0.6 finish.1
  (50 shorter events, 2.2 us)
Async XLA Ops:
  0.6 1.1 %copy-start.1 = (bf16[1,16,32,768]{3,2,1,0:T(8,128)(2,1)S(1)}, bf16[1,16,32,768]{3,2,1,0:T(8,128)(2,1)}, u32[]{:S(2)}) copy-start(bf16[1,16,32,768]{3,2,1,0:T(8,128)(2,1)} %param.5) | copy-start | bytes 2359300
  1.8 9.6 %copy-start.3 = (bf16[768,768]{1,0:T(8,128)(2,1)S(1)}, bf16[768,768]{1,0:T(8,128)(2,1)}, u32[]{:S(2)}) copy-start(bf16[768,768]{1,0:T(8,128)(2,1)} %wp_ref.1) | copy-start | bytes 3538948
  1.8 9.6 %copy-start.4 = (bf16[1,16,32,768]{3,2,1,0:T(8,128)(2,1)S(1)}, bf16[1,16,32,768]{3,2,1,0:T(8,128)(2,1)}, u32[]{:S(2)}) copy-start(bf16[1,16,32,768]{3,2,1,0:T(8,128)(2,1)} %param.6) | copy-start | bytes 2359300
  1.8 9.6 %copy-start.5 = (s32[1,16,32]{2,1,0:T(8,128)S(1)}, s32[1,16,32]{2,1,0:T(8,128)}, u32[]{:S(2)}) copy-start(s32[1,16,32]{2,1,0:T(8,128)} %param.7) | copy-start | bytes 6148
  1.8 11.1 %collective-permute-start = (bf16[8,24,768]{2,1,0:T(8,128)(2,1)S(1)}, bf16[8,24,768]{2,1,0:T(8,128)(2,1)S(1)}, u32[]{:S(2)}, u32[]{:S(2)}) collective-permute-start(bf16[8,24,768]{2,1,0:T(8,128)(2,1)S(1)} %above.1.after_ref), channel_id=1, source_target_pairs={{0,56},{8,0},{16,8},{24,16},{32,24},{40,32},{48,40},{56,48},{1,57}... | collective-permute-start | bytes 884744 | tf_op jit(solution)/shard_map/ppermute | solution.py:433
  4.3 12.7 %collective-permute-start.2 = (bf16[8,8,768]{2,1,0:T(8,128)(2,1)S(1)}, bf16[8,8,768]{2,1,0:T(8,128)(2,1)S(1)}, u32[]{:S(2)}, u32[]{:S(2)}) collective-permute-start(bf16[8,8,768]{2,1,0:T(8,128)(2,1)S(1)} %corner.1.after_ref), channel_id=1, source_target_pairs={{0,63},{1,56},{2,57},{3,58},{4,59},{5,60},{6,61},{7,62},{8,7},{9,0... | collective-permute-start | bytes 294920 | tf_op jit(solution)/shard_map/ppermute | solution.py:496
  10.3 6.7 %collective-permute-start.1 = (bf16[8,8,768]{2,1,0:T(8,128)(2,1)S(1)}, bf16[8,8,768]{2,1,0:T(8,128)(2,1)S(1)}, u32[]{:S(2)}, u32[]{:S(2)}) collective-permute-start(bf16[8,8,768]{2,1,0:T(8,128)(2,1)S(1)} %left.1), channel_id=1, source_target_pairs={{0,7},{1,0},{2,1},{3,2},{4,3},{5,4},{6,5},{7,6},{8,15},{9,8},{10,9... | collective-permute-start | bytes 294920 | tf_op jit(solution)/shard_map/ppermute | solution.py:433
  11.4 2.0 %copy-start = (bf16[768,2304]{1,0:T(8,128)(2,1)S(1)}, bf16[768,2304]{1,0:T(8,128)(2,1)}, u32[]{:S(2)}) copy-start(bf16[768,2304]{1,0:T(8,128)(2,1)} %wv_ref.3) | copy-start | bytes 10616836
  11.4 2.2 %copy-start.2 = (bf16[1,16,32,768]{3,2,1,0:T(8,128)(2,1)S(1)}, bf16[1,16,32,768]{3,2,1,0:T(8,128)(2,1)}, u32[]{:S(2)}) copy-start(bf16[1,16,32,768]{3,2,1,0:T(8,128)(2,1)} %param.5) | copy-start | bytes 2359300
  21.7 5.1 %collective-permute-start.3 = (bf16[384,1536]{1,0:T(8,128)(2,1)S(1)}, bf16[384,1536]{1,0:T(8,128)(2,1)S(1)}, u32[]{:S(2)}, u32[]{:S(2)}) collective-permute-start(bf16[384,1536]{1,0:T(8,128)(2,1)S(1)} %get-tuple-element.53), channel_id=1, source_target_pairs={{0,8},{8,0},{16,24},{24,16},{32,40},{40,32},{48,56},{56,48},{1,9},... | collective-permute-start | bytes 3538952 | tf_op jit(solution)/shard_map/ppermute | solution.py:433
  26.8 3.1 %collective-permute-start.4 = (bf16[384,1536]{1,0:T(8,128)(2,1)S(1)}, bf16[384,1536]{1,0:T(8,128)(2,1)S(1)}, u32[]{:S(2)}, u32[]{:S(2)}) collective-permute-start(bf16[384,1536]{1,0:T(8,128)(2,1)S(1)} %get-tuple-element.55), channel_id=1, source_target_pairs={{0,8},{8,0},{16,24},{24,16},{32,40},{40,32},{48,56},{56,48},{1,9},... | collective-permute-start | bytes 3538952 | tf_op jit(solution)/shard_map/ppermute | solution.py:433
  27.7 12.3 %collective-permute-start.9 = (bf16[96,768]{1,0:T(8,128)(2,1)S(1)}, bf16[96,768]{1,0:T(8,128)(2,1)S(1)}, u32[]{:S(2)}, u32[]{:S(2)}) collective-permute-start(bf16[96,768]{1,0:T(8,128)(2,1)S(1)} %get-tuple-element.86), channel_id=1, source_target_pairs={{0,64},{64,0},{128,192},{192,128},{1,65},{65,1},{129,193},{193,129... | collective-permute-start | bytes 442376 | tf_op jit(solution)/shard_map/ppermute | solution.py:433
  28.6 12.6 %collective-permute-start.7 = (bf16[96,768]{1,0:T(8,128)(2,1)S(1)}, bf16[96,768]{1,0:T(8,128)(2,1)S(1)}, u32[]{:S(2)}, u32[]{:S(2)}) collective-permute-start(bf16[96,768]{1,0:T(8,128)(2,1)S(1)} %get-tuple-element.87), channel_id=1, source_target_pairs={{0,192},{64,128},{128,64},{192,0},{1,193},{65,129},{129,65},{193,1... | collective-permute-start | bytes 442376 | tf_op jit(solution)/shard_map/ppermute | solution.py:433
  30.2 7.4 %collective-permute-start.6 = (bf16[96,768]{1,0:T(8,128)(2,1)S(1)}, bf16[96,768]{1,0:T(8,128)(2,1)S(1)}, u32[]{:S(2)}, u32[]{:S(2)}) collective-permute-start(bf16[96,768]{1,0:T(8,128)(2,1)S(1)} %get-tuple-element.84), channel_id=1, source_target_pairs={{0,48},{8,56},{16,32},{24,40},{32,16},{40,24},{48,0},{56,8},{1,49}... | collective-permute-start | bytes 442376 | tf_op jit(solution)/shard_map/ppermute | solution.py:433
  31.1 6.6 %collective-permute-start.5 = (bf16[96,768]{1,0:T(8,128)(2,1)S(1)}, bf16[96,768]{1,0:T(8,128)(2,1)S(1)}, u32[]{:S(2)}, u32[]{:S(2)}) collective-permute-start(bf16[96,768]{1,0:T(8,128)(2,1)S(1)} %get-tuple-element.85), channel_id=1, source_target_pairs={{0,16},{8,24},{16,0},{24,8},{32,48},{40,56},{48,32},{56,40},{1,17}... | collective-permute-start | bytes 442376 | tf_op jit(solution)/shard_map/ppermute | solution.py:433
  37.7 9.3 %collective-permute-start.11 = (bf16[96,1536]{1,0:T(8,128)(2,1)S(1)}, bf16[96,1536]{1,0:T(8,128)(2,1)S(1)}, u32[]{:S(2)}, u32[]{:S(2)}) collective-permute-start(bf16[96,1536]{1,0:T(8,128)(2,1)S(1)} %pad_maximum_fusion.2), channel_id=1, source_target_pairs={{0,16},{8,24},{16,0},{24,8},{32,48},{40,56},{48,32},{56,40},{1,17}... | collective-permute-start | bytes 884744 | tf_op jit(solution)/shard_map/ppermute | solution.py:433
  37.9 9.8 %collective-permute-start.12 = (bf16[96,1536]{1,0:T(8,128)(2,1)S(1)}, bf16[96,1536]{1,0:T(8,128)(2,1)S(1)}, u32[]{:S(2)}, u32[]{:S(2)}) collective-permute-start(bf16[96,1536]{1,0:T(8,128)(2,1)S(1)} %pad_maximum_fusion.3), channel_id=1, source_target_pairs={{0,48},{8,56},{16,32},{24,40},{32,16},{40,24},{48,0},{56,8},{1,49}... | collective-permute-start | bytes 884744 | tf_op jit(solution)/shard_map/ppermute | solution.py:433
  40.1 9.2 %collective-permute-start.10 = (bf16[96,1536]{1,0:T(8,128)(2,1)S(1)}, bf16[96,1536]{1,0:T(8,128)(2,1)S(1)}, u32[]{:S(2)}, u32[]{:S(2)}) collective-permute-start(bf16[96,1536]{1,0:T(8,128)(2,1)S(1)} %pad_maximum_fusion.1), channel_id=1, source_target_pairs={{0,192},{64,128},{128,64},{192,0},{1,193},{65,129},{129,65},{193,1... | collective-permute-start | bytes 884744 | tf_op jit(solution)/shard_map/ppermute | solution.py:433
  41.3 7.9 %collective-permute-start.8 = (bf16[96,1536]{1,0:T(8,128)(2,1)S(1)}, bf16[96,1536]{1,0:T(8,128)(2,1)S(1)}, u32[]{:S(2)}, u32[]{:S(2)}) collective-permute-start(bf16[96,1536]{1,0:T(8,128)(2,1)S(1)} %pad_maximum_fusion), channel_id=1, source_target_pairs={{0,64},{64,0},{128,192},{192,128},{1,65},{65,1},{129,193},{193,129... | collective-permute-start | bytes 884744 | tf_op jit(solution)/shard_map/ppermute | solution.py:433
  49.5 7.3 %collective-permute-start.13 = (bf16[24,1536]{1,0:T(8,128)(2,1)S(1)}, bf16[24,1536]{1,0:T(8,128)(2,1)S(1)}, u32[]{:S(2)}, u32[]{:S(2)}) collective-permute-start(bf16[24,1536]{1,0:T(8,128)(2,1)S(1)} %get-tuple-element.92), channel_id=1, source_target_pairs={{0,32},{8,40},{16,48},{24,56},{32,0},{40,8},{48,16},{56,24},{1,33}... | collective-permute-start | bytes 221192 | tf_op jit(solution)/shard_map/ppermute | solution.py:433
  51.7 6.2 %collective-permute-start.15 = (bf16[24,1536]{1,0:T(8,128)(2,1)S(1)}, bf16[24,1536]{1,0:T(8,128)(2,1)S(1)}, u32[]{:S(2)}, u32[]{:S(2)}) collective-permute-start(bf16[24,1536]{1,0:T(8,128)(2,1)S(1)} %get-tuple-element.93), channel_id=1, source_target_pairs={{0,16},{8,24},{16,0},{24,8},{32,48},{40,56},{48,32},{56,40},{1,17}... | collective-permute-start | bytes 221192 | tf_op jit(solution)/shard_map/ppermute | solution.py:433
  52.0 5.9 %collective-permute-start.14 = (bf16[24,1536]{1,0:T(8,128)(2,1)S(1)}, bf16[24,1536]{1,0:T(8,128)(2,1)S(1)}, u32[]{:S(2)}, u32[]{:S(2)}) collective-permute-start(bf16[24,1536]{1,0:T(8,128)(2,1)S(1)} %get-tuple-element.94), channel_id=1, source_target_pairs={{0,48},{8,56},{16,32},{24,40},{32,16},{40,24},{48,0},{56,8},{1,49}... | collective-permute-start | bytes 221192 | tf_op jit(solution)/shard_map/ppermute | solution.py:433
  53.7 5.9 %collective-permute-start.16 = (bf16[24,1536]{1,0:T(8,128)(2,1)S(1)}, bf16[24,1536]{1,0:T(8,128)(2,1)S(1)}, u32[]{:S(2)}, u32[]{:S(2)}) collective-permute-start(bf16[24,1536]{1,0:T(8,128)(2,1)S(1)} %get-tuple-element.95), channel_id=1, source_target_pairs={{0,128},{64,192},{128,0},{192,64},{1,129},{65,193},{129,1},{193,65... | collective-permute-start | bytes 221192 | tf_op jit(solution)/shard_map/ppermute | solution.py:433
  55.7 4.4 %collective-permute-start.18 = (bf16[24,1536]{1,0:T(8,128)(2,1)S(1)}, bf16[24,1536]{1,0:T(8,128)(2,1)S(1)}, u32[]{:S(2)}, u32[]{:S(2)}) collective-permute-start(bf16[24,1536]{1,0:T(8,128)(2,1)S(1)} %get-tuple-element.96), channel_id=1, source_target_pairs={{0,64},{64,0},{128,192},{192,128},{1,65},{65,1},{129,193},{193,129... | collective-permute-start | bytes 221192 | tf_op jit(solution)/shard_map/ppermute | solution.py:433
  56.8 5.6 %collective-permute-start.17 = (bf16[24,1536]{1,0:T(8,128)(2,1)S(1)}, bf16[24,1536]{1,0:T(8,128)(2,1)S(1)}, u32[]{:S(2)}, u32[]{:S(2)}) collective-permute-start(bf16[24,1536]{1,0:T(8,128)(2,1)S(1)} %get-tuple-element.97), channel_id=1, source_target_pairs={{0,192},{64,128},{128,64},{192,0},{1,193},{65,129},{129,65},{193,1... | collective-permute-start | bytes 221192 | tf_op jit(solution)/shard_map/ppermute | solution.py:433

commit v13 on v12

--- a/solution.py
+++ b/solution.py
@@ -16,6 +16,7 @@
 GW = D // GROUPS
 HEAD_SCALE = 0.125
 VMEM = 32 * 1024 * 1024
+LATE_VMEM = 60 * 1024 * 1024
 
 
 def nn(a, b):
@@ -343,7 +344,7 @@
     out = pl.pallas_call(
         out_kernel,
         out_shape=jax.ShapeDtypeStruct((WIN, 2, WIN, D), BF),
-        compiler_params=pltpu.CompilerParams(vmem_limit_bytes=VMEM),
+        compiler_params=pltpu.CompilerParams(vmem_limit_bytes=LATE_VMEM),
         cost_estimate=cost(1e3, 1e3),
         name="out_part",
     )(*xws, tis, *atts, att2, w_proj)
@@ -396,7 +397,7 @@
         out_specs=full((WIN, 2, WIN, D)),
         out_shape=jax.ShapeDtypeStruct((WIN, 2, WIN, D), BF),
         scratch_shapes=[pltpu.VMEM((2 * CELLS, D), F32)],
-        compiler_params=pltpu.CompilerParams(vmem_limit_bytes=VMEM),
+        compiler_params=pltpu.CompilerParams(vmem_limit_bytes=LATE_VMEM),
         cost_estimate=cost(1e3, 1e3),
         name="grad_part",
     )(*xws, cot, tis, *dqkvs, dqkv2, w_qkv, w_qkv, w_qkv)
@@ -518,21 +519,22 @@
     low_a, high_a = blocks(first[:, :D]), blocks(first[:, D:])
     came_a = ring_start(low_a, high_a, *along_x)
     second = add(keep1, send(send1, "gy", lambda i: i ^ 1))
-    second, att2 = tie(second, att2)
     low_b, high_b = blocks(second[:, :D]), blocks(second[:, D:])
     came_b = ring_start(low_b, high_b, *along_y)
-    out = out_part((xw0, xw1), tis, (att0, att1), att2, w_proj)
-    came_b, out, xw0, low_a, high_a = tie(came_b, out, xw0, low_a, high_a)
+    came_b, low_a, high_a = tie(came_b, low_a, high_a)
     came_b = ring_pass(low_b, high_b, came_b, *along_y)
     came_a = ring_pass(low_a, high_a, came_a, *along_x)
-    grad = grad_part((xw0, xw1), cot, tis, (dqkv0, dqkv1), dqkv2, w_qkv)
-    came_a, came_b, grad = tie(came_a, came_b, grad)
     rows_a = ring_end(low_a, high_a, came_a)
+    came_a = direct_start(rows_a, *along_y)
     rows_b = ring_end(low_b, high_b, came_b)
-    came_a = direct_start(rows_a, *along_y)
     came_b = direct_start(rows_b, *along_x)
     rows = jnp.concatenate([direct_end(rows_a, came_a), direct_end(rows_b, came_b)], 1)
-    grad_qkv, grad_proj = finish(exchange(rows, ("gx",)))
+    rows, xw0, att2 = tie(rows, xw0, att2)
+    parts = exchange(rows, ("gx",))
+    out = out_part((xw0, xw1), tis, (att0, att1), att2, w_proj)
+    grad = grad_part((xw0, xw1), cot, tis, (dqkv0, dqkv1), dqkv2, w_qkv)
+    out, grad, parts = tie(out, grad, parts)
+    grad_qkv, grad_proj = finish(parts)
     return out, grad, grad_qkv, grad_proj
 
 

time: 78.8 us -> 81.2 us (1.030); the launches traced: 78.4 us -> 79.9 us
  blocking collectives: 15.2 us -> 0 us
  starting transfers between devices: 25.6 us -> 30.7 us
  waiting for transfers between devices: 11.6 us -> 16.5 us
  Pallas kernels: 21.8 us -> 26.1 us
  local copies, waits for them, and re-layouts: 2.07 us -> 4.52 us
    all_to_all x1 -> x0, blocking collectives: 15.2 us -> none  [exchange(): return lax.all_to_all(rows, axis, 0, 0, axis_index_groups=groups)]
    all_to_all x0 -> x1, starting transfers between devices: none -> 5.5 us  [exchange(): return lax.all_to_all(rows, axis, 0, 0, axis_index_groups=groups)]
    ppermute x18, waiting for transfers between devices: 11.6 us -> 16.5 us  [send(): lax.ppermute(value, axis, [(i, move(i) % devices) for i in range(devices)])]
    pallas_call x1, Pallas kernels: 5.11 us -> 7.57 us  [grad_part(): pl.pallas_call(grad_kernel, grid=(GROUPS,), in_specs=[rows, rows, full((W...]
    pallas_call x1, Pallas kernels: 1.68 us -> 3.45 us  [out_part(): pl.pallas_call(out_kernel, out_shape=jax.ShapeDtypeStruct((WIN, 2, WIN, D...]
    unnamed x12 -> x30, local copies, waits for them, and re-layouts: 1.81 us -> 3.58 us
  transfers between devices with their start and end apart: 19 -> 20, of which waited for: 7 -> 6; matrix products, arithmetic and copies ran while one was open for 1% -> 2% of each run, Pallas kernels for 21% -> 26%
where the time goes in v13:
time: 81.2 us; the launch traced here: 79.9 us
  starting transfers between devices  30.7 us (38%)
  Pallas kernels  26.1 us (32%)
  waiting for transfers between devices  16.5 us (20%)
  local copies, waits for them, and re-layouts  4.52 us (6%)
  other arithmetic  1.15 us (1%)
  between operations  0.99 us (1%)
    ppermute x18, starting transfers between devices, send(): lax.ppermute(value, axis, [(i, move(i) % devices) for i in range(devices)])  19.1 us
    ppermute x18, waiting for transfers between devices, send(): lax.ppermute(value, axis, [(i, move(i) % devices) for i in range(devices)])  16.5 us
    pallas_call x1, Pallas kernels, grad_part(): pl.pallas_call(grad_kernel, grid=(GROUPS,), in_specs=[rows, rows, full((W...  7.57 us
    ppermute x1, starting transfers between devices, shards(): lax.ppermute(corner, ('gy', 'gx'), [(a * nx + b, (a - 1) % ny * nx + (b -...  6.04 us
    all_to_all x1, starting transfers between devices, exchange(): return lax.all_to_all(rows, axis, 0, 0, axis_index_groups=groups)  5.5 us
    pallas_call x1, Pallas kernels, last_heads(): pl.pallas_call(last_kernel, grid=(1,), in_specs=[rows, rows, turned, turn...  4.86 us
    pallas_call x1, Pallas kernels, right_window(): pl.pallas_call(right_window_kernel, grid=(1,), in_specs=[full((16, 32, D)...  4.63 us
    unnamed x30, local copies, waits for them, and re-layouts  3.58 us
  transfers between devices with their start and end apart: 20, of which 6 were waited for; matrix products, arithmetic and copies ran while one was open for 2% of the time, Pallas kernels for 26%

profile of v13, /device:TPU:6, one launch (start us, length us, event | category | flops | bytes accessed | tf_op | source)
XLA Modules:
  0.0 79.9 jit_solution(6782053985158514794)
XLA Ops:
  0.6 1.1 %copy-done.1 = bf16[1,16,32,768]{3,2,1,0:T(8,128)(2,1)S(1)} copy-done((bf16[1,16,32,768]{3,2,1,0:T(8,128)(2,1)S(1)}, bf16[1,16,32,768]{3,2,1,0:T(8,128)(2,1)}, u32[]{:S(2)}) %copy-start.1) | copy-done | bytes 786456
  1.8 2.5 %collective-permute-start = (bf16[8,24,768]{2,1,0:T(8,128)(2,1)S(1)}, bf16[8,24,768]{2,1,0:T(8,128)(2,1)S(1)}, u32[]{:S(2)}, u32[]{:S(2)}) collective-permute-start(bf16[8,24,768]{2,1,0:T(8,128)(2,1)S(1)} %above.1.after_ref), channel_id=1, source_target_pairs={{0,56},{8,0},{16,8},{24,16},{32,24},{40,32},{48,40},{56,48},{1,57}... | collective-permute-start | bytes 884744 | tf_op jit(solution)/shard_map/ppermute | solution.py:434
  4.3 6.0 %collective-permute-start.2 = (bf16[8,8,768]{2,1,0:T(8,128)(2,1)S(1)}, bf16[8,8,768]{2,1,0:T(8,128)(2,1)S(1)}, u32[]{:S(2)}, u32[]{:S(2)}) collective-permute-start(bf16[8,8,768]{2,1,0:T(8,128)(2,1)S(1)} %corner.1.after_ref), channel_id=1, source_target_pairs={{0,63},{1,56},{2,57},{3,58},{4,59},{5,60},{6,61},{7,62},{8,7},{9,0... | collective-permute-start | bytes 294920 | tf_op jit(solution)/shard_map/ppermute | solution.py:497
  10.3 1.1 %collective-permute-start.1 = (bf16[8,8,768]{2,1,0:T(8,128)(2,1)S(1)}, bf16[8,8,768]{2,1,0:T(8,128)(2,1)S(1)}, u32[]{:S(2)}, u32[]{:S(2)}) collective-permute-start(bf16[8,8,768]{2,1,0:T(8,128)(2,1)S(1)} %left.1), channel_id=1, source_target_pairs={{0,7},{1,0},{2,1},{3,2},{4,3},{5,4},{6,5},{7,6},{8,15},{9,8},{10,9... | collective-permute-start | bytes 294920 | tf_op jit(solution)/shard_map/ppermute | solution.py:434
  11.5 1.5 %branch.1 = (bf16[2,256,768]{2,1,0:T(8,128)(2,1)S(1)}, bf16[2,256,768]{2,1,0:T(8,128)(2,1)S(1)}, bf16[2,256,128]{2,1,0:T(8,128)(2,1)S(1)}, bf16[2,256,128]{2,1,0:T(8,128)(2,1)S(1)}) custom-call(bf16[16,2,16,768]{3,2,1,0:T(8,128)(2,1)S(1)} %bitcast.29, s32[16,32]{1,0:T(8,128)S(1)} %bitcast.30, bf16[768,768]{1,0:T(8,128)(2,1)S(1)} %copy-done.7), custom_call_target="tpu_custom_call" | custom-call | flops 20000000000 | bytes 4000000 | tf_op jit(solution)/shard_map/branch/pallas_call | solution.py:108
  13.6 3.4 %left_window.1 = (bf16[256,512]{1,0:T(8,128)(2,1)S(1)}, bf16[2,256,768]{2,1,0:T(8,128)(2,1)S(1)}, bf16[256,768]{1,0:T(8,128)(2,1)S(1)}, bf16[256,768]{1,0:T(8,128)(2,1)S(1)}, bf16[768,256]{1,0:T(8,128)(2,1)S(1)}) custom-call(bf16[16,32,768]{2,1,0:T(8,128)(2,1)S(1)} %bitcast.26, bf16[8,24,768]{2,1,0:T(8,128)(2,1)S(1)} %collective-permute-done.below_ref, ...), custom_call_target="tpu_custom_call" | custom-call | flops 3000000000 | bytes 5000000 | tf_op jit(solution)/shard_map/left_window/pallas_call | solution.py:285
  17.1 4.6 %right_window.1 = (bf16[384,1536]{1,0:T(8,128)(2,1)S(1)}, bf16[384,1536]{1,0:T(8,128)(2,1)S(1)}, bf16[256,512]{1,0:T(8,128)(2,1)S(1)}, bf16[2,256,768]{2,1,0:T(8...) custom-call(bf16[16,32,768]{2,1,0:T(8,128)(2,1)S(1)} %bitcast.27, ...), custom_call_target="tpu_custom_call" | custom-call | flops 4000000000 | bytes 6000000 | tf_op jit(solution)/shard_map/right_window/pallas_call | solution.py:301
  21.7 0.7 copy-done.6
  22.5 0.9 %copy-done.9 = bf16[2,256,768]{2,1,0:T(8,128)(2,1)} copy-done((bf16[2,256,768]{2,1,0:T(8,128)(2,1)}, bf16[2,256,768]{2,1,0:T(8,128)(2,1)S(1)}, u32[]{:S(2)}) %copy-start.9) | copy-done | bytes 786456
  23.4 4.9 %last_heads.1 = (bf16[384,1536]{1,0:T(8,128)(2,1)S(1)}, bf16[384,1536]{1,0:T(8,128)(2,1)S(1)}, bf16[2,256,256]{2,1,0:T(8,128)(2,1)S(1)}, bf16[2,256,768]{2,1,0:T(8,128)(2,1)S(1)}) custom-call(bf16[256,768]{1,0:T(8,128)(2,1)S(1)} %get-tuple-element.41.hid0_ref, bf16[256,768]{1,0:T(8,128)(2,1)S(1)} %get-tuple-element.44.hid1_ref, ...), custom_call_target="tpu_custom_call" | custom-call | flops 4000000000 | bytes 6000000 | tf_op jit(solution)/shard_map/last_heads/pallas_call | solution.py:320
  28.3 0.6 collective-permute-start.4
  29.9 0.9 %collective-permute-start.9 = (bf16[96,768]{1,0:T(8,128)(2,1)S(1)}, bf16[96,768]{1,0:T(8,128)(2,1)S(1)}, u32[]{:S(2)}, u32[]{:S(2)}) collective-permute-start(bf16[96,768]{1,0:T(8,128)(2,1)S(1)} %get-tuple-element.75), channel_id=1, source_target_pairs={{0,64},{64,0},{128,192},{192,128},{1,65},{65,1},{129,193},{193,129... | collective-permute-start | bytes 442376 | tf_op jit(solution)/shard_map/ppermute | solution.py:434
  30.8 0.6 collective-permute-done.4
  31.7 0.8 %collective-permute-start.6 = (bf16[96,768]{1,0:T(8,128)(2,1)S(1)}, bf16[96,768]{1,0:T(8,128)(2,1)S(1)}, u32[]{:S(2)}, u32[]{:S(2)}) collective-permute-start(bf16[96,768]{1,0:T(8,128)(2,1)S(1)} %get-tuple-element.78), channel_id=1, source_target_pairs={{0,48},{8,56},{16,32},{24,40},{32,16},{40,24},{48,0},{56,8},{1,49}... | collective-permute-start | bytes 442376 | tf_op jit(solution)/shard_map/ppermute | solution.py:434
  32.6 6.5 %collective-permute-done.6 = bf16[96,768]{1,0:T(8,128)(2,1)S(1)} collective-permute-done((bf16[96,768]{1,0:T(8,128)(2,1)S(1)}, bf16[96,768]{1,0:T(8,128)(2,1)S(1)}, u32[]{:S(2)}, u32[]{:S(2)}) %collective-permute-start.6) | collective-permute-done | bytes 147488 | tf_op jit(solution)/shard_map/ppermute | solution.py:434
  39.2 1.2 %collective-permute-start.10 = (bf16[96,1536]{1,0:T(8,128)(2,1)S(1)}, bf16[96,1536]{1,0:T(8,128)(2,1)S(1)}, u32[]{:S(2)}, u32[]{:S(2)}) collective-permute-start(bf16[96,1536]{1,0:T(8,128)(2,1)S(1)} %pad_maximum_fusion.1), channel_id=1, source_target_pairs={{0,192},{64,128},{128,64},{192,0},{1,193},{65,129},{129,65},{193,1... | collective-permute-start | bytes 884744 | tf_op jit(solution)/shard_map/ppermute | solution.py:434
  40.5 1.2 %collective-permute-start.8 = (bf16[96,1536]{1,0:T(8,128)(2,1)S(1)}, bf16[96,1536]{1,0:T(8,128)(2,1)S(1)}, u32[]{:S(2)}, u32[]{:S(2)}) collective-permute-start(bf16[96,1536]{1,0:T(8,128)(2,1)S(1)} %pad_maximum_fusion), channel_id=1, source_target_pairs={{0,64},{64,0},{128,192},{192,128},{1,65},{65,1},{129,193},{193,129... | collective-permute-start | bytes 884744 | tf_op jit(solution)/shard_map/ppermute | solution.py:434
  41.8 1.8 %collective-permute-start.15 = (bf16[96,1536]{1,0:T(8,128)(2,1)S(1)}, bf16[96,1536]{1,0:T(8,128)(2,1)S(1)}, u32[]{:S(2)}, u32[]{:S(2)}) collective-permute-start(bf16[96,1536]{1,0:T(8,128)(2,1)S(1)} %pad_maximum_fusion.3), channel_id=1, source_target_pairs={{0,48},{8,56},{16,32},{24,40},{32,16},{40,24},{48,0},{56,8},{1,49}... | collective-permute-start | bytes 884744 | tf_op jit(solution)/shard_map/ppermute | solution.py:434
  43.8 5.2 %collective-permute-done.10 = bf16[96,1536]{1,0:T(8,128)(2,1)S(1)} collective-permute-done((bf16[96,1536]{1,0:T(8,128)(2,1)S(1)}, bf16[96,1536]{1,0:T(8,128)(2,1)S(1)}, u32[]{:S(2)}, u32[]{:S(2)}) %collective-permute-start.10) | collective-permute-done | bytes 294944 | tf_op jit(solution)/shard_map/ppermute | solution.py:434
  49.1 1.5 %collective-permute-start.11 = (bf16[24,1536]{1,0:T(8,128)(2,1)S(1)}, bf16[24,1536]{1,0:T(8,128)(2,1)S(1)}, u32[]{:S(2)}, u32[]{:S(2)}) collective-permute-start(bf16[24,1536]{1,0:T(8,128)(2,1)S(1)} %get-tuple-element.86), channel_id=1, source_target_pairs={{0,32},{8,40},{16,48},{24,56},{32,0},{40,8},{48,16},{56,24},{1,33}... | collective-permute-start | bytes 221192 | tf_op jit(solution)/shard_map/ppermute | solution.py:434
  50.7 0.8 %collective-permute-start.13 = (bf16[24,1536]{1,0:T(8,128)(2,1)S(1)}, bf16[24,1536]{1,0:T(8,128)(2,1)S(1)}, u32[]{:S(2)}, u32[]{:S(2)}) collective-permute-start(bf16[24,1536]{1,0:T(8,128)(2,1)S(1)} %get-tuple-element.87), channel_id=1, source_target_pairs={{0,16},{8,24},{16,0},{24,8},{32,48},{40,56},{48,32},{56,40},{1,17}... | collective-permute-start | bytes 221192 | tf_op jit(solution)/shard_map/ppermute | solution.py:434
  51.5 1.8 %collective-permute-start.12 = (bf16[24,1536]{1,0:T(8,128)(2,1)S(1)}, bf16[24,1536]{1,0:T(8,128)(2,1)S(1)}, u32[]{:S(2)}, u32[]{:S(2)}) collective-permute-start(bf16[24,1536]{1,0:T(8,128)(2,1)S(1)} %get-tuple-element.88), channel_id=1, source_target_pairs={{0,48},{8,56},{16,32},{24,40},{32,16},{40,24},{48,0},{56,8},{1,49}... | collective-permute-start | bytes 221192 | tf_op jit(solution)/shard_map/ppermute | solution.py:434
  53.5 1.9 %collective-permute-start.16 = (bf16[24,1536]{1,0:T(8,128)(2,1)S(1)}, bf16[24,1536]{1,0:T(8,128)(2,1)S(1)}, u32[]{:S(2)}, u32[]{:S(2)}) collective-permute-start(bf16[24,1536]{1,0:T(8,128)(2,1)S(1)} %get-tuple-element.89), channel_id=1, source_target_pairs={{0,128},{64,192},{128,0},{192,64},{1,129},{65,193},{129,1},{193,65... | collective-permute-start | bytes 221192 | tf_op jit(solution)/shard_map/ppermute | solution.py:434
  55.4 1.0 %collective-permute-start.18 = (bf16[24,1536]{1,0:T(8,128)(2,1)S(1)}, bf16[24,1536]{1,0:T(8,128)(2,1)S(1)}, u32[]{:S(2)}, u32[]{:S(2)}) collective-permute-start(bf16[24,1536]{1,0:T(8,128)(2,1)S(1)} %get-tuple-element.90), channel_id=1, source_target_pairs={{0,64},{64,0},{128,192},{192,128},{1,65},{65,1},{129,193},{193,129... | collective-permute-start | bytes 221192 | tf_op jit(solution)/shard_map/ppermute | solution.py:434
  56.3 1.3 %collective-permute-start.17 = (bf16[24,1536]{1,0:T(8,128)(2,1)S(1)}, bf16[24,1536]{1,0:T(8,128)(2,1)S(1)}, u32[]{:S(2)}, u32[]{:S(2)}) collective-permute-start(bf16[24,1536]{1,0:T(8,128)(2,1)S(1)} %get-tuple-element.91), channel_id=1, source_target_pairs={{0,192},{64,128},{128,64},{192,0},{1,193},{65,129},{129,65},{193,1... | collective-permute-start | bytes 221192 | tf_op jit(solution)/shard_map/ppermute | solution.py:434
  57.7 1.7 %collective-permute-done.16 = bf16[24,1536]{1,0:T(8,128)(2,1)S(1)} collective-permute-done((bf16[24,1536]{1,0:T(8,128)(2,1)S(1)}, bf16[24,1536]{1,0:T(8,128)(2,1)S(1)}, u32[]{:S(2)}, u32[]{:S(2)}) %collective-permute-start.16) | collective-permute-done | bytes 73760 | tf_op jit(solution)/shard_map/ppermute | solution.py:434
  59.7 2.2 %collective-permute-done.17 = bf16[24,1536]{1,0:T(8,128)(2,1)S(1)} collective-permute-done((bf16[24,1536]{1,0:T(8,128)(2,1)S(1)}, bf16[24,1536]{1,0:T(8,128)(2,1)S(1)}, u32[]{:S(2)}, u32[]{:S(2)}) %collective-permute-start.17) | collective-permute-done | bytes 73760 | tf_op jit(solution)/shard_map/ppermute | solution.py:434
  62.0 0.8 reshape.81
  62.8 5.5 %all-to-all-start = ((bf16[8,3,3072]{2,1,0:T(4,128)(2,1)}), bf16[8,3,3072]{2,1,0:T(4,128)(2,1)S(1)}, u32[]{:S(2)}, u32[]{:S(2)}) async-start(bf16[8,3,3072]{2,1,0:T(4,128)(2,1)} %reshape.81), calls=%async_computation | async-start | bytes 393216 | tf_op jit(solution)/shard_map/all_to_all | solution.py:480
  68.3 3.5 %out_part.1 = bf16[16,2,16,768]{3,2,1,0:T(8,128)(2,1)} custom-call(bf16[256,768]{1,0:T(8,128)(2,1)} %copy-done.5, bf16[256,768]{1,0:T(8,128)(2,1)} %copy-done.6, bf16[2,256,128]{2,1,0:T(8,128)(2,1)} %copy-done.4, bf16[256,512]{1,0:T(8,128)(2,1)} %copy-done.11, bf16[256,512]{1,0:T(8,128)(2,1)} %copy-done.12, bf16[2,256,256]{2,1,0:T(8,128)(2,1)} %copy-done.13, ...), custom_call_target="tpu_custom_call" | custom-call | flops 1000 | bytes 1000 | tf_op jit(solution)/shard_map/out_part/pallas_call | solution.py:344
  71.7 7.6 %grad_part.1 = bf16[16,2,16,768]{3,2,1,0:T(8,128)(2,1)} custom-call(bf16[256,768]{1,0:T(8,128)(2,1)} %copy-done.5, bf16[256,768]{1,0:T(8,128)(2,1)} %copy-done.6, bf16[16,2,16,768]{3,2,1,0:T(8,128)(2,1)} %bitcast.28, bf16[2,256,128]{2,1,0:T(8,128)(2,1)} %copy-done.4, bf16[2,256,768]{2,1,0:T(8,128)(2,1)} %copy-done.3, bf16[2,256,768]{2,1,0:T(8,128)(2,1)} %copy-done.9, ...), custom_call_target="tpu_custom_call" | custom-call | flops 1000 | bytes 1000 | tf_op jit(solution)/shard_map/grad_part/pallas_call | solution.py:390
  79.3 0.6 finish.1
  (70 shorter events, 3.2 us)
Async XLA Ops:
  0.6 1.1 %copy-start.1 = (bf16[1,16,32,768]{3,2,1,0:T(8,128)(2,1)S(1)}, bf16[1,16,32,768]{3,2,1,0:T(8,128)(2,1)}, u32[]{:S(2)}) copy-start(bf16[1,16,32,768]{3,2,1,0:T(8,128)(2,1)} %param.5) | copy-start | bytes 2359300
  1.8 9.6 %copy-start.7 = (bf16[768,768]{1,0:T(8,128)(2,1)S(1)}, bf16[768,768]{1,0:T(8,128)(2,1)}, u32[]{:S(2)}) copy-start(bf16[768,768]{1,0:T(8,128)(2,1)} %wp_ref.1) | copy-start | bytes 3538948
  1.8 9.6 %copy-start.8 = (bf16[1,16,32,768]{3,2,1,0:T(8,128)(2,1)S(1)}, bf16[1,16,32,768]{3,2,1,0:T(8,128)(2,1)}, u32[]{:S(2)}) copy-start(bf16[1,16,32,768]{3,2,1,0:T(8,128)(2,1)} %param.6) | copy-start | bytes 2359300
  1.8 9.6 %copy-start.14 = (s32[1,16,32]{2,1,0:T(8,128)S(1)}, s32[1,16,32]{2,1,0:T(8,128)}, u32[]{:S(2)}) copy-start(s32[1,16,32]{2,1,0:T(8,128)} %param.7) | copy-start | bytes 6148
  1.8 11.2 %collective-permute-start = (bf16[8,24,768]{2,1,0:T(8,128)(2,1)S(1)}, bf16[8,24,768]{2,1,0:T(8,128)(2,1)S(1)}, u32[]{:S(2)}, u32[]{:S(2)}) collective-permute-start(bf16[8,24,768]{2,1,0:T(8,128)(2,1)S(1)} %above.1.after_ref), channel_id=1, source_target_pairs={{0,56},{8,0},{16,8},{24,16},{32,24},{40,32},{48,40},{56,48},{1,57}... | collective-permute-start | bytes 884744 | tf_op jit(solution)/shard_map/ppermute | solution.py:434
  4.3 12.8 %collective-permute-start.2 = (bf16[8,8,768]{2,1,0:T(8,128)(2,1)S(1)}, bf16[8,8,768]{2,1,0:T(8,128)(2,1)S(1)}, u32[]{:S(2)}, u32[]{:S(2)}) collective-permute-start(bf16[8,8,768]{2,1,0:T(8,128)(2,1)S(1)} %corner.1.after_ref), channel_id=1, source_target_pairs={{0,63},{1,56},{2,57},{3,58},{4,59},{5,60},{6,61},{7,62},{8,7},{9,0... | collective-permute-start | bytes 294920 | tf_op jit(solution)/shard_map/ppermute | solution.py:497
  10.3 6.7 %collective-permute-start.1 = (bf16[8,8,768]{2,1,0:T(8,128)(2,1)S(1)}, bf16[8,8,768]{2,1,0:T(8,128)(2,1)S(1)}, u32[]{:S(2)}, u32[]{:S(2)}) collective-permute-start(bf16[8,8,768]{2,1,0:T(8,128)(2,1)S(1)} %left.1), channel_id=1, source_target_pairs={{0,7},{1,0},{2,1},{3,2},{4,3},{5,4},{6,5},{7,6},{8,15},{9,8},{10,9... | collective-permute-start | bytes 294920 | tf_op jit(solution)/shard_map/ppermute | solution.py:434
  11.4 2.0 %copy-start = (bf16[768,2304]{1,0:T(8,128)(2,1)S(1)}, bf16[768,2304]{1,0:T(8,128)(2,1)}, u32[]{:S(2)}) copy-start(bf16[768,2304]{1,0:T(8,128)(2,1)} %wv_ref.3) | copy-start | bytes 10616836
  11.4 2.2 %copy-start.2 = (bf16[1,16,32,768]{3,2,1,0:T(8,128)(2,1)S(1)}, bf16[1,16,32,768]{3,2,1,0:T(8,128)(2,1)}, u32[]{:S(2)}) copy-start(bf16[1,16,32,768]{3,2,1,0:T(8,128)(2,1)} %param.5) | copy-start | bytes 2359300
  13.0 10.4 %copy-start.4 = (bf16[2,256,128]{2,1,0:T(8,128)(2,1)}, bf16[2,256,128]{2,1,0:T(8,128)(2,1)S(1)}, u32[]{:S(2)}) copy-start(bf16[2,256,128]{2,1,0:T(8,128)(2,1)S(1)} %get-tuple-element.38.tis_ref) | copy-start | bytes 393220
  17.0 4.7 %copy-start.3 = (bf16[2,256,768]{2,1,0:T(8,128)(2,1)}, bf16[2,256,768]{2,1,0:T(8,128)(2,1)S(1)}, u32[]{:S(2)}) copy-start(bf16[2,256,768]{2,1,0:T(8,128)(2,1)S(1)} %get-tuple-element.43.dqkv0_ref) | copy-start | bytes 2359300
  17.0 4.7 %copy-start.5 = (bf16[256,768]{1,0:T(8,128)(2,1)}, bf16[256,768]{1,0:T(8,128)(2,1)S(1)}, u32[]{:S(2)}) copy-start(bf16[256,768]{1,0:T(8,128)(2,1)S(1)} %get-tuple-element.61.xw0_ref) | copy-start | bytes 1179652
  17.0 6.3 %copy-start.11 = (bf16[256,512]{1,0:T(8,128)(2,1)}, bf16[256,512]{1,0:T(8,128)(2,1)S(1)}, u32[]{:S(2)}) copy-start(bf16[256,512]{1,0:T(8,128)(2,1)S(1)} %get-tuple-element.46.att0_ref) | copy-start | bytes 786436
  23.4 4.9 %copy-start.12 = (bf16[256,512]{1,0:T(8,128)(2,1)}, bf16[256,512]{1,0:T(8,128)(2,1)S(1)}, u32[]{:S(2)}) copy-start(bf16[256,512]{1,0:T(8,128)(2,1)S(1)} %get-tuple-element.47.att1_ref) | copy-start | bytes 786436
  23.4 4.9 %collective-permute-start.3 = (bf16[384,1536]{1,0:T(8,128)(2,1)S(1)}, bf16[384,1536]{1,0:T(8,128)(2,1)S(1)}, u32[]{:S(2)}, u32[]{:S(2)}) collective-permute-start(bf16[384,1536]{1,0:T(8,128)(2,1)S(1)} %get-tuple-element.50), channel_id=1, source_target_pairs={{0,8},{8,0},{16,24},{24,16},{32,40},{40,32},{48,56},{56,48},{1,9},... | collective-permute-start | bytes 3538952 | tf_op jit(solution)/shard_map/ppermute | solution.py:434
  28.3 1.0 %copy-start.13 = (bf16[2,256,256]{2,1,0:T(8,128)(2,1)}, bf16[2,256,256]{2,1,0:T(8,128)(2,1)S(1)}, u32[]{:S(2)}) copy-start(bf16[2,256,256]{2,1,0:T(8,128)(2,1)S(1)} %get-tuple-element.63.att2_ref) | copy-start | bytes 786436
  28.3 3.1 %collective-permute-start.4 = (bf16[384,1536]{1,0:T(8,128)(2,1)S(1)}, bf16[384,1536]{1,0:T(8,128)(2,1)S(1)}, u32[]{:S(2)}, u32[]{:S(2)}) collective-permute-start(bf16[384,1536]{1,0:T(8,128)(2,1)S(1)} %get-tuple-element.52), channel_id=1, source_target_pairs={{0,8},{8,0},{16,24},{24,16},{32,40},{40,32},{48,56},{56,48},{1,9},... | collective-permute-start | bytes 3538952 | tf_op jit(solution)/shard_map/ppermute | solution.py:434
  29.3 11.1 %collective-permute-start.7 = (bf16[96,768]{1,0:T(8,128)(2,1)S(1)}, bf16[96,768]{1,0:T(8,128)(2,1)S(1)}, u32[]{:S(2)}, u32[]{:S(2)}) collective-permute-start(bf16[96,768]{1,0:T(8,128)(2,1)S(1)} %get-tuple-element.74), channel_id=1, source_target_pairs={{0,192},{64,128},{128,64},{192,0},{1,193},{65,129},{129,65},{193,1... | collective-permute-start | bytes 442376 | tf_op jit(solution)/shard_map/ppermute | solution.py:434
  29.9 9.3 %collective-permute-start.9 = (bf16[96,768]{1,0:T(8,128)(2,1)S(1)}, bf16[96,768]{1,0:T(8,128)(2,1)S(1)}, u32[]{:S(2)}, u32[]{:S(2)}) collective-permute-start(bf16[96,768]{1,0:T(8,128)(2,1)S(1)} %get-tuple-element.75), channel_id=1, source_target_pairs={{0,64},{64,0},{128,192},{192,128},{1,65},{65,1},{129,193},{193,129... | collective-permute-start | bytes 442376 | tf_op jit(solution)/shard_map/ppermute | solution.py:434
  31.7 7.4 %collective-permute-start.6 = (bf16[96,768]{1,0:T(8,128)(2,1)S(1)}, bf16[96,768]{1,0:T(8,128)(2,1)S(1)}, u32[]{:S(2)}, u32[]{:S(2)}) collective-permute-start(bf16[96,768]{1,0:T(8,128)(2,1)S(1)} %get-tuple-element.78), channel_id=1, source_target_pairs={{0,48},{8,56},{16,32},{24,40},{32,16},{40,24},{48,0},{56,8},{1,49}... | collective-permute-start | bytes 442376 | tf_op jit(solution)/shard_map/ppermute | solution.py:434
  32.5 6.6 %collective-permute-start.5 = (bf16[96,768]{1,0:T(8,128)(2,1)S(1)}, bf16[96,768]{1,0:T(8,128)(2,1)S(1)}, u32[]{:S(2)}, u32[]{:S(2)}) collective-permute-start(bf16[96,768]{1,0:T(8,128)(2,1)S(1)} %get-tuple-element.79), channel_id=1, source_target_pairs={{0,16},{8,24},{16,0},{24,8},{32,48},{40,56},{48,32},{56,40},{1,17}... | collective-permute-start | bytes 442376 | tf_op jit(solution)/shard_map/ppermute | solution.py:434
  39.2 9.8 %collective-permute-start.10 = (bf16[96,1536]{1,0:T(8,128)(2,1)S(1)}, bf16[96,1536]{1,0:T(8,128)(2,1)S(1)}, u32[]{:S(2)}, u32[]{:S(2)}) collective-permute-start(bf16[96,1536]{1,0:T(8,128)(2,1)S(1)} %pad_maximum_fusion.1), channel_id=1, source_target_pairs={{0,192},{64,128},{128,64},{192,0},{1,193},{65,129},{129,65},{193,1... | collective-permute-start | bytes 884744 | tf_op jit(solution)/shard_map/ppermute | solution.py:434
  40.5 8.5 %collective-permute-start.8 = (bf16[96,1536]{1,0:T(8,128)(2,1)S(1)}, bf16[96,1536]{1,0:T(8,128)(2,1)S(1)}, u32[]{:S(2)}, u32[]{:S(2)}) collective-permute-start(bf16[96,1536]{1,0:T(8,128)(2,1)S(1)} %pad_maximum_fusion), channel_id=1, source_target_pairs={{0,64},{64,0},{128,192},{192,128},{1,65},{65,1},{129,193},{193,129... | collective-permute-start | bytes 884744 | tf_op jit(solution)/shard_map/ppermute | solution.py:434
  41.8 11.5 %collective-permute-start.15 = (bf16[96,1536]{1,0:T(8,128)(2,1)S(1)}, bf16[96,1536]{1,0:T(8,128)(2,1)S(1)}, u32[]{:S(2)}, u32[]{:S(2)}) collective-permute-start(bf16[96,1536]{1,0:T(8,128)(2,1)S(1)} %pad_maximum_fusion.3), channel_id=1, source_target_pairs={{0,48},{8,56},{16,32},{24,40},{32,16},{40,24},{48,0},{56,8},{1,49}... | collective-permute-start | bytes 884744 | tf_op jit(solution)/shard_map/ppermute | solution.py:434
  43.7 9.6 %collective-permute-start.14 = (bf16[96,1536]{1,0:T(8,128)(2,1)S(1)}, bf16[96,1536]{1,0:T(8,128)(2,1)S(1)}, u32[]{:S(2)}, u32[]{:S(2)}) collective-permute-start(bf16[96,1536]{1,0:T(8,128)(2,1)S(1)} %pad_maximum_fusion.2), channel_id=1, source_target_pairs={{0,16},{8,24},{16,0},{24,8},{32,48},{40,56},{48,32},{56,40},{1,17}... | collective-permute-start | bytes 884744 | tf_op jit(solution)/shard_map/ppermute | solution.py:434
  49.1 7.2 %collective-permute-start.11 = (bf16[24,1536]{1,0:T(8,128)(2,1)S(1)}, bf16[24,1536]{1,0:T(8,128)(2,1)S(1)}, u32[]{:S(2)}, u32[]{:S(2)}) collective-permute-start(bf16[24,1536]{1,0:T(8,128)(2,1)S(1)} %get-tuple-element.86), channel_id=1, source_target_pairs={{0,32},{8,40},{16,48},{24,56},{32,0},{40,8},{48,16},{56,24},{1,33}... | collective-permute-start | bytes 221192 | tf_op jit(solution)/shard_map/ppermute | solution.py:434
  50.7 7.0 %collective-permute-start.13 = (bf16[24,1536]{1,0:T(8,128)(2,1)S(1)}, bf16[24,1536]{1,0:T(8,128)(2,1)S(1)}, u32[]{:S(2)}, u32[]{:S(2)}) collective-permute-start(bf16[24,1536]{1,0:T(8,128)(2,1)S(1)} %get-tuple-element.87), channel_id=1, source_target_pairs={{0,16},{8,24},{16,0},{24,8},{32,48},{40,56},{48,32},{56,40},{1,17}... | collective-permute-start | bytes 221192 | tf_op jit(solution)/shard_map/ppermute | solution.py:434
  51.5 6.2 %collective-permute-start.12 = (bf16[24,1536]{1,0:T(8,128)(2,1)S(1)}, bf16[24,1536]{1,0:T(8,128)(2,1)S(1)}, u32[]{:S(2)}, u32[]{:S(2)}) collective-permute-start(bf16[24,1536]{1,0:T(8,128)(2,1)S(1)} %get-tuple-element.88), channel_id=1, source_target_pairs={{0,48},{8,56},{16,32},{24,40},{32,16},{40,24},{48,0},{56,8},{1,49}... | collective-permute-start | bytes 221192 | tf_op jit(solution)/shard_map/ppermute | solution.py:434
  53.5 5.9 %collective-permute-start.16 = (bf16[24,1536]{1,0:T(8,128)(2,1)S(1)}, bf16[24,1536]{1,0:T(8,128)(2,1)S(1)}, u32[]{:S(2)}, u32[]{:S(2)}) collective-permute-start(bf16[24,1536]{1,0:T(8,128)(2,1)S(1)} %get-tuple-element.89), channel_id=1, source_target_pairs={{0,128},{64,192},{128,0},{192,64},{1,129},{65,193},{129,1},{193,65... | collective-permute-start | bytes 221192 | tf_op jit(solution)/shard_map/ppermute | solution.py:434
  55.4 4.4 %collective-permute-start.18 = (bf16[24,1536]{1,0:T(8,128)(2,1)S(1)}, bf16[24,1536]{1,0:T(8,128)(2,1)S(1)}, u32[]{:S(2)}, u32[]{:S(2)}) collective-permute-start(bf16[24,1536]{1,0:T(8,128)(2,1)S(1)} %get-tuple-element.90), channel_id=1, source_target_pairs={{0,64},{64,0},{128,192},{192,128},{1,65},{65,1},{129,193},{193,129... | collective-permute-start | bytes 221192 | tf_op jit(solution)/shard_map/ppermute | solution.py:434
  56.3 5.6 %collective-permute-start.17 = (bf16[24,1536]{1,0:T(8,128)(2,1)S(1)}, bf16[24,1536]{1,0:T(8,128)(2,1)S(1)}, u32[]{:S(2)}, u32[]{:S(2)}) collective-permute-start(bf16[24,1536]{1,0:T(8,128)(2,1)S(1)} %get-tuple-element.91), channel_id=1, source_target_pairs={{0,192},{64,128},{128,64},{192,0},{1,193},{65,129},{129,65},{193,1... | collective-permute-start | bytes 221192 | tf_op jit(solution)/shard_map/ppermute | solution.py:434
  62.8 16.5 %all-to-all-start = ((bf16[8,3,3072]{2,1,0:T(4,128)(2,1)}), bf16[8,3,3072]{2,1,0:T(4,128)(2,1)S(1)}, u32[]{:S(2)}, u32[]{:S(2)}) async-start(bf16[8,3,3072]{2,1,0:T(4,128)(2,1)} %reshape.81), calls=%async_computation | async-start | bytes 393216 | tf_op jit(solution)/shard_map/all_to_all | solution.py:480
  (3 other events, 2.5 us)

commit v14 on v12

--- a/solution.py
+++ b/solution.py
@@ -344,7 +344,7 @@
         out_kernel,
         out_shape=jax.ShapeDtypeStruct((WIN, 2, WIN, D), BF),
         compiler_params=pltpu.CompilerParams(vmem_limit_bytes=VMEM),
-        cost_estimate=cost(1e3, 1e3),
+        cost_estimate=cost(3e9, 1e6),
         name="out_part",
     )(*xws, tis, *atts, att2, w_proj)
     return out.reshape(1, WIN, 2 * WIN, D)
@@ -397,7 +397,7 @@
         out_shape=jax.ShapeDtypeStruct((WIN, 2, WIN, D), BF),
         scratch_shapes=[pltpu.VMEM((2 * CELLS, D), F32)],
         compiler_params=pltpu.CompilerParams(vmem_limit_bytes=VMEM),
-        cost_estimate=cost(1e3, 1e3),
+        cost_estimate=cost(6e9, 1e6),
         name="grad_part",
     )(*xws, cot, tis, *dqkvs, dqkv2, w_qkv, w_qkv, w_qkv)
     return grad.reshape(1, WIN, 2 * WIN, D)
@@ -442,22 +442,19 @@
 
 def ring_start(low, high, axis, flips):
     one, three = flips
-    return send(low[3], axis, lambda j: j ^ one), send(high[3], axis, lambda j: j ^ three)
+    return send(low[2:], axis, lambda j: j ^ one), send(high[1::2], axis, lambda j: j ^ three)
 
 
 def ring_pass(low, high, came, axis, flips):
     one, three = flips
-    to_one = jnp.concatenate([low[2], add(high[2], came[1])], 1)
-    to_three = jnp.concatenate([add(low[1], came[0]), high[1]], 1)
-    return send(to_one, axis, lambda j: j ^ one), send(to_three, axis, lambda j: j ^ three)
-
-
-def ring_end(low, high, came):
-    n = low.shape[2]
-    up, down = came
-    low = add(low[0], up[:, :n], down[:, :n])
-    high = add(high[0], up[:, n:], down[:, n:])
-    return jnp.concatenate([low, high], 1)
+    low = add(low[:2], came[0])
+    high = add(high[::2], came[1])
+    came = send(low[1], axis, lambda j: j ^ three), send(high[1], axis, lambda j: j ^ one)
+    return (low[0], high[0]), came
+
+
+def ring_end(kept, came):
+    return jnp.concatenate([add(kept[0], came[0]), add(kept[1], came[1])], 1)
 
 
 def direct_start(rows, axis, flips):
@@ -518,17 +515,16 @@
     low_a, high_a = blocks(first[:, :D]), blocks(first[:, D:])
     came_a = ring_start(low_a, high_a, *along_x)
     second = add(keep1, send(send1, "gy", lambda i: i ^ 1))
-    second, att2 = tie(second, att2)
+    second, att2, dqkv2 = tie(second, att2, dqkv2)
     low_b, high_b = blocks(second[:, :D]), blocks(second[:, D:])
     came_b = ring_start(low_b, high_b, *along_y)
     out = out_part((xw0, xw1), tis, (att0, att1), att2, w_proj)
-    came_b, out, xw0, low_a, high_a = tie(came_b, out, xw0, low_a, high_a)
-    came_b = ring_pass(low_b, high_b, came_b, *along_y)
-    came_a = ring_pass(low_a, high_a, came_a, *along_x)
     grad = grad_part((xw0, xw1), cot, tis, (dqkv0, dqkv1), dqkv2, w_qkv)
-    came_a, came_b, grad = tie(came_a, came_b, grad)
-    rows_a = ring_end(low_a, high_a, came_a)
-    rows_b = ring_end(low_b, high_b, came_b)
+    came_b, out, grad, low_a, high_a = tie(came_b, out, grad, low_a, high_a)
+    kept_b, came_b = ring_pass(low_b, high_b, came_b, *along_y)
+    kept_a, came_a = ring_pass(low_a, high_a, came_a, *along_x)
+    rows_a = ring_end(kept_a, came_a)
+    rows_b = ring_end(kept_b, came_b)
     came_a = direct_start(rows_a, *along_y)
     came_b = direct_start(rows_b, *along_x)
     rows = jnp.concatenate([direct_end(rows_a, came_a), direct_end(rows_b, came_b)], 1)

time: 78.8 us -> 80.7 us (1.024)
  starting transfers between devices: 25.6 us -> 26.5 us
    ppermute x18, starting transfers between devices: 19.6 us -> 20.5 us  [send(): lax.ppermute(value, axis, [(i, move(i) % devices) for i in range(devices)])]
  transfers between devices with their start and end apart: 19 -> 19, of which waited for: 7 -> 7; matrix products, arithmetic and copies ran while one was open for 1% -> 2% of each run, Pallas kernels for 21% -> 21%
where the time goes in v14:
time: 80.7 us; the launch traced here: 79.8 us
  starting transfers between devices  26.5 us (33%)
  Pallas kernels  21.9 us (27%)
  blocking collectives  15 us (19%)
  waiting for transfers between devices  12.2 us (15%)
  local copies, waits for them, and re-layouts  2.18 us (3%)
  other arithmetic  1.12 us (1%)
  between operations  0.94 us (1%)
    ppermute x18, starting transfers between devices, send(): lax.ppermute(value, axis, [(i, move(i) % devices) for i in range(devices)])  20.5 us
    all_to_all x1, blocking collectives, exchange(): return lax.all_to_all(rows, axis, 0, 0, axis_index_groups=groups)  15 us
    ppermute x18, waiting for transfers between devices, send(): lax.ppermute(value, axis, [(i, move(i) % devices) for i in range(devices)])  12.2 us
    ppermute x1, starting transfers between devices, shards(): lax.ppermute(corner, ('gy', 'gx'), [(a * nx + b, (a - 1) % ny * nx + (b -...  6.04 us
    pallas_call x1, Pallas kernels, grad_part(): pl.pallas_call(grad_kernel, grid=(GROUPS,), in_specs=[rows, rows, full((W...  5.12 us
    pallas_call x1, Pallas kernels, last_heads(): pl.pallas_call(last_kernel, grid=(1,), in_specs=[rows, rows, turned, turn...  4.87 us
    pallas_call x1, Pallas kernels, right_window(): pl.pallas_call(right_window_kernel, grid=(1,), in_specs=[full((16, 32, D)...  4.64 us
    pallas_call x1, Pallas kernels, left_window(): pl.pallas_call(left_window_kernel, grid=(1,), in_specs=[full((16, 32, D))...  3.38 us
  transfers between devices with their start and end apart: 19, of which 7 were waited for; matrix products, arithmetic and copies ran while one was open for 2% of the time, Pallas kernels for 21%

profile of v14, /device:TPU:6, one launch (start us, length us, event | category | flops | bytes accessed | tf_op | source)
XLA Modules:
  0.0 79.8 jit_solution(6086883608678408053)
XLA Ops:
  0.6 1.1 %copy-done.1 = bf16[1,16,32,768]{3,2,1,0:T(8,128)(2,1)S(1)} copy-done((bf16[1,16,32,768]{3,2,1,0:T(8,128)(2,1)S(1)}, bf16[1,16,32,768]{3,2,1,0:T(8,128)(2,1)}, u32[]{:S(2)}) %copy-start.1) | copy-done | bytes 786456
  1.8 2.5 %collective-permute-start = (bf16[8,24,768]{2,1,0:T(8,128)(2,1)S(1)}, bf16[8,24,768]{2,1,0:T(8,128)(2,1)S(1)}, u32[]{:S(2)}, u32[]{:S(2)}) collective-permute-start(bf16[8,24,768]{2,1,0:T(8,128)(2,1)S(1)} %above.1.after_ref), channel_id=1, source_target_pairs={{0,56},{8,0},{16,8},{24,16},{32,24},{40,32},{48,40},{56,48},{1,57}... | collective-permute-start | bytes 884744 | tf_op jit(solution)/shard_map/ppermute | solution.py:433
  4.3 6.0 %collective-permute-start.2 = (bf16[8,8,768]{2,1,0:T(8,128)(2,1)S(1)}, bf16[8,8,768]{2,1,0:T(8,128)(2,1)S(1)}, u32[]{:S(2)}, u32[]{:S(2)}) collective-permute-start(bf16[8,8,768]{2,1,0:T(8,128)(2,1)S(1)} %corner.1.after_ref), channel_id=1, source_target_pairs={{0,63},{1,56},{2,57},{3,58},{4,59},{5,60},{6,61},{7,62},{8,7},{9,0... | collective-permute-start | bytes 294920 | tf_op jit(solution)/shard_map/ppermute | solution.py:493
  10.3 1.1 %collective-permute-start.1 = (bf16[8,8,768]{2,1,0:T(8,128)(2,1)S(1)}, bf16[8,8,768]{2,1,0:T(8,128)(2,1)S(1)}, u32[]{:S(2)}, u32[]{:S(2)}) collective-permute-start(bf16[8,8,768]{2,1,0:T(8,128)(2,1)S(1)} %left.1), channel_id=1, source_target_pairs={{0,7},{1,0},{2,1},{3,2},{4,3},{5,4},{6,5},{7,6},{8,15},{9,8},{10,9... | collective-permute-start | bytes 294920 | tf_op jit(solution)/shard_map/ppermute | solution.py:433
  11.5 1.5 %branch.1 = (bf16[2,256,768]{2,1,0:T(8,128)(2,1)S(1)}, bf16[2,256,768]{2,1,0:T(8,128)(2,1)S(1)}, bf16[2,256,128]{2,1,0:T(8,128)(2,1)S(1)}, bf16[2,256,128]{2,1,0:T(8,128)(2,1)S(1)}) custom-call(bf16[16,2,16,768]{3,2,1,0:T(8,128)(2,1)S(1)} %bitcast.45, s32[16,32]{1,0:T(8,128)S(1)} %bitcast.47, bf16[768,768]{1,0:T(8,128)(2,1)S(1)} %copy-done.3), custom_call_target="tpu_custom_call" | custom-call | flops 20000000000 | bytes 4000000 | tf_op jit(solution)/shard_map/branch/pallas_call | solution.py:107
  13.0 0.5 copy-done
  13.6 3.4 %left_window.1 = (bf16[256,512]{1,0:T(8,128)(2,1)S(1)}, bf16[2,256,768]{2,1,0:T(8,128)(2,1)S(1)}, bf16[256,768]{1,0:T(8,128)(2,1)S(1)}, bf16[256,768]{1,0:T(8,128)(2,1)S(1)}, bf16[768,256]{1,0:T(8,128)(2,1)S(1)}) custom-call(bf16[16,32,768]{2,1,0:T(8,128)(2,1)S(1)} %bitcast.43, bf16[8,24,768]{2,1,0:T(8,128)(2,1)S(1)} %collective-permute-done.below_ref, ...), custom_call_target="tpu_custom_call" | custom-call | flops 3000000000 | bytes 5000000 | tf_op jit(solution)/shard_map/left_window/pallas_call | solution.py:284
  17.0 4.6 %right_window.1 = (bf16[384,1536]{1,0:T(8,128)(2,1)S(1)}, bf16[384,1536]{1,0:T(8,128)(2,1)S(1)}, bf16[256,512]{1,0:T(8,128)(2,1)S(1)}, bf16[2,256,768]{2,1,0:T(8...) custom-call(bf16[16,32,768]{2,1,0:T(8,128)(2,1)S(1)} %bitcast.44, ...), custom_call_target="tpu_custom_call" | custom-call | flops 4000000000 | bytes 6000000 | tf_op jit(solution)/shard_map/right_window/pallas_call | solution.py:300
  21.7 0.3 collective-permute-start.3
  22.0 4.9 %last_heads.1 = (bf16[384,1536]{1,0:T(8,128)(2,1)S(1)}, bf16[384,1536]{1,0:T(8,128)(2,1)S(1)}, bf16[2,256,256]{2,1,0:T(8,128)(2,1)S(1)}, bf16[2,256,768]{2,1,0:T(8,128)(2,1)S(1)}) custom-call(bf16[256,768]{1,0:T(8,128)(2,1)S(1)} %get-tuple-element.40.hid0_ref, bf16[256,768]{1,0:T(8,128)(2,1)S(1)} %get-tuple-element.43.hid1_ref, ...), custom_call_target="tpu_custom_call" | custom-call | flops 4000000000 | bytes 6000000 | tf_op jit(solution)/shard_map/last_heads/pallas_call | solution.py:319
  26.8 0.6 collective-permute-start.4
  27.8 0.6 collective-permute-start.9
  28.4 0.9 %collective-permute-start.7 = (bf16[2,96,768]{2,1,0:T(8,128)(2,1)S(1)}, bf16[2,96,768]{2,1,0:T(8,128)(2,1)S(1)}, u32[]{:S(2)}, u32[]{:S(2)}) collective-permute-start(bf16[2,96,768]{2,1,0:T(8,128)(2,1)S(1)} %bitcast.54), channel_id=1, source_target_pairs={{0,64},{64,0},{128,192},{192,128},{1,65},{65,1},{129,193},{193,129... | collective-permute-start | bytes 884744 | tf_op jit(solution)/shard_map/ppermute | solution.py:433
  29.3 0.6 collective-permute-done.4
  30.3 0.8 %collective-permute-start.6 = (bf16[2,96,768]{2,1,0:T(8,128)(2,1)S(1)}, bf16[2,96,768]{2,1,0:T(8,128)(2,1)S(1)}, u32[]{:S(2)}, u32[]{:S(2)}) collective-permute-start(bf16[2,96,768]{2,1,0:T(8,128)(2,1)S(1)} %slice.103), channel_id=1, source_target_pairs={{0,48},{8,56},{16,32},{24,40},{32,16},{40,24},{48,0},{56,8},{1,49}... | collective-permute-start | bytes 884744 | tf_op jit(solution)/shard_map/ppermute | solution.py:433
  31.2 5.1 %grad_part.1 = bf16[16,2,16,768]{3,2,1,0:T(8,128)(2,1)} custom-call(bf16[256,768]{1,0:T(8,128)(2,1)S(1)} %get-tuple-element.55.xw0_ref, bf16[256,768]{1,0:T(8,128)(2,1)S(1)} %get-tuple-element.56.xw1_ref, bf16[16,2,16,768]{3,2,1,0:T(8,128)(2,1)S(1)} %bitcast.46, bf16[2,256,128]{2,1,0:T(8,128)(2,1)S(1)} %get-tuple-element.37.tis_ref, ...), custom_call_target="tpu_custom_call" | custom-call | flops 6000000000 | bytes 1000000 | tf_op jit(solution)/shard_map/grad_part/pallas_call | solution.py:389
  36.3 1.7 %out_part.1 = bf16[16,2,16,768]{3,2,1,0:T(8,128)(2,1)} custom-call(bf16[256,768]{1,0:T(8,128)(2,1)S(1)} %get-tuple-element.55.xw0_ref, bf16[256,768]{1,0:T(8,128)(2,1)S(1)} %get-tuple-element.56.xw1_ref, bf16[2,256,128]{2,1,0:T(8,128)(2,1)S(1)} %get-tuple-element.37.tis_ref, bf16[256,512]{1,0:T(8,128)(2,1)S(1)} %get-tuple-element.45.att0_ref, ...), custom_call_target="tpu_custom_call" | custom-call | flops 3000000000 | bytes 1000000 | tf_op jit(solution)/shard_map/out_part/pallas_call | solution.py:343
  37.9 2.9 %collective-permute-done.6 = bf16[2,96,768]{2,1,0:T(8,128)(2,1)S(1)} collective-permute-done((bf16[2,96,768]{2,1,0:T(8,128)(2,1)S(1)}, bf16[2,96,768]{2,1,0:T(8,128)(2,1)S(1)}, u32[]{:S(2)}, u32[]{:S(2)}) %collective-permute-start.6) | collective-permute-done | bytes 294944 | tf_op jit(solution)/shard_map/ppermute | solution.py:433
  41.2 2.1 %collective-permute-start.14 = (bf16[96,768]{1,0:T(8,128)(2,1)S(1)}, bf16[96,768]{1,0:T(8,128)(2,1)S(1)}, u32[]{:S(2)}, u32[]{:S(2)}) collective-permute-start(bf16[96,768]{1,0:T(8,128)(2,1)S(1)} %slice_bitcast_fusion.2), channel_id=1, source_target_pairs={{0,48},{8,56},{16,32},{24,40},{32,16},{40,24},{48,0},{56,8},{1,49}... | collective-permute-start | bytes 442376 | tf_op jit(solution)/shard_map/ppermute | solution.py:433
  43.4 1.1 %collective-permute-start.10 = (bf16[96,768]{1,0:T(8,128)(2,1)S(1)}, bf16[96,768]{1,0:T(8,128)(2,1)S(1)}, u32[]{:S(2)}, u32[]{:S(2)}) collective-permute-start(bf16[96,768]{1,0:T(8,128)(2,1)S(1)} %slice_bitcast_fusion.4), channel_id=1, source_target_pairs={{0,64},{64,0},{128,192},{192,128},{1,65},{65,1},{129,193},{193,129... | collective-permute-start | bytes 442376 | tf_op jit(solution)/shard_map/ppermute | solution.py:433
  44.6 2.1 %collective-permute-start.8 = (bf16[96,768]{1,0:T(8,128)(2,1)S(1)}, bf16[96,768]{1,0:T(8,128)(2,1)S(1)}, u32[]{:S(2)}, u32[]{:S(2)}) collective-permute-start(bf16[96,768]{1,0:T(8,128)(2,1)S(1)} %slice_bitcast_fusion.6), channel_id=1, source_target_pairs={{0,192},{64,128},{128,64},{192,0},{1,193},{65,129},{129,65},{193,1... | collective-permute-start | bytes 442376 | tf_op jit(solution)/shard_map/ppermute | solution.py:433
  46.7 2.1 %collective-permute-done.10 = bf16[96,768]{1,0:T(8,128)(2,1)S(1)} collective-permute-done((bf16[96,768]{1,0:T(8,128)(2,1)S(1)}, bf16[96,768]{1,0:T(8,128)(2,1)S(1)}, u32[]{:S(2)}, u32[]{:S(2)}) %collective-permute-start.10) | collective-permute-done | bytes 147488 | tf_op jit(solution)/shard_map/ppermute | solution.py:433
  48.9 2.2 %collective-permute-done.8 = bf16[96,768]{1,0:T(8,128)(2,1)S(1)} collective-permute-done((bf16[96,768]{1,0:T(8,128)(2,1)S(1)}, bf16[96,768]{1,0:T(8,128)(2,1)S(1)}, u32[]{:S(2)}, u32[]{:S(2)}) %collective-permute-start.8) | collective-permute-done | bytes 147488 | tf_op jit(solution)/shard_map/ppermute | solution.py:433
  51.1 2.2 %collective-permute-start.11 = (bf16[24,1536]{1,0:T(8,128)(2,1)S(1)}, bf16[24,1536]{1,0:T(8,128)(2,1)S(1)}, u32[]{:S(2)}, u32[]{:S(2)}) collective-permute-start(bf16[24,1536]{1,0:T(8,128)(2,1)S(1)} %get-tuple-element.74), channel_id=1, source_target_pairs={{0,32},{8,40},{16,48},{24,56},{32,0},{40,8},{48,16},{56,24},{1,33}... | collective-permute-start | bytes 221192 | tf_op jit(solution)/shard_map/ppermute | solution.py:433
  53.3 2.0 %collective-permute-start.12 = (bf16[24,1536]{1,0:T(8,128)(2,1)S(1)}, bf16[24,1536]{1,0:T(8,128)(2,1)S(1)}, u32[]{:S(2)}, u32[]{:S(2)}) collective-permute-start(bf16[24,1536]{1,0:T(8,128)(2,1)S(1)} %get-tuple-element.76), channel_id=1, source_target_pairs={{0,48},{8,56},{16,32},{24,40},{32,16},{40,24},{48,0},{56,8},{1,49}... | collective-permute-start | bytes 221192 | tf_op jit(solution)/shard_map/ppermute | solution.py:433
  55.4 0.5 collective-permute-start.16
  56.0 2.4 %collective-permute-start.18 = (bf16[24,1536]{1,0:T(8,128)(2,1)S(1)}, bf16[24,1536]{1,0:T(8,128)(2,1)S(1)}, u32[]{:S(2)}, u32[]{:S(2)}) collective-permute-start(bf16[24,1536]{1,0:T(8,128)(2,1)S(1)} %get-tuple-element.78), channel_id=1, source_target_pairs={{0,64},{64,0},{128,192},{192,128},{1,65},{65,1},{129,193},{193,129... | collective-permute-start | bytes 221192 | tf_op jit(solution)/shard_map/ppermute | solution.py:433
  58.4 1.2 %collective-permute-start.17 = (bf16[24,1536]{1,0:T(8,128)(2,1)S(1)}, bf16[24,1536]{1,0:T(8,128)(2,1)S(1)}, u32[]{:S(2)}, u32[]{:S(2)}) collective-permute-start(bf16[24,1536]{1,0:T(8,128)(2,1)S(1)} %get-tuple-element.79), channel_id=1, source_target_pairs={{0,192},{64,128},{128,64},{192,0},{1,193},{65,129},{129,65},{193,1... | collective-permute-start | bytes 221192 | tf_op jit(solution)/shard_map/ppermute | solution.py:433
  59.7 1.7 %collective-permute-done.16 = bf16[24,1536]{1,0:T(8,128)(2,1)S(1)} collective-permute-done((bf16[24,1536]{1,0:T(8,128)(2,1)S(1)}, bf16[24,1536]{1,0:T(8,128)(2,1)S(1)}, u32[]{:S(2)}, u32[]{:S(2)}) %collective-permute-start.16) | collective-permute-done | bytes 73760 | tf_op jit(solution)/shard_map/ppermute | solution.py:433
  61.5 2.5 %collective-permute-done.17 = bf16[24,1536]{1,0:T(8,128)(2,1)S(1)} collective-permute-done((bf16[24,1536]{1,0:T(8,128)(2,1)S(1)}, bf16[24,1536]{1,0:T(8,128)(2,1)S(1)}, u32[]{:S(2)}, u32[]{:S(2)}) %collective-permute-start.17) | collective-permute-done | bytes 73760 | tf_op jit(solution)/shard_map/ppermute | solution.py:433
  64.1 15.0 %all_to_all.5.parts_ref = bf16[8,3,3072]{2,1,0:T(4,128)(2,1)S(1)} all-to-all(bf16[8,3,3072]{2,1,0:T(4,128)(2,1)S(1)} %reshape.69), channel_id=1, replica_groups=mesh['dp'=4,'gy'=8,'gx'=8] {'gx'}, dimensions={0} | all-to-all | bytes 294912 | tf_op jit(solution)/shard_map/all_to_all | solution.py:476
  79.2 0.6 finish.1
  (55 shorter events, 2.0 us)
Async XLA Ops:
  0.6 1.1 %copy-start.1 = (bf16[1,16,32,768]{3,2,1,0:T(8,128)(2,1)S(1)}, bf16[1,16,32,768]{3,2,1,0:T(8,128)(2,1)}, u32[]{:S(2)}) copy-start(bf16[1,16,32,768]{3,2,1,0:T(8,128)(2,1)} %param.5) | copy-start | bytes 2359300
  1.8 9.6 %copy-start.3 = (bf16[768,768]{1,0:T(8,128)(2,1)S(1)}, bf16[768,768]{1,0:T(8,128)(2,1)}, u32[]{:S(2)}) copy-start(bf16[768,768]{1,0:T(8,128)(2,1)} %wp_ref.1) | copy-start | bytes 3538948
  1.8 9.6 %copy-start.4 = (bf16[1,16,32,768]{3,2,1,0:T(8,128)(2,1)S(1)}, bf16[1,16,32,768]{3,2,1,0:T(8,128)(2,1)}, u32[]{:S(2)}) copy-start(bf16[1,16,32,768]{3,2,1,0:T(8,128)(2,1)} %param.6) | copy-start | bytes 2359300
  1.8 9.6 %copy-start.5 = (s32[1,16,32]{2,1,0:T(8,128)S(1)}, s32[1,16,32]{2,1,0:T(8,128)}, u32[]{:S(2)}) copy-start(s32[1,16,32]{2,1,0:T(8,128)} %param.7) | copy-start | bytes 6148
  1.8 11.1 %collective-permute-start = (bf16[8,24,768]{2,1,0:T(8,128)(2,1)S(1)}, bf16[8,24,768]{2,1,0:T(8,128)(2,1)S(1)}, u32[]{:S(2)}, u32[]{:S(2)}) collective-permute-start(bf16[8,24,768]{2,1,0:T(8,128)(2,1)S(1)} %above.1.after_ref), channel_id=1, source_target_pairs={{0,56},{8,0},{16,8},{24,16},{32,24},{40,32},{48,40},{56,48},{1,57}... | collective-permute-start | bytes 884744 | tf_op jit(solution)/shard_map/ppermute | solution.py:433
  4.3 12.7 %collective-permute-start.2 = (bf16[8,8,768]{2,1,0:T(8,128)(2,1)S(1)}, bf16[8,8,768]{2,1,0:T(8,128)(2,1)S(1)}, u32[]{:S(2)}, u32[]{:S(2)}) collective-permute-start(bf16[8,8,768]{2,1,0:T(8,128)(2,1)S(1)} %corner.1.after_ref), channel_id=1, source_target_pairs={{0,63},{1,56},{2,57},{3,58},{4,59},{5,60},{6,61},{7,62},{8,7},{9,0... | collective-permute-start | bytes 294920 | tf_op jit(solution)/shard_map/ppermute | solution.py:493
  10.3 6.7 %collective-permute-start.1 = (bf16[8,8,768]{2,1,0:T(8,128)(2,1)S(1)}, bf16[8,8,768]{2,1,0:T(8,128)(2,1)S(1)}, u32[]{:S(2)}, u32[]{:S(2)}) collective-permute-start(bf16[8,8,768]{2,1,0:T(8,128)(2,1)S(1)} %left.1), channel_id=1, source_target_pairs={{0,7},{1,0},{2,1},{3,2},{4,3},{5,4},{6,5},{7,6},{8,15},{9,8},{10,9... | collective-permute-start | bytes 294920 | tf_op jit(solution)/shard_map/ppermute | solution.py:433
  11.4 2.0 %copy-start = (bf16[768,2304]{1,0:T(8,128)(2,1)S(1)}, bf16[768,2304]{1,0:T(8,128)(2,1)}, u32[]{:S(2)}) copy-start(bf16[768,2304]{1,0:T(8,128)(2,1)} %wv_ref.3) | copy-start | bytes 10616836
  11.4 2.2 %copy-start.2 = (bf16[1,16,32,768]{3,2,1,0:T(8,128)(2,1)S(1)}, bf16[1,16,32,768]{3,2,1,0:T(8,128)(2,1)}, u32[]{:S(2)}) copy-start(bf16[1,16,32,768]{3,2,1,0:T(8,128)(2,1)} %param.5) | copy-start | bytes 2359300
  21.7 5.2 %collective-permute-start.3 = (bf16[384,1536]{1,0:T(8,128)(2,1)S(1)}, bf16[384,1536]{1,0:T(8,128)(2,1)S(1)}, u32[]{:S(2)}, u32[]{:S(2)}) collective-permute-start(bf16[384,1536]{1,0:T(8,128)(2,1)S(1)} %get-tuple-element.49), channel_id=1, source_target_pairs={{0,8},{8,0},{16,24},{24,16},{32,40},{40,32},{48,56},{56,48},{1,9},... | collective-permute-start | bytes 3538952 | tf_op jit(solution)/shard_map/ppermute | solution.py:433
  26.8 3.1 %collective-permute-start.4 = (bf16[384,1536]{1,0:T(8,128)(2,1)S(1)}, bf16[384,1536]{1,0:T(8,128)(2,1)S(1)}, u32[]{:S(2)}, u32[]{:S(2)}) collective-permute-start(bf16[384,1536]{1,0:T(8,128)(2,1)S(1)} %get-tuple-element.51), channel_id=1, source_target_pairs={{0,8},{8,0},{16,24},{24,16},{32,40},{40,32},{48,56},{56,48},{1,9},... | collective-permute-start | bytes 3538952 | tf_op jit(solution)/shard_map/ppermute | solution.py:433
  27.8 15.4 %collective-permute-start.9 = (bf16[2,96,768]{2,1,0:T(8,128)(2,1)S(1)}, bf16[2,96,768]{2,1,0:T(8,128)(2,1)S(1)}, u32[]{:S(2)}, u32[]{:S(2)}) collective-permute-start(bf16[2,96,768]{2,1,0:T(8,128)(2,1)S(1)} %slice.112), channel_id=1, source_target_pairs={{0,192},{64,128},{128,64},{192,0},{1,193},{65,129},{129,65},{193,1... | collective-permute-start | bytes 884744 | tf_op jit(solution)/shard_map/ppermute | solution.py:433
  28.4 16.1 %collective-permute-start.7 = (bf16[2,96,768]{2,1,0:T(8,128)(2,1)S(1)}, bf16[2,96,768]{2,1,0:T(8,128)(2,1)S(1)}, u32[]{:S(2)}, u32[]{:S(2)}) collective-permute-start(bf16[2,96,768]{2,1,0:T(8,128)(2,1)S(1)} %bitcast.54), channel_id=1, source_target_pairs={{0,64},{64,0},{128,192},{192,128},{1,65},{65,1},{129,193},{193,129... | collective-permute-start | bytes 884744 | tf_op jit(solution)/shard_map/ppermute | solution.py:433
  30.3 10.6 %collective-permute-start.6 = (bf16[2,96,768]{2,1,0:T(8,128)(2,1)S(1)}, bf16[2,96,768]{2,1,0:T(8,128)(2,1)S(1)}, u32[]{:S(2)}, u32[]{:S(2)}) collective-permute-start(bf16[2,96,768]{2,1,0:T(8,128)(2,1)S(1)} %slice.103), channel_id=1, source_target_pairs={{0,48},{8,56},{16,32},{24,40},{32,16},{40,24},{48,0},{56,8},{1,49}... | collective-permute-start | bytes 884744 | tf_op jit(solution)/shard_map/ppermute | solution.py:433
  31.1 9.7 %collective-permute-start.5 = (bf16[2,96,768]{2,1,0:T(8,128)(2,1)S(1)}, bf16[2,96,768]{2,1,0:T(8,128)(2,1)S(1)}, u32[]{:S(2)}, u32[]{:S(2)}) collective-permute-start(bf16[2,96,768]{2,1,0:T(8,128)(2,1)S(1)} %bitcast.55), channel_id=1, source_target_pairs={{0,16},{8,24},{16,0},{24,8},{32,48},{40,56},{48,32},{56,40},{1,17}... | collective-permute-start | bytes 884744 | tf_op jit(solution)/shard_map/ppermute | solution.py:433
  41.0 14.3 %collective-permute-start.15 = (bf16[96,768]{1,0:T(8,128)(2,1)S(1)}, bf16[96,768]{1,0:T(8,128)(2,1)S(1)}, u32[]{:S(2)}, u32[]{:S(2)}) collective-permute-start(bf16[96,768]{1,0:T(8,128)(2,1)S(1)} %slice_bitcast_fusion), channel_id=1, source_target_pairs={{0,16},{8,24},{16,0},{24,8},{32,48},{40,56},{48,32},{56,40},{1,17}... | collective-permute-start | bytes 442376 | tf_op jit(solution)/shard_map/ppermute | solution.py:433
  41.2 14.2 %collective-permute-start.14 = (bf16[96,768]{1,0:T(8,128)(2,1)S(1)}, bf16[96,768]{1,0:T(8,128)(2,1)S(1)}, u32[]{:S(2)}, u32[]{:S(2)}) collective-permute-start(bf16[96,768]{1,0:T(8,128)(2,1)S(1)} %slice_bitcast_fusion.2), channel_id=1, source_target_pairs={{0,48},{8,56},{16,32},{24,40},{32,16},{40,24},{48,0},{56,8},{1,49}... | collective-permute-start | bytes 442376 | tf_op jit(solution)/shard_map/ppermute | solution.py:433
  43.4 5.5 %collective-permute-start.10 = (bf16[96,768]{1,0:T(8,128)(2,1)S(1)}, bf16[96,768]{1,0:T(8,128)(2,1)S(1)}, u32[]{:S(2)}, u32[]{:S(2)}) collective-permute-start(bf16[96,768]{1,0:T(8,128)(2,1)S(1)} %slice_bitcast_fusion.4), channel_id=1, source_target_pairs={{0,64},{64,0},{128,192},{192,128},{1,65},{65,1},{129,193},{193,129... | collective-permute-start | bytes 442376 | tf_op jit(solution)/shard_map/ppermute | solution.py:433
  44.6 6.4 %collective-permute-start.8 = (bf16[96,768]{1,0:T(8,128)(2,1)S(1)}, bf16[96,768]{1,0:T(8,128)(2,1)S(1)}, u32[]{:S(2)}, u32[]{:S(2)}) collective-permute-start(bf16[96,768]{1,0:T(8,128)(2,1)S(1)} %slice_bitcast_fusion.6), channel_id=1, source_target_pairs={{0,192},{64,128},{128,64},{192,0},{1,193},{65,129},{129,65},{193,1... | collective-permute-start | bytes 442376 | tf_op jit(solution)/shard_map/ppermute | solution.py:433
  51.1 7.3 %collective-permute-start.11 = (bf16[24,1536]{1,0:T(8,128)(2,1)S(1)}, bf16[24,1536]{1,0:T(8,128)(2,1)S(1)}, u32[]{:S(2)}, u32[]{:S(2)}) collective-permute-start(bf16[24,1536]{1,0:T(8,128)(2,1)S(1)} %get-tuple-element.74), channel_id=1, source_target_pairs={{0,32},{8,40},{16,48},{24,56},{32,0},{40,8},{48,16},{56,24},{1,33}... | collective-permute-start | bytes 221192 | tf_op jit(solution)/shard_map/ppermute | solution.py:433
  53.3 6.3 %collective-permute-start.13 = (bf16[24,1536]{1,0:T(8,128)(2,1)S(1)}, bf16[24,1536]{1,0:T(8,128)(2,1)S(1)}, u32[]{:S(2)}, u32[]{:S(2)}) collective-permute-start(bf16[24,1536]{1,0:T(8,128)(2,1)S(1)} %get-tuple-element.75), channel_id=1, source_target_pairs={{0,16},{8,24},{16,0},{24,8},{32,48},{40,56},{48,32},{56,40},{1,17}... | collective-permute-start | bytes 221192 | tf_op jit(solution)/shard_map/ppermute | solution.py:433
  53.3 6.3 %collective-permute-start.12 = (bf16[24,1536]{1,0:T(8,128)(2,1)S(1)}, bf16[24,1536]{1,0:T(8,128)(2,1)S(1)}, u32[]{:S(2)}, u32[]{:S(2)}) collective-permute-start(bf16[24,1536]{1,0:T(8,128)(2,1)S(1)} %get-tuple-element.76), channel_id=1, source_target_pairs={{0,48},{8,56},{16,32},{24,40},{32,16},{40,24},{48,0},{56,8},{1,49}... | collective-permute-start | bytes 221192 | tf_op jit(solution)/shard_map/ppermute | solution.py:433
  55.4 5.9 %collective-permute-start.16 = (bf16[24,1536]{1,0:T(8,128)(2,1)S(1)}, bf16[24,1536]{1,0:T(8,128)(2,1)S(1)}, u32[]{:S(2)}, u32[]{:S(2)}) collective-permute-start(bf16[24,1536]{1,0:T(8,128)(2,1)S(1)} %get-tuple-element.77), channel_id=1, source_target_pairs={{0,128},{64,192},{128,0},{192,64},{1,129},{65,193},{129,1},{193,65... | collective-permute-start | bytes 221192 | tf_op jit(solution)/shard_map/ppermute | solution.py:433
  56.0 5.5 %collective-permute-start.18 = (bf16[24,1536]{1,0:T(8,128)(2,1)S(1)}, bf16[24,1536]{1,0:T(8,128)(2,1)S(1)}, u32[]{:S(2)}, u32[]{:S(2)}) collective-permute-start(bf16[24,1536]{1,0:T(8,128)(2,1)S(1)} %get-tuple-element.78), channel_id=1, source_target_pairs={{0,64},{64,0},{128,192},{192,128},{1,65},{65,1},{129,193},{193,129... | collective-permute-start | bytes 221192 | tf_op jit(solution)/shard_map/ppermute | solution.py:433
  58.4 5.6 %collective-permute-start.17 = (bf16[24,1536]{1,0:T(8,128)(2,1)S(1)}, bf16[24,1536]{1,0:T(8,128)(2,1)S(1)}, u32[]{:S(2)}, u32[]{:S(2)}) collective-permute-start(bf16[24,1536]{1,0:T(8,128)(2,1)S(1)} %get-tuple-element.79), channel_id=1, source_target_pairs={{0,192},{64,128},{128,64},{192,0},{1,193},{65,129},{129,65},{193,1... | collective-permute-start | bytes 221192 | tf_op jit(solution)/shard_map/ppermute | solution.py:433

commit v15 on v12

--- a/solution.py
+++ b/solution.py
@@ -408,15 +408,21 @@
     for part in range(1, parts_ref.shape[0]):
         total = total + parts_ref[part].astype(F32)
     total = total * (1.0 / math.sqrt(512))
-    for i in range(3):
-        for g in range(GROUPS):
-            at = g * D + i * GW
-            qkv_ref[:, i * D + g * GW : i * D + (g + 1) * GW] = total[:, at : at + GW]
-    proj_ref[...] = total[:, 3 * D :]
+    wide = (GROUPS + 1) * D // 128
+    for row in range(total.shape[0] // wide):
+        for c in range(wide):
+            line = total[row * wide + c : row * wide + c + 1]
+            g, i, half = c // 6, c % 6 // 2, c % 2
+            if g < GROUPS:
+                at = i * D + g * GW + half * 128
+                qkv_ref[row : row + 1, at : at + 128] = line
+            else:
+                at = (c - 6 * GROUPS) * 128
+                proj_ref[row : row + 1, at : at + 128] = line
 
 
 def finish(parts):
-    rows = parts.shape[1]
+    rows = parts.shape[1] * 128 // ((GROUPS + 1) * D)
     return pl.pallas_call(
         finish_kernel,
         out_shape=[
@@ -532,7 +538,7 @@
     came_a = direct_start(rows_a, *along_y)
     came_b = direct_start(rows_b, *along_x)
     rows = jnp.concatenate([direct_end(rows_a, came_a), direct_end(rows_b, came_b)], 1)
-    grad_qkv, grad_proj = finish(exchange(rows, ("gx",)))
+    grad_qkv, grad_proj = finish(lax.all_to_all(rows.reshape(nx, -1, 128), "gx", 0, 0))
     return out, grad, grad_qkv, grad_proj
 
 

time: 78.8 us -> 78.3 us (level)
  no operation moved by 1% of the time
where the time goes in v15:
time: 78.3 us; the launch traced here: 77.8 us
  starting transfers between devices  25.6 us (33%)
  Pallas kernels  21.8 us (28%)
  blocking collectives  14.6 us (19%)
  waiting for transfers between devices  11.6 us (15%)
  local copies, waits for them, and re-layouts  2.04 us (3%)
  other arithmetic  1.15 us (1%)
  between operations  0.91 us (1%)
    ppermute x18, starting transfers between devices, send(): lax.ppermute(value, axis, [(i, move(i) % devices) for i in range(devices)])  19.6 us
    all_to_all x1, blocking collectives, shards(): lax.all_to_all(rows.reshape(nx, -1, 128), 'gx', 0, 0)  14.6 us
    ppermute x18, waiting for transfers between devices, send(): lax.ppermute(value, axis, [(i, move(i) % devices) for i in range(devices)])  11.6 us
    ppermute x1, starting transfers between devices, shards(): lax.ppermute(corner, ('gy', 'gx'), [(a * nx + b, (a - 1) % ny * nx + (b -...  6.04 us
    pallas_call x1, Pallas kernels, grad_part(): pl.pallas_call(grad_kernel, grid=(GROUPS,), in_specs=[rows, rows, full((W...  5.11 us
    pallas_call x1, Pallas kernels, last_heads(): pl.pallas_call(last_kernel, grid=(1,), in_specs=[rows, rows, turned, turn...  4.86 us
    pallas_call x1, Pallas kernels, right_window(): pl.pallas_call(right_window_kernel, grid=(1,), in_specs=[full((16, 32, D)...  4.63 us
    pallas_call x1, Pallas kernels, left_window(): pl.pallas_call(left_window_kernel, grid=(1,), in_specs=[full((16, 32, D))...  3.38 us
  transfers between devices with their start and end apart: 19, of which 7 were waited for; matrix products, arithmetic and copies ran while one was open for 1% of the time, Pallas kernels for 21%

profile of v15, /device:TPU:6, one launch (start us, length us, event | category | flops | bytes accessed | tf_op | source)
XLA Modules:
  0.0 77.8 jit_solution(13478020089891531838)
XLA Ops:
  0.6 1.1 %copy-done.1 = bf16[1,16,32,768]{3,2,1,0:T(8,128)(2,1)S(1)} copy-done((bf16[1,16,32,768]{3,2,1,0:T(8,128)(2,1)S(1)}, bf16[1,16,32,768]{3,2,1,0:T(8,128)(2,1)}, u32[]{:S(2)}) %copy-start.1) | copy-done | bytes 786456
  1.8 2.5 %collective-permute-start = (bf16[8,24,768]{2,1,0:T(8,128)(2,1)S(1)}, bf16[8,24,768]{2,1,0:T(8,128)(2,1)S(1)}, u32[]{:S(2)}, u32[]{:S(2)}) collective-permute-start(bf16[8,24,768]{2,1,0:T(8,128)(2,1)S(1)} %above.1.after_ref), channel_id=1, source_target_pairs={{0,56},{8,0},{16,8},{24,16},{32,24},{40,32},{48,40},{56,48},{1,57}... | collective-permute-start | bytes 884744 | tf_op jit(solution)/shard_map/ppermute | solution.py:439
  4.3 6.0 %collective-permute-start.2 = (bf16[8,8,768]{2,1,0:T(8,128)(2,1)S(1)}, bf16[8,8,768]{2,1,0:T(8,128)(2,1)S(1)}, u32[]{:S(2)}, u32[]{:S(2)}) collective-permute-start(bf16[8,8,768]{2,1,0:T(8,128)(2,1)S(1)} %corner.1.after_ref), channel_id=1, source_target_pairs={{0,63},{1,56},{2,57},{3,58},{4,59},{5,60},{6,61},{7,62},{8,7},{9,0... | collective-permute-start | bytes 294920 | tf_op jit(solution)/shard_map/ppermute | solution.py:502
  10.3 1.1 %collective-permute-start.1 = (bf16[8,8,768]{2,1,0:T(8,128)(2,1)S(1)}, bf16[8,8,768]{2,1,0:T(8,128)(2,1)S(1)}, u32[]{:S(2)}, u32[]{:S(2)}) collective-permute-start(bf16[8,8,768]{2,1,0:T(8,128)(2,1)S(1)} %left.1), channel_id=1, source_target_pairs={{0,7},{1,0},{2,1},{3,2},{4,3},{5,4},{6,5},{7,6},{8,15},{9,8},{10,9... | collective-permute-start | bytes 294920 | tf_op jit(solution)/shard_map/ppermute | solution.py:439
  11.5 1.5 %branch.1 = (bf16[2,256,768]{2,1,0:T(8,128)(2,1)S(1)}, bf16[2,256,768]{2,1,0:T(8,128)(2,1)S(1)}, bf16[2,256,128]{2,1,0:T(8,128)(2,1)S(1)}, bf16[2,256,128]{2,1,0:T(8,128)(2,1)S(1)}) custom-call(bf16[16,2,16,768]{3,2,1,0:T(8,128)(2,1)S(1)} %bitcast.28, s32[16,32]{1,0:T(8,128)S(1)} %bitcast.30, bf16[768,768]{1,0:T(8,128)(2,1)S(1)} %copy-done.3), custom_call_target="tpu_custom_call" | custom-call | flops 20000000000 | bytes 4000000 | tf_op jit(solution)/shard_map/branch/pallas_call | solution.py:107
  13.0 0.5 copy-done
  13.6 3.4 %left_window.1 = (bf16[256,512]{1,0:T(8,128)(2,1)S(1)}, bf16[2,256,768]{2,1,0:T(8,128)(2,1)S(1)}, bf16[256,768]{1,0:T(8,128)(2,1)S(1)}, bf16[256,768]{1,0:T(8,128)(2,1)S(1)}, bf16[768,256]{1,0:T(8,128)(2,1)S(1)}) custom-call(bf16[16,32,768]{2,1,0:T(8,128)(2,1)S(1)} %bitcast.26, bf16[8,24,768]{2,1,0:T(8,128)(2,1)S(1)} %collective-permute-done.below_ref, ...), custom_call_target="tpu_custom_call" | custom-call | flops 3000000000 | bytes 5000000 | tf_op jit(solution)/shard_map/left_window/pallas_call | solution.py:284
  17.0 4.6 %right_window.1 = (bf16[384,1536]{1,0:T(8,128)(2,1)S(1)}, bf16[384,1536]{1,0:T(8,128)(2,1)S(1)}, bf16[256,512]{1,0:T(8,128)(2,1)S(1)}, bf16[2,256,768]{2,1,0:T(8...) custom-call(bf16[16,32,768]{2,1,0:T(8,128)(2,1)S(1)} %bitcast.27, ...), custom_call_target="tpu_custom_call" | custom-call | flops 4000000000 | bytes 6000000 | tf_op jit(solution)/shard_map/right_window/pallas_call | solution.py:300
  21.9 4.9 %last_heads.1 = (bf16[384,1536]{1,0:T(8,128)(2,1)S(1)}, bf16[384,1536]{1,0:T(8,128)(2,1)S(1)}, bf16[2,256,256]{2,1,0:T(8,128)(2,1)S(1)}, bf16[2,256,768]{2,1,0:T(8,128)(2,1)S(1)}) custom-call(bf16[256,768]{1,0:T(8,128)(2,1)S(1)} %get-tuple-element.44.hid0_ref, bf16[256,768]{1,0:T(8,128)(2,1)S(1)} %get-tuple-element.47.hid1_ref, ...), custom_call_target="tpu_custom_call" | custom-call | flops 4000000000 | bytes 6000000 | tf_op jit(solution)/shard_map/last_heads/pallas_call | solution.py:319
  26.8 0.6 collective-permute-start.4
  27.7 0.9 %collective-permute-start.9 = (bf16[96,768]{1,0:T(8,128)(2,1)S(1)}, bf16[96,768]{1,0:T(8,128)(2,1)S(1)}, u32[]{:S(2)}, u32[]{:S(2)}) collective-permute-start(bf16[96,768]{1,0:T(8,128)(2,1)S(1)} %get-tuple-element.86), channel_id=1, source_target_pairs={{0,64},{64,0},{128,192},{192,128},{1,65},{65,1},{129,193},{193,129... | collective-permute-start | bytes 442376 | tf_op jit(solution)/shard_map/ppermute | solution.py:439
  28.6 1.1 %collective-permute-start.7 = (bf16[96,768]{1,0:T(8,128)(2,1)S(1)}, bf16[96,768]{1,0:T(8,128)(2,1)S(1)}, u32[]{:S(2)}, u32[]{:S(2)}) collective-permute-start(bf16[96,768]{1,0:T(8,128)(2,1)S(1)} %get-tuple-element.87), channel_id=1, source_target_pairs={{0,192},{64,128},{128,64},{192,0},{1,193},{65,129},{129,65},{193,1... | collective-permute-start | bytes 442376 | tf_op jit(solution)/shard_map/ppermute | solution.py:439
  30.2 0.8 %collective-permute-start.6 = (bf16[96,768]{1,0:T(8,128)(2,1)S(1)}, bf16[96,768]{1,0:T(8,128)(2,1)S(1)}, u32[]{:S(2)}, u32[]{:S(2)}) collective-permute-start(bf16[96,768]{1,0:T(8,128)(2,1)S(1)} %get-tuple-element.84), channel_id=1, source_target_pairs={{0,48},{8,56},{16,32},{24,40},{32,16},{40,24},{48,0},{56,8},{1,49}... | collective-permute-start | bytes 442376 | tf_op jit(solution)/shard_map/ppermute | solution.py:439
  31.1 1.7 %out_part.1 = bf16[16,2,16,768]{3,2,1,0:T(8,128)(2,1)} custom-call(bf16[256,768]{1,0:T(8,128)(2,1)S(1)} %get-tuple-element.68.xw0_ref, bf16[256,768]{1,0:T(8,128)(2,1)S(1)} %get-tuple-element.59.xw1_ref, bf16[2,256,128]{2,1,0:T(8,128)(2,1)S(1)} %get-tuple-element.41.tis_ref, bf16[256,512]{1,0:T(8,128)(2,1)S(1)} %get-tuple-element.49.att0_ref, ...), custom_call_target="tpu_custom_call" | custom-call | flops 1000 | bytes 1000 | tf_op jit(solution)/shard_map/out_part/pallas_call | solution.py:343
  32.8 4.8 %collective-permute-done.6 = bf16[96,768]{1,0:T(8,128)(2,1)S(1)} collective-permute-done((bf16[96,768]{1,0:T(8,128)(2,1)S(1)}, bf16[96,768]{1,0:T(8,128)(2,1)S(1)}, u32[]{:S(2)}, u32[]{:S(2)}) %collective-permute-start.6) | collective-permute-done | bytes 147488 | tf_op jit(solution)/shard_map/ppermute | solution.py:439
  37.9 2.1 %collective-permute-start.12 = (bf16[96,1536]{1,0:T(8,128)(2,1)S(1)}, bf16[96,1536]{1,0:T(8,128)(2,1)S(1)}, u32[]{:S(2)}, u32[]{:S(2)}) collective-permute-start(bf16[96,1536]{1,0:T(8,128)(2,1)S(1)} %pad_maximum_fusion.3), channel_id=1, source_target_pairs={{0,48},{8,56},{16,32},{24,40},{32,16},{40,24},{48,0},{56,8},{1,49}... | collective-permute-start | bytes 884744 | tf_op jit(solution)/shard_map/ppermute | solution.py:439
  40.1 1.2 %collective-permute-start.10 = (bf16[96,1536]{1,0:T(8,128)(2,1)S(1)}, bf16[96,1536]{1,0:T(8,128)(2,1)S(1)}, u32[]{:S(2)}, u32[]{:S(2)}) collective-permute-start(bf16[96,1536]{1,0:T(8,128)(2,1)S(1)} %pad_maximum_fusion.1), channel_id=1, source_target_pairs={{0,192},{64,128},{128,64},{192,0},{1,193},{65,129},{129,65},{193,1... | collective-permute-start | bytes 884744 | tf_op jit(solution)/shard_map/ppermute | solution.py:439
  41.3 0.6 collective-permute-start.8
  41.9 5.1 %grad_part.1 = bf16[16,2,16,768]{3,2,1,0:T(8,128)(2,1)} custom-call(bf16[256,768]{1,0:T(8,128)(2,1)S(1)} %get-tuple-element.68.xw0_ref, bf16[256,768]{1,0:T(8,128)(2,1)S(1)} %get-tuple-element.59.xw1_ref, bf16[16,2,16,768]{3,2,1,0:T(8,128)(2,1)S(1)} %bitcast.29, bf16[2,256,128]{2,1,0:T(8,128)(2,1)S(1)} %get-tuple-element.41.tis_ref, ...), custom_call_target="tpu_custom_call" | custom-call | flops 1000 | bytes 1000 | tf_op jit(solution)/shard_map/grad_part/pallas_call | solution.py:389
  47.0 0.6 collective-permute-done.12
  47.6 1.6 %collective-permute-done.10 = bf16[96,1536]{1,0:T(8,128)(2,1)S(1)} collective-permute-done((bf16[96,1536]{1,0:T(8,128)(2,1)S(1)}, bf16[96,1536]{1,0:T(8,128)(2,1)S(1)}, u32[]{:S(2)}, u32[]{:S(2)}) %collective-permute-start.10) | collective-permute-done | bytes 294944 | tf_op jit(solution)/shard_map/ppermute | solution.py:439
  49.5 2.2 %collective-permute-start.13 = (bf16[24,1536]{1,0:T(8,128)(2,1)S(1)}, bf16[24,1536]{1,0:T(8,128)(2,1)S(1)}, u32[]{:S(2)}, u32[]{:S(2)}) collective-permute-start(bf16[24,1536]{1,0:T(8,128)(2,1)S(1)} %get-tuple-element.92), channel_id=1, source_target_pairs={{0,32},{8,40},{16,48},{24,56},{32,0},{40,8},{48,16},{56,24},{1,33}... | collective-permute-start | bytes 221192 | tf_op jit(solution)/shard_map/ppermute | solution.py:439
  51.7 0.3 collective-permute-start.15
  52.0 1.7 %collective-permute-start.14 = (bf16[24,1536]{1,0:T(8,128)(2,1)S(1)}, bf16[24,1536]{1,0:T(8,128)(2,1)S(1)}, u32[]{:S(2)}, u32[]{:S(2)}) collective-permute-start(bf16[24,1536]{1,0:T(8,128)(2,1)S(1)} %get-tuple-element.94), channel_id=1, source_target_pairs={{0,48},{8,56},{16,32},{24,40},{32,16},{40,24},{48,0},{56,8},{1,49}... | collective-permute-start | bytes 221192 | tf_op jit(solution)/shard_map/ppermute | solution.py:439
  53.7 2.0 %collective-permute-start.16 = (bf16[24,1536]{1,0:T(8,128)(2,1)S(1)}, bf16[24,1536]{1,0:T(8,128)(2,1)S(1)}, u32[]{:S(2)}, u32[]{:S(2)}) collective-permute-start(bf16[24,1536]{1,0:T(8,128)(2,1)S(1)} %get-tuple-element.95), channel_id=1, source_target_pairs={{0,128},{64,192},{128,0},{192,64},{1,129},{65,193},{129,1},{193,65... | collective-permute-start | bytes 221192 | tf_op jit(solution)/shard_map/ppermute | solution.py:439
  55.7 1.1 %collective-permute-start.18 = (bf16[24,1536]{1,0:T(8,128)(2,1)S(1)}, bf16[24,1536]{1,0:T(8,128)(2,1)S(1)}, u32[]{:S(2)}, u32[]{:S(2)}) collective-permute-start(bf16[24,1536]{1,0:T(8,128)(2,1)S(1)} %get-tuple-element.96), channel_id=1, source_target_pairs={{0,64},{64,0},{128,192},{192,128},{1,65},{65,1},{129,193},{193,129... | collective-permute-start | bytes 221192 | tf_op jit(solution)/shard_map/ppermute | solution.py:439
  56.8 1.1 %collective-permute-start.17 = (bf16[24,1536]{1,0:T(8,128)(2,1)S(1)}, bf16[24,1536]{1,0:T(8,128)(2,1)S(1)}, u32[]{:S(2)}, u32[]{:S(2)}) collective-permute-start(bf16[24,1536]{1,0:T(8,128)(2,1)S(1)} %get-tuple-element.97), channel_id=1, source_target_pairs={{0,192},{64,128},{128,64},{192,0},{1,193},{65,129},{129,65},{193,1... | collective-permute-start | bytes 221192 | tf_op jit(solution)/shard_map/ppermute | solution.py:439
  58.0 1.7 %collective-permute-done.16 = bf16[24,1536]{1,0:T(8,128)(2,1)S(1)} collective-permute-done((bf16[24,1536]{1,0:T(8,128)(2,1)S(1)}, bf16[24,1536]{1,0:T(8,128)(2,1)S(1)}, u32[]{:S(2)}, u32[]{:S(2)}) %collective-permute-start.16) | collective-permute-done | bytes 73760 | tf_op jit(solution)/shard_map/ppermute | solution.py:439
  59.7 0.4 collective-permute-done.18
  60.0 2.3 %collective-permute-done.17 = bf16[24,1536]{1,0:T(8,128)(2,1)S(1)} collective-permute-done((bf16[24,1536]{1,0:T(8,128)(2,1)S(1)}, bf16[24,1536]{1,0:T(8,128)(2,1)S(1)}, u32[]{:S(2)}, u32[]{:S(2)}) %collective-permute-start.17) | collective-permute-done | bytes 73760 | tf_op jit(solution)/shard_map/ppermute | solution.py:439
  62.5 14.6 %all_to_all.5.parts_ref = bf16[8,72,128]{2,1,0:T(8,128)(2,1)S(1)} all-to-all(bf16[8,72,128]{2,1,0:T(8,128)(2,1)S(1)} %reshape.81), channel_id=1, replica_groups=mesh['dp'=4,'gy'=8,'gx'=8] {'gx'}, dimensions={0} | all-to-all | bytes 294912 | tf_op jit(solution)/shard_map/all_to_all | solution.py:541
  77.2 0.7 finish.1
  (50 shorter events, 2.1 us)
Async XLA Ops:
  0.6 1.1 %copy-start.1 = (bf16[1,16,32,768]{3,2,1,0:T(8,128)(2,1)S(1)}, bf16[1,16,32,768]{3,2,1,0:T(8,128)(2,1)}, u32[]{:S(2)}) copy-start(bf16[1,16,32,768]{3,2,1,0:T(8,128)(2,1)} %param.5) | copy-start | bytes 2359300
  1.8 9.6 %copy-start.3 = (bf16[768,768]{1,0:T(8,128)(2,1)S(1)}, bf16[768,768]{1,0:T(8,128)(2,1)}, u32[]{:S(2)}) copy-start(bf16[768,768]{1,0:T(8,128)(2,1)} %wp_ref.1) | copy-start | bytes 3538948
  1.8 9.6 %copy-start.4 = (bf16[1,16,32,768]{3,2,1,0:T(8,128)(2,1)S(1)}, bf16[1,16,32,768]{3,2,1,0:T(8,128)(2,1)}, u32[]{:S(2)}) copy-start(bf16[1,16,32,768]{3,2,1,0:T(8,128)(2,1)} %param.6) | copy-start | bytes 2359300
  1.8 9.6 %copy-start.5 = (s32[1,16,32]{2,1,0:T(8,128)S(1)}, s32[1,16,32]{2,1,0:T(8,128)}, u32[]{:S(2)}) copy-start(s32[1,16,32]{2,1,0:T(8,128)} %param.7) | copy-start | bytes 6148
  1.8 11.1 %collective-permute-start = (bf16[8,24,768]{2,1,0:T(8,128)(2,1)S(1)}, bf16[8,24,768]{2,1,0:T(8,128)(2,1)S(1)}, u32[]{:S(2)}, u32[]{:S(2)}) collective-permute-start(bf16[8,24,768]{2,1,0:T(8,128)(2,1)S(1)} %above.1.after_ref), channel_id=1, source_target_pairs={{0,56},{8,0},{16,8},{24,16},{32,24},{40,32},{48,40},{56,48},{1,57}... | collective-permute-start | bytes 884744 | tf_op jit(solution)/shard_map/ppermute | solution.py:439
  4.3 12.7 %collective-permute-start.2 = (bf16[8,8,768]{2,1,0:T(8,128)(2,1)S(1)}, bf16[8,8,768]{2,1,0:T(8,128)(2,1)S(1)}, u32[]{:S(2)}, u32[]{:S(2)}) collective-permute-start(bf16[8,8,768]{2,1,0:T(8,128)(2,1)S(1)} %corner.1.after_ref), channel_id=1, source_target_pairs={{0,63},{1,56},{2,57},{3,58},{4,59},{5,60},{6,61},{7,62},{8,7},{9,0... | collective-permute-start | bytes 294920 | tf_op jit(solution)/shard_map/ppermute | solution.py:502
  10.3 6.7 %collective-permute-start.1 = (bf16[8,8,768]{2,1,0:T(8,128)(2,1)S(1)}, bf16[8,8,768]{2,1,0:T(8,128)(2,1)S(1)}, u32[]{:S(2)}, u32[]{:S(2)}) collective-permute-start(bf16[8,8,768]{2,1,0:T(8,128)(2,1)S(1)} %left.1), channel_id=1, source_target_pairs={{0,7},{1,0},{2,1},{3,2},{4,3},{5,4},{6,5},{7,6},{8,15},{9,8},{10,9... | collective-permute-start | bytes 294920 | tf_op jit(solution)/shard_map/ppermute | solution.py:439
  11.4 2.0 %copy-start = (bf16[768,2304]{1,0:T(8,128)(2,1)S(1)}, bf16[768,2304]{1,0:T(8,128)(2,1)}, u32[]{:S(2)}) copy-start(bf16[768,2304]{1,0:T(8,128)(2,1)} %wv_ref.3) | copy-start | bytes 10616836
  11.4 2.2 %copy-start.2 = (bf16[1,16,32,768]{3,2,1,0:T(8,128)(2,1)S(1)}, bf16[1,16,32,768]{3,2,1,0:T(8,128)(2,1)}, u32[]{:S(2)}) copy-start(bf16[1,16,32,768]{3,2,1,0:T(8,128)(2,1)} %param.5) | copy-start | bytes 2359300
  21.7 5.1 %collective-permute-start.3 = (bf16[384,1536]{1,0:T(8,128)(2,1)S(1)}, bf16[384,1536]{1,0:T(8,128)(2,1)S(1)}, u32[]{:S(2)}, u32[]{:S(2)}) collective-permute-start(bf16[384,1536]{1,0:T(8,128)(2,1)S(1)} %get-tuple-element.53), channel_id=1, source_target_pairs={{0,8},{8,0},{16,24},{24,16},{32,40},{40,32},{48,56},{56,48},{1,9},... | collective-permute-start | bytes 3538952 | tf_op jit(solution)/shard_map/ppermute | solution.py:439
  26.8 3.1 %collective-permute-start.4 = (bf16[384,1536]{1,0:T(8,128)(2,1)S(1)}, bf16[384,1536]{1,0:T(8,128)(2,1)S(1)}, u32[]{:S(2)}, u32[]{:S(2)}) collective-permute-start(bf16[384,1536]{1,0:T(8,128)(2,1)S(1)} %get-tuple-element.55), channel_id=1, source_target_pairs={{0,8},{8,0},{16,24},{24,16},{32,40},{40,32},{48,56},{56,48},{1,9},... | collective-permute-start | bytes 3538952 | tf_op jit(solution)/shard_map/ppermute | solution.py:439
  27.7 12.3 %collective-permute-start.9 = (bf16[96,768]{1,0:T(8,128)(2,1)S(1)}, bf16[96,768]{1,0:T(8,128)(2,1)S(1)}, u32[]{:S(2)}, u32[]{:S(2)}) collective-permute-start(bf16[96,768]{1,0:T(8,128)(2,1)S(1)} %get-tuple-element.86), channel_id=1, source_target_pairs={{0,64},{64,0},{128,192},{192,128},{1,65},{65,1},{129,193},{193,129... | collective-permute-start | bytes 442376 | tf_op jit(solution)/shard_map/ppermute | solution.py:439
  28.6 12.6 %collective-permute-start.7 = (bf16[96,768]{1,0:T(8,128)(2,1)S(1)}, bf16[96,768]{1,0:T(8,128)(2,1)S(1)}, u32[]{:S(2)}, u32[]{:S(2)}) collective-permute-start(bf16[96,768]{1,0:T(8,128)(2,1)S(1)} %get-tuple-element.87), channel_id=1, source_target_pairs={{0,192},{64,128},{128,64},{192,0},{1,193},{65,129},{129,65},{193,1... | collective-permute-start | bytes 442376 | tf_op jit(solution)/shard_map/ppermute | solution.py:439
  30.2 7.4 %collective-permute-start.6 = (bf16[96,768]{1,0:T(8,128)(2,1)S(1)}, bf16[96,768]{1,0:T(8,128)(2,1)S(1)}, u32[]{:S(2)}, u32[]{:S(2)}) collective-permute-start(bf16[96,768]{1,0:T(8,128)(2,1)S(1)} %get-tuple-element.84), channel_id=1, source_target_pairs={{0,48},{8,56},{16,32},{24,40},{32,16},{40,24},{48,0},{56,8},{1,49}... | collective-permute-start | bytes 442376 | tf_op jit(solution)/shard_map/ppermute | solution.py:439
  31.1 6.6 %collective-permute-start.5 = (bf16[96,768]{1,0:T(8,128)(2,1)S(1)}, bf16[96,768]{1,0:T(8,128)(2,1)S(1)}, u32[]{:S(2)}, u32[]{:S(2)}) collective-permute-start(bf16[96,768]{1,0:T(8,128)(2,1)S(1)} %get-tuple-element.85), channel_id=1, source_target_pairs={{0,16},{8,24},{16,0},{24,8},{32,48},{40,56},{48,32},{56,40},{1,17}... | collective-permute-start | bytes 442376 | tf_op jit(solution)/shard_map/ppermute | solution.py:439
  37.7 9.3 %collective-permute-start.11 = (bf16[96,1536]{1,0:T(8,128)(2,1)S(1)}, bf16[96,1536]{1,0:T(8,128)(2,1)S(1)}, u32[]{:S(2)}, u32[]{:S(2)}) collective-permute-start(bf16[96,1536]{1,0:T(8,128)(2,1)S(1)} %pad_maximum_fusion.2), channel_id=1, source_target_pairs={{0,16},{8,24},{16,0},{24,8},{32,48},{40,56},{48,32},{56,40},{1,17}... | collective-permute-start | bytes 884744 | tf_op jit(solution)/shard_map/ppermute | solution.py:439
  37.9 9.8 %collective-permute-start.12 = (bf16[96,1536]{1,0:T(8,128)(2,1)S(1)}, bf16[96,1536]{1,0:T(8,128)(2,1)S(1)}, u32[]{:S(2)}, u32[]{:S(2)}) collective-permute-start(bf16[96,1536]{1,0:T(8,128)(2,1)S(1)} %pad_maximum_fusion.3), channel_id=1, source_target_pairs={{0,48},{8,56},{16,32},{24,40},{32,16},{40,24},{48,0},{56,8},{1,49}... | collective-permute-start | bytes 884744 | tf_op jit(solution)/shard_map/ppermute | solution.py:439
  40.1 9.2 %collective-permute-start.10 = (bf16[96,1536]{1,0:T(8,128)(2,1)S(1)}, bf16[96,1536]{1,0:T(8,128)(2,1)S(1)}, u32[]{:S(2)}, u32[]{:S(2)}) collective-permute-start(bf16[96,1536]{1,0:T(8,128)(2,1)S(1)} %pad_maximum_fusion.1), channel_id=1, source_target_pairs={{0,192},{64,128},{128,64},{192,0},{1,193},{65,129},{129,65},{193,1... | collective-permute-start | bytes 884744 | tf_op jit(solution)/shard_map/ppermute | solution.py:439
  41.3 7.9 %collective-permute-start.8 = (bf16[96,1536]{1,0:T(8,128)(2,1)S(1)}, bf16[96,1536]{1,0:T(8,128)(2,1)S(1)}, u32[]{:S(2)}, u32[]{:S(2)}) collective-permute-start(bf16[96,1536]{1,0:T(8,128)(2,1)S(1)} %pad_maximum_fusion), channel_id=1, source_target_pairs={{0,64},{64,0},{128,192},{192,128},{1,65},{65,1},{129,193},{193,129... | collective-permute-start | bytes 884744 | tf_op jit(solution)/shard_map/ppermute | solution.py:439
  49.5 7.3 %collective-permute-start.13 = (bf16[24,1536]{1,0:T(8,128)(2,1)S(1)}, bf16[24,1536]{1,0:T(8,128)(2,1)S(1)}, u32[]{:S(2)}, u32[]{:S(2)}) collective-permute-start(bf16[24,1536]{1,0:T(8,128)(2,1)S(1)} %get-tuple-element.92), channel_id=1, source_target_pairs={{0,32},{8,40},{16,48},{24,56},{32,0},{40,8},{48,16},{56,24},{1,33}... | collective-permute-start | bytes 221192 | tf_op jit(solution)/shard_map/ppermute | solution.py:439
  51.7 6.2 %collective-permute-start.15 = (bf16[24,1536]{1,0:T(8,128)(2,1)S(1)}, bf16[24,1536]{1,0:T(8,128)(2,1)S(1)}, u32[]{:S(2)}, u32[]{:S(2)}) collective-permute-start(bf16[24,1536]{1,0:T(8,128)(2,1)S(1)} %get-tuple-element.93), channel_id=1, source_target_pairs={{0,16},{8,24},{16,0},{24,8},{32,48},{40,56},{48,32},{56,40},{1,17}... | collective-permute-start | bytes 221192 | tf_op jit(solution)/shard_map/ppermute | solution.py:439
  52.0 5.9 %collective-permute-start.14 = (bf16[24,1536]{1,0:T(8,128)(2,1)S(1)}, bf16[24,1536]{1,0:T(8,128)(2,1)S(1)}, u32[]{:S(2)}, u32[]{:S(2)}) collective-permute-start(bf16[24,1536]{1,0:T(8,128)(2,1)S(1)} %get-tuple-element.94), channel_id=1, source_target_pairs={{0,48},{8,56},{16,32},{24,40},{32,16},{40,24},{48,0},{56,8},{1,49}... | collective-permute-start | bytes 221192 | tf_op jit(solution)/shard_map/ppermute | solution.py:439
  53.7 5.9 %collective-permute-start.16 = (bf16[24,1536]{1,0:T(8,128)(2,1)S(1)}, bf16[24,1536]{1,0:T(8,128)(2,1)S(1)}, u32[]{:S(2)}, u32[]{:S(2)}) collective-permute-start(bf16[24,1536]{1,0:T(8,128)(2,1)S(1)} %get-tuple-element.95), channel_id=1, source_target_pairs={{0,128},{64,192},{128,0},{192,64},{1,129},{65,193},{129,1},{193,65... | collective-permute-start | bytes 221192 | tf_op jit(solution)/shard_map/ppermute | solution.py:439
  55.7 4.4 %collective-permute-start.18 = (bf16[24,1536]{1,0:T(8,128)(2,1)S(1)}, bf16[24,1536]{1,0:T(8,128)(2,1)S(1)}, u32[]{:S(2)}, u32[]{:S(2)}) collective-permute-start(bf16[24,1536]{1,0:T(8,128)(2,1)S(1)} %get-tuple-element.96), channel_id=1, source_target_pairs={{0,64},{64,0},{128,192},{192,128},{1,65},{65,1},{129,193},{193,129... | collective-permute-start | bytes 221192 | tf_op jit(solution)/shard_map/ppermute | solution.py:439
  56.8 5.6 %collective-permute-start.17 = (bf16[24,1536]{1,0:T(8,128)(2,1)S(1)}, bf16[24,1536]{1,0:T(8,128)(2,1)S(1)}, u32[]{:S(2)}, u32[]{:S(2)}) collective-permute-start(bf16[24,1536]{1,0:T(8,128)(2,1)S(1)} %get-tuple-element.97), channel_id=1, source_target_pairs={{0,192},{64,128},{128,64},{192,0},{1,193},{65,129},{129,65},{193,1... | collective-permute-start | bytes 221192 | tf_op jit(solution)/shard_map/ppermute | solution.py:439
